TPU v7x, 32 devices: a whole 2x2x4 slice. The times are simulated.
32 devices in a mesh: groups: 2 (over x), blk: 16 (over z, y, core).
Axes of the slice: x: 2, y: 2, z: 4, core: 2. Of those that a mesh axis runs over, the one named last changes fastest.
Arguments:
- tokens: bfloat16 [4096, 2048], P(('groups', 'blk')), parts along dimension 0, may hold values from -6 to 6
- expert_ids: int32 [4096, 4], P(('groups', 'blk')), parts along dimension 0, may hold values from 0 to 7, all different within a row; in each aligned block of 128 rows (0 to 127, 128 to 255, ...) at most 96 rows name the same one
- route_gate: float32 [4096, 4], P(('groups', 'blk')), parts along dimension 0, may hold values from 0.1 to 1
- gate_up: bfloat16 [2, 12288, 2048], P(None, 'blk'), may hold values from -0.125 to 0.125
- down_proj: bfloat16 [12288, 2048], P('blk'), may hold values from -0.15625 to 0.15625
Outputs:
- combined: bfloat16 [4096, 2048], P(('groups', 'blk')), parts along dimension 0
There are 2 independent parts, one for each index of `groups`. A program takes and returns all parts, laid end to end along the dimension named above; an argument that names none is the same for every part. Nothing has to cross between parts.
Inputs may be any that keep to these rules, and one draw needn't show every extreme that they name: `expert_ids`: each row names 4 different experts. Among the 128 rows of one device, no expert is named more than 96 times, and in every draw some expert reaches 96 on some device.
All inputs are finite; a program needn't handle non-finite values.
Results may differ from a plain program's by a relative error of at most 0.0057.
Values may be sent and summed in bfloat16 or wider, within the bound.
No kernel may reach another device: no remote copies, remote signals or barrier semaphores. Data moves between devices by JAX's collectives and lax.ppermute only.
A program may use at most 64 MiB of HBM per device.

v0:
```python
import jax
import jax.numpy as jnp
from jax import lax
from jax.sharding import PartitionSpec as P


def expert_half(slot_block, gate_up, down_proj):
    contract = (((1,), (1,)), ((), ()))
    gating = lax.dot_general(slot_block, gate_up[0], contract, preferred_element_type=jnp.float32)
    lifted = lax.dot_general(slot_block, gate_up[1], contract, preferred_element_type=jnp.float32)
    hidden = (jax.nn.silu(gating) * lifted).astype(jnp.bfloat16)
    return jnp.dot(hidden, down_proj, preferred_element_type=jnp.float32).astype(jnp.bfloat16)


def per_device(tokens, expert_ids, route_gate, gate_up, down_proj):
    tok_count, per_token = expert_ids.shape
    feature_width = tokens.shape[1]
    devices = lax.axis_size("blk")
    experts = devices // 2
    capacity = 3 * tok_count * per_token // devices
    placements = tok_count * per_token
    chosen_ids = expert_ids.reshape(placements)
    onehot = (chosen_ids[:, None] == jnp.arange(experts, dtype=jnp.int32)[None, :]).astype(
        jnp.int32
    )
    ranked = jnp.sum((jnp.cumsum(onehot, axis=0) - 1) * onehot, axis=1)
    slot_index = chosen_ids * capacity + ranked
    token_of = jnp.arange(placements, dtype=jnp.int32) // per_token
    slot_table = jnp.full((experts * capacity,), tok_count, jnp.int32).at[slot_index].set(token_of)
    outgoing = jnp.take(tokens, slot_table, axis=0, mode="fill", fill_value=0)
    outgoing = outgoing.reshape(experts, capacity, feature_width)
    doubled = jnp.repeat(outgoing, 2, axis=0)
    received = lax.all_to_all(doubled, "blk", split_axis=0, concat_axis=0, tiled=True)
    item_count = received.shape[1]
    partial_value = expert_half(received.reshape(-1, feature_width), gate_up, down_proj)
    partial_value = partial_value.reshape(devices, item_count, feature_width)
    returned_rows = lax.all_to_all(partial_value, "blk", split_axis=0, concat_axis=0, tiled=True)
    halves = returned_rows.reshape(experts, 2, capacity, feature_width).astype(jnp.float32)
    results = halves[:, 0] + halves[:, 1]
    flattened = results.reshape(experts * capacity, feature_width)
    picked = jnp.take(flattened, slot_index, axis=0)
    weighted = picked.reshape(tok_count, per_token, feature_width) * route_gate[:, :, None]
    return jnp.sum(weighted, axis=1).astype(jnp.bfloat16)


def solution(mesh):
    placed = (
        P(("groups", "blk"), None),
        P(("groups", "blk"), None),
        P(("groups", "blk"), None),
        P(None, "blk", None),
        P("blk", None),
    )
    return jax.shard_map(
        per_device,
        mesh=mesh,
        in_specs=placed,
        out_specs=P(("groups", "blk"), None),
        check_vma=False,
    )
```

profile of v0, /device:TPU:13, one launch (start us, length us, event | category | flops | bytes accessed | tf_op | source)
XLA Modules:
  0.0 351.1 jit_solution(4430551264600560813)
XLA Ops:
  0.0 0.9 copy.16
  1.0 0.1 reshape.93
  1.2 0.7 broadcast_multiply_fusion
  1.9 1.1 reduce-window.6
  3.0 0.2 slice_reduce_fusion
  3.3 0.1 copy.20
  3.4 0.1 mul.40
  3.6 2.4 scatter_custom_fusion
  6.2 8.2 %gather_fusion = bf16[768,2048]{1,0:T(8,128)(2,1)} fusion(bf16[128,2048]{1,0:T(8,128)(2,1)} %param.5, s32[1024]{0:T(1024)S(1)} %pad_clamp_fusion.1), kind=kCustom, calls=%fused_computation | custom fusion | bytes 6294528 | tf_op jit(solution)/shard_map/jit(_take)/gather | solution.py:30
  14.4 2.2 broadcast_select_fusion
  16.6 0.9 broadcast_in_dim.39
  17.5 143.8 %all_to_all.10 = bf16[16,96,2048]{2,1,0:T(8,128)(2,1)S(1)} all-to-all(bf16[16,96,2048]{2,1,0:T(8,128)(2,1)S(1)} %bitcast.34), channel_id=1, replica_groups=mesh['groups'=2,'blk'=16] {'blk'}, dimensions={0} | all-to-all | bytes 12582912 | tf_op jit(solution)/shard_map/all_to_all | solution.py:33
  161.3 5.3 %fusion.2 = f32[1536,768]{1,0:T(8,128)S(1)} fusion(bf16[1536,2048]{1,0:T(8,128)(2,1)S(1)} %bitcast.37, bf16[2,768,2048]{2,1,0:T(8,128)(2,1)S(1)} %bitcast.43), kind=kOutput, calls=%fused_computation.10 | convolution fusion | flops 4831838208 | bytes 14155776 | tf_op jit(solution)/shard_map/dot_general | solution.py:9
  166.7 5.7 %multiply_convert_fusion = bf16[1536,768]{1,0:T(8,128)(2,1)S(1)} fusion(f32[1536,768]{1,0:T(8,128)S(1)} %fusion.2, bf16[1536,2048]{1,0:T(8,128)(2,1)S(1)} %bitcast.38, bf16[2,768,2048]{2,1,0:T(8,128)(2,1)S(1)} %bitcast.43), kind=kOutput, calls=%fused_computation.7 | convolution fusion | flops 4838916096 | bytes 16515072 | tf_op jit(solution)/shard_map/dot_general | solution.py:10
  172.4 7.1 %convolution_convert_fusion = bf16[1536,2048]{1,0:T(8,128)(2,1)} fusion(bf16[1536,768]{1,0:T(8,128)(2,1)S(1)} %multiply_convert_fusion, bf16[768,2048]{1,0:T(8,128)(2,1)S(1)} %copy-done), kind=kOutput, calls=%fused_computation.3 | convolution fusion | flops 4834983936 | bytes 11796480 | tf_op jit(solution)/shard_map/dot_general | solution.py:12
  179.5 5.6 %all-to-all-start.1 = ((bf16[16,96,2048]{2,1,0:T(8,128)(2,1)}), bf16[16,96,2048]{2,1,0:T(8,128)(2,1)}, u32[]{:S(2)}, u32[]{:S(2)}) async-start(bf16[16,96,2048]{2,1,0:T(8,128)(2,1)} %bitcast.36), calls=%async_computation.1 | async-start | bytes 12582912 | tf_op jit(solution)/shard_map/all_to_all | solution.py:37
  185.3 0.1 copy.19
  185.5 0.1 copy.23
  185.6 136.9 %all-to-all-done.1 = bf16[16,96,2048]{2,1,0:T(8,128)(2,1)} async-done(((bf16[16,96,2048]{2,1,0:T(8,128)(2,1)}), bf16[16,96,2048]{2,1,0:T(8,128)(2,1)}, u32[]{:S(2)}, u32[]{:S(2)}) %all-to-all-start.1) | async-done | bytes 6291488 | tf_op jit(solution)/shard_map/all_to_all | solution.py:37
  322.5 4.2 %convert.1 = f32[8,2,96,2048]{3,2,1,0:T(8,128)S(1)} convert(bf16[8,2,96,2048]{3,2,1,0:T(8,128)(2,1)} %bitcast.11) | non-fusion elementwise | flops 3145728 | bytes 18874368 | tf_op jit(solution)/shard_map/convert_element_type | solution.py:38
  326.8 4.0 %fusion = f32[8,1,96,2048]{3,2,0,1:T(8,128)} fusion(f32[8,2,96,2048]{3,2,1,0:T(8,128)S(1)} %convert.1), kind=kLoop, calls=%fused_computation.5 | loop fusion | flops 1572864 | bytes 18874368 | tf_op jit(solution)/shard_map/add | solution.py:39
  330.8 8.4 %gather_fusion.1 = f32[512,2048]{1,0:T(8,128)} fusion(f32[768,2048]{1,0:T(8,128)} %bitcast.33, s32[1024]{0:T(1024)S(1)} %pad_clamp_fusion), kind=kCustom, calls=%fused_computation.1 | custom fusion | bytes 8390656 | tf_op jit(solution)/shard_map/jit(_take)/gather | solution.py:41
  339.2 5.2 %gather.15 = f32[128,4,2048]{2,1,0:T(4,128)} reshape(f32[512,2048]{1,0:T(8,128)} %gather_fusion.1) | data formatting | bytes 8388608 | tf_op jit(solution)/shard_map/jit(_take)/gather | solution.py:41
  344.3 6.7 %multiply_reduce_fusion = bf16[128,2048]{1,0:T(8,128)(2,1)} fusion(f32[128,4,2048]{2,1,0:T(4,128)} %gather.15, f32[128,4]{1,0:T(8,128)S(1)} %copy.23, pred[128,4]{1,0:T(8,128)(4,1)S(1)} %copy.19), kind=kLoop, calls=%fused_computation.8 | loop fusion | flops 2883584 | bytes 4721152 | tf_op jit(solution)/shard_map/reduce_sum | solution.py:43
  (28 shorter events, 0.6 us)
Async XLA Ops:
  0.0 172.4 %copy-start = (bf16[768,2048]{1,0:T(8,128)(2,1)S(1)}, bf16[768,2048]{1,0:T(8,128)(2,1)}, u32[]{:S(2)}) copy-start(bf16[768,2048]{1,0:T(8,128)(2,1)} %param.9) | copy-start | bytes 9437188
  16.6 144.8 %slice-start = ((s8[6291456]{0:T(1024)(128)(4,1)}), s8[2097152]{0:T(1024)(128)(4,1)S(1)}, s32[]{:S(2)}) async-start(s8[6291456]{0:T(1024)(128)(4,1)} %bitcast.42), calls=%async_computation.2 | async-start | bytes 4194304
  17.5 143.8 %slice-start.1 = ((s8[6291456]{0:T(1024)(128)(4,1)}), s8[4194304]{0:T(1024)(128)(4,1)S(1)}, s32[]{:S(2)}) async-start(s8[6291456]{0:T(1024)(128)(4,1)} %bitcast.42), calls=%async_computation.3 | async-start | bytes 8388608
  179.5 5.8 %copy-start.2 = (s32[128,4]{0,1:T(4,128)S(1)}, s32[128,4]{0,1:T(4,128)}, u32[]{:S(2)}) copy-start(s32[128,4]{0,1:T(4,128)} %param.6) | copy-start | bytes 6148
  179.5 6.0 %copy-start.3 = (f32[128,4]{0,1:T(4,128)S(1)}, f32[128,4]{0,1:T(4,128)}, u32[]{:S(2)}) copy-start(f32[128,4]{0,1:T(4,128)} %param.7) | copy-start | bytes 6148
  179.5 143.0 %all-to-all-start.1 = ((bf16[16,96,2048]{2,1,0:T(8,128)(2,1)}), bf16[16,96,2048]{2,1,0:T(8,128)(2,1)}, u32[]{:S(2)}, u32[]{:S(2)}) async-start(bf16[16,96,2048]{2,1,0:T(8,128)(2,1)} %bitcast.36), calls=%async_computation.1 | async-start | bytes 12582912 | tf_op jit(solution)/shard_map/all_to_all | solution.py:37
  330.8 20.3 %copy-start.1 = (bf16[768,2048]{1,0:T(8,128)(2,1)S(1)}, bf16[768,2048]{1,0:T(8,128)(2,1)}, u32[]{:S(2)}) copy-start(bf16[768,2048]{1,0:T(8,128)(2,1)} %param.9) | copy-start | bytes 9437188
where the time goes:
time: 352 us; the launch traced here: 351 us
  blocking collectives  144 us (41%)
  waiting for transfers between devices  137 us (39%)
  local copies, waits for them, and re-layouts  27.3 us (8%)
  other arithmetic  19.1 us (5%)
  matrix products  18.1 us (5%)
  starting transfers between devices  5.63 us (2%)
    all_to_all x1, blocking collectives, per_device(): lax.all_to_all(doubled, 'blk', split_axis=0, concat_axis=0, tiled=True)  144 us
    all_to_all x1, waiting for transfers between devices, per_device(): lax.all_to_all(partial_value, 'blk', split_axis=0, concat_axis=0, tiled=T...  137 us
    gather x2, local copies, waits for them, and re-layouts, per_device(): picked = jnp.take(flattened, slot_index, axis=0)  13.6 us
    gather x1, local copies, waits for them, and re-layouts, per_device(): outgoing = jnp.take(tokens, slot_table, axis=0, mode='fill', fill_value=0)  8.21 us
    dot_general x1, matrix products, expert_half(): jnp.dot(hidden, down_proj, preferred_element_type=jnp.float32)  7.09 us
  transfers between devices with their start and end apart: 1, of which 1 were waited for; matrix products, arithmetic and copies ran while one was open for 0% of the time, Pallas kernels for 0%

commit v1 on v0

--- a/solution.py
+++ b/solution.py
@@ -12,7 +12,7 @@
     return jnp.dot(hidden, down_proj, preferred_element_type=jnp.float32).astype(jnp.bfloat16)
 
 
-def per_device(tokens, expert_ids, route_gate, gate_up, down_proj):
+def by_slots(tokens, expert_ids, route_gate, gate_up, down_proj):
     tok_count, per_token = expert_ids.shape
     feature_width = tokens.shape[1]
     devices = lax.axis_size("blk")
@@ -43,6 +43,23 @@
     return jnp.sum(weighted, axis=1).astype(jnp.bfloat16)
 
 
+def by_tokens(tokens, expert_ids, route_gate, gate_up, down_proj):
+    devices = lax.axis_size("blk")
+    experts = devices // 2
+    mine = lax.axis_index("blk") // 2
+    chosen = expert_ids[:, :, None] == jnp.arange(experts, dtype=jnp.int32)[None, None, :]
+    weight = jnp.sum(jnp.where(chosen, route_gate[:, :, None], 0.0), axis=1)
+    weights = lax.all_gather(weight.T, "blk", axis=0, tiled=False)
+    weights = lax.dynamic_index_in_dim(weights, mine, 1, keepdims=False).reshape(-1, 1)
+    rows = lax.all_gather(tokens, "blk", axis=0, tiled=True)
+    contract = (((1,), (1,)), ((), ()))
+    gating = lax.dot_general(rows, gate_up[0], contract, preferred_element_type=jnp.float32)
+    lifted = lax.dot_general(rows, gate_up[1], contract, preferred_element_type=jnp.float32)
+    hidden = (jax.nn.silu(gating) * lifted * weights).astype(jnp.bfloat16)
+    partial_value = jnp.dot(hidden, down_proj, preferred_element_type=jnp.float32).astype(jnp.bfloat16)
+    return lax.psum_scatter(partial_value, "blk", scatter_dimension=0, tiled=True)
+
+
 def solution(mesh):
     placed = (
         P(("groups", "blk"), None),
@@ -51,6 +68,12 @@
         P(None, "blk", None),
         P("blk", None),
     )
+
+    def per_device(tokens, expert_ids, route_gate, gate_up, down_proj):
+        experts = mesh.shape["blk"] // 2
+        body = by_tokens if experts <= 2 * expert_ids.shape[1] else by_slots
+        return body(tokens, expert_ids, route_gate, gate_up, down_proj)
+
     return jax.shard_map(
         per_device,
         mesh=mesh,

time: 352 us -> 231 us (0.66)
  the two profiles are of different devices: /device:TPU:13 before, /device:TPU:0 now
where the time goes in v1:
time: 231 us; the launch traced here: 230 us
  waiting for transfers between devices  159 us (69%)
  matrix products  33.1 us (14%)
  blocking collectives  23.5 us (10%)
  between operations  13.4 us (6%)
    reduce_scatter x1, waiting for transfers between devices, by_tokens(): lax.psum_scatter(partial_value, 'blk', scatter_dimension=0, tiled=True)  103 us
    all_gather x1, waiting for transfers between devices, by_tokens(): rows = lax.all_gather(tokens, 'blk', axis=0, tiled=True)  55.5 us
    all_gather x1, blocking collectives, by_tokens(): weights = lax.all_gather(weight.T, 'blk', axis=0, tiled=False)  23.5 us
    dot_general x1, matrix products, by_tokens(): jnp.dot(hidden, down_proj, preferred_element_type=jnp.float32)  21.4 us
    dot_general x1, matrix products, by_tokens(): lax.dot_general(rows, gate_up[0], contract, preferred_element_type=jnp.fl...  11.8 us
  transfers between devices with their start and end apart: 2, of which 2 were waited for; matrix products, arithmetic and copies ran while one was open for 0% of the time, Pallas kernels for 0%

profile of v1, /device:TPU:0, one launch (start us, length us, event | category | flops | bytes accessed | tf_op | source)
XLA Modules:
  0.0 230.3 jit_solution(11799240682841361339)
XLA Ops:
  6.5 0.0 copy-start
  6.5 0.0 all-gather.3.cloned.1.call-start
  6.5 0.7 all-gather.3.cloned.1.call-update
  7.3 0.0 reduce-scatter.2.cloned.1.call-start
  7.3 0.9 select_reduce_fusion
  8.2 23.5 %all-gather = f32[128,128]{1,0:T(8,128)S(1)} all-gather(f32[8,128]{1,0:T(8,128)S(1)} %bitcast.14), channel_id=2, replica_groups=mesh['groups'=2,'blk'=16] {'blk'}, dimensions={0}, use_global_device_ids=true | all-gather | bytes 69632 | tf_op jit(solution)/shard_map/all_gather | solution.py:52
  31.7 55.5 %all-gather.3.cloned.1.call-done = bf16[2048,2048]{1,0:T(8,128)(2,1)} async-done(((bf16[128,2048]{1,0:T(8,128)(2,1)}), bf16[2048,2048]{1,0:T(8,128)(2,1)}) %all-gather.3.cloned.1.call-update) | async-done | bytes 8388624 | tf_op jit(solution)/shard_map/all_gather | solution.py:54
  87.2 11.8 %fusion.2 = f32[2048,768]{1,0:T(8,128)} fusion(bf16[2048,2048]{1,0:T(8,128)(2,1)} %all-gather.3.cloned.1.call-done, bf16[2,768,2048]{2,1,0:T(8,128)(2,1)} %param.8), kind=kOutput, calls=%fused_computation.3 | convolution fusion | flops 6442450944 | bytes 17825792 | tf_op jit(solution)/shard_map/dot_general | solution.py:56
  99.0 0.0 copy-done
  99.0 21.4 %convolution_convert_fusion = bf16[2048,2048]{1,0:T(8,128)(2,1)} fusion(bf16[768,2048]{1,0:T(8,128)(2,1)S(1)} %copy-done, f32[2048,768]{1,0:T(8,128)} %fusion.2, bf16[2048,2048]{1,0:T(8,128)(2,1)} %all-gather.3.cloned.1.call-done, f32[2048]{0:T(1024)S(1)} %bitcast.15, bf16[2,768,2048]{2,1,0:T(8,128)(2,1)} %param.8), kind=kOutput, calls=%fused_computation | convolution fusion | flops 12900106240 | bytes 29368320 | tf_op jit(solution)/shard_map/dot_general | solution.py:59
  120.4 0.0 reduce-scatter.2.cloned.1.call-update
  120.4 103.1 %reduce-scatter.2.cloned.1.call-done = bf16[128,2048]{1,0:T(8,128)(2,1)} async-done(((bf16[2048,2048]{1,0:T(8,128)(2,1)}), bf16[128,2048]{1,0:T(8,128)(2,1)}) %reduce-scatter.2.cloned.1.call-update) | async-done | bytes 524304 | tf_op jit(solution)/shard_map/reduce_scatter | solution.py:60
  (1 shorter events, 0.0 us)
Async XLA Ops:
  6.5 92.5 %copy-start = (bf16[768,2048]{1,0:T(8,128)(2,1)S(1)}, bf16[768,2048]{1,0:T(8,128)(2,1)}, u32[]{:S(2)}) copy-start(bf16[768,2048]{1,0:T(8,128)(2,1)} %param.9) | copy-start | bytes 9437188
  6.5 80.7 %all-gather.3.cloned.1.call-start = ((), (), s32[]{:S(2)}) async-start(), calls=%async_computation.1 | async-start | bytes 8912896 | tf_op jit(solution)/shard_map/all_gather | solution.py:54
  7.3 216.2 %reduce-scatter.2.cloned.1.call-start = ((), (), s32[]{:S(2)}) async-start(), calls=%async_computation.2 | async-start | bytes 8912896 | tf_op jit(solution)/shard_map/reduce_scatter | solution.py:60
Sparse Core Ops, SparseCore 0:
  9.5 77.6 all-gather.2
  120.5 102.9 reduce-scatter.1

commit v2 on v0

--- a/solution.py
+++ b/solution.py
@@ -1,6 +1,10 @@
+import functools
+
 import jax
 import jax.numpy as jnp
 from jax import lax
+from jax.experimental import pallas as pl
+from jax.experimental.pallas import tpu as pltpu
 from jax.sharding import PartitionSpec as P
 
 
@@ -12,7 +16,7 @@
     return jnp.dot(hidden, down_proj, preferred_element_type=jnp.float32).astype(jnp.bfloat16)
 
 
-def per_device(tokens, expert_ids, route_gate, gate_up, down_proj):
+def by_slots(tokens, expert_ids, route_gate, gate_up, down_proj):
     tok_count, per_token = expert_ids.shape
     feature_width = tokens.shape[1]
     devices = lax.axis_size("blk")
@@ -43,6 +47,133 @@
     return jnp.sum(weighted, axis=1).astype(jnp.bfloat16)
 
 
+def snake(chips):
+    return list(range(0, chips, 2)) + list(range(chips - 1, 0, -2))
+
+
+def half_expert_kernel(count, mine_ref, *refs):
+    blocks, gates = refs[:count], refs[count : count + 2]
+    gate_up_ref, down_ref, out_own, out_other, rows, total = refs[count + 2 :]
+    step, steps = pl.program_id(0), pl.num_programs(0)
+
+    @pl.when(step == 0)
+    def _():
+        at = 0
+        for block in blocks:
+            rows[at : at + block.shape[0], :] = block[...]
+            at += block.shape[0]
+
+    contract = (((1,), (1,)), ((), ()))
+    taken = rows[...]
+    gating = lax.dot_general(taken, gate_up_ref[0], contract, preferred_element_type=jnp.float32)
+    lifted = lax.dot_general(taken, gate_up_ref[1], contract, preferred_element_type=jnp.float32)
+    hidden = (gating / (1.0 + jnp.exp(-gating)) * lifted).astype(jnp.bfloat16)
+    product = jnp.dot(hidden, down_ref[...], preferred_element_type=jnp.float32)
+
+    @pl.when(step == 0)
+    def _():
+        total[...] = product
+
+    @pl.when(step > 0)
+    def _():
+        total[...] += product
+
+    @pl.when(step == steps - 1)
+    def _():
+        tokens = gates[0].shape[1]
+        experts = gates[0].shape[0] // 2
+        for core, out in enumerate((out_own, out_other)):
+            for place in range(out.shape[0] // tokens):
+                columns = gates[place][...].T
+                column = lax.broadcasted_iota(jnp.int32, columns.shape, 1)
+                wanted = column == mine_ref[0] + core * experts
+                weight = jnp.sum(jnp.where(wanted, columns, 0.0), axis=1, keepdims=True)
+                low = place * tokens
+                here = core * out.shape[0] + low
+                out[low : low + tokens, :] = (total[here : here + tokens, :] * weight).astype(out.dtype)
+
+
+def half_expert(mine, blocks, gates, gate_up, down_proj):
+    if len(gates) == 1:
+        gates = gates * 2
+    height = sum(block.shape[0] for block in blocks)
+    units, width = down_proj.shape
+    tile = 256 if units % 256 == 0 else units
+    whole = pl.BlockSpec(memory_space=pltpu.VMEM)
+    out = jax.ShapeDtypeStruct((height // 2, width), jnp.bfloat16)
+    return pl.pallas_call(
+        functools.partial(half_expert_kernel, len(blocks)),
+        grid=(units // tile,),
+        out_shape=(out, out),
+        in_specs=[pl.BlockSpec(memory_space=pltpu.SMEM)]
+        + [whole] * (len(blocks) + 2)
+        + [
+            pl.BlockSpec((2, tile, width), lambda i: (0, i, 0)),
+            pl.BlockSpec((tile, width), lambda i: (i, 0)),
+        ],
+        out_specs=(whole, whole),
+        scratch_shapes=[
+            pltpu.VMEM((height, width), jnp.bfloat16),
+            pltpu.VMEM((height, width), jnp.float32),
+        ],
+        compiler_params=pltpu.CompilerParams(vmem_limit_bytes=32 << 20),
+        cost_estimate=pl.CostEstimate(
+            flops=6 * height * units * width,
+            bytes_accessed=6 * units * width + 4 * height * width,
+            transcendentals=height * units,
+        ),
+    )(mine, *blocks, *gates, gate_up, down_proj)
+
+
+def by_tokens(tokens, expert_ids, route_gate, gate_up, down_proj):
+    chips = lax.axis_size("blk") // 2
+    order = snake(chips)
+    far = chips // 2
+    up = [(2 * order[r] + c, 2 * order[(r + 1) % chips] + c) for r in range(chips) for c in (0, 1)]
+    down = [(b, a) for a, b in up]
+    cores = [(d, d ^ 1) for d in range(2 * chips)]
+
+    def send(value, pairs):
+        return lax.ppermute(value, "blk", pairs)
+
+    mine = (lax.axis_index("blk") // 2).astype(jnp.int32).reshape(1)
+    chosen = jnp.arange(chips, dtype=jnp.int32)[:, None, None] == expert_ids.T[None]
+    weight = jnp.sum(jnp.where(chosen, route_gate.T[None], 0.0), axis=1)
+    gates = jnp.concatenate([weight, send(weight, cores)])
+    middle = tokens.shape[0] // 2
+
+    def partials(blocks, weights):
+        others = [send(block, cores) for block in blocks]
+        own, other = half_expert(mine, blocks + others, weights, gate_up, down_proj)
+        return own, send(other, cores)
+
+    results = [partials([tokens], [gates])]
+    above, below, gates_above, gates_below = tokens, tokens, gates, gates
+    for step in range(1, far):
+        above, below = send(above, down), send(below, up)
+        gates_above, gates_below = send(gates_above, down), send(gates_below, up)
+        results.append(partials([above, below], [gates_above, gates_below]))
+    above, below = send(above[:middle], down), send(below[middle:], up)
+    gates_above = send(gates_above, down)
+    results.append(partials([above, below], [gates_above]))
+
+    def both(pair, low, high):
+        return pair[0][low:high].astype(jnp.float32) + pair[1][low:high].astype(jnp.float32)
+
+    rows = tokens.shape[0]
+    above = send(both(results[far], 0, middle).astype(jnp.bfloat16), up)
+    below = send(both(results[far], middle, rows).astype(jnp.bfloat16), down)
+    for step in range(far - 1, 0, -1):
+        to_above, to_below = both(results[step], 0, rows), both(results[step], rows, 2 * rows)
+        if step == far - 1:
+            to_above = jnp.concatenate([to_above[:middle] + above, to_above[middle:]])
+            to_below = jnp.concatenate([to_below[:middle], to_below[middle:] + below])
+        else:
+            to_above, to_below = to_above + above, to_below + below
+        above, below = send(to_above.astype(jnp.bfloat16), up), send(to_below.astype(jnp.bfloat16), down)
+    return (both(results[0], 0, rows) + above + below).astype(jnp.bfloat16)
+
+
 def solution(mesh):
     placed = (
         P(("groups", "blk"), None),
@@ -51,6 +182,12 @@
         P(None, "blk", None),
         P("blk", None),
     )
+
+    def per_device(tokens, expert_ids, route_gate, gate_up, down_proj):
+        experts = mesh.shape["blk"] // 2
+        body = by_tokens if experts <= 2 * expert_ids.shape[1] else by_slots
+        return body(tokens, expert_ids, route_gate, gate_up, down_proj)
+
     return jax.shard_map(
         per_device,
         mesh=mesh,

time: 352 us -> 150 us (0.43)
  the two profiles are of different devices: /device:TPU:13 before, /device:TPU:0 now
where the time goes in v2:
time: 150 us; the launch traced here: 149 us
  waiting for transfers between devices  76.9 us (51%)
  Pallas kernels  33.3 us (22%)
  starting transfers between devices  29.9 us (20%)
  local copies, waits for them, and re-layouts  5.5 us (4%)
  other arithmetic  3.62 us (2%)
    ppermute x38, waiting for transfers between devices, send(): return lax.ppermute(value, 'blk', pairs)  76.9 us
    pallas_call x5, Pallas kernels, half_expert(): pl.pallas_call(functools.partial(half_expert_kernel, len(blocks)), grid=(...  33.3 us
    ppermute x38, starting transfers between devices, send(): return lax.ppermute(value, 'blk', pairs)  29.9 us
    unnamed x14, local copies, waits for them, and re-layouts  4.7 us
  transfers between devices with their start and end apart: 38, of which 18 were waited for; matrix products, arithmetic and copies ran while one was open for 2% of the time, Pallas kernels for 22%

profile of v2, /device:TPU:0, one launch (start us, length us, event | category | flops | bytes accessed | tf_op | source)
XLA Modules:
  0.0 149.4 jit_solution(7029287413057893998)
XLA Ops:
  0.0 3.0 %collective-permute-start.3 = (bf16[128,2048]{1,0:T(8,128)(2,1)}, bf16[128,2048]{1,0:T(8,128)(2,1)S(1)}, u32[]{:S(2)}, u32[]{:S(2)}) collective-permute-start(bf16[128,2048]{1,0:T(8,128)(2,1)} %refs_0_.1), channel_id=1, source_target_pairs={{4,0},{5,1},{8,4},{9,5},{12,8},{13,9},{14,12},{15,13},{10,14},{11,... | collective-permute-start | bytes 1572872 | tf_op jit(solution)/shard_map/ppermute | solution.py:137
  3.0 12.1 %collective-permute-done.3.refs_0_ = bf16[128,2048]{1,0:T(8,128)(2,1)S(1)} collective-permute-done((bf16[128,2048]{1,0:T(8,128)(2,1)}, bf16[128,2048]{1,0:T(8,128)(2,1)S(1)}, u32[]{:S(2)}, u32[]{:S(2)}) %collective-permute-start.3) | collective-permute-done | bytes 524320 | tf_op jit(solution)/shard_map/ppermute | solution.py:137
  15.2 1.7 %collective-permute-start.10 = (bf16[128,2048]{1,0:T(8,128)(2,1)S(1)}, bf16[128,2048]{1,0:T(8,128)(2,1)S(1)}, u32[]{:S(2)}, u32[]{:S(2)}) collective-permute-start(bf16[128,2048]{1,0:T(8,128)(2,1)S(1)} %collective-permute-done.3.refs_0_), channel_id=1, source_target_pairs={{4,0},{5,1},{8,4},{9,5},{12,8},{13,9},{14,12},{15,13},{10,14},{11,... | collective-permute-start | bytes 1572872 | tf_op jit(solution)/shard_map/ppermute | solution.py:137
  17.2 11.1 %collective-permute-done.10.refs_0_ = bf16[128,2048]{1,0:T(8,128)(2,1)S(1)} collective-permute-done((bf16[128,2048]{1,0:T(8,128)(2,1)S(1)}, bf16[128,2048]{1,0:T(8,128)(2,1)S(1)}, u32[]{:S(2)}, u32[]{:S(2)}) %collective-permute-start.10) | collective-permute-done | bytes 524320 | tf_op jit(solution)/shard_map/ppermute | solution.py:137
  30.3 10.2 %collective-permute-done.17.refs_0_ = bf16[128,2048]{1,0:T(8,128)(2,1)S(1)} collective-permute-done((bf16[128,2048]{1,0:T(8,128)(2,1)S(1)}, bf16[128,2048]{1,0:T(8,128)(2,1)S(1)}, u32[]{:S(2)}, u32[]{:S(2)}) %collective-permute-start.17) | collective-permute-done | bytes 524320 | tf_op jit(solution)/shard_map/ppermute | solution.py:137
  47.5 3.5 %collective-permute-done.7.refs_4_ = f32[16,128]{1,0:T(8,128)S(1)} collective-permute-done((f32[16,128]{1,0:T(8,128)S(1)}, f32[16,128]{1,0:T(8,128)S(1)}, u32[]{:S(2)}, u32[]{:S(2)}) %collective-permute-start.7) | collective-permute-done | bytes 8224 | tf_op jit(solution)/shard_map/ppermute | solution.py:137
  52.0 2.7 %collective-permute-done.8.refs_5_ = f32[16,128]{1,0:T(8,128)S(1)} collective-permute-done((f32[16,128]{1,0:T(8,128)S(1)}, f32[16,128]{1,0:T(8,128)S(1)}, u32[]{:S(2)}, u32[]{:S(2)}) %collective-permute-start.8) | collective-permute-done | bytes 8224 | tf_op jit(solution)/shard_map/ppermute | solution.py:137
  56.3 2.1 %collective-permute-done.14.refs_4_ = f32[16,128]{1,0:T(8,128)S(1)} collective-permute-done((f32[16,128]{1,0:T(8,128)S(1)}, f32[16,128]{1,0:T(8,128)S(1)}, u32[]{:S(2)}, u32[]{:S(2)}) %collective-permute-start.14) | collective-permute-done | bytes 8224 | tf_op jit(solution)/shard_map/ppermute | solution.py:137
  59.3 2.7 %collective-permute-done.15.refs_5_ = f32[16,128]{1,0:T(8,128)S(1)} collective-permute-done((f32[16,128]{1,0:T(8,128)S(1)}, f32[16,128]{1,0:T(8,128)S(1)}, u32[]{:S(2)}, u32[]{:S(2)}) %collective-permute-start.15) | collective-permute-done | bytes 8224 | tf_op jit(solution)/shard_map/ppermute | solution.py:137
  63.6 2.1 %collective-permute-done.21.refs_4_ = f32[16,128]{1,0:T(8,128)S(1)} collective-permute-done((f32[16,128]{1,0:T(8,128)S(1)}, f32[16,128]{1,0:T(8,128)S(1)}, u32[]{:S(2)}, u32[]{:S(2)}) %collective-permute-start.21) | collective-permute-done | bytes 8224 | tf_op jit(solution)/shard_map/ppermute | solution.py:137
  66.7 2.7 %collective-permute-done.22.refs_5_ = f32[16,128]{1,0:T(8,128)S(1)} collective-permute-done((f32[16,128]{1,0:T(8,128)S(1)}, f32[16,128]{1,0:T(8,128)S(1)}, u32[]{:S(2)}, u32[]{:S(2)}) %collective-permute-start.22) | collective-permute-done | bytes 8224 | tf_op jit(solution)/shard_map/ppermute | solution.py:137
  71.9 2.8 %copy-done = bf16[2,768,2048]{2,1,0:T(8,128)(2,1)S(1)} copy-done((bf16[2,768,2048]{2,1,0:T(8,128)(2,1)S(1)}, bf16[2,768,2048]{2,1,0:T(8,128)(2,1)}, u32[]{:S(2)}) %copy-start) | copy-done | bytes 6291480
  74.7 1.9 %copy-done.2 = bf16[768,2048]{1,0:T(8,128)(2,1)S(1)} copy-done((bf16[768,2048]{1,0:T(8,128)(2,1)S(1)}, bf16[768,2048]{1,0:T(8,128)(2,1)}, u32[]{:S(2)}) %copy-start.2) | copy-done | bytes 3145752
  76.6 8.8 %shard_map.58 = (bf16[256,2048]{1,0:T(8,128)(2,1)S(1)}, bf16[256,2048]{1,0:T(8,128)(2,1)S(1)}) custom-call(s32[1]{0:T(128)} %bitcast.mine_ref, bf16[128,2048]{1,0:T(8,128)(2,1)S(1)} %collective-permute-done.17.refs_0_, bf16[128,2048]{1,0:T(8,128)(2,1)S(1)} %collective-permute-done.18.refs_1_, bf16[128,2048]{1,0:T(8,128)(2,1)} %collective-permute-done.19.refs_2_, ...), custom_call_target="tpu_custom_call" | custom-call | flops 4831838208 | bytes 13631488 | tf_op jit(solution)/shard_map/pallas_call | solution.py:104
  85.6 4.7 %shard_map.59 = (bf16[128,2048]{1,0:T(8,128)(2,1)S(1)}, bf16[128,2048]{1,0:T(8,128)(2,1)S(1)}) custom-call(s32[1]{0:T(128)} %bitcast.mine_ref, bf16[64,2048]{1,0:T(8,128)(2,1)S(1)} %collective-permute-done.24.refs_0_, bf16[64,2048]{1,0:T(8,128)(2,1)S(1)} %collective-permute-done.25.refs_1_, bf16[64,2048]{1,0:T(8,128)(2,1)S(1)} %collective-permute-done.26.refs_2_, ...), custom_call_target="tpu_custom_call" | custom-call | flops 2415919104 | bytes 11534336 | tf_op jit(solution)/shard_map/pallas_call | solution.py:104
  91.3 7.6 %shard_map.57 = (bf16[256,2048]{1,0:T(8,128)(2,1)S(1)}, bf16[256,2048]{1,0:T(8,128)(2,1)S(1)}) custom-call(s32[1]{0:T(128)} %bitcast.mine_ref, bf16[128,2048]{1,0:T(8,128)(2,1)S(1)} %collective-permute-done.10.refs_0_, bf16[128,2048]{1,0:T(8,128)(2,1)S(1)} %copy-done.6, bf16[128,2048]{1,0:T(8,128)(2,1)S(1)} %collective-permute-done.12.refs_2_, ...), custom_call_target="tpu_custom_call" | custom-call | flops 4831838208 | bytes 13631488 | tf_op jit(solution)/shard_map/pallas_call | solution.py:104
  99.2 1.6 %collective-permute-start.34 = (bf16[64,2048]{1,0:T(8,128)(2,1)S(1)}, bf16[64,2048]{1,0:T(8,128)(2,1)S(1)}, u32[]{:S(2)}, u32[]{:S(2)}) collective-permute-start(bf16[64,2048]{1,0:T(8,128)(2,1)S(1)} %get-tuple-element.32), channel_id=1, source_target_pairs={{4,0},{5,1},{8,4},{9,5},{12,8},{13,9},{14,12},{15,13},{10,14},{11,... | collective-permute-start | bytes 786440 | tf_op jit(solution)/shard_map/ppermute | solution.py:137
  101.6 6.3 %collective-permute-done.34 = bf16[64,2048]{1,0:T(8,128)(2,1)S(1)} collective-permute-done((bf16[64,2048]{1,0:T(8,128)(2,1)S(1)}, bf16[64,2048]{1,0:T(8,128)(2,1)S(1)}, u32[]{:S(2)}, u32[]{:S(2)}) %collective-permute-start.34) | collective-permute-done | bytes 262176 | tf_op jit(solution)/shard_map/ppermute | solution.py:137
  110.5 7.6 %shard_map.56 = (bf16[256,2048]{1,0:T(8,128)(2,1)S(1)}, bf16[256,2048]{1,0:T(8,128)(2,1)S(1)}) custom-call(s32[1]{0:T(128)} %bitcast.mine_ref, bf16[128,2048]{1,0:T(8,128)(2,1)S(1)} %collective-permute-done.3.refs_0_, bf16[128,2048]{1,0:T(8,128)(2,1)S(1)} %collective-permute-done.4.refs_1_, bf16[128,2048]{1,0:T(8,128)(2,1)S(1)} %collective-permute-done.5.refs_2_, ...), custom_call_target="tpu_custom_call" | custom-call | flops 4831838208 | bytes 13631488 | tf_op jit(solution)/shard_map/pallas_call | solution.py:104
  118.7 2.9 %collective-permute-done.35 = bf16[128,2048]{1,0:T(8,128)(2,1)S(1)} collective-permute-done((bf16[128,2048]{1,0:T(8,128)(2,1)S(1)}, bf16[128,2048]{1,0:T(8,128)(2,1)S(1)}, u32[]{:S(2)}, u32[]{:S(2)}) %collective-permute-start.35) | collective-permute-done | bytes 524320 | tf_op jit(solution)/shard_map/ppermute | solution.py:137
  121.6 1.7 %collective-permute-done.31 = bf16[128,2048]{1,0:T(8,128)(2,1)S(1)} collective-permute-done((bf16[128,2048]{1,0:T(8,128)(2,1)S(1)}, bf16[128,2048]{1,0:T(8,128)(2,1)S(1)}, u32[]{:S(2)}, u32[]{:S(2)}) %collective-permute-start.31) | collective-permute-done | bytes 524320 | tf_op jit(solution)/shard_map/ppermute | solution.py:137
  125.9 4.7 %shard_map.55 = (bf16[128,2048]{1,0:T(8,128)(2,1)S(1)}, bf16[128,2048]{1,0:T(8,128)(2,1)S(1)}) custom-call(s32[1]{0:T(128)} %bitcast.mine_ref, bf16[128,2048]{1,0:T(8,128)(2,1)S(1)} %copy-done.4, bf16[128,2048]{1,0:T(8,128)(2,1)S(1)} %collective-permute-done.refs_1_, f32[16,128]{1,0:T(8,128)S(1)} %pad_maximum_fusion.2.refs_2_.refs_3_, ...), custom_call_target="tpu_custom_call" | custom-call | flops 2415919104 | bytes 11534336 | tf_op jit(solution)/shard_map/pallas_call | solution.py:104
  130.6 5.5 %collective-permute-done.32 = bf16[128,2048]{1,0:T(8,128)(2,1)S(1)} collective-permute-done((bf16[128,2048]{1,0:T(8,128)(2,1)S(1)}, bf16[128,2048]{1,0:T(8,128)(2,1)S(1)}, u32[]{:S(2)}, u32[]{:S(2)}) %collective-permute-start.32) | collective-permute-done | bytes 524320 | tf_op jit(solution)/shard_map/ppermute | solution.py:137
  139.0 9.1 %collective-permute-done.33 = bf16[128,2048]{1,0:T(8,128)(2,1)S(1)} collective-permute-done((bf16[128,2048]{1,0:T(8,128)(2,1)S(1)}, bf16[128,2048]{1,0:T(8,128)(2,1)S(1)}, u32[]{:S(2)}, u32[]{:S(2)}) %collective-permute-start.33) | collective-permute-done | bytes 524320 | tf_op jit(solution)/shard_map/ppermute | solution.py:137
  (86 shorter events, 30.5 us)
Async XLA Ops:
  0.0 15.2 %collective-permute-start.3 = (bf16[128,2048]{1,0:T(8,128)(2,1)}, bf16[128,2048]{1,0:T(8,128)(2,1)S(1)}, u32[]{:S(2)}, u32[]{:S(2)}) collective-permute-start(bf16[128,2048]{1,0:T(8,128)(2,1)} %refs_0_.1), channel_id=1, source_target_pairs={{4,0},{5,1},{8,4},{9,5},{12,8},{13,9},{14,12},{15,13},{10,14},{11,... | collective-permute-start | bytes 1572872 | tf_op jit(solution)/shard_map/ppermute | solution.py:137
  3.0 13.9 %collective-permute-start.4 = (bf16[128,2048]{1,0:T(8,128)(2,1)}, bf16[128,2048]{1,0:T(8,128)(2,1)S(1)}, u32[]{:S(2)}, u32[]{:S(2)}) collective-permute-start(bf16[128,2048]{1,0:T(8,128)(2,1)} %refs_0_.1), channel_id=1, source_target_pairs={{0,4},{1,5},{4,8},{5,9},{8,12},{9,13},{12,14},{13,15},{14,10},{15,... | collective-permute-start | bytes 1572872 | tf_op jit(solution)/shard_map/ppermute | solution.py:137
  15.2 13.1 %collective-permute-start.10 = (bf16[128,2048]{1,0:T(8,128)(2,1)S(1)}, bf16[128,2048]{1,0:T(8,128)(2,1)S(1)}, u32[]{:S(2)}, u32[]{:S(2)}) collective-permute-start(bf16[128,2048]{1,0:T(8,128)(2,1)S(1)} %collective-permute-done.3.refs_0_), channel_id=1, source_target_pairs={{4,0},{5,1},{8,4},{9,5},{12,8},{13,9},{14,12},{15,13},{10,14},{11,... | collective-permute-start | bytes 1572872 | tf_op jit(solution)/shard_map/ppermute | solution.py:137
  16.8 12.8 %collective-permute-start.11 = (bf16[128,2048]{1,0:T(8,128)(2,1)S(1)}, bf16[128,2048]{1,0:T(8,128)(2,1)S(1)}, u32[]{:S(2)}, u32[]{:S(2)}) collective-permute-start(bf16[128,2048]{1,0:T(8,128)(2,1)S(1)} %collective-permute-done.4.refs_1_), channel_id=1, source_target_pairs={{0,4},{1,5},{4,8},{5,9},{8,12},{9,13},{12,14},{13,15},{14,10},{15,... | collective-permute-start | bytes 1572872 | tf_op jit(solution)/shard_map/ppermute | solution.py:137
  28.3 12.2 %collective-permute-start.17 = (bf16[128,2048]{1,0:T(8,128)(2,1)S(1)}, bf16[128,2048]{1,0:T(8,128)(2,1)S(1)}, u32[]{:S(2)}, u32[]{:S(2)}) collective-permute-start(bf16[128,2048]{1,0:T(8,128)(2,1)S(1)} %collective-permute-done.10.refs_0_), channel_id=1, source_target_pairs={{4,0},{5,1},{8,4},{9,5},{12,8},{13,9},{14,12},{15,13},{10,14},{11,... | collective-permute-start | bytes 1572872 | tf_op jit(solution)/shard_map/ppermute | solution.py:137
  40.5 31.0 %collective-permute-start.19 = (bf16[128,2048]{1,0:T(8,128)(2,1)S(1)}, bf16[128,2048]{1,0:T(8,128)(2,1)}, u32[]{:S(2)}, u32[]{:S(2)}) collective-permute-start(bf16[128,2048]{1,0:T(8,128)(2,1)S(1)} %collective-permute-done.17.refs_0_), channel_id=1, source_target_pairs={{0,1},{1,0},{2,3},{3,2},{4,5},{5,4},{6,7},{7,6},{8,9},{9,8},{10,11... | collective-permute-start | bytes 1572872 | tf_op jit(solution)/shard_map/ppermute | solution.py:137
  41.2 30.3 %collective-permute-start.20 = (bf16[128,2048]{1,0:T(8,128)(2,1)S(1)}, bf16[128,2048]{1,0:T(8,128)(2,1)}, u32[]{:S(2)}, u32[]{:S(2)}) collective-permute-start(bf16[128,2048]{1,0:T(8,128)(2,1)S(1)} %collective-permute-done.18.refs_1_), channel_id=1, source_target_pairs={{0,1},{1,0},{2,3},{3,2},{4,5},{5,4},{6,7},{7,6},{8,9},{9,8},{10,11... | collective-permute-start | bytes 1572872 | tf_op jit(solution)/shard_map/ppermute | solution.py:137
  42.0 28.9 %collective-permute-start.24 = (bf16[64,2048]{1,0:T(8,128)(2,1)}, bf16[64,2048]{1,0:T(8,128)(2,1)S(1)}, u32[]{:S(2)}, u32[]{:S(2)}) collective-permute-start(bf16[64,2048]{1,0:T(8,128)(2,1)} %slice.94), channel_id=1, source_target_pairs={{4,0},{5,1},{8,4},{9,5},{12,8},{13,9},{14,12},{15,13},{10,14},{11,... | collective-permute-start | bytes 786440 | tf_op jit(solution)/shard_map/ppermute | solution.py:137
  43.6 27.4 %collective-permute-start.25 = (bf16[64,2048]{1,0:T(8,128)(2,1)S(1)}, bf16[64,2048]{1,0:T(8,128)(2,1)S(1)}, u32[]{:S(2)}, u32[]{:S(2)}) collective-permute-start(bf16[64,2048]{1,0:T(8,128)(2,1)S(1)} %slice.95), channel_id=1, source_target_pairs={{0,4},{1,5},{4,8},{5,9},{8,12},{9,13},{12,14},{13,15},{14,10},{15,... | collective-permute-start | bytes 786440 | tf_op jit(solution)/shard_map/ppermute | solution.py:137
  69.3 16.1 %collective-permute-start.28 = (f32[16,128]{1,0:T(8,128)S(1)}, f32[16,128]{1,0:T(8,128)S(1)}, u32[]{:S(2)}, u32[]{:S(2)}) collective-permute-start(f32[16,128]{1,0:T(8,128)S(1)} %collective-permute-done.21.refs_4_), channel_id=1, source_target_pairs={{4,0},{5,1},{8,4},{9,5},{12,8},{13,9},{14,12},{15,13},{10,14},{11,... | collective-permute-start | bytes 24584 | tf_op jit(solution)/shard_map/ppermute | solution.py:137
  70.9 20.0 %collective-permute-start.12 = (bf16[128,2048]{1,0:T(8,128)(2,1)S(1)}, bf16[128,2048]{1,0:T(8,128)(2,1)S(1)}, u32[]{:S(2)}, u32[]{:S(2)}) collective-permute-start(bf16[128,2048]{1,0:T(8,128)(2,1)S(1)} %collective-permute-done.10.refs_0_), channel_id=1, source_target_pairs={{0,1},{1,0},{2,3},{3,2},{4,5},{5,4},{6,7},{7,6},{8,9},{9,8},{10,11... | collective-permute-start | bytes 1572872 | tf_op jit(solution)/shard_map/ppermute | solution.py:137
  70.9 20.4 %collective-permute-start.13 = (bf16[128,2048]{1,0:T(8,128)(2,1)}, bf16[128,2048]{1,0:T(8,128)(2,1)S(1)}, u32[]{:S(2)}, u32[]{:S(2)}) collective-permute-start(bf16[128,2048]{1,0:T(8,128)(2,1)} %copy-done.5), channel_id=1, source_target_pairs={{0,1},{1,0},{2,3},{3,2},{4,5},{5,4},{6,7},{7,6},{8,9},{9,8},{10,11... | collective-permute-start | bytes 1572872 | tf_op jit(solution)/shard_map/ppermute | solution.py:137
  71.4 14.1 %collective-permute-start.26 = (bf16[64,2048]{1,0:T(8,128)(2,1)S(1)}, bf16[64,2048]{1,0:T(8,128)(2,1)S(1)}, u32[]{:S(2)}, u32[]{:S(2)}) collective-permute-start(bf16[64,2048]{1,0:T(8,128)(2,1)S(1)} %collective-permute-done.24.refs_0_), channel_id=1, source_target_pairs={{0,1},{1,0},{2,3},{3,2},{4,5},{5,4},{6,7},{7,6},{8,9},{9,8},{10,11... | collective-permute-start | bytes 786440 | tf_op jit(solution)/shard_map/ppermute | solution.py:137
  71.5 14.1 %collective-permute-start.27 = (bf16[64,2048]{1,0:T(8,128)(2,1)S(1)}, bf16[64,2048]{1,0:T(8,128)(2,1)S(1)}, u32[]{:S(2)}, u32[]{:S(2)}) collective-permute-start(bf16[64,2048]{1,0:T(8,128)(2,1)S(1)} %collective-permute-done.25.refs_1_), channel_id=1, source_target_pairs={{0,1},{1,0},{2,3},{3,2},{4,5},{5,4},{6,7},{7,6},{8,9},{9,8},{10,11... | collective-permute-start | bytes 786440 | tf_op jit(solution)/shard_map/ppermute | solution.py:137
  85.4 15.4 %collective-permute-start.23 = (bf16[256,2048]{1,0:T(8,128)(2,1)S(1)}, bf16[256,2048]{1,0:T(8,128)(2,1)S(1)}, u32[]{:S(2)}, u32[]{:S(2)}) collective-permute-start(bf16[256,2048]{1,0:T(8,128)(2,1)S(1)} %get-tuple-element.22), channel_id=1, source_target_pairs={{0,1},{1,0},{2,3},{3,2},{4,5},{5,4},{6,7},{7,6},{8,9},{9,8},{10,11... | collective-permute-start | bytes 3145736 | tf_op jit(solution)/shard_map/ppermute | solution.py:137
  90.8 19.7 %collective-permute-start.5 = (bf16[128,2048]{1,0:T(8,128)(2,1)S(1)}, bf16[128,2048]{1,0:T(8,128)(2,1)S(1)}, u32[]{:S(2)}, u32[]{:S(2)}) collective-permute-start(bf16[128,2048]{1,0:T(8,128)(2,1)S(1)} %collective-permute-done.3.refs_0_), channel_id=1, source_target_pairs={{0,1},{1,0},{2,3},{3,2},{4,5},{5,4},{6,7},{7,6},{8,9},{9,8},{10,11... | collective-permute-start | bytes 1572872 | tf_op jit(solution)/shard_map/ppermute | solution.py:137
  90.9 19.6 %collective-permute-start.6 = (bf16[128,2048]{1,0:T(8,128)(2,1)S(1)}, bf16[128,2048]{1,0:T(8,128)(2,1)S(1)}, u32[]{:S(2)}, u32[]{:S(2)}) collective-permute-start(bf16[128,2048]{1,0:T(8,128)(2,1)S(1)} %collective-permute-done.4.refs_1_), channel_id=1, source_target_pairs={{0,1},{1,0},{2,3},{3,2},{4,5},{5,4},{6,7},{7,6},{8,9},{9,8},{10,11... | collective-permute-start | bytes 1572872 | tf_op jit(solution)/shard_map/ppermute | solution.py:137
  98.9 19.8 %collective-permute-start.16 = (bf16[256,2048]{1,0:T(8,128)(2,1)S(1)}, bf16[256,2048]{1,0:T(8,128)(2,1)S(1)}, u32[]{:S(2)}, u32[]{:S(2)}) collective-permute-start(bf16[256,2048]{1,0:T(8,128)(2,1)S(1)} %get-tuple-element.20), channel_id=1, source_target_pairs={{0,1},{1,0},{2,3},{3,2},{4,5},{5,4},{6,7},{7,6},{8,9},{9,8},{10,11... | collective-permute-start | bytes 3145736 | tf_op jit(solution)/shard_map/ppermute | solution.py:137
  108.0 13.5 %collective-permute-start.35 = (bf16[128,2048]{1,0:T(8,128)(2,1)S(1)}, bf16[128,2048]{1,0:T(8,128)(2,1)S(1)}, u32[]{:S(2)}, u32[]{:S(2)}) collective-permute-start(bf16[128,2048]{1,0:T(8,128)(2,1)S(1)} %pad_maximum_fusion.1), channel_id=1, source_target_pairs={{4,0},{5,1},{8,4},{9,5},{12,8},{13,9},{14,12},{15,13},{10,14},{11,... | collective-permute-start | bytes 1572872 | tf_op jit(solution)/shard_map/ppermute | solution.py:137
  109.8 13.4 %collective-permute-start.31 = (bf16[128,2048]{1,0:T(8,128)(2,1)S(1)}, bf16[128,2048]{1,0:T(8,128)(2,1)S(1)}, u32[]{:S(2)}, u32[]{:S(2)}) collective-permute-start(bf16[128,2048]{1,0:T(8,128)(2,1)S(1)} %pad_maximum_fusion), channel_id=1, source_target_pairs={{0,4},{1,5},{4,8},{5,9},{8,12},{9,13},{12,14},{13,15},{14,10},{15,... | collective-permute-start | bytes 1572872 | tf_op jit(solution)/shard_map/ppermute | solution.py:137
  110.5 15.3 %collective-permute-start = (bf16[128,2048]{1,0:T(8,128)(2,1)S(1)}, bf16[128,2048]{1,0:T(8,128)(2,1)S(1)}, u32[]{:S(2)}, u32[]{:S(2)}) collective-permute-start(bf16[128,2048]{1,0:T(8,128)(2,1)S(1)} %copy-done.4), channel_id=1, source_target_pairs={{0,1},{1,0},{2,3},{3,2},{4,5},{5,4},{6,7},{7,6},{8,9},{9,8},{10,11... | collective-permute-start | bytes 1572872 | tf_op jit(solution)/shard_map/ppermute | solution.py:137
  118.1 12.5 %collective-permute-start.9 = (bf16[256,2048]{1,0:T(8,128)(2,1)S(1)}, bf16[256,2048]{1,0:T(8,128)(2,1)S(1)}, u32[]{:S(2)}, u32[]{:S(2)}) collective-permute-start(bf16[256,2048]{1,0:T(8,128)(2,1)S(1)} %get-tuple-element.18), channel_id=1, source_target_pairs={{0,1},{1,0},{2,3},{3,2},{4,5},{5,4},{6,7},{7,6},{8,9},{9,8},{10,11... | collective-permute-start | bytes 3145736 | tf_op jit(solution)/shard_map/ppermute | solution.py:137
  123.8 12.3 %collective-permute-start.32 = (bf16[128,2048]{1,0:T(8,128)(2,1)S(1)}, bf16[128,2048]{1,0:T(8,128)(2,1)S(1)}, u32[]{:S(2)}, u32[]{:S(2)}) collective-permute-start(bf16[128,2048]{1,0:T(8,128)(2,1)S(1)} %get-tuple-element.27), channel_id=1, source_target_pairs={{0,4},{1,5},{4,8},{5,9},{8,12},{9,13},{12,14},{13,15},{14,10},{15,... | collective-permute-start | bytes 1572872 | tf_op jit(solution)/shard_map/ppermute | solution.py:137
  124.3 12.0 %collective-permute-start.36 = (bf16[128,2048]{1,0:T(8,128)(2,1)S(1)}, bf16[128,2048]{1,0:T(8,128)(2,1)S(1)}, u32[]{:S(2)}, u32[]{:S(2)}) collective-permute-start(bf16[128,2048]{1,0:T(8,128)(2,1)S(1)} %get-tuple-element.28), channel_id=1, source_target_pairs={{4,0},{5,1},{8,4},{9,5},{12,8},{13,9},{14,12},{15,13},{10,14},{11,... | collective-permute-start | bytes 1572872 | tf_op jit(solution)/shard_map/ppermute | solution.py:137
  (21 other events, 144.8 us)

commit v3 on v0

--- a/solution.py
+++ b/solution.py
@@ -1,6 +1,11 @@
+import functools
+
 import jax
 import jax.numpy as jnp
+import numpy as np
 from jax import lax
+from jax.experimental import pallas as pl
+from jax.experimental.pallas import tpu as pltpu
 from jax.sharding import PartitionSpec as P
 
 
@@ -12,7 +17,7 @@
     return jnp.dot(hidden, down_proj, preferred_element_type=jnp.float32).astype(jnp.bfloat16)
 
 
-def per_device(tokens, expert_ids, route_gate, gate_up, down_proj):
+def by_slots(tokens, expert_ids, route_gate, gate_up, down_proj):
     tok_count, per_token = expert_ids.shape
     feature_width = tokens.shape[1]
     devices = lax.axis_size("blk")
@@ -43,6 +48,176 @@
     return jnp.sum(weighted, axis=1).astype(jnp.bfloat16)
 
 
+def snake(chips):
+    return list(range(0, chips, 2)) + list(range(chips - 1, 0, -2))
+
+
+def sources(chips):
+    order = snake(chips)
+    table = np.zeros((2 * chips, 2 * chips), np.int32)
+    for place in range(chips):
+        for core in (0, 1):
+            turn = 1 - 2 * core
+            row = [(0, core), (0, 1 - core)]
+            for step in range(1, chips // 2):
+                row += [(-step, core), (-step, 1 - core), (step, 1 - core), (step, core)]
+            row += [(chips // 2, core), (chips // 2, 1 - core)]
+            table[2 * order[place] + core] = [2 * order[(place + turn * d) % chips] + c for d, c in row]
+    return table
+
+
+def half_expert_kernel(pieces, keep, sources_ref, gates_ref, *refs):
+    blocks, (gate_up_ref, down_ref, out_keep, out_give, rows, hidden) = refs[:-6], refs[-6:]
+    weights = []
+    at = 0
+    for operand, first, count, source, token in pieces:
+        rows[at : at + count, :] = blocks[operand][first : first + count, :]
+        at += count
+        line = gates_ref[pl.ds(sources_ref[source], 1), :]
+        column = jnp.broadcast_to(line, (8, line.shape[1])).T[:, :1]
+        weights.append(column[token : token + count])
+    weight = jnp.concatenate(weights)
+
+    units, width = down_ref.shape
+    tile = 256 if units % 256 == 0 else units
+    contract = (((1,), (1,)), ((), ()))
+    taken = rows[...]
+    for low in range(0, units, tile):
+        gating = lax.dot_general(taken, gate_up_ref[0, low : low + tile], contract, preferred_element_type=jnp.float32)
+        lifted = lax.dot_general(taken, gate_up_ref[1, low : low + tile], contract, preferred_element_type=jnp.float32)
+        hidden[:, low : low + tile] = (gating / (1.0 + jnp.exp(-gating)) * lifted).astype(jnp.bfloat16)
+    inner = hidden[...]
+    tile = 512 if width % 512 == 0 else width
+    for low in range(0, width, tile):
+        product = jnp.dot(inner, down_ref[:, low : low + tile], preferred_element_type=jnp.float32) * weight
+        product = product.astype(jnp.bfloat16)
+        out_keep[:, low : low + tile] = product[:keep]
+        out_give[:, low : low + tile] = product[keep:]
+
+
+def half_expert(places, gates, pieces, keep, blocks, gate_up, down_proj):
+    height = sum(piece[2] for piece in pieces)
+    units, width = down_proj.shape
+    whole = pl.BlockSpec(memory_space=pltpu.VMEM)
+    return pl.pallas_call(
+        functools.partial(half_expert_kernel, tuple(pieces), keep),
+        out_shape=(
+            jax.ShapeDtypeStruct((keep, width), jnp.bfloat16),
+            jax.ShapeDtypeStruct((height - keep, width), jnp.bfloat16),
+        ),
+        in_specs=[pl.BlockSpec(memory_space=pltpu.SMEM)] + [whole] * (len(blocks) + 3),
+        out_specs=(whole, whole),
+        scratch_shapes=[
+            pltpu.VMEM((height, width), jnp.bfloat16),
+            pltpu.VMEM((height, units), jnp.bfloat16),
+        ],
+        compiler_params=pltpu.CompilerParams(vmem_limit_bytes=32 << 20),
+        cost_estimate=pl.CostEstimate(
+            flops=6 * height * units * width,
+            bytes_accessed=6 * units * width + 4 * height * width,
+            transcendentals=height * units,
+        ),
+    )(places, gates, *blocks, gate_up, down_proj)
+
+
+def by_tokens(tokens, expert_ids, route_gate, gate_up, down_proj):
+    chips = lax.axis_size("blk") // 2
+    order, far = snake(chips), chips // 2
+    rows = tokens.shape[0]
+    half = rows // 2
+    chains = (0, 1)
+    forth, back, across, home, cores = [], [], [], [], []
+    for place in range(chips):
+        for core in (0, 1):
+            device = 2 * order[place] + core
+            ahead, behind = order[(place + 1 - 2 * core) % chips], order[(place - 1 + 2 * core) % chips]
+            forth.append((device, 2 * ahead + core))
+            back.append((device, 2 * behind + core))
+            across.append((device, 2 * behind + 1 - core))
+            home.append((device, 2 * behind + 1 - core))
+            cores.append((device, device ^ 1))
+
+    def send(value, pairs):
+        return lax.ppermute(value, "blk", pairs)
+
+    def total(*terms):
+        return sum(term.astype(jnp.float32) for term in terms)
+
+    def rounded(value):
+        return value.astype(jnp.bfloat16)
+
+    def after(value, *earlier):
+        return lax.optimization_barrier((value, *earlier))[0]
+
+    parts = [tokens[c * half : (c + 1) * half] for c in chains]
+    ring = [jnp.concatenate([send(part, forth), send(part, across)]) for part in parts]
+
+    places = lax.dynamic_index_in_dim(jnp.asarray(sources(chips)), lax.axis_index("blk"), 0, keepdims=False)
+    chosen = jnp.arange(chips, dtype=jnp.int32)[:, None, None] == expert_ids.T[None]
+    weight = jnp.sum(jnp.where(chosen, route_gate.T[None], 0.0), axis=1)
+    gates = lax.all_to_all(jnp.repeat(weight, 2, axis=0), "blk", split_axis=0, concat_axis=0, tiled=True)
+    gates = gates.reshape(-1, rows)
+
+    def partials(pieces, keep, blocks):
+        kept, given = half_expert(places, gates, pieces, keep, blocks, gate_up, down_proj)
+        return kept, send(given, cores)
+
+    def of(chain, operand, source):
+        return [(operand, i * half, half, source + i, chain * half) for i in (0, 1)]
+
+    own = partials([(0, 0, rows, 0, 0), (1, 0, rows, 1, 0)], rows, [tokens, send(tokens, cores)])
+    ring[0] = after(ring[0], own[0])
+
+    results = {}
+    for step in range(1, far):
+        swapped = [send(block, cores) for block in ring]
+        base = 2 + 4 * (step - 1)
+        blocks = ring + swapped
+        ring = [send(block if step < far - 1 else block[:half], forth) for block in ring]
+        if step < far - 1:
+            pieces = of(0, 0, base) + of(1, 1, base) + of(0, 2, base + 2) + of(1, 3, base + 2)
+            kept, given = partials(pieces, 2 * rows, blocks)
+            for c in chains:
+                results[step, c] = kept[c * rows : (c + 1) * rows], given[c * rows : (c + 1) * rows]
+            ring[0] = after(ring[0], kept)
+        else:
+            last = blocks
+    earlier = ring[0]
+    base = 2 + 4 * (far - 2)
+    for c in chains:
+        block = ring[c]
+        swapped = send(block, cores)
+        inputs = [after(last[c], earlier), last[2 + c]]
+        results[far - 1, c] = partials(of(c, 0, base) + of(c, 1, base + 2), rows, inputs)
+        swapped = after(swapped, results[far - 1, c][0])
+        pieces = [(0, 0, half, base + 4, c * half), (1, 0, half, base + 5, c * half)]
+        results[far, c] = partials(pieces, half, [block, swapped])
+        earlier = results[far, c][0]
+
+    sums = [None, None]
+    earlier = tokens
+    for step in range(far, 1, -1):
+        for c in chains:
+            kept, given = results[step, c]
+            value = total(after(kept, earlier), given)
+            if step == far - 1:
+                value = jnp.concatenate([value[:half] + total(sums[c]), value[half:]])
+            elif step < far - 1:
+                value = value + total(sums[c])
+            earlier = rounded(value)
+            sums[c] = send(earlier, back)
+    outs = []
+    for c in chains:
+        kept, given = results[1, c]
+        kept = after(kept, earlier)
+        mine = [part[c * half : (c + 1) * half] for part in own]
+        for low, pairs in ((half, home), (0, back)):
+            earlier = rounded(sum(total(term[low : low + half]) for term in (kept, given, sums[c])))
+            mine.append(send(earlier, pairs))
+        outs.append(rounded(total(*mine)))
+    return jnp.concatenate(outs)
+
+
 def solution(mesh):
     placed = (
         P(("groups", "blk"), None),
@@ -51,6 +226,12 @@
         P(None, "blk", None),
         P("blk", None),
     )
+
+    def per_device(tokens, expert_ids, route_gate, gate_up, down_proj):
+        experts = mesh.shape["blk"] // 2
+        body = by_tokens if experts <= 2 * expert_ids.shape[1] else by_slots
+        return body(tokens, expert_ids, route_gate, gate_up, down_proj)
+
     return jax.shard_map(
         per_device,
         mesh=mesh,

time: 352 us -> 124 us (0.35)
  the two profiles are of different devices: /device:TPU:13 before, /device:TPU:0 now
where the time goes in v3:
time: 124 us; the launch traced here: 123 us
  waiting for transfers between devices  55.7 us (45%)
  starting transfers between devices  28 us (23%)
  Pallas kernels  27.6 us (22%)
  local copies, waits for them, and re-layouts  8.42 us (7%)
  other arithmetic  3.48 us (3%)
    ppermute x36, waiting for transfers between devices, send(): return lax.ppermute(value, 'blk', pairs)  54.5 us
    pallas_call x7, Pallas kernels, half_expert(): pl.pallas_call(functools.partial(half_expert_kernel, tuple(pieces), keep)...  27.6 us
    ppermute x36, starting transfers between devices, send(): return lax.ppermute(value, 'blk', pairs)  23.3 us
    unnamed x11, local copies, waits for them, and re-layouts  5.74 us
    all_to_all x1, starting transfers between devices, by_tokens(): lax.all_to_all(jnp.repeat(weight, 2, axis=0), 'blk', split_axis=0, concat...  4.64 us
  transfers between devices with their start and end apart: 37, of which 20 were waited for; matrix products, arithmetic and copies ran while one was open for 3% of the time, Pallas kernels for 22%

profile of v3, /device:TPU:0, one launch (start us, length us, event | category | flops | bytes accessed | tf_op | source)
XLA Modules:
  0.0 123.5 jit_solution(15449277662653052195)
XLA Ops:
  1.1 3.1 %collective-permute-start.4 = (bf16[64,2048]{1,0:T(8,128)(2,1)S(1)}, bf16[64,2048]{1,0:T(8,128)(2,1)S(1)}, u32[]{:S(2)}, u32[]{:S(2)}) collective-permute-start(bf16[64,2048]{1,0:T(8,128)(2,1)S(1)} %get-tuple-element.74), channel_id=1, source_target_pairs={{0,4},{1,3},{4,8},{5,1},{8,12},{9,5},{12,14},{13,9},{14,10},{15,13... | collective-permute-start | bytes 786440 | tf_op jit(solution)/shard_map/ppermute | solution.py:141
  8.8 4.6 %all-to-all-start = ((f32[16,1,128]{2,1,0:T(1,128)}), f32[16,1,128]{2,1,0:T(1,128)S(1)}, u32[]{:S(2)}, u32[]{:S(2)}) async-start(f32[16,1,128]{2,1,0:T(1,128)} %bitcast.3), calls=%async_computation | async-start | bytes 16384 | tf_op jit(solution)/shard_map/all_to_all | solution.py:158
  14.2 2.7 %collective-permute-done.5 = bf16[64,2048]{1,0:T(8,128)(2,1)S(1)} collective-permute-done((bf16[64,2048]{1,0:T(8,128)(2,1)S(1)}, bf16[64,2048]{1,0:T(8,128)(2,1)S(1)}, u32[]{:S(2)}, u32[]{:S(2)}) %collective-permute-start.5) | collective-permute-done | bytes 262176 | tf_op jit(solution)/shard_map/ppermute | solution.py:141
  17.0 2.2 %collective-permute-start.9 = (bf16[128,2048]{1,0:T(8,128)(2,1)S(1)}, bf16[128,2048]{1,0:T(8,128)(2,1)S(1)}, u32[]{:S(2)}, u32[]{:S(2)}) collective-permute-start(bf16[128,2048]{1,0:T(8,128)(2,1)S(1)} %constant_dynamic-update-slice_fusion.refs_1_), channel_id=1, source_target_pairs={{0,4},{1,3},{4,8},{5,1},{8,12},{9,5},{12,14},{13,9},{14,10},{15,13... | collective-permute-start | bytes 1572872 | tf_op jit(solution)/shard_map/ppermute | solution.py:141
  20.4 2.8 %copy-done = bf16[2,768,2048]{2,1,0:T(8,128)(2,1)S(1)} copy-done((bf16[2,768,2048]{2,1,0:T(8,128)(2,1)S(1)}, bf16[2,768,2048]{2,1,0:T(8,128)(2,1)}, u32[]{:S(2)}) %copy-start) | copy-done | bytes 6291480
  26.1 3.2 %shard_map.64 = (bf16[128,2048]{1,0:T(8,128)(2,1)S(1)}, bf16[128,2048]{1,0:T(8,128)(2,1)S(1)}) custom-call(s32[16]{0:T(128)S(1)} %dynamic-slice_bitcast_fusion.sources_ref, f32[16,128]{1,0:T(8,128)S(1)} %bitcast.8, bf16[128,2048]{1,0:T(8,128)(2,1)S(1)} %copy-done.2, bf16[128,2048]{1,0:T(8,128)(2,1)S(1)} %collective-permute-done.refs_1_, ...), custom_call_target="tpu_custom_call" | custom-call | flops 2415919104 | bytes 11534336 | tf_op jit(solution)/shard_map/pallas_call | solution.py:102
  31.4 5.7 %shard_map.65 = (bf16[256,2048]{1,0:T(8,128)(2,1)S(1)}, bf16[256,2048]{1,0:T(8,128)(2,1)S(1)}) custom-call(s32[16]{0:T(128)S(1)} %dynamic-slice_bitcast_fusion.sources_ref, f32[16,128]{1,0:T(8,128)S(1)} %bitcast.9, bf16[128,2048]{1,0:T(8,128)(2,1)S(1)} %pad_maximum_fusion.refs_0_, bf16[128,2048]{1,0:T(8,128)(2,1)S(1)} %constant_dynamic-update-slice_fusion.refs_1_, ...), custom_call_target="tpu_custom_call" | custom-call | flops 4831838208 | bytes 13631488 | tf_op jit(solution)/shard_map/pallas_call | solution.py:102
  40.7 5.7 %shard_map.66 = (bf16[256,2048]{1,0:T(8,128)(2,1)S(1)}, bf16[256,2048]{1,0:T(8,128)(2,1)S(1)}) custom-call(s32[16]{0:T(128)S(1)} %dynamic-slice_bitcast_fusion.sources_ref, f32[16,128]{1,0:T(8,128)S(1)} %bitcast.10, bf16[128,2048]{1,0:T(8,128)(2,1)S(1)} %collective-permute-done.8.refs_0_, bf16[128,2048]{1,0:T(8,128)(2,1)S(1)} %collective-permute-done.9.refs_1_, ...), custom_call_target="tpu_custom_call" | custom-call | flops 4831838208 | bytes 13631488 | tf_op jit(solution)/shard_map/pallas_call | solution.py:102
  48.6 5.0 %collective-permute-done.12.refs_0_ = bf16[128,2048]{1,0:T(8,128)(2,1)S(1)} collective-permute-done((bf16[128,2048]{1,0:T(8,128)(2,1)S(1)}, bf16[128,2048]{1,0:T(8,128)(2,1)S(1)}, u32[]{:S(2)}, u32[]{:S(2)}) %collective-permute-start.12) | collective-permute-done | bytes 524320 | tf_op jit(solution)/shard_map/ppermute | solution.py:141
  54.4 2.0 %collective-permute-done.14.refs_0_ = bf16[64,2048]{1,0:T(8,128)(2,1)S(1)} collective-permute-done((bf16[64,2048]{1,0:T(8,128)(2,1)S(1)}, bf16[64,2048]{1,0:T(8,128)(2,1)S(1)}, u32[]{:S(2)}, u32[]{:S(2)}) %collective-permute-start.14) | collective-permute-done | bytes 262176 | tf_op jit(solution)/shard_map/ppermute | solution.py:141
  56.9 3.2 %shard_map.67 = (bf16[128,2048]{1,0:T(8,128)(2,1)S(1)}, bf16[128,2048]{1,0:T(8,128)(2,1)S(1)}) custom-call(s32[16]{0:T(128)S(1)} %dynamic-slice_bitcast_fusion.sources_ref, f32[16,128]{1,0:T(8,128)S(1)} %bitcast.11, bf16[128,2048]{1,0:T(8,128)(2,1)S(1)} %collective-permute-done.13.refs_0_, bf16[128,2048]{1,0:T(8,128)(2,1)S(1)} %collective-permute-done.16.refs_1_, ...), custom_call_target="tpu_custom_call" | custom-call | flops 2415919104 | bytes 11534336 | tf_op jit(solution)/shard_map/pallas_call | solution.py:102
  60.8 3.2 %shard_map.68 = (bf16[64,2048]{1,0:T(8,128)(2,1)S(1)}, bf16[64,2048]{1,0:T(8,128)(2,1)S(1)}) custom-call(s32[16]{0:T(128)S(1)} %dynamic-slice_bitcast_fusion.sources_ref, f32[16,128]{1,0:T(8,128)S(1)} %bitcast.12, bf16[64,2048]{1,0:T(8,128)(2,1)S(1)} %collective-permute-done.14.refs_0_, bf16[64,2048]{1,0:T(8,128)(2,1)S(1)} %collective-permute-done.15.refs_1_, ...), custom_call_target="tpu_custom_call" | custom-call | flops 1207959552 | bytes 10485760 | tf_op jit(solution)/shard_map/pallas_call | solution.py:102
  64.5 3.2 %shard_map.69 = (bf16[128,2048]{1,0:T(8,128)(2,1)S(1)}, bf16[128,2048]{1,0:T(8,128)(2,1)S(1)}) custom-call(s32[16]{0:T(128)S(1)} %dynamic-slice_bitcast_fusion.sources_ref, f32[16,128]{1,0:T(8,128)S(1)} %bitcast.13, bf16[128,2048]{1,0:T(8,128)(2,1)S(1)} %collective-permute-done.12.refs_0_, bf16[128,2048]{1,0:T(8,128)(2,1)S(1)} %collective-permute-done.17.refs_1_, ...), custom_call_target="tpu_custom_call" | custom-call | flops 2415919104 | bytes 11534336 | tf_op jit(solution)/shard_map/pallas_call | solution.py:102
  67.8 3.2 %shard_map.70 = (bf16[64,2048]{1,0:T(8,128)(2,1)S(1)}, bf16[64,2048]{1,0:T(8,128)(2,1)S(1)}) custom-call(s32[16]{0:T(128)S(1)} %dynamic-slice_bitcast_fusion.sources_ref, f32[16,128]{1,0:T(8,128)S(1)} %bitcast.14, bf16[64,2048]{1,0:T(8,128)(2,1)S(1)} %collective-permute-done.18.refs_0_, bf16[64,2048]{1,0:T(8,128)(2,1)S(1)} %collective-permute-done.19.refs_1_, ...), custom_call_target="tpu_custom_call" | custom-call | flops 1207959552 | bytes 10485760 | tf_op jit(solution)/shard_map/pallas_call | solution.py:102
  74.1 5.6 %collective-permute-done.23 = bf16[64,2048]{1,0:T(8,128)(2,1)S(1)} collective-permute-done((bf16[64,2048]{1,0:T(8,128)(2,1)S(1)}, bf16[64,2048]{1,0:T(8,128)(2,1)S(1)}, u32[]{:S(2)}, u32[]{:S(2)}) %collective-permute-start.23) | collective-permute-done | bytes 262176 | tf_op jit(solution)/shard_map/ppermute | solution.py:141
  82.1 4.0 %collective-permute-done.25 = bf16[64,2048]{1,0:T(8,128)(2,1)S(1)} collective-permute-done((bf16[64,2048]{1,0:T(8,128)(2,1)S(1)}, bf16[64,2048]{1,0:T(8,128)(2,1)S(1)}, u32[]{:S(2)}, u32[]{:S(2)}) %collective-permute-start.25) | collective-permute-done | bytes 262176 | tf_op jit(solution)/shard_map/ppermute | solution.py:141
  86.9 4.8 %collective-permute-done.27 = bf16[128,2048]{1,0:T(8,128)(2,1)S(1)} collective-permute-done((bf16[128,2048]{1,0:T(8,128)(2,1)S(1)}, bf16[128,2048]{1,0:T(8,128)(2,1)S(1)}, u32[]{:S(2)}, u32[]{:S(2)}) %collective-permute-start.27) | collective-permute-done | bytes 524320 | tf_op jit(solution)/shard_map/ppermute | solution.py:141
  92.6 4.8 %collective-permute-done.28 = bf16[128,2048]{1,0:T(8,128)(2,1)S(1)} collective-permute-done((bf16[128,2048]{1,0:T(8,128)(2,1)S(1)}, bf16[128,2048]{1,0:T(8,128)(2,1)S(1)}, u32[]{:S(2)}, u32[]{:S(2)}) %collective-permute-start.28) | collective-permute-done | bytes 524320 | tf_op jit(solution)/shard_map/ppermute | solution.py:141
  98.3 4.6 %collective-permute-done.30 = bf16[128,2048]{1,0:T(8,128)(2,1)S(1)} collective-permute-done((bf16[128,2048]{1,0:T(8,128)(2,1)S(1)}, bf16[128,2048]{1,0:T(8,128)(2,1)S(1)}, u32[]{:S(2)}, u32[]{:S(2)}) %collective-permute-start.30) | collective-permute-done | bytes 524320 | tf_op jit(solution)/shard_map/ppermute | solution.py:141
  103.2 5.4 %collective-permute-done.33 = bf16[128,2048]{1,0:T(8,128)(2,1)S(1)} collective-permute-done((bf16[128,2048]{1,0:T(8,128)(2,1)S(1)}, bf16[128,2048]{1,0:T(8,128)(2,1)S(1)}, u32[]{:S(2)}, u32[]{:S(2)}) %collective-permute-start.33) | collective-permute-done | bytes 524320 | tf_op jit(solution)/shard_map/ppermute | solution.py:141
  112.4 2.3 %collective-permute-done.34 = bf16[64,2048]{1,0:T(8,128)(2,1)S(1)} collective-permute-done((bf16[64,2048]{1,0:T(8,128)(2,1)S(1)}, bf16[64,2048]{1,0:T(8,128)(2,1)S(1)}, u32[]{:S(2)}, u32[]{:S(2)}) %collective-permute-start.34) | collective-permute-done | bytes 262176 | tf_op jit(solution)/shard_map/ppermute | solution.py:141
  114.7 1.9 %collective-permute-done.35 = bf16[64,2048]{1,0:T(8,128)(2,1)S(1)} collective-permute-done((bf16[64,2048]{1,0:T(8,128)(2,1)S(1)}, bf16[64,2048]{1,0:T(8,128)(2,1)S(1)}, u32[]{:S(2)}, u32[]{:S(2)}) %collective-permute-start.35) | collective-permute-done | bytes 262176 | tf_op jit(solution)/shard_map/ppermute | solution.py:141
  116.6 3.7 %collective-permute-done.31 = bf16[64,2048]{1,0:T(8,128)(2,1)S(1)} collective-permute-done((bf16[64,2048]{1,0:T(8,128)(2,1)S(1)}, bf16[64,2048]{1,0:T(8,128)(2,1)S(1)}, u32[]{:S(2)}, u32[]{:S(2)}) %collective-permute-start.31) | collective-permute-done | bytes 262176 | tf_op jit(solution)/shard_map/ppermute | solution.py:141
  120.3 1.9 %collective-permute-done.32 = bf16[64,2048]{1,0:T(8,128)(2,1)S(1)} collective-permute-done((bf16[64,2048]{1,0:T(8,128)(2,1)S(1)}, bf16[64,2048]{1,0:T(8,128)(2,1)S(1)}, u32[]{:S(2)}, u32[]{:S(2)}) %collective-permute-start.32) | collective-permute-done | bytes 262176 | tf_op jit(solution)/shard_map/ppermute | solution.py:141
  (95 shorter events, 34.2 us)
Async XLA Ops:
  1.1 13.1 %collective-permute-start.4 = (bf16[64,2048]{1,0:T(8,128)(2,1)S(1)}, bf16[64,2048]{1,0:T(8,128)(2,1)S(1)}, u32[]{:S(2)}, u32[]{:S(2)}) collective-permute-start(bf16[64,2048]{1,0:T(8,128)(2,1)S(1)} %get-tuple-element.74), channel_id=1, source_target_pairs={{0,4},{1,3},{4,8},{5,1},{8,12},{9,5},{12,14},{13,9},{14,10},{15,13... | collective-permute-start | bytes 786440 | tf_op jit(solution)/shard_map/ppermute | solution.py:141
  4.2 16.3 %collective-permute-start = (bf16[128,2048]{1,0:T(8,128)(2,1)}, bf16[128,2048]{1,0:T(8,128)(2,1)S(1)}, u32[]{:S(2)}, u32[]{:S(2)}) collective-permute-start(bf16[128,2048]{1,0:T(8,128)(2,1)} %refs_0_.1), channel_id=1, source_target_pairs={{0,1},{1,0},{4,5},{5,4},{8,9},{9,8},{12,13},{13,12},{14,15},{15,14... | collective-permute-start | bytes 1572872 | tf_op jit(solution)/shard_map/ppermute | solution.py:141
  4.2 15.0 %collective-permute-start.2 = (bf16[64,2048]{1,0:T(8,128)(2,1)S(1)}, bf16[64,2048]{1,0:T(8,128)(2,1)S(1)}, u32[]{:S(2)}, u32[]{:S(2)}) collective-permute-start(bf16[64,2048]{1,0:T(8,128)(2,1)S(1)} %get-tuple-element.73), channel_id=1, source_target_pairs={{0,4},{1,3},{4,8},{5,1},{8,12},{9,5},{12,14},{13,9},{14,10},{15,13... | collective-permute-start | bytes 786440 | tf_op jit(solution)/shard_map/ppermute | solution.py:141
  5.7 13.4 %collective-permute-start.3 = (bf16[64,2048]{1,0:T(8,128)(2,1)S(1)}, bf16[64,2048]{1,0:T(8,128)(2,1)S(1)}, u32[]{:S(2)}, u32[]{:S(2)}) collective-permute-start(bf16[64,2048]{1,0:T(8,128)(2,1)S(1)} %get-tuple-element.73), channel_id=1, source_target_pairs={{0,3},{1,4},{4,1},{5,8},{8,5},{9,12},{12,9},{13,14},{14,13},{15,10... | collective-permute-start | bytes 786440 | tf_op jit(solution)/shard_map/ppermute | solution.py:141
  6.1 10.7 %collective-permute-start.5 = (bf16[64,2048]{1,0:T(8,128)(2,1)S(1)}, bf16[64,2048]{1,0:T(8,128)(2,1)S(1)}, u32[]{:S(2)}, u32[]{:S(2)}) collective-permute-start(bf16[64,2048]{1,0:T(8,128)(2,1)S(1)} %get-tuple-element.74), channel_id=1, source_target_pairs={{0,3},{1,4},{4,1},{5,8},{8,5},{9,12},{12,9},{13,14},{14,13},{15,10... | collective-permute-start | bytes 786440 | tf_op jit(solution)/shard_map/ppermute | solution.py:141
  8.8 11.6 %all-to-all-start = ((f32[16,1,128]{2,1,0:T(1,128)}), f32[16,1,128]{2,1,0:T(1,128)S(1)}, u32[]{:S(2)}, u32[]{:S(2)}) async-start(f32[16,1,128]{2,1,0:T(1,128)} %bitcast.3), calls=%async_computation | async-start | bytes 16384 | tf_op jit(solution)/shard_map/all_to_all | solution.py:158
  16.9 13.4 %collective-permute-start.7 = (bf16[128,2048]{1,0:T(8,128)(2,1)S(1)}, bf16[128,2048]{1,0:T(8,128)(2,1)S(1)}, u32[]{:S(2)}, u32[]{:S(2)}) collective-permute-start(bf16[128,2048]{1,0:T(8,128)(2,1)S(1)} %constant_dynamic-update-slice_fusion.refs_1_), channel_id=1, source_target_pairs={{0,1},{1,0},{4,5},{5,4},{8,9},{9,8},{12,13},{13,12},{14,15},{15,14... | collective-permute-start | bytes 1572872 | tf_op jit(solution)/shard_map/ppermute | solution.py:141
  17.0 13.1 %collective-permute-start.9 = (bf16[128,2048]{1,0:T(8,128)(2,1)S(1)}, bf16[128,2048]{1,0:T(8,128)(2,1)S(1)}, u32[]{:S(2)}, u32[]{:S(2)}) collective-permute-start(bf16[128,2048]{1,0:T(8,128)(2,1)S(1)} %constant_dynamic-update-slice_fusion.refs_1_), channel_id=1, source_target_pairs={{0,4},{1,3},{4,8},{5,1},{8,12},{9,5},{12,14},{13,9},{14,10},{15,13... | collective-permute-start | bytes 1572872 | tf_op jit(solution)/shard_map/ppermute | solution.py:141
  29.5 9.2 %collective-permute-start.8 = (bf16[128,2048]{1,0:T(8,128)(2,1)S(1)}, bf16[128,2048]{1,0:T(8,128)(2,1)S(1)}, u32[]{:S(2)}, u32[]{:S(2)}) collective-permute-start(bf16[128,2048]{1,0:T(8,128)(2,1)S(1)} %pad_maximum_fusion.refs_0_), channel_id=1, source_target_pairs={{0,4},{1,3},{4,8},{5,1},{8,12},{9,5},{12,14},{13,9},{14,10},{15,13... | collective-permute-start | bytes 1572872 | tf_op jit(solution)/shard_map/ppermute | solution.py:141
  30.1 10.6 %collective-permute-start.11 = (bf16[128,2048]{1,0:T(8,128)(2,1)S(1)}, bf16[128,2048]{1,0:T(8,128)(2,1)S(1)}, u32[]{:S(2)}, u32[]{:S(2)}) collective-permute-start(bf16[128,2048]{1,0:T(8,128)(2,1)S(1)} %collective-permute-done.9.refs_1_), channel_id=1, source_target_pairs={{0,1},{1,0},{4,5},{5,4},{8,9},{9,8},{12,13},{13,12},{14,15},{15,14... | collective-permute-start | bytes 1572872 | tf_op jit(solution)/shard_map/ppermute | solution.py:141
  38.7 9.2 %collective-permute-start.13 = (bf16[128,2048]{1,0:T(8,128)(2,1)S(1)}, bf16[128,2048]{1,0:T(8,128)(2,1)S(1)}, u32[]{:S(2)}, u32[]{:S(2)}) collective-permute-start(bf16[128,2048]{1,0:T(8,128)(2,1)S(1)} %collective-permute-done.8.refs_0_), channel_id=1, source_target_pairs={{0,4},{1,3},{4,8},{5,1},{8,12},{9,5},{12,14},{13,9},{14,10},{15,13... | collective-permute-start | bytes 1572872 | tf_op jit(solution)/shard_map/ppermute | solution.py:141
  39.3 14.2 %collective-permute-start.12 = (bf16[128,2048]{1,0:T(8,128)(2,1)S(1)}, bf16[128,2048]{1,0:T(8,128)(2,1)S(1)}, u32[]{:S(2)}, u32[]{:S(2)}) collective-permute-start(bf16[128,2048]{1,0:T(8,128)(2,1)S(1)} %collective-permute-done.9.refs_1_), channel_id=1, source_target_pairs={{0,4},{1,3},{4,8},{5,1},{8,12},{9,5},{12,14},{13,9},{14,10},{15,13... | collective-permute-start | bytes 1572872 | tf_op jit(solution)/shard_map/ppermute | solution.py:141
  47.9 8.9 %collective-permute-start.16 = (bf16[128,2048]{1,0:T(8,128)(2,1)S(1)}, bf16[128,2048]{1,0:T(8,128)(2,1)S(1)}, u32[]{:S(2)}, u32[]{:S(2)}) collective-permute-start(bf16[128,2048]{1,0:T(8,128)(2,1)S(1)} %collective-permute-done.13.refs_0_), channel_id=1, source_target_pairs={{0,1},{1,0},{4,5},{5,4},{8,9},{9,8},{12,13},{13,12},{14,15},{15,14... | collective-permute-start | bytes 1572872 | tf_op jit(solution)/shard_map/ppermute | solution.py:141
  48.0 8.4 %collective-permute-start.14 = (bf16[64,2048]{1,0:T(8,128)(2,1)S(1)}, bf16[64,2048]{1,0:T(8,128)(2,1)S(1)}, u32[]{:S(2)}, u32[]{:S(2)}) collective-permute-start(bf16[64,2048]{1,0:T(8,128)(2,1)S(1)} %slice.105), channel_id=1, source_target_pairs={{0,4},{1,3},{4,8},{5,1},{8,12},{9,5},{12,14},{13,9},{14,10},{15,13... | collective-permute-start | bytes 786440 | tf_op jit(solution)/shard_map/ppermute | solution.py:141
  53.6 10.5 %collective-permute-start.17 = (bf16[128,2048]{1,0:T(8,128)(2,1)S(1)}, bf16[128,2048]{1,0:T(8,128)(2,1)S(1)}, u32[]{:S(2)}, u32[]{:S(2)}) collective-permute-start(bf16[128,2048]{1,0:T(8,128)(2,1)S(1)} %collective-permute-done.12.refs_0_), channel_id=1, source_target_pairs={{0,1},{1,0},{4,5},{5,4},{8,9},{9,8},{12,13},{13,12},{14,15},{15,14... | collective-permute-start | bytes 1572872 | tf_op jit(solution)/shard_map/ppermute | solution.py:141
  56.4 56.0 %collective-permute-start.1 = (bf16[128,2048]{1,0:T(8,128)(2,1)S(1)}, bf16[128,2048]{1,0:T(8,128)(2,1)S(1)}, u32[]{:S(2)}, u32[]{:S(2)}) collective-permute-start(bf16[128,2048]{1,0:T(8,128)(2,1)S(1)} %get-tuple-element.35), channel_id=1, source_target_pairs={{0,1},{1,0},{4,5},{5,4},{8,9},{9,8},{12,13},{13,12},{14,15},{15,14... | collective-permute-start | bytes 1572872 | tf_op jit(solution)/shard_map/ppermute | solution.py:141
  56.9 41.4 %collective-permute-start.29 = (bf16[256,2048]{1,0:T(8,128)(2,1)S(1)}, bf16[256,2048]{1,0:T(8,128)(2,1)S(1)}, u32[]{:S(2)}, u32[]{:S(2)}) collective-permute-start(bf16[256,2048]{1,0:T(8,128)(2,1)S(1)} %get-tuple-element.61), channel_id=1, source_target_pairs={{0,1},{1,0},{4,5},{5,4},{8,9},{9,8},{12,13},{13,12},{14,15},{15,14... | collective-permute-start | bytes 3145736 | tf_op jit(solution)/shard_map/ppermute | solution.py:141
  60.2 26.7 %collective-permute-start.26 = (bf16[256,2048]{1,0:T(8,128)(2,1)S(1)}, bf16[256,2048]{1,0:T(8,128)(2,1)S(1)}, u32[]{:S(2)}, u32[]{:S(2)}) collective-permute-start(bf16[256,2048]{1,0:T(8,128)(2,1)S(1)} %get-tuple-element.58), channel_id=1, source_target_pairs={{0,1},{1,0},{4,5},{5,4},{8,9},{9,8},{12,13},{13,12},{14,15},{15,14... | collective-permute-start | bytes 3145736 | tf_op jit(solution)/shard_map/ppermute | solution.py:141
  80.4 11.3 %collective-permute-start.27 = (bf16[128,2048]{1,0:T(8,128)(2,1)S(1)}, bf16[128,2048]{1,0:T(8,128)(2,1)S(1)}, u32[]{:S(2)}, u32[]{:S(2)}) collective-permute-start(bf16[128,2048]{1,0:T(8,128)(2,1)S(1)} %pad_maximum_fusion.1), channel_id=1, source_target_pairs={{0,2},{1,5},{4,0},{5,9},{8,4},{9,13},{12,8},{13,15},{14,12},{15,11... | collective-permute-start | bytes 1572872 | tf_op jit(solution)/shard_map/ppermute | solution.py:141
  86.2 11.1 %collective-permute-start.28 = (bf16[128,2048]{1,0:T(8,128)(2,1)S(1)}, bf16[128,2048]{1,0:T(8,128)(2,1)S(1)}, u32[]{:S(2)}, u32[]{:S(2)}) collective-permute-start(bf16[128,2048]{1,0:T(8,128)(2,1)S(1)} %pad_maximum_fusion.2), channel_id=1, source_target_pairs={{0,2},{1,5},{4,0},{5,9},{8,4},{9,13},{12,8},{13,15},{14,12},{15,11... | collective-permute-start | bytes 1572872 | tf_op jit(solution)/shard_map/ppermute | solution.py:141
  92.0 11.0 %collective-permute-start.30 = (bf16[128,2048]{1,0:T(8,128)(2,1)S(1)}, bf16[128,2048]{1,0:T(8,128)(2,1)S(1)}, u32[]{:S(2)}, u32[]{:S(2)}) collective-permute-start(bf16[128,2048]{1,0:T(8,128)(2,1)S(1)} %add_convert_fusion.1), channel_id=1, source_target_pairs={{0,2},{1,5},{4,0},{5,9},{8,4},{9,13},{12,8},{13,15},{14,12},{15,11... | collective-permute-start | bytes 1572872 | tf_op jit(solution)/shard_map/ppermute | solution.py:141
  97.6 11.0 %collective-permute-start.33 = (bf16[128,2048]{1,0:T(8,128)(2,1)S(1)}, bf16[128,2048]{1,0:T(8,128)(2,1)S(1)}, u32[]{:S(2)}, u32[]{:S(2)}) collective-permute-start(bf16[128,2048]{1,0:T(8,128)(2,1)S(1)} %add_convert_fusion), channel_id=1, source_target_pairs={{0,2},{1,5},{4,0},{5,9},{8,4},{9,13},{12,8},{13,15},{14,12},{15,11... | collective-permute-start | bytes 1572872 | tf_op jit(solution)/shard_map/ppermute | solution.py:141
  109.5 10.8 %collective-permute-start.31 = (bf16[64,2048]{1,0:T(8,128)(2,1)S(1)}, bf16[64,2048]{1,0:T(8,128)(2,1)S(1)}, u32[]{:S(2)}, u32[]{:S(2)}) collective-permute-start(bf16[64,2048]{1,0:T(8,128)(2,1)S(1)} %get-tuple-element.63), channel_id=1, source_target_pairs={{0,3},{1,4},{4,1},{5,8},{8,5},{9,12},{12,9},{13,14},{14,13},{15,10... | collective-permute-start | bytes 786440 | tf_op jit(solution)/shard_map/ppermute | solution.py:141
  110.9 11.3 %collective-permute-start.32 = (bf16[64,2048]{1,0:T(8,128)(2,1)S(1)}, bf16[64,2048]{1,0:T(8,128)(2,1)S(1)}, u32[]{:S(2)}, u32[]{:S(2)}) collective-permute-start(bf16[64,2048]{1,0:T(8,128)(2,1)S(1)} %get-tuple-element.64), channel_id=1, source_target_pairs={{0,2},{1,5},{4,0},{5,9},{8,4},{9,13},{12,8},{13,15},{14,12},{15,11... | collective-permute-start | bytes 786440 | tf_op jit(solution)/shard_map/ppermute | solution.py:141
  (18 other events, 109.1 us)

commit v4 on v0

--- a/solution.py
+++ b/solution.py
@@ -1,6 +1,11 @@
+import functools
+
 import jax
 import jax.numpy as jnp
+import numpy as np
 from jax import lax
+from jax.experimental import pallas as pl
+from jax.experimental.pallas import tpu as pltpu
 from jax.sharding import PartitionSpec as P
 
 
@@ -12,7 +17,7 @@
     return jnp.dot(hidden, down_proj, preferred_element_type=jnp.float32).astype(jnp.bfloat16)
 
 
-def per_device(tokens, expert_ids, route_gate, gate_up, down_proj):
+def by_slots(tokens, expert_ids, route_gate, gate_up, down_proj):
     tok_count, per_token = expert_ids.shape
     feature_width = tokens.shape[1]
     devices = lax.axis_size("blk")
@@ -43,6 +48,221 @@
     return jnp.sum(weighted, axis=1).astype(jnp.bfloat16)
 
 
+def snake(chips):
+    return list(range(0, chips, 2)) + list(range(chips - 1, 0, -2))
+
+
+def sources(chips):
+    order = snake(chips)
+    table = np.zeros((2 * chips, 2 + 2 * chips), np.int32)
+    for place in range(chips):
+        for core in (0, 1):
+            turn = 1 - 2 * core
+            row = [(0, core), (0, 1 - core)]
+            for step in range(1, chips // 2 + 1):
+                row += [(-step, core), (-step, 1 - core), (step, 1 - core), (step, core)]
+            table[2 * order[place] + core] = [2 * order[(place + turn * d) % chips] + c for d, c in row]
+    return table
+
+
+def half_expert_kernel(pieces, load, sources_ref, gates_ref, *refs):
+    blocks, refs = refs[: len(pieces)], refs[len(pieces) :]
+    if load:
+        gate_up_far, down_far, out_keep, out_give, gate_up_ref, down_ref, rows, hidden, arrived = refs
+    else:
+        gate_up_ref, down_ref, out_keep, out_give, rows, hidden = refs
+    units, width = down_ref.shape
+    tile = 256 if units % 256 == 0 else units
+    tiles = units // tile
+    copies = []
+    if load:
+        for t in range(tiles):
+            near = pl.ds(t * tile, tile)
+            copies.append(pltpu.make_async_copy(gate_up_far.at[:, near], gate_up_ref.at[:, near], arrived.at[t]))
+        copies.append(pltpu.make_async_copy(down_far, down_ref, arrived.at[tiles]))
+        for copy in copies:
+            copy.start()
+
+    weights = []
+    at = 0
+    for block, (source, token) in zip(blocks, pieces):
+        count = block.shape[0]
+        rows[at : at + count, :] = block[...]
+        at += count
+        line = gates_ref[pl.ds(sources_ref[source], 1), :]
+        column = jnp.broadcast_to(line, (8, line.shape[1])).T[:, :1]
+        weights.append(column[token : token + count])
+    weight = jnp.concatenate(weights)
+
+    contract = (((1,), (1,)), ((), ()))
+    taken = rows[...]
+    for t in range(tiles):
+        if load:
+            copies[t].wait()
+        near = slice(t * tile, (t + 1) * tile)
+        gating = lax.dot_general(taken, gate_up_ref[0, near], contract, preferred_element_type=jnp.float32)
+        lifted = lax.dot_general(taken, gate_up_ref[1, near], contract, preferred_element_type=jnp.float32)
+        hidden[:, near] = (gating / (1.0 + jnp.exp(-gating)) * lifted).astype(jnp.bfloat16)
+    if load:
+        copies[tiles].wait()
+    inner = hidden[...]
+    keep = out_keep.shape[0]
+    tile = 512 if width % 512 == 0 else width
+    for low in range(0, width, tile):
+        product = jnp.dot(inner, down_ref[:, low : low + tile], preferred_element_type=jnp.float32) * weight
+        product = product.astype(jnp.bfloat16)
+        out_keep[:, low : low + tile] = product[:keep]
+        out_give[:, low : low + tile] = product[keep:]
+
+
+def half_expert(places, gates, pieces, blocks, gate_up, down_proj, load=False):
+    height = sum(block.shape[0] for block in blocks)
+    units, width = down_proj.shape
+    whole = pl.BlockSpec(memory_space=pltpu.VMEM)
+    out = jax.ShapeDtypeStruct((height // 2, width), jnp.bfloat16)
+    weights = [jax.ShapeDtypeStruct(array.shape, array.dtype) for array in (gate_up, down_proj)] if load else []
+    scratch = [pltpu.VMEM((height, width), jnp.bfloat16), pltpu.VMEM((height, units), jnp.bfloat16)]
+    if load:
+        scratch.append(pltpu.SemaphoreType.DMA((units // 256 + 1 if units % 256 == 0 else 2,)))
+    return pl.pallas_call(
+        functools.partial(half_expert_kernel, tuple(pieces), load),
+        out_shape=[out, out] + weights,
+        in_specs=[pl.BlockSpec(memory_space=pltpu.SMEM)]
+        + [whole] * (len(blocks) + 1)
+        + [pl.BlockSpec(memory_space=pltpu.HBM) if load else whole] * 2,
+        out_specs=[whole] * (2 + len(weights)),
+        scratch_shapes=scratch,
+        compiler_params=pltpu.CompilerParams(vmem_limit_bytes=(34 if load else 14) << 20),
+        cost_estimate=pl.CostEstimate(
+            flops=6 * height * units * width,
+            bytes_accessed=6 * units * width + 4 * height * width,
+            transcendentals=height * units,
+        ),
+    )(places, gates, *blocks, gate_up, down_proj)
+
+
+def sum_kernel(*refs):
+    *terms, out = refs
+    out[...] = sum(term[...].astype(jnp.float32) for term in terms)
+
+
+def summed(*terms):
+    whole = pl.BlockSpec(memory_space=pltpu.VMEM)
+    size = terms[0].size
+    return pl.pallas_call(
+        sum_kernel,
+        out_shape=jax.ShapeDtypeStruct(terms[0].shape, jnp.float32),
+        in_specs=[whole] * len(terms),
+        out_specs=whole,
+        compiler_params=pltpu.CompilerParams(vmem_limit_bytes=8 << 20),
+        cost_estimate=pl.CostEstimate(flops=size * 20000, bytes_accessed=size * 100, transcendentals=0),
+    )(*terms)
+
+
+def by_tokens(tokens, expert_ids, route_gate, gate_up, down_proj):
+    chips = lax.axis_size("blk") // 2
+    order, far = snake(chips), chips // 2
+    rows = tokens.shape[0]
+    half = rows // 2
+    chains = (0, 1)
+    forth, back, across, cores = [], [], [], []
+    for place in range(chips):
+        for core in (0, 1):
+            device = 2 * order[place] + core
+            ahead, behind = order[(place + 1 - 2 * core) % chips], order[(place - 1 + 2 * core) % chips]
+            forth.append((device, 2 * ahead + core))
+            back.append((device, 2 * behind + core))
+            across.append((device, 2 * behind + 1 - core))
+            cores.append((device, device ^ 1))
+
+    def send(value, pairs):
+        return lax.ppermute(value, "blk", pairs)
+
+    def total(*terms):
+        return sum(term.astype(jnp.float32) for term in terms)
+
+    def rounded(value):
+        return value.astype(jnp.bfloat16)
+
+    def after(value, *earlier):
+        return lax.optimization_barrier((value, *earlier))[0]
+
+    ring = [send(tokens, forth), send(tokens, across)]
+    other = send(tokens, cores)
+
+    places = lax.dynamic_index_in_dim(jnp.asarray(sources(chips)), lax.axis_index("blk"), 0, keepdims=False)
+    chosen = jnp.arange(chips, dtype=jnp.int32)[:, None, None] == expert_ids.T[None]
+    weight = jnp.sum(jnp.where(chosen, route_gate.T[None], 0.0), axis=1)
+    gates = lax.all_to_all(jnp.repeat(weight, 2, axis=0), "blk", split_axis=0, concat_axis=0, tiled=True)
+    gates = gates.reshape(-1, rows)
+    ring[0] = after(ring[0], gates)
+
+    near = None
+    results = {}
+    for step in range(1, far - 1):
+        swapped = [send(block, cores) for block in ring]
+        pieces = [(4 * step - 2 + i, 0) for i in range(4)]
+        blocks = ring + swapped
+        ring = [send(block, forth) for block in ring]
+        if near is None:
+            kept, given, *near = half_expert(places, gates, pieces, blocks, gate_up, down_proj, load=True)
+        else:
+            kept, given = half_expert(places, gates, pieces, blocks, *near)
+        given = send(given, cores)
+        for c in chains:
+            results[step, c] = kept[c * rows : (c + 1) * rows], given[c * rows : (c + 1) * rows]
+        ring[0] = after(ring[0], kept)
+
+    first, second = slice(0, half), slice(half, rows)
+    swapped = [send(block, cores) for block in ring]
+    blocks = ring + swapped
+    ring = [send(ring[0][first], forth), send(ring[1][second], forth)]
+    for c in chains:
+        pieces = [(4 * far - 6 + c, 0), (4 * far - 4 + c, 0)]
+        mine, theirs = half_expert(places, gates, pieces, [blocks[c], blocks[2 + c]], *near)
+        results[far - 1, c] = mine, send(theirs, cores)
+        if c == 0:
+            ring[0] = after(ring[0], mine)
+            blocks[1] = after(blocks[1], ring[0])
+    swapped = [send(block, cores) for block in ring]
+    mine, theirs = results[far - 1, 0]
+    earlier = rounded(total(after(mine, results[far - 1, 1][0])[second], theirs[second]))
+    early = [send(earlier, back)]
+    swapped[0] = after(swapped[0], earlier)
+    base = 4 * far - 2
+    pieces = [(base, 0), (base + 1, half), (base + 2, 0), (base + 3, half)]
+    kept, given = half_expert(places, gates, pieces, ring + swapped, *near)
+    given = send(given, cores)
+    mine, theirs = results[far - 1, 1]
+    earlier = rounded(total(after(mine, kept)[first], theirs[first]))
+    early.append(send(earlier, back))
+
+    late = []
+    for part in (first, second):
+        earlier = rounded(total(after(kept[part], earlier, early[0]), given[part]))
+        late.append(send(earlier, back))
+    sums = []
+    for c in chains:
+        mine, theirs = results[far - 1, c]
+        part = (first, second)[c]
+        earlier = rounded(total(after(mine[part], earlier, early[1]), theirs[part], late[c]))
+        pair = [send(earlier, back), early[c]]
+        sums.append(jnp.concatenate(pair if c == 0 else pair[::-1]))
+    for step in range(far - 2, 1, -1):
+        for c in chains:
+            mine, theirs = results[step, c]
+            earlier = rounded(total(after(mine, earlier), theirs, sums[c]))
+            sums[c] = send(earlier, back)
+    kept, given = half_expert(places, gates, [(0, 0), (1, 0)], [after(tokens, earlier), other], *near)
+    given = send(given, cores)
+    earlier = kept
+    for c, pairs in zip(chains, (back, across)):
+        mine, theirs = results[1, c]
+        earlier = rounded(total(after(mine, earlier), theirs, sums[c]))
+        sums[c] = send(earlier, pairs)
+    return rounded(total(summed(kept, given, sums[0]), sums[1]))
+
+
 def solution(mesh):
     placed = (
         P(("groups", "blk"), None),
@@ -51,6 +271,12 @@
         P(None, "blk", None),
         P("blk", None),
     )
+
+    def per_device(tokens, expert_ids, route_gate, gate_up, down_proj):
+        experts = mesh.shape["blk"] // 2
+        body = by_tokens if experts <= 2 * expert_ids.shape[1] else by_slots
+        return body(tokens, expert_ids, route_gate, gate_up, down_proj)
+
     return jax.shard_map(
         per_device,
         mesh=mesh,

time: 352 us -> 115 us (0.33)
  the two profiles are of different devices: /device:TPU:13 before, /device:TPU:0 now
where the time goes in v4:
time: 115 us; the launch traced here: 113 us
  waiting for transfers between devices  49.7 us (43%)
  Pallas kernels  26.8 us (23%)
  starting transfers between devices  15.3 us (13%)
  blocking collectives  15 us (13%)
  other arithmetic  3.06 us (3%)
  local copies, waits for them, and re-layouts  2.84 us (2%)
    ppermute x33, waiting for transfers between devices, send(): return lax.ppermute(value, 'blk', pairs)  49.7 us
    pallas_call x6, Pallas kernels, half_expert(): pl.pallas_call(functools.partial(half_expert_kernel, tuple(pieces), load)...  26.6 us
    ppermute x33, starting transfers between devices, send(): return lax.ppermute(value, 'blk', pairs)  15.3 us
    all_to_all x1, blocking collectives, by_tokens(): lax.all_to_all(jnp.repeat(weight, 2, axis=0), 'blk', split_axis=0, concat...  15 us
    convert_element_type x11, other arithmetic, rounded(): return value.astype(jnp.bfloat16)  2.35 us
  transfers between devices with their start and end apart: 33, of which 17 were waited for; matrix products, arithmetic and copies ran while one was open for 3% of the time, Pallas kernels for 24%

profile of v4, /device:TPU:0, one launch (start us, length us, event | category | flops | bytes accessed | tf_op | source)
XLA Modules:
  0.0 112.9 jit_solution(3196697932533666729)
XLA Ops:
  0.0 3.0 %collective-permute-start = (bf16[128,2048]{1,0:T(8,128)(2,1)}, bf16[128,2048]{1,0:T(8,128)(2,1)S(1)}, u32[]{:S(2)}, u32[]{:S(2)}) collective-permute-start(bf16[128,2048]{1,0:T(8,128)(2,1)} %refs_0_), channel_id=1, source_target_pairs={{0,4},{1,3},{4,8},{5,1},{8,12},{9,5},{12,14},{13,9},{14,10},{15,13... | collective-permute-start | bytes 1572872 | tf_op jit(solution)/shard_map/ppermute | solution.py:179
  4.4 15.0 %all_to_all.11 = f32[16,1,128]{2,1,0:T(1,128)S(1)} all-to-all(f32[16,1,128]{2,1,0:T(1,128)S(1)} %bitcast.12), channel_id=1, replica_groups=mesh['groups'=2,'blk'=16] {'blk'}, dimensions={0} | all-to-all | bytes 16384 | tf_op jit(solution)/shard_map/all_to_all | solution.py:196
  22.1 1.9 %copy-done.1 = bf16[768,2048]{1,0:T(8,128)(2,1)S(1)} copy-done((bf16[768,2048]{1,0:T(8,128)(2,1)S(1)}, bf16[768,2048]{1,0:T(8,128)(2,1)}, u32[]{:S(2)}) %copy-start.1) | copy-done | bytes 3145752
  24.0 7.9 %shard_map.64 = (bf16[256,2048]{1,0:T(8,128)(2,1)S(1)}, bf16[256,2048]{1,0:T(8,128)(2,1)S(1)}, bf16[2,768,2048]{2,1,0:T(8,128)(2,1)S(1)}, bf16[768,2048]{1,0:T(8,128)(2,1)S(1)}) custom-call(s32[18]{0:T(128)S(1)} %dynamic-slice_bitcast_fusion.sources_ref, f32[16,128]{1,0:T(8,128)S(1)} %bitcast.6, bf16[128,2048]{1,0:T(8,128)(2,1)S(1)} %collective-permute-done.refs_0_, ...), custom_call_target="tpu_custom_call" | custom-call | flops 4831838208 | bytes 13631488 | tf_op jit(solution)/shard_map/pallas_call | solution.py:127
  32.1 2.6 %collective-permute-done.5.refs_1_ = bf16[128,2048]{1,0:T(8,128)(2,1)S(1)} collective-permute-done((bf16[128,2048]{1,0:T(8,128)(2,1)S(1)}, bf16[128,2048]{1,0:T(8,128)(2,1)S(1)}, u32[]{:S(2)}, u32[]{:S(2)}) %collective-permute-start.5) | collective-permute-done | bytes 524320 | tf_op jit(solution)/shard_map/ppermute | solution.py:179
  36.6 5.6 %shard_map.65 = (bf16[256,2048]{1,0:T(8,128)(2,1)S(1)}, bf16[256,2048]{1,0:T(8,128)(2,1)S(1)}) custom-call(s32[18]{0:T(128)S(1)} %dynamic-slice_bitcast_fusion.sources_ref, f32[16,128]{1,0:T(8,128)S(1)} %bitcast.7, bf16[128,2048]{1,0:T(8,128)(2,1)S(1)} %collective-permute-done.1.refs_0_, bf16[128,2048]{1,0:T(8,128)(2,1)S(1)} %collective-permute-done.5.refs_1_, ...), custom_call_target="tpu_custom_call" | custom-call | flops 4831838208 | bytes 13631488 | tf_op jit(solution)/shard_map/pallas_call | solution.py:127
  42.3 1.6 %collective-permute-done.9.refs_0_ = bf16[128,2048]{1,0:T(8,128)(2,1)S(1)} collective-permute-done((bf16[128,2048]{1,0:T(8,128)(2,1)S(1)}, bf16[128,2048]{1,0:T(8,128)(2,1)S(1)}, u32[]{:S(2)}, u32[]{:S(2)}) %collective-permute-start.9) | collective-permute-done | bytes 524320 | tf_op jit(solution)/shard_map/ppermute | solution.py:179
  45.1 4.4 %collective-permute-done.8.refs_0_ = bf16[128,2048]{1,0:T(8,128)(2,1)S(1)} collective-permute-done((bf16[128,2048]{1,0:T(8,128)(2,1)S(1)}, bf16[128,2048]{1,0:T(8,128)(2,1)S(1)}, u32[]{:S(2)}, u32[]{:S(2)}) %collective-permute-start.8) | collective-permute-done | bytes 524320 | tf_op jit(solution)/shard_map/ppermute | solution.py:179
  50.3 3.3 %shard_map.66 = (bf16[128,2048]{1,0:T(8,128)(2,1)S(1)}, bf16[128,2048]{1,0:T(8,128)(2,1)S(1)}) custom-call(s32[18]{0:T(128)S(1)} %dynamic-slice_bitcast_fusion.sources_ref, f32[16,128]{1,0:T(8,128)S(1)} %bitcast.8, bf16[128,2048]{1,0:T(8,128)(2,1)S(1)} %collective-permute-done.9.refs_0_, bf16[128,2048]{1,0:T(8,128)(2,1)S(1)} %collective-permute-done.11.refs_1_, ...), custom_call_target="tpu_custom_call" | custom-call | flops 2415919104 | bytes 11534336 | tf_op jit(solution)/shard_map/pallas_call | solution.py:127
  54.4 1.8 %collective-permute-done.13.refs_1_ = bf16[64,2048]{1,0:T(8,128)(2,1)S(1)} collective-permute-done((bf16[64,2048]{1,0:T(8,128)(2,1)S(1)}, bf16[64,2048]{1,0:T(8,128)(2,1)S(1)}, u32[]{:S(2)}, u32[]{:S(2)}) %collective-permute-start.13) | collective-permute-done | bytes 262176 | tf_op jit(solution)/shard_map/ppermute | solution.py:179
  56.7 3.3 %shard_map.67 = (bf16[128,2048]{1,0:T(8,128)(2,1)S(1)}, bf16[128,2048]{1,0:T(8,128)(2,1)S(1)}) custom-call(s32[18]{0:T(128)S(1)} %dynamic-slice_bitcast_fusion.sources_ref, f32[16,128]{1,0:T(8,128)S(1)} %bitcast.9, bf16[128,2048]{1,0:T(8,128)(2,1)S(1)} %collective-permute-done.8.refs_0_, bf16[128,2048]{1,0:T(8,128)(2,1)S(1)} %collective-permute-done.12.refs_1_, ...), custom_call_target="tpu_custom_call" | custom-call | flops 2415919104 | bytes 11534336 | tf_op jit(solution)/shard_map/pallas_call | solution.py:127
  60.1 1.4 %collective-permute-done.14.refs_2_ = bf16[64,2048]{1,0:T(8,128)(2,1)S(1)} collective-permute-done((bf16[64,2048]{1,0:T(8,128)(2,1)S(1)}, bf16[64,2048]{1,0:T(8,128)(2,1)S(1)}, u32[]{:S(2)}, u32[]{:S(2)}) %collective-permute-start.14) | collective-permute-done | bytes 262176 | tf_op jit(solution)/shard_map/ppermute | solution.py:179
  61.7 3.3 %shard_map.68 = (bf16[128,2048]{1,0:T(8,128)(2,1)S(1)}, bf16[128,2048]{1,0:T(8,128)(2,1)S(1)}) custom-call(s32[18]{0:T(128)S(1)} %dynamic-slice_bitcast_fusion.sources_ref, f32[16,128]{1,0:T(8,128)S(1)} %bitcast.10, bf16[64,2048]{1,0:T(8,128)(2,1)S(1)} %collective-permute-done.10.refs_0_, bf16[64,2048]{1,0:T(8,128)(2,1)S(1)} %collective-permute-done.13.refs_1_, ...), custom_call_target="tpu_custom_call" | custom-call | flops 2415919104 | bytes 11534336 | tf_op jit(solution)/shard_map/pallas_call | solution.py:127
  66.1 5.8 %collective-permute-done.18 = bf16[64,2048]{1,0:T(8,128)(2,1)S(1)} collective-permute-done((bf16[64,2048]{1,0:T(8,128)(2,1)S(1)}, bf16[64,2048]{1,0:T(8,128)(2,1)S(1)}, u32[]{:S(2)}, u32[]{:S(2)}) %collective-permute-start.18) | collective-permute-done | bytes 262176 | tf_op jit(solution)/shard_map/ppermute | solution.py:179
  73.2 5.1 %collective-permute-done.20 = bf16[64,2048]{1,0:T(8,128)(2,1)S(1)} collective-permute-done((bf16[64,2048]{1,0:T(8,128)(2,1)S(1)}, bf16[64,2048]{1,0:T(8,128)(2,1)S(1)}, u32[]{:S(2)}, u32[]{:S(2)}) %collective-permute-start.20) | collective-permute-done | bytes 262176 | tf_op jit(solution)/shard_map/ppermute | solution.py:179
  78.8 2.3 %collective-permute-done.21 = bf16[64,2048]{1,0:T(8,128)(2,1)S(1)} collective-permute-done((bf16[64,2048]{1,0:T(8,128)(2,1)S(1)}, bf16[64,2048]{1,0:T(8,128)(2,1)S(1)}, u32[]{:S(2)}, u32[]{:S(2)}) %collective-permute-start.21) | collective-permute-done | bytes 262176 | tf_op jit(solution)/shard_map/ppermute | solution.py:179
  81.8 2.9 %collective-permute-done.22 = bf16[64,2048]{1,0:T(8,128)(2,1)S(1)} collective-permute-done((bf16[64,2048]{1,0:T(8,128)(2,1)S(1)}, bf16[64,2048]{1,0:T(8,128)(2,1)S(1)}, u32[]{:S(2)}, u32[]{:S(2)}) %collective-permute-start.22) | collective-permute-done | bytes 262176 | tf_op jit(solution)/shard_map/ppermute | solution.py:179
  85.3 2.3 %collective-permute-done.24 = bf16[64,2048]{1,0:T(8,128)(2,1)S(1)} collective-permute-done((bf16[64,2048]{1,0:T(8,128)(2,1)S(1)}, bf16[64,2048]{1,0:T(8,128)(2,1)S(1)}, u32[]{:S(2)}, u32[]{:S(2)}) %collective-permute-start.24) | collective-permute-done | bytes 262176 | tf_op jit(solution)/shard_map/ppermute | solution.py:179
  88.4 2.8 %collective-permute-done.25 = bf16[64,2048]{1,0:T(8,128)(2,1)S(1)} collective-permute-done((bf16[64,2048]{1,0:T(8,128)(2,1)S(1)}, bf16[64,2048]{1,0:T(8,128)(2,1)S(1)}, u32[]{:S(2)}, u32[]{:S(2)}) %collective-permute-start.25) | collective-permute-done | bytes 262176 | tf_op jit(solution)/shard_map/ppermute | solution.py:179
  92.0 3.2 %shard_map.69 = (bf16[128,2048]{1,0:T(8,128)(2,1)S(1)}, bf16[128,2048]{1,0:T(8,128)(2,1)S(1)}) custom-call(s32[18]{0:T(128)S(1)} %dynamic-slice_bitcast_fusion.sources_ref, f32[16,128]{1,0:T(8,128)S(1)} %bitcast.11, bf16[128,2048]{1,0:T(8,128)(2,1)S(1)} %copy-done, bf16[128,2048]{1,0:T(8,128)(2,1)S(1)} %collective-permute-done.26.refs_1_, ...), custom_call_target="tpu_custom_call" | custom-call | flops 2415919104 | bytes 11534336 | tf_op jit(solution)/shard_map/pallas_call | solution.py:127
  95.3 1.8 %collective-permute-done.29 = bf16[128,2048]{1,0:T(8,128)(2,1)S(1)} collective-permute-done((bf16[128,2048]{1,0:T(8,128)(2,1)S(1)}, bf16[128,2048]{1,0:T(8,128)(2,1)S(1)}, u32[]{:S(2)}, u32[]{:S(2)}) %collective-permute-start.29) | collective-permute-done | bytes 524320 | tf_op jit(solution)/shard_map/ppermute | solution.py:179
  97.9 4.8 %collective-permute-done.31 = bf16[128,2048]{1,0:T(8,128)(2,1)S(1)} collective-permute-done((bf16[128,2048]{1,0:T(8,128)(2,1)S(1)}, bf16[128,2048]{1,0:T(8,128)(2,1)S(1)}, u32[]{:S(2)}, u32[]{:S(2)}) %collective-permute-start.31) | collective-permute-done | bytes 524320 | tf_op jit(solution)/shard_map/ppermute | solution.py:179
  103.1 5.3 %collective-permute-done.30.refs_2_ = bf16[128,2048]{1,0:T(8,128)(2,1)S(1)} collective-permute-done((bf16[128,2048]{1,0:T(8,128)(2,1)S(1)}, bf16[128,2048]{1,0:T(8,128)(2,1)S(1)}, u32[]{:S(2)}, u32[]{:S(2)}) %collective-permute-start.30) | collective-permute-done | bytes 524320 | tf_op jit(solution)/shard_map/ppermute | solution.py:179
  108.5 3.5 %collective-permute-done.32 = bf16[128,2048]{1,0:T(8,128)(2,1)S(1)} collective-permute-done((bf16[128,2048]{1,0:T(8,128)(2,1)S(1)}, bf16[128,2048]{1,0:T(8,128)(2,1)S(1)}, u32[]{:S(2)}, u32[]{:S(2)}) %collective-permute-start.32) | collective-permute-done | bytes 524320 | tf_op jit(solution)/shard_map/ppermute | solution.py:179
  (75 shorter events, 17.7 us)
Async XLA Ops:
  0.0 19.4 %collective-permute-start = (bf16[128,2048]{1,0:T(8,128)(2,1)}, bf16[128,2048]{1,0:T(8,128)(2,1)S(1)}, u32[]{:S(2)}, u32[]{:S(2)}) collective-permute-start(bf16[128,2048]{1,0:T(8,128)(2,1)} %refs_0_), channel_id=1, source_target_pairs={{0,4},{1,3},{4,8},{5,1},{8,12},{9,5},{12,14},{13,9},{14,10},{15,13... | collective-permute-start | bytes 1572872 | tf_op jit(solution)/shard_map/ppermute | solution.py:179
  3.0 16.4 %collective-permute-start.2 = (bf16[128,2048]{1,0:T(8,128)(2,1)}, bf16[128,2048]{1,0:T(8,128)(2,1)S(1)}, u32[]{:S(2)}, u32[]{:S(2)}) collective-permute-start(bf16[128,2048]{1,0:T(8,128)(2,1)} %refs_0_), channel_id=1, source_target_pairs={{0,3},{1,4},{4,1},{5,8},{8,5},{9,12},{12,9},{13,14},{14,13},{15,10... | collective-permute-start | bytes 1572872 | tf_op jit(solution)/shard_map/ppermute | solution.py:179
  19.9 12.0 %collective-permute-start.1 = (bf16[128,2048]{1,0:T(8,128)(2,1)S(1)}, bf16[128,2048]{1,0:T(8,128)(2,1)S(1)}, u32[]{:S(2)}, u32[]{:S(2)}) collective-permute-start(bf16[128,2048]{1,0:T(8,128)(2,1)S(1)} %collective-permute-done.refs_0_), channel_id=1, source_target_pairs={{0,4},{1,3},{4,8},{5,1},{8,12},{9,5},{12,14},{13,9},{14,10},{15,13... | collective-permute-start | bytes 1572872 | tf_op jit(solution)/shard_map/ppermute | solution.py:179
  20.4 14.3 %collective-permute-start.5 = (bf16[128,2048]{1,0:T(8,128)(2,1)S(1)}, bf16[128,2048]{1,0:T(8,128)(2,1)S(1)}, u32[]{:S(2)}, u32[]{:S(2)}) collective-permute-start(bf16[128,2048]{1,0:T(8,128)(2,1)S(1)} %collective-permute-done.2.refs_1_), channel_id=1, source_target_pairs={{0,4},{1,3},{4,8},{5,1},{8,12},{9,5},{12,14},{13,9},{14,10},{15,13... | collective-permute-start | bytes 1572872 | tf_op jit(solution)/shard_map/ppermute | solution.py:179
  34.7 9.2 %collective-permute-start.9 = (bf16[128,2048]{1,0:T(8,128)(2,1)S(1)}, bf16[128,2048]{1,0:T(8,128)(2,1)S(1)}, u32[]{:S(2)}, u32[]{:S(2)}) collective-permute-start(bf16[128,2048]{1,0:T(8,128)(2,1)S(1)} %collective-permute-done.1.refs_0_), channel_id=1, source_target_pairs={{0,4},{1,3},{4,8},{5,1},{8,12},{9,5},{12,14},{13,9},{14,10},{15,13... | collective-permute-start | bytes 1572872 | tf_op jit(solution)/shard_map/ppermute | solution.py:179
  35.2 14.3 %collective-permute-start.8 = (bf16[128,2048]{1,0:T(8,128)(2,1)S(1)}, bf16[128,2048]{1,0:T(8,128)(2,1)S(1)}, u32[]{:S(2)}, u32[]{:S(2)}) collective-permute-start(bf16[128,2048]{1,0:T(8,128)(2,1)S(1)} %collective-permute-done.5.refs_1_), channel_id=1, source_target_pairs={{0,4},{1,3},{4,8},{5,1},{8,12},{9,5},{12,14},{13,9},{14,10},{15,13... | collective-permute-start | bytes 1572872 | tf_op jit(solution)/shard_map/ppermute | solution.py:179
  43.9 6.4 %collective-permute-start.11 = (bf16[128,2048]{1,0:T(8,128)(2,1)S(1)}, bf16[128,2048]{1,0:T(8,128)(2,1)S(1)}, u32[]{:S(2)}, u32[]{:S(2)}) collective-permute-start(bf16[128,2048]{1,0:T(8,128)(2,1)S(1)} %collective-permute-done.9.refs_0_), channel_id=1, source_target_pairs={{0,1},{1,0},{4,5},{5,4},{8,9},{9,8},{12,13},{13,12},{14,15},{15,14... | collective-permute-start | bytes 1572872 | tf_op jit(solution)/shard_map/ppermute | solution.py:179
  43.9 48.1 %collective-permute-start.26 = (bf16[128,2048]{1,0:T(8,128)(2,1)S(1)}, bf16[128,2048]{1,0:T(8,128)(2,1)S(1)}, u32[]{:S(2)}, u32[]{:S(2)}) collective-permute-start(bf16[128,2048]{1,0:T(8,128)(2,1)S(1)} %copy-done), channel_id=1, source_target_pairs={{0,1},{1,0},{4,5},{5,4},{8,9},{9,8},{12,13},{13,12},{14,15},{15,14... | collective-permute-start | bytes 1572872 | tf_op jit(solution)/shard_map/ppermute | solution.py:179
  44.5 9.7 %collective-permute-start.10 = (bf16[64,2048]{1,0:T(8,128)(2,1)S(1)}, bf16[64,2048]{1,0:T(8,128)(2,1)S(1)}, u32[]{:S(2)}, u32[]{:S(2)}) collective-permute-start(bf16[64,2048]{1,0:T(8,128)(2,1)S(1)} %slice.68), channel_id=1, source_target_pairs={{0,4},{1,3},{4,8},{5,1},{8,12},{9,5},{12,14},{13,9},{14,10},{15,13... | collective-permute-start | bytes 786440 | tf_op jit(solution)/shard_map/ppermute | solution.py:179
  49.6 6.6 %collective-permute-start.13 = (bf16[64,2048]{1,0:T(8,128)(2,1)S(1)}, bf16[64,2048]{1,0:T(8,128)(2,1)S(1)}, u32[]{:S(2)}, u32[]{:S(2)}) collective-permute-start(bf16[64,2048]{1,0:T(8,128)(2,1)S(1)} %slice.88), channel_id=1, source_target_pairs={{0,4},{1,3},{4,8},{5,1},{8,12},{9,5},{12,14},{13,9},{14,10},{15,13... | collective-permute-start | bytes 786440 | tf_op jit(solution)/shard_map/ppermute | solution.py:179
  53.6 6.4 %collective-permute-start.15 = (bf16[128,2048]{1,0:T(8,128)(2,1)S(1)}, bf16[128,2048]{1,0:T(8,128)(2,1)S(1)}, u32[]{:S(2)}, u32[]{:S(2)}) collective-permute-start(bf16[128,2048]{1,0:T(8,128)(2,1)S(1)} %get-tuple-element.48), channel_id=1, source_target_pairs={{0,1},{1,0},{4,5},{5,4},{8,9},{9,8},{12,13},{13,12},{14,15},{15,14... | collective-permute-start | bytes 1572872 | tf_op jit(solution)/shard_map/ppermute | solution.py:179
  54.3 41.0 %collective-permute-start.28 = (bf16[256,2048]{1,0:T(8,128)(2,1)S(1)}, bf16[256,2048]{1,0:T(8,128)(2,1)S(1)}, u32[]{:S(2)}, u32[]{:S(2)}) collective-permute-start(bf16[256,2048]{1,0:T(8,128)(2,1)S(1)} %get-tuple-element.65), channel_id=1, source_target_pairs={{0,1},{1,0},{4,5},{5,4},{8,9},{9,8},{12,13},{13,12},{14,15},{15,14... | collective-permute-start | bytes 3145736 | tf_op jit(solution)/shard_map/ppermute | solution.py:179
  56.2 29.2 %collective-permute-start.23 = (bf16[256,2048]{1,0:T(8,128)(2,1)S(1)}, bf16[256,2048]{1,0:T(8,128)(2,1)S(1)}, u32[]{:S(2)}, u32[]{:S(2)}) collective-permute-start(bf16[256,2048]{1,0:T(8,128)(2,1)S(1)} %get-tuple-element.59), channel_id=1, source_target_pairs={{0,1},{1,0},{4,5},{5,4},{8,9},{9,8},{12,13},{13,12},{14,15},{15,14... | collective-permute-start | bytes 3145736 | tf_op jit(solution)/shard_map/ppermute | solution.py:179
  65.0 7.4 %collective-permute-start.19 = (bf16[128,2048]{1,0:T(8,128)(2,1)S(1)}, bf16[128,2048]{1,0:T(8,128)(2,1)S(1)}, u32[]{:S(2)}, u32[]{:S(2)}) collective-permute-start(bf16[128,2048]{1,0:T(8,128)(2,1)S(1)} %get-tuple-element.54), channel_id=1, source_target_pairs={{0,1},{1,0},{4,5},{5,4},{8,9},{9,8},{12,13},{13,12},{14,15},{15,14... | collective-permute-start | bytes 1572872 | tf_op jit(solution)/shard_map/ppermute | solution.py:179
  65.5 6.4 %collective-permute-start.18 = (bf16[64,2048]{1,0:T(8,128)(2,1)S(1)}, bf16[64,2048]{1,0:T(8,128)(2,1)S(1)}, u32[]{:S(2)}, u32[]{:S(2)}) collective-permute-start(bf16[64,2048]{1,0:T(8,128)(2,1)S(1)} %add_convert_fusion.10), channel_id=1, source_target_pairs={{0,2},{1,5},{4,0},{5,9},{8,4},{9,13},{12,8},{13,15},{14,12},{15,11... | collective-permute-start | bytes 786440 | tf_op jit(solution)/shard_map/ppermute | solution.py:179
  71.9 6.4 %collective-permute-start.20 = (bf16[64,2048]{1,0:T(8,128)(2,1)S(1)}, bf16[64,2048]{1,0:T(8,128)(2,1)S(1)}, u32[]{:S(2)}, u32[]{:S(2)}) collective-permute-start(bf16[64,2048]{1,0:T(8,128)(2,1)S(1)} %add_convert_fusion.9), channel_id=1, source_target_pairs={{0,2},{1,5},{4,0},{5,9},{8,4},{9,13},{12,8},{13,15},{14,12},{15,11... | collective-permute-start | bytes 786440 | tf_op jit(solution)/shard_map/ppermute | solution.py:179
  72.5 8.6 %collective-permute-start.21 = (bf16[64,2048]{1,0:T(8,128)(2,1)S(1)}, bf16[64,2048]{1,0:T(8,128)(2,1)S(1)}, u32[]{:S(2)}, u32[]{:S(2)}) collective-permute-start(bf16[64,2048]{1,0:T(8,128)(2,1)S(1)} %add_convert_fusion.8), channel_id=1, source_target_pairs={{0,2},{1,5},{4,0},{5,9},{8,4},{9,13},{12,8},{13,15},{14,12},{15,11... | collective-permute-start | bytes 786440 | tf_op jit(solution)/shard_map/ppermute | solution.py:179
  81.2 6.4 %collective-permute-start.24 = (bf16[64,2048]{1,0:T(8,128)(2,1)S(1)}, bf16[64,2048]{1,0:T(8,128)(2,1)S(1)}, u32[]{:S(2)}, u32[]{:S(2)}) collective-permute-start(bf16[64,2048]{1,0:T(8,128)(2,1)S(1)} %add_convert_fusion.6), channel_id=1, source_target_pairs={{0,2},{1,5},{4,0},{5,9},{8,4},{9,13},{12,8},{13,15},{14,12},{15,11... | collective-permute-start | bytes 786440 | tf_op jit(solution)/shard_map/ppermute | solution.py:179
  84.8 6.4 %collective-permute-start.25 = (bf16[64,2048]{1,0:T(8,128)(2,1)S(1)}, bf16[64,2048]{1,0:T(8,128)(2,1)S(1)}, u32[]{:S(2)}, u32[]{:S(2)}) collective-permute-start(bf16[64,2048]{1,0:T(8,128)(2,1)S(1)} %add_convert_fusion.5), channel_id=1, source_target_pairs={{0,2},{1,5},{4,0},{5,9},{8,4},{9,13},{12,8},{13,15},{14,12},{15,11... | collective-permute-start | bytes 786440 | tf_op jit(solution)/shard_map/ppermute | solution.py:179
  87.9 9.2 %collective-permute-start.29 = (bf16[128,2048]{1,0:T(8,128)(2,1)S(1)}, bf16[128,2048]{1,0:T(8,128)(2,1)S(1)}, u32[]{:S(2)}, u32[]{:S(2)}) collective-permute-start(bf16[128,2048]{1,0:T(8,128)(2,1)S(1)} %add_convert_fusion.4), channel_id=1, source_target_pairs={{0,2},{1,5},{4,0},{5,9},{8,4},{9,13},{12,8},{13,15},{14,12},{15,11... | collective-permute-start | bytes 1572872 | tf_op jit(solution)/shard_map/ppermute | solution.py:179
  91.4 11.3 %collective-permute-start.31 = (bf16[128,2048]{1,0:T(8,128)(2,1)S(1)}, bf16[128,2048]{1,0:T(8,128)(2,1)S(1)}, u32[]{:S(2)}, u32[]{:S(2)}) collective-permute-start(bf16[128,2048]{1,0:T(8,128)(2,1)S(1)} %add_convert_fusion.3), channel_id=1, source_target_pairs={{0,2},{1,5},{4,0},{5,9},{8,4},{9,13},{12,8},{13,15},{14,12},{15,11... | collective-permute-start | bytes 1572872 | tf_op jit(solution)/shard_map/ppermute | solution.py:179
  95.2 7.8 %collective-permute-start.27 = (bf16[128,2048]{1,0:T(8,128)(2,1)S(1)}, bf16[128,2048]{1,0:T(8,128)(2,1)S(1)}, u32[]{:S(2)}, u32[]{:S(2)}) collective-permute-start(bf16[128,2048]{1,0:T(8,128)(2,1)S(1)} %get-tuple-element.63), channel_id=1, source_target_pairs={{0,1},{1,0},{4,5},{5,4},{8,9},{9,8},{12,13},{13,12},{14,15},{15,14... | collective-permute-start | bytes 1572872 | tf_op jit(solution)/shard_map/ppermute | solution.py:179
  97.4 11.0 %collective-permute-start.30 = (bf16[128,2048]{1,0:T(8,128)(2,1)S(1)}, bf16[128,2048]{1,0:T(8,128)(2,1)S(1)}, u32[]{:S(2)}, u32[]{:S(2)}) collective-permute-start(bf16[128,2048]{1,0:T(8,128)(2,1)S(1)} %add_convert_fusion.2), channel_id=1, source_target_pairs={{0,2},{1,5},{4,0},{5,9},{8,4},{9,13},{12,8},{13,15},{14,12},{15,11... | collective-permute-start | bytes 1572872 | tf_op jit(solution)/shard_map/ppermute | solution.py:179
  103.0 9.0 %collective-permute-start.32 = (bf16[128,2048]{1,0:T(8,128)(2,1)S(1)}, bf16[128,2048]{1,0:T(8,128)(2,1)S(1)}, u32[]{:S(2)}, u32[]{:S(2)}) collective-permute-start(bf16[128,2048]{1,0:T(8,128)(2,1)S(1)} %add_convert_fusion.1), channel_id=1, source_target_pairs={{0,3},{1,4},{4,1},{5,8},{8,5},{9,12},{12,9},{13,14},{14,13},{15,10... | collective-permute-start | bytes 1572872 | tf_op jit(solution)/shard_map/ppermute | solution.py:179
  (11 other events, 43.3 us)

commit v5 on v4

--- a/solution.py
+++ b/solution.py
@@ -65,12 +65,13 @@
     return table
 
 
-def half_expert_kernel(pieces, load, sources_ref, gates_ref, *refs):
+def half_expert_kernel(pieces, load, split, sources_ref, gates_ref, *refs):
     blocks, refs = refs[: len(pieces)], refs[len(pieces) :]
     if load:
-        gate_up_far, down_far, out_keep, out_give, gate_up_ref, down_ref, rows, hidden, arrived = refs
+        (gate_up_far, down_far), refs = refs[:2], refs[2:]
+        outs, (gate_up_ref, down_ref, rows, hidden, arrived) = refs[:split], refs[split:]
     else:
-        gate_up_ref, down_ref, out_keep, out_give, rows, hidden = refs
+        (gate_up_ref, down_ref), outs, (rows, hidden) = refs[:2], refs[2:-2], refs[-2:]
     units, width = down_ref.shape
     tile = 256 if units % 256 == 0 else units
     tiles = units // tile
@@ -106,36 +107,36 @@
     if load:
         copies[tiles].wait()
     inner = hidden[...]
-    keep = out_keep.shape[0]
+    share = outs[0].shape[0]
     tile = 512 if width % 512 == 0 else width
     for low in range(0, width, tile):
         product = jnp.dot(inner, down_ref[:, low : low + tile], preferred_element_type=jnp.float32) * weight
         product = product.astype(jnp.bfloat16)
-        out_keep[:, low : low + tile] = product[:keep]
-        out_give[:, low : low + tile] = product[keep:]
-
-
-def half_expert(places, gates, pieces, blocks, gate_up, down_proj, load=False):
+        for i, out in enumerate(outs):
+            out[:, low : low + tile] = product[i * share : (i + 1) * share]
+
+
+def half_expert(places, gates, pieces, blocks, gate_up, down_proj, load=False, cost=6, split=2):
     height = sum(block.shape[0] for block in blocks)
     units, width = down_proj.shape
     whole = pl.BlockSpec(memory_space=pltpu.VMEM)
-    out = jax.ShapeDtypeStruct((height // 2, width), jnp.bfloat16)
+    outs = [jax.ShapeDtypeStruct((height // split, width), jnp.bfloat16)] * split
     weights = [jax.ShapeDtypeStruct(array.shape, array.dtype) for array in (gate_up, down_proj)] if load else []
     scratch = [pltpu.VMEM((height, width), jnp.bfloat16), pltpu.VMEM((height, units), jnp.bfloat16)]
     if load:
         scratch.append(pltpu.SemaphoreType.DMA((units // 256 + 1 if units % 256 == 0 else 2,)))
     return pl.pallas_call(
-        functools.partial(half_expert_kernel, tuple(pieces), load),
-        out_shape=[out, out] + weights,
+        functools.partial(half_expert_kernel, tuple(pieces), load, split),
+        out_shape=outs + weights,
         in_specs=[pl.BlockSpec(memory_space=pltpu.SMEM)]
         + [whole] * (len(blocks) + 1)
         + [pl.BlockSpec(memory_space=pltpu.HBM) if load else whole] * 2,
-        out_specs=[whole] * (2 + len(weights)),
+        out_specs=[whole] * (split + len(weights)),
         scratch_shapes=scratch,
         compiler_params=pltpu.CompilerParams(vmem_limit_bytes=(34 if load else 14) << 20),
         cost_estimate=pl.CostEstimate(
-            flops=6 * height * units * width,
-            bytes_accessed=6 * units * width + 4 * height * width,
+            flops=cost * height * units * width,
+            bytes_accessed=cost * units * width,
             transcendentals=height * units,
         ),
     )(places, gates, *blocks, gate_up, down_proj)
@@ -195,59 +196,60 @@
     weight = jnp.sum(jnp.where(chosen, route_gate.T[None], 0.0), axis=1)
     gates = lax.all_to_all(jnp.repeat(weight, 2, axis=0), "blk", split_axis=0, concat_axis=0, tiled=True)
     gates = gates.reshape(-1, rows)
-    ring[0] = after(ring[0], gates)
-
-    near = None
-    results = {}
-    for step in range(1, far - 1):
+
+    results, near = {}, None
+    earlier = ring[1]
+    for step in range(1, far):
         swapped = [send(block, cores) for block in ring]
-        pieces = [(4 * step - 2 + i, 0) for i in range(4)]
-        blocks = ring + swapped
-        ring = [send(block, forth) for block in ring]
-        if near is None:
-            kept, given, *near = half_expert(places, gates, pieces, blocks, gate_up, down_proj, load=True)
+        blocks = ring
+        if step < far - 1:
+            ring = [send(block, forth) for block in ring]
         else:
-            kept, given = half_expert(places, gates, pieces, blocks, *near)
-        given = send(given, cores)
+            ring = [send(ring[0][:half], forth), send(ring[1][half:], forth)]
         for c in chains:
-            results[step, c] = kept[c * rows : (c + 1) * rows], given[c * rows : (c + 1) * rows]
-        ring[0] = after(ring[0], kept)
+            pieces = [(4 * step - 2 + c, 0), (4 * step + c, 0)]
+            inputs = [after(blocks[c], earlier), swapped[c]]
+            if near is None:
+                kept, given, *near = half_expert(places, gates, pieces, inputs, gate_up, down_proj, load=True)
+            elif (step, c) != (far - 1, 1):
+                kept, given = half_expert(places, gates, pieces, inputs, *near)
+            else:
+                last = pieces, [blocks[c], swapped[c]]
+                break
+            results[step, c] = kept, send(given, cores)
+            ring[c] = earlier = after(ring[c], kept)
+
+    base = 4 * far - 2
+    pieces = [(base, 0), (base + 1, half)]
+    (given,) = half_expert(places, gates, pieces, ring, *near, split=1)
+    swapped = [send(block, cores) for block in ring]
+    swapped[0] = after(swapped[0], given)
+    given = send(given, cores)
+    pieces = [(base + 2, 0), (base + 3, half)]
+    (kept,) = half_expert(places, gates, pieces, swapped, *near, split=1)
 
     first, second = slice(0, half), slice(half, rows)
-    swapped = [send(block, cores) for block in ring]
-    blocks = ring + swapped
-    ring = [send(ring[0][first], forth), send(ring[1][second], forth)]
-    for c in chains:
-        pieces = [(4 * far - 6 + c, 0), (4 * far - 4 + c, 0)]
-        mine, theirs = half_expert(places, gates, pieces, [blocks[c], blocks[2 + c]], *near)
-        results[far - 1, c] = mine, send(theirs, cores)
-        if c == 0:
-            ring[0] = after(ring[0], mine)
-            blocks[1] = after(blocks[1], ring[0])
-    swapped = [send(block, cores) for block in ring]
-    mine, theirs = results[far - 1, 0]
-    earlier = rounded(total(after(mine, results[far - 1, 1][0])[second], theirs[second]))
-    early = [send(earlier, back)]
-    swapped[0] = after(swapped[0], earlier)
-    base = 4 * far - 2
-    pieces = [(base, 0), (base + 1, half), (base + 2, 0), (base + 3, half)]
-    kept, given = half_expert(places, gates, pieces, ring + swapped, *near)
-    given = send(given, cores)
-    mine, theirs = results[far - 1, 1]
-    earlier = rounded(total(after(mine, kept)[first], theirs[first]))
-    early.append(send(earlier, back))
-
     late = []
-    for part in (first, second):
-        earlier = rounded(total(after(kept[part], earlier, early[0]), given[part]))
+    earlier = kept
+    for part in (second, first):
+        earlier = rounded(total(after(kept[part], earlier), given[part]))
         late.append(send(earlier, back))
+    pieces, inputs = last
+    inputs[0] = after(inputs[0], earlier)
+    kept, given = half_expert(places, gates, pieces, inputs, *near, cost=1)
+    results[far - 1, 1] = kept, send(given, cores)
+
     sums = []
+    earlier = kept
     for c in chains:
         mine, theirs = results[far - 1, c]
-        part = (first, second)[c]
-        earlier = rounded(total(after(mine[part], earlier, early[1]), theirs[part], late[c]))
-        pair = [send(earlier, back), early[c]]
-        sums.append(jnp.concatenate(pair if c == 0 else pair[::-1]))
+        value = total(after(mine, earlier), theirs)
+        if c == 0:
+            value = jnp.concatenate([value[first], value[second] + total(late[c])])
+        else:
+            value = jnp.concatenate([value[first] + total(late[c]), value[second]])
+        earlier = rounded(value)
+        sums.append(send(earlier, back))
     for step in range(far - 2, 1, -1):
         for c in chains:
             mine, theirs = results[step, c]

time: 115 us -> 112 us (0.974)
  blocking collectives: 15 us -> 0 us
  starting transfers between devices: 15.3 us -> 23.7 us
  Pallas kernels: 26.8 us -> 31.5 us
    all_to_all x1 -> x0, blocking collectives: 15 us -> none  [by_tokens(): lax.all_to_all(jnp.repeat(weight, 2, axis=0), 'blk', split_axis=0, concat...]
    all_to_all x0 -> x1, starting transfers between devices: none -> 5.8 us  [by_tokens(): lax.all_to_all(jnp.repeat(weight, 2, axis=0), 'blk', split_axis=0, concat...]
    pallas_call x6 -> x9, Pallas kernels: 26.6 us -> 31.3 us  [half_expert(): pl.pallas_call(functools.partial(half_expert_kernel, tuple(pieces), load,...]
    ppermute x33, waiting for transfers between devices: 49.7 us -> 45.1 us  [send(): return lax.ppermute(value, 'blk', pairs)]
    all_to_all x0 -> x1, waiting for transfers between devices: none -> 3.57 us  [by_tokens(): lax.all_to_all(jnp.repeat(weight, 2, axis=0), 'blk', split_axis=0, concat...]
    ppermute x33, starting transfers between devices: 15.3 us -> 17.9 us  [send(): return lax.ppermute(value, 'blk', pairs)]
    convert_element_type x11 -> x7, other arithmetic: 2.35 us -> 2.02 us  [rounded(): return value.astype(jnp.bfloat16)]
  transfers between devices with their start and end apart: 33 -> 34, of which waited for: 17 -> 13; matrix products, arithmetic and copies ran while one was open for 3% -> 3% of each run, Pallas kernels for 24% -> 28%
where the time goes in v5:
time: 112 us; the launch traced here: 111 us
  waiting for transfers between devices  48.7 us (43%)
  Pallas kernels  31.5 us (28%)
  starting transfers between devices  23.7 us (21%)
  local copies, waits for them, and re-layouts  3.32 us (3%)
  other arithmetic  3.16 us (3%)
    ppermute x33, waiting for transfers between devices, send(): return lax.ppermute(value, 'blk', pairs)  45.1 us
    pallas_call x9, Pallas kernels, half_expert(): pl.pallas_call(functools.partial(half_expert_kernel, tuple(pieces), load,...  31.3 us
    ppermute x33, starting transfers between devices, send(): return lax.ppermute(value, 'blk', pairs)  17.9 us
    all_to_all x1, starting transfers between devices, by_tokens(): lax.all_to_all(jnp.repeat(weight, 2, axis=0), 'blk', split_axis=0, concat...  5.8 us
    all_to_all x1, waiting for transfers between devices, by_tokens(): lax.all_to_all(jnp.repeat(weight, 2, axis=0), 'blk', split_axis=0, concat...  3.57 us
  transfers between devices with their start and end apart: 34, of which 13 were waited for; matrix products, arithmetic and copies ran while one was open for 3% of the time, Pallas kernels for 28%

profile of v5, /device:TPU:0, one launch (start us, length us, event | category | flops | bytes accessed | tf_op | source)
XLA Modules:
  0.0 110.8 jit_solution(1799478256509535516)
XLA Ops:
  0.0 3.0 %collective-permute-start.2 = (bf16[128,2048]{1,0:T(8,128)(2,1)}, bf16[128,2048]{1,0:T(8,128)(2,1)S(1)}, u32[]{:S(2)}, u32[]{:S(2)}) collective-permute-start(bf16[128,2048]{1,0:T(8,128)(2,1)} %refs_0_), channel_id=1, source_target_pairs={{0,4},{1,3},{4,8},{5,1},{8,12},{9,5},{12,14},{13,9},{14,10},{15,13... | collective-permute-start | bytes 1572872 | tf_op jit(solution)/shard_map/ppermute | solution.py:180
  3.7 10.9 %collective-permute-done.2.refs_0_ = bf16[128,2048]{1,0:T(8,128)(2,1)S(1)} collective-permute-done((bf16[128,2048]{1,0:T(8,128)(2,1)}, bf16[128,2048]{1,0:T(8,128)(2,1)S(1)}, u32[]{:S(2)}, u32[]{:S(2)}) %collective-permute-start.2) | collective-permute-done | bytes 524320 | tf_op jit(solution)/shard_map/ppermute | solution.py:180
  14.7 2.4 %collective-permute-start.3 = (bf16[128,2048]{1,0:T(8,128)(2,1)S(1)}, bf16[128,2048]{1,0:T(8,128)(2,1)S(1)}, u32[]{:S(2)}, u32[]{:S(2)}) collective-permute-start(bf16[128,2048]{1,0:T(8,128)(2,1)S(1)} %collective-permute-done.2.refs_0_), channel_id=1, source_target_pairs={{0,4},{1,3},{4,8},{5,1},{8,12},{9,5},{12,14},{13,9},{14,10},{15,13... | collective-permute-start | bytes 1572872 | tf_op jit(solution)/shard_map/ppermute | solution.py:180
  18.3 5.8 %all-to-all-start = ((f32[16,1,128]{2,1,0:T(1,128)}), f32[16,1,128]{2,1,0:T(1,128)S(1)}, u32[]{:S(2)}, u32[]{:S(2)}) async-start(f32[16,1,128]{2,1,0:T(1,128)} %bitcast.3), calls=%async_computation | async-start | bytes 16384 | tf_op jit(solution)/shard_map/all_to_all | solution.py:197
  25.3 1.7 %collective-permute-start.1 = (bf16[128,2048]{1,0:T(8,128)(2,1)S(1)}, bf16[128,2048]{1,0:T(8,128)(2,1)S(1)}, u32[]{:S(2)}, u32[]{:S(2)}) collective-permute-start(bf16[128,2048]{1,0:T(8,128)(2,1)S(1)} %collective-permute-done.refs_0_), channel_id=1, source_target_pairs={{0,4},{1,3},{4,8},{5,1},{8,12},{9,5},{12,14},{13,9},{14,10},{15,13... | collective-permute-start | bytes 1572872 | tf_op jit(solution)/shard_map/ppermute | solution.py:180
  27.0 3.6 %all-to-all-done = f32[16,1,128]{2,1,0:T(1,128)S(1)} async-done(((f32[16,1,128]{2,1,0:T(1,128)}), f32[16,1,128]{2,1,0:T(1,128)S(1)}, u32[]{:S(2)}, u32[]{:S(2)}) %all-to-all-start) | async-done | bytes 8224 | tf_op jit(solution)/shard_map/all_to_all | solution.py:197
  30.6 1.9 %copy-done = bf16[768,2048]{1,0:T(8,128)(2,1)S(1)} copy-done((bf16[768,2048]{1,0:T(8,128)(2,1)S(1)}, bf16[768,2048]{1,0:T(8,128)(2,1)}, u32[]{:S(2)}) %copy-start) | copy-done | bytes 3145752
  32.5 5.5 %shard_map.64 = (bf16[128,2048]{1,0:T(8,128)(2,1)S(1)}, bf16[128,2048]{1,0:T(8,128)(2,1)S(1)}, bf16[2,768,2048]{2,1,0:T(8,128)(2,1)S(1)}, bf16[768,2048]{1,0:T(8,128)(2,1)S(1)}) custom-call(s32[18]{0:T(128)S(1)} %dynamic-slice_bitcast_fusion.sources_ref, f32[16,128]{1,0:T(8,128)S(1)} %bitcast.6, bf16[128,2048]{1,0:T(8,128)(2,1)S(1)} %collective-permute-done.2.refs_0_, ...), custom_call_target="tpu_custom_call" | custom-call | flops 2415919104 | bytes 9437184 | tf_op jit(solution)/shard_map/pallas_call | solution.py:128
  38.5 3.2 %shard_map.65 = (bf16[128,2048]{1,0:T(8,128)(2,1)S(1)}, bf16[128,2048]{1,0:T(8,128)(2,1)S(1)}) custom-call(s32[18]{0:T(128)S(1)} %dynamic-slice_bitcast_fusion.sources_ref, f32[16,128]{1,0:T(8,128)S(1)} %bitcast.7, bf16[128,2048]{1,0:T(8,128)(2,1)S(1)} %collective-permute-done.refs_0_, bf16[128,2048]{1,0:T(8,128)(2,1)S(1)} %collective-permute-done.5.refs_1_, ...), custom_call_target="tpu_custom_call" | custom-call | flops 2415919104 | bytes 9437184 | tf_op jit(solution)/shard_map/pallas_call | solution.py:128
  43.6 3.2 %shard_map.66 = (bf16[128,2048]{1,0:T(8,128)(2,1)S(1)}, bf16[128,2048]{1,0:T(8,128)(2,1)S(1)}) custom-call(s32[18]{0:T(128)S(1)} %dynamic-slice_bitcast_fusion.sources_ref, f32[16,128]{1,0:T(8,128)S(1)} %bitcast.8, bf16[128,2048]{1,0:T(8,128)(2,1)S(1)} %collective-permute-done.3.refs_0_, bf16[128,2048]{1,0:T(8,128)(2,1)S(1)} %collective-permute-done.7.refs_1_, ...), custom_call_target="tpu_custom_call" | custom-call | flops 2415919104 | bytes 9437184 | tf_op jit(solution)/shard_map/pallas_call | solution.py:128
  47.8 3.2 %shard_map.67 = (bf16[128,2048]{1,0:T(8,128)(2,1)S(1)}, bf16[128,2048]{1,0:T(8,128)(2,1)S(1)}) custom-call(s32[18]{0:T(128)S(1)} %dynamic-slice_bitcast_fusion.sources_ref, f32[16,128]{1,0:T(8,128)S(1)} %bitcast.9, bf16[128,2048]{1,0:T(8,128)(2,1)S(1)} %collective-permute-done.1.refs_0_, bf16[128,2048]{1,0:T(8,128)(2,1)S(1)} %collective-permute-done.8.refs_1_, ...), custom_call_target="tpu_custom_call" | custom-call | flops 2415919104 | bytes 9437184 | tf_op jit(solution)/shard_map/pallas_call | solution.py:128
  51.0 1.9 %collective-permute-done.9.refs_0_ = bf16[128,2048]{1,0:T(8,128)(2,1)S(1)} collective-permute-done((bf16[128,2048]{1,0:T(8,128)(2,1)S(1)}, bf16[128,2048]{1,0:T(8,128)(2,1)S(1)}, u32[]{:S(2)}, u32[]{:S(2)}) %collective-permute-start.9) | collective-permute-done | bytes 524320 | tf_op jit(solution)/shard_map/ppermute | solution.py:180
  53.6 3.2 %shard_map.68 = (bf16[128,2048]{1,0:T(8,128)(2,1)S(1)}, bf16[128,2048]{1,0:T(8,128)(2,1)S(1)}) custom-call(s32[18]{0:T(128)S(1)} %dynamic-slice_bitcast_fusion.sources_ref, f32[16,128]{1,0:T(8,128)S(1)} %bitcast.10, bf16[128,2048]{1,0:T(8,128)(2,1)S(1)} %collective-permute-done.6.refs_0_, bf16[128,2048]{1,0:T(8,128)(2,1)S(1)} %collective-permute-done.11.refs_1_, ...), custom_call_target="tpu_custom_call" | custom-call | flops 2415919104 | bytes 9437184 | tf_op jit(solution)/shard_map/pallas_call | solution.py:128
  56.9 2.6 %collective-permute-done.13.refs_1_ = bf16[64,2048]{1,0:T(8,128)(2,1)S(1)} collective-permute-done((bf16[64,2048]{1,0:T(8,128)(2,1)S(1)}, bf16[64,2048]{1,0:T(8,128)(2,1)S(1)}, u32[]{:S(2)}, u32[]{:S(2)}) %collective-permute-start.13) | collective-permute-done | bytes 262176 | tf_op jit(solution)/shard_map/ppermute | solution.py:180
  60.5 3.2 %shard_map.69 = bf16[128,2048]{1,0:T(8,128)(2,1)S(1)} custom-call(s32[18]{0:T(128)S(1)} %dynamic-slice_bitcast_fusion.sources_ref, f32[16,128]{1,0:T(8,128)S(1)} %bitcast.11, bf16[64,2048]{1,0:T(8,128)(2,1)S(1)} %collective-permute-done.10.refs_0_, bf16[64,2048]{1,0:T(8,128)(2,1)S(1)} %collective-permute-done.13.refs_1_, ...), custom_call_target="tpu_custom_call" | custom-call | flops 1207959552 | bytes 9437184 | tf_op jit(solution)/shard_map/pallas_call | solution.py:128
  64.4 3.2 %shard_map.70 = bf16[128,2048]{1,0:T(8,128)(2,1)S(1)} custom-call(s32[18]{0:T(128)S(1)} %dynamic-slice_bitcast_fusion.sources_ref, f32[16,128]{1,0:T(8,128)S(1)} %bitcast.12, bf16[64,2048]{1,0:T(8,128)(2,1)S(1)} %collective-permute-done.12.refs_0_, bf16[64,2048]{1,0:T(8,128)(2,1)S(1)} %collective-permute-done.14.refs_1_, ...), custom_call_target="tpu_custom_call" | custom-call | flops 1207959552 | bytes 9437184 | tf_op jit(solution)/shard_map/pallas_call | solution.py:128
  69.0 3.2 %shard_map.71 = (bf16[128,2048]{1,0:T(8,128)(2,1)S(1)}, bf16[128,2048]{1,0:T(8,128)(2,1)S(1)}) custom-call(s32[18]{0:T(128)S(1)} %dynamic-slice_bitcast_fusion.sources_ref, f32[16,128]{1,0:T(8,128)S(1)} %bitcast.13, bf16[128,2048]{1,0:T(8,128)(2,1)S(1)} %collective-permute-done.9.refs_0_, bf16[128,2048]{1,0:T(8,128)(2,1)S(1)} %collective-permute-done.16.refs_1_, ...), custom_call_target="tpu_custom_call" | custom-call | flops 402653184 | bytes 1572864 | tf_op jit(solution)/shard_map/pallas_call | solution.py:128
  74.9 2.1 %collective-permute-done.20 = bf16[64,2048]{1,0:T(8,128)(2,1)S(1)} collective-permute-done((bf16[64,2048]{1,0:T(8,128)(2,1)S(1)}, bf16[64,2048]{1,0:T(8,128)(2,1)S(1)}, u32[]{:S(2)}, u32[]{:S(2)}) %collective-permute-start.20) | collective-permute-done | bytes 262176 | tf_op jit(solution)/shard_map/ppermute | solution.py:180
  78.1 5.4 %collective-permute-done.22 = bf16[128,2048]{1,0:T(8,128)(2,1)S(1)} collective-permute-done((bf16[128,2048]{1,0:T(8,128)(2,1)S(1)}, bf16[128,2048]{1,0:T(8,128)(2,1)S(1)}, u32[]{:S(2)}, u32[]{:S(2)}) %collective-permute-start.22) | collective-permute-done | bytes 524320 | tf_op jit(solution)/shard_map/ppermute | solution.py:180
  84.2 4.9 %collective-permute-done.24 = bf16[128,2048]{1,0:T(8,128)(2,1)S(1)} collective-permute-done((bf16[128,2048]{1,0:T(8,128)(2,1)S(1)}, bf16[128,2048]{1,0:T(8,128)(2,1)S(1)}, u32[]{:S(2)}, u32[]{:S(2)}) %collective-permute-start.24) | collective-permute-done | bytes 524320 | tf_op jit(solution)/shard_map/ppermute | solution.py:180
  90.1 3.3 %shard_map.72 = (bf16[128,2048]{1,0:T(8,128)(2,1)S(1)}, bf16[128,2048]{1,0:T(8,128)(2,1)S(1)}) custom-call(s32[18]{0:T(128)S(1)} %dynamic-slice_bitcast_fusion.sources_ref, f32[16,128]{1,0:T(8,128)S(1)} %bitcast.14, bf16[128,2048]{1,0:T(8,128)(2,1)S(1)} %copy-done.1, bf16[128,2048]{1,0:T(8,128)(2,1)S(1)} %collective-permute-done.25.refs_1_, ...), custom_call_target="tpu_custom_call" | custom-call | flops 2415919104 | bytes 9437184 | tf_op jit(solution)/shard_map/pallas_call | solution.py:128
  95.4 4.9 %collective-permute-done.31 = bf16[128,2048]{1,0:T(8,128)(2,1)S(1)} collective-permute-done((bf16[128,2048]{1,0:T(8,128)(2,1)S(1)}, bf16[128,2048]{1,0:T(8,128)(2,1)S(1)}, u32[]{:S(2)}, u32[]{:S(2)}) %collective-permute-start.31) | collective-permute-done | bytes 524320 | tf_op jit(solution)/shard_map/ppermute | solution.py:180
  100.7 5.3 %collective-permute-done.29.refs_2_ = bf16[128,2048]{1,0:T(8,128)(2,1)S(1)} collective-permute-done((bf16[128,2048]{1,0:T(8,128)(2,1)S(1)}, bf16[128,2048]{1,0:T(8,128)(2,1)S(1)}, u32[]{:S(2)}, u32[]{:S(2)}) %collective-permute-start.29) | collective-permute-done | bytes 524320 | tf_op jit(solution)/shard_map/ppermute | solution.py:180
  106.2 3.6 %collective-permute-done.32 = bf16[128,2048]{1,0:T(8,128)(2,1)S(1)} collective-permute-done((bf16[128,2048]{1,0:T(8,128)(2,1)S(1)}, bf16[128,2048]{1,0:T(8,128)(2,1)S(1)}, u32[]{:S(2)}, u32[]{:S(2)}) %collective-permute-start.32) | collective-permute-done | bytes 524320 | tf_op jit(solution)/shard_map/ppermute | solution.py:180
  (79 shorter events, 19.2 us)
Async XLA Ops:
  0.0 14.7 %collective-permute-start.2 = (bf16[128,2048]{1,0:T(8,128)(2,1)}, bf16[128,2048]{1,0:T(8,128)(2,1)S(1)}, u32[]{:S(2)}, u32[]{:S(2)}) collective-permute-start(bf16[128,2048]{1,0:T(8,128)(2,1)} %refs_0_), channel_id=1, source_target_pairs={{0,4},{1,3},{4,8},{5,1},{8,12},{9,5},{12,14},{13,9},{14,10},{15,13... | collective-permute-start | bytes 1572872 | tf_op jit(solution)/shard_map/ppermute | solution.py:180
  3.0 21.1 %collective-permute-start = (bf16[128,2048]{1,0:T(8,128)(2,1)}, bf16[128,2048]{1,0:T(8,128)(2,1)S(1)}, u32[]{:S(2)}, u32[]{:S(2)}) collective-permute-start(bf16[128,2048]{1,0:T(8,128)(2,1)} %refs_0_), channel_id=1, source_target_pairs={{0,3},{1,4},{4,1},{5,8},{8,5},{9,12},{12,9},{13,14},{14,13},{15,10... | collective-permute-start | bytes 1572872 | tf_op jit(solution)/shard_map/ppermute | solution.py:180
  14.7 15.9 %collective-permute-start.4 = (bf16[128,2048]{1,0:T(8,128)(2,1)S(1)}, bf16[128,2048]{1,0:T(8,128)(2,1)S(1)}, u32[]{:S(2)}, u32[]{:S(2)}) collective-permute-start(bf16[128,2048]{1,0:T(8,128)(2,1)S(1)} %collective-permute-done.2.refs_0_), channel_id=1, source_target_pairs={{0,1},{1,0},{4,5},{5,4},{8,9},{9,8},{12,13},{13,12},{14,15},{15,14... | collective-permute-start | bytes 1572872 | tf_op jit(solution)/shard_map/ppermute | solution.py:180
  14.7 23.3 %collective-permute-start.3 = (bf16[128,2048]{1,0:T(8,128)(2,1)S(1)}, bf16[128,2048]{1,0:T(8,128)(2,1)S(1)}, u32[]{:S(2)}, u32[]{:S(2)}) collective-permute-start(bf16[128,2048]{1,0:T(8,128)(2,1)S(1)} %collective-permute-done.2.refs_0_), channel_id=1, source_target_pairs={{0,4},{1,3},{4,8},{5,1},{8,12},{9,5},{12,14},{13,9},{14,10},{15,13... | collective-permute-start | bytes 1572872 | tf_op jit(solution)/shard_map/ppermute | solution.py:180
  18.3 12.2 %all-to-all-start = ((f32[16,1,128]{2,1,0:T(1,128)}), f32[16,1,128]{2,1,0:T(1,128)S(1)}, u32[]{:S(2)}, u32[]{:S(2)}) async-start(f32[16,1,128]{2,1,0:T(1,128)} %bitcast.3), calls=%async_computation | async-start | bytes 16384 | tf_op jit(solution)/shard_map/all_to_all | solution.py:197
  24.2 14.3 %collective-permute-start.5 = (bf16[128,2048]{1,0:T(8,128)(2,1)S(1)}, bf16[128,2048]{1,0:T(8,128)(2,1)S(1)}, u32[]{:S(2)}, u32[]{:S(2)}) collective-permute-start(bf16[128,2048]{1,0:T(8,128)(2,1)S(1)} %collective-permute-done.refs_0_), channel_id=1, source_target_pairs={{0,1},{1,0},{4,5},{5,4},{8,9},{9,8},{12,13},{13,12},{14,15},{15,14... | collective-permute-start | bytes 1572872 | tf_op jit(solution)/shard_map/ppermute | solution.py:180
  25.3 16.4 %collective-permute-start.1 = (bf16[128,2048]{1,0:T(8,128)(2,1)S(1)}, bf16[128,2048]{1,0:T(8,128)(2,1)S(1)}, u32[]{:S(2)}, u32[]{:S(2)}) collective-permute-start(bf16[128,2048]{1,0:T(8,128)(2,1)S(1)} %collective-permute-done.refs_0_), channel_id=1, source_target_pairs={{0,4},{1,3},{4,8},{5,1},{8,12},{9,5},{12,14},{13,9},{14,10},{15,13... | collective-permute-start | bytes 1572872 | tf_op jit(solution)/shard_map/ppermute | solution.py:180
  38.0 9.2 %collective-permute-start.6 = (bf16[128,2048]{1,0:T(8,128)(2,1)S(1)}, bf16[128,2048]{1,0:T(8,128)(2,1)S(1)}, u32[]{:S(2)}, u32[]{:S(2)}) collective-permute-start(bf16[128,2048]{1,0:T(8,128)(2,1)S(1)} %collective-permute-done.3.refs_0_), channel_id=1, source_target_pairs={{0,4},{1,3},{4,8},{5,1},{8,12},{9,5},{12,14},{13,9},{14,10},{15,13... | collective-permute-start | bytes 1572872 | tf_op jit(solution)/shard_map/ppermute | solution.py:180
  42.0 10.9 %collective-permute-start.9 = (bf16[128,2048]{1,0:T(8,128)(2,1)S(1)}, bf16[128,2048]{1,0:T(8,128)(2,1)S(1)}, u32[]{:S(2)}, u32[]{:S(2)}) collective-permute-start(bf16[128,2048]{1,0:T(8,128)(2,1)S(1)} %collective-permute-done.1.refs_0_), channel_id=1, source_target_pairs={{0,4},{1,3},{4,8},{5,1},{8,12},{9,5},{12,14},{13,9},{14,10},{15,13... | collective-permute-start | bytes 1572872 | tf_op jit(solution)/shard_map/ppermute | solution.py:180
  47.3 9.5 %collective-permute-start.10 = (bf16[64,2048]{1,0:T(8,128)(2,1)S(1)}, bf16[64,2048]{1,0:T(8,128)(2,1)S(1)}, u32[]{:S(2)}, u32[]{:S(2)}) collective-permute-start(bf16[64,2048]{1,0:T(8,128)(2,1)S(1)} %slice.32), channel_id=1, source_target_pairs={{0,4},{1,3},{4,8},{5,1},{8,12},{9,5},{12,14},{13,9},{14,10},{15,13... | collective-permute-start | bytes 786440 | tf_op jit(solution)/shard_map/ppermute | solution.py:180
  59.5 8.8 %collective-permute-start.16 = (bf16[128,2048]{1,0:T(8,128)(2,1)S(1)}, bf16[128,2048]{1,0:T(8,128)(2,1)S(1)}, u32[]{:S(2)}, u32[]{:S(2)}) collective-permute-start(bf16[128,2048]{1,0:T(8,128)(2,1)S(1)} %collective-permute-done.9.refs_0_), channel_id=1, source_target_pairs={{0,1},{1,0},{4,5},{5,4},{8,9},{9,8},{12,13},{13,12},{14,15},{15,14... | collective-permute-start | bytes 1572872 | tf_op jit(solution)/shard_map/ppermute | solution.py:180
  60.0 17.5 %collective-permute-start.21 = (bf16[128,2048]{1,0:T(8,128)(2,1)S(1)}, bf16[128,2048]{1,0:T(8,128)(2,1)S(1)}, u32[]{:S(2)}, u32[]{:S(2)}) collective-permute-start(bf16[128,2048]{1,0:T(8,128)(2,1)S(1)} %get-tuple-element.69), channel_id=1, source_target_pairs={{0,1},{1,0},{4,5},{5,4},{8,9},{9,8},{12,13},{13,12},{14,15},{15,14... | collective-permute-start | bytes 1572872 | tf_op jit(solution)/shard_map/ppermute | solution.py:180
  60.0 23.7 %collective-permute-start.23 = (bf16[128,2048]{1,0:T(8,128)(2,1)S(1)}, bf16[128,2048]{1,0:T(8,128)(2,1)S(1)}, u32[]{:S(2)}, u32[]{:S(2)}) collective-permute-start(bf16[128,2048]{1,0:T(8,128)(2,1)S(1)} %get-tuple-element.71), channel_id=1, source_target_pairs={{0,1},{1,0},{4,5},{5,4},{8,9},{9,8},{12,13},{13,12},{14,15},{15,14... | collective-permute-start | bytes 1572872 | tf_op jit(solution)/shard_map/ppermute | solution.py:180
  63.9 8.4 %collective-permute-start.17 = (bf16[128,2048]{1,0:T(8,128)(2,1)S(1)}, bf16[128,2048]{1,0:T(8,128)(2,1)S(1)}, u32[]{:S(2)}, u32[]{:S(2)}) collective-permute-start(bf16[128,2048]{1,0:T(8,128)(2,1)S(1)} %get-tuple-element.65), channel_id=1, source_target_pairs={{0,1},{1,0},{4,5},{5,4},{8,9},{9,8},{12,13},{13,12},{14,15},{15,14... | collective-permute-start | bytes 1572872 | tf_op jit(solution)/shard_map/ppermute | solution.py:180
  68.3 8.7 %collective-permute-start.20 = (bf16[64,2048]{1,0:T(8,128)(2,1)S(1)}, bf16[64,2048]{1,0:T(8,128)(2,1)S(1)}, u32[]{:S(2)}, u32[]{:S(2)}) collective-permute-start(bf16[64,2048]{1,0:T(8,128)(2,1)S(1)} %add_convert_fusion.5), channel_id=1, source_target_pairs={{0,2},{1,5},{4,0},{5,9},{8,4},{9,13},{12,8},{13,15},{14,12},{15,11... | collective-permute-start | bytes 786440 | tf_op jit(solution)/shard_map/ppermute | solution.py:180
  74.3 9.2 %collective-permute-start.22 = (bf16[128,2048]{1,0:T(8,128)(2,1)S(1)}, bf16[128,2048]{1,0:T(8,128)(2,1)S(1)}, u32[]{:S(2)}, u32[]{:S(2)}) collective-permute-start(bf16[128,2048]{1,0:T(8,128)(2,1)S(1)} %pad_maximum_fusion), channel_id=1, source_target_pairs={{0,2},{1,5},{4,0},{5,9},{8,4},{9,13},{12,8},{13,15},{14,12},{15,11... | collective-permute-start | bytes 1572872 | tf_op jit(solution)/shard_map/ppermute | solution.py:180
  77.1 12.0 %collective-permute-start.24 = (bf16[128,2048]{1,0:T(8,128)(2,1)S(1)}, bf16[128,2048]{1,0:T(8,128)(2,1)S(1)}, u32[]{:S(2)}, u32[]{:S(2)}) collective-permute-start(bf16[128,2048]{1,0:T(8,128)(2,1)S(1)} %pad_maximum_fusion.1), channel_id=1, source_target_pairs={{0,2},{1,5},{4,0},{5,9},{8,4},{9,13},{12,8},{13,15},{14,12},{15,11... | collective-permute-start | bytes 1572872 | tf_op jit(solution)/shard_map/ppermute | solution.py:180
  77.5 12.5 %collective-permute-start.25 = (bf16[128,2048]{1,0:T(8,128)(2,1)S(1)}, bf16[128,2048]{1,0:T(8,128)(2,1)S(1)}, u32[]{:S(2)}, u32[]{:S(2)}) collective-permute-start(bf16[128,2048]{1,0:T(8,128)(2,1)S(1)} %copy-done.1), channel_id=1, source_target_pairs={{0,1},{1,0},{4,5},{5,4},{8,9},{9,8},{12,13},{13,12},{14,15},{15,14... | collective-permute-start | bytes 1572872 | tf_op jit(solution)/shard_map/ppermute | solution.py:180
  77.6 15.9 %collective-permute-start.27 = (bf16[128,2048]{1,0:T(8,128)(2,1)S(1)}, bf16[128,2048]{1,0:T(8,128)(2,1)S(1)}, u32[]{:S(2)}, u32[]{:S(2)}) collective-permute-start(bf16[128,2048]{1,0:T(8,128)(2,1)S(1)} %get-tuple-element.76), channel_id=1, source_target_pairs={{0,1},{1,0},{4,5},{5,4},{8,9},{9,8},{12,13},{13,12},{14,15},{15,14... | collective-permute-start | bytes 1572872 | tf_op jit(solution)/shard_map/ppermute | solution.py:180
  83.5 12.0 %collective-permute-start.30 = (bf16[128,2048]{1,0:T(8,128)(2,1)S(1)}, bf16[128,2048]{1,0:T(8,128)(2,1)S(1)}, u32[]{:S(2)}, u32[]{:S(2)}) collective-permute-start(bf16[128,2048]{1,0:T(8,128)(2,1)S(1)} %get-tuple-element.78), channel_id=1, source_target_pairs={{0,1},{1,0},{4,5},{5,4},{8,9},{9,8},{12,13},{13,12},{14,15},{15,14... | collective-permute-start | bytes 1572872 | tf_op jit(solution)/shard_map/ppermute | solution.py:180
  83.8 11.0 %collective-permute-start.28 = (bf16[128,2048]{1,0:T(8,128)(2,1)S(1)}, bf16[128,2048]{1,0:T(8,128)(2,1)S(1)}, u32[]{:S(2)}, u32[]{:S(2)}) collective-permute-start(bf16[128,2048]{1,0:T(8,128)(2,1)S(1)} %add_convert_fusion.4), channel_id=1, source_target_pairs={{0,2},{1,5},{4,0},{5,9},{8,4},{9,13},{12,8},{13,15},{14,12},{15,11... | collective-permute-start | bytes 1572872 | tf_op jit(solution)/shard_map/ppermute | solution.py:180
  89.4 11.0 %collective-permute-start.31 = (bf16[128,2048]{1,0:T(8,128)(2,1)S(1)}, bf16[128,2048]{1,0:T(8,128)(2,1)S(1)}, u32[]{:S(2)}, u32[]{:S(2)}) collective-permute-start(bf16[128,2048]{1,0:T(8,128)(2,1)S(1)} %add_convert_fusion.3), channel_id=1, source_target_pairs={{0,2},{1,5},{4,0},{5,9},{8,4},{9,13},{12,8},{13,15},{14,12},{15,11... | collective-permute-start | bytes 1572872 | tf_op jit(solution)/shard_map/ppermute | solution.py:180
  95.0 11.0 %collective-permute-start.29 = (bf16[128,2048]{1,0:T(8,128)(2,1)S(1)}, bf16[128,2048]{1,0:T(8,128)(2,1)S(1)}, u32[]{:S(2)}, u32[]{:S(2)}) collective-permute-start(bf16[128,2048]{1,0:T(8,128)(2,1)S(1)} %add_convert_fusion.2), channel_id=1, source_target_pairs={{0,2},{1,5},{4,0},{5,9},{8,4},{9,13},{12,8},{13,15},{14,12},{15,11... | collective-permute-start | bytes 1572872 | tf_op jit(solution)/shard_map/ppermute | solution.py:180
  100.6 9.2 %collective-permute-start.32 = (bf16[128,2048]{1,0:T(8,128)(2,1)S(1)}, bf16[128,2048]{1,0:T(8,128)(2,1)S(1)}, u32[]{:S(2)}, u32[]{:S(2)}) collective-permute-start(bf16[128,2048]{1,0:T(8,128)(2,1)S(1)} %add_convert_fusion.1), channel_id=1, source_target_pairs={{0,3},{1,4},{4,1},{5,8},{8,5},{9,12},{12,9},{13,14},{14,13},{15,10... | collective-permute-start | bytes 1572872 | tf_op jit(solution)/shard_map/ppermute | solution.py:180
  (12 other events, 63.0 us)

commit v6 on v5

--- a/solution.py
+++ b/solution.py
@@ -52,20 +52,8 @@
     return list(range(0, chips, 2)) + list(range(chips - 1, 0, -2))
 
 
-def sources(chips):
-    order = snake(chips)
-    table = np.zeros((2 * chips, 2 + 2 * chips), np.int32)
-    for place in range(chips):
-        for core in (0, 1):
-            turn = 1 - 2 * core
-            row = [(0, core), (0, 1 - core)]
-            for step in range(1, chips // 2 + 1):
-                row += [(-step, core), (-step, 1 - core), (step, 1 - core), (step, core)]
-            table[2 * order[place] + core] = [2 * order[(place + turn * d) % chips] + c for d, c in row]
-    return table
-
-
-def half_expert_kernel(pieces, load, split, sources_ref, gates_ref, *refs):
+def half_expert_kernel(pieces, gate_count, load, split, mine_ref, *refs):
+    gates, refs = refs[:gate_count], refs[gate_count:]
     blocks, refs = refs[: len(pieces)], refs[len(pieces) :]
     if load:
         (gate_up_far, down_far), refs = refs[:2], refs[2:]
@@ -86,11 +74,12 @@
 
     weights = []
     at = 0
-    for block, (source, token) in zip(blocks, pieces):
+    for block, (place, kind, token) in zip(blocks, pieces):
         count = block.shape[0]
         rows[at : at + count, :] = block[...]
         at += count
-        line = gates_ref[pl.ds(sources_ref[source], 1), :]
+        experts = gates[place].shape[0] // 2
+        line = gates[place][pl.ds(mine_ref[0] + kind * experts, 1), :]
         column = jnp.broadcast_to(line, (8, line.shape[1])).T[:, :1]
         weights.append(column[token : token + count])
     weight = jnp.concatenate(weights)
@@ -116,7 +105,7 @@
             out[:, low : low + tile] = product[i * share : (i + 1) * share]
 
 
-def half_expert(places, gates, pieces, blocks, gate_up, down_proj, load=False, cost=6, split=2):
+def half_expert(mine, gates, pieces, blocks, gate_up, down_proj, load=False, cost=2, split=2):
     height = sum(block.shape[0] for block in blocks)
     units, width = down_proj.shape
     whole = pl.BlockSpec(memory_space=pltpu.VMEM)
@@ -126,10 +115,10 @@
     if load:
         scratch.append(pltpu.SemaphoreType.DMA((units // 256 + 1 if units % 256 == 0 else 2,)))
     return pl.pallas_call(
-        functools.partial(half_expert_kernel, tuple(pieces), load, split),
+        functools.partial(half_expert_kernel, tuple(pieces), len(gates), load, split),
         out_shape=outs + weights,
         in_specs=[pl.BlockSpec(memory_space=pltpu.SMEM)]
-        + [whole] * (len(blocks) + 1)
+        + [whole] * (len(gates) + len(blocks))
         + [pl.BlockSpec(memory_space=pltpu.HBM) if load else whole] * 2,
         out_specs=[whole] * (split + len(weights)),
         scratch_shapes=scratch,
@@ -139,7 +128,7 @@
             bytes_accessed=cost * units * width,
             transcendentals=height * units,
         ),
-    )(places, gates, *blocks, gate_up, down_proj)
+    )(mine, *gates, *blocks, gate_up, down_proj)
 
 
 def sum_kernel(*refs):
@@ -166,15 +155,16 @@
     rows = tokens.shape[0]
     half = rows // 2
     chains = (0, 1)
-    forth, back, across, cores = [], [], [], []
-    for place in range(chips):
-        for core in (0, 1):
-            device = 2 * order[place] + core
-            ahead, behind = order[(place + 1 - 2 * core) % chips], order[(place - 1 + 2 * core) % chips]
-            forth.append((device, 2 * ahead + core))
-            back.append((device, 2 * behind + core))
-            across.append((device, 2 * behind + 1 - core))
-            cores.append((device, device ^ 1))
+
+    def moved(steps, swap=False):
+        pairs = []
+        for place in range(chips):
+            for core in (0, 1):
+                target = order[(place + steps * (1 - 2 * core)) % chips]
+                pairs.append((2 * order[place] + core, 2 * target + (1 - core if swap else core)))
+        return pairs
+
+    forth, back, across, cores = moved(1), moved(-1), moved(-1, True), moved(0, True)
 
     def send(value, pairs):
         return lax.ppermute(value, "blk", pairs)
@@ -191,42 +181,49 @@
     ring = [send(tokens, forth), send(tokens, across)]
     other = send(tokens, cores)
 
-    places = lax.dynamic_index_in_dim(jnp.asarray(sources(chips)), lax.axis_index("blk"), 0, keepdims=False)
+    expert = (lax.axis_index("blk") // 2).astype(jnp.int32).reshape(1)
     chosen = jnp.arange(chips, dtype=jnp.int32)[:, None, None] == expert_ids.T[None]
     weight = jnp.sum(jnp.where(chosen, route_gate.T[None], 0.0), axis=1)
-    gates = lax.all_to_all(jnp.repeat(weight, 2, axis=0), "blk", split_axis=0, concat_axis=0, tiled=True)
-    gates = gates.reshape(-1, rows)
-
-    results, near = {}, None
+    weight = jnp.concatenate([weight, send(weight, cores)])
+    gates = [[weight]]
+    for step in range(1, far):
+        gates.append([send(weight, moved(step)), send(weight, moved(-step))])
+    gates.append([send(weight, moved(far))])
+    ring[0] = after(ring[0], ring[1], *sum(gates, []))
+
+    def expert_rows(step, c, inputs, **options):
+        pieces = [(0, c, 0), (1, 1 - c, 0)]
+        return half_expert(expert, gates[step], pieces, inputs, *near, **options)
+
+    results, near = {}, (gate_up, down_proj)
     earlier = ring[1]
     for step in range(1, far):
         swapped = [send(block, cores) for block in ring]
-        blocks = ring
+        blocks = list(ring)
         if step < far - 1:
             ring = [send(block, forth) for block in ring]
         else:
-            ring = [send(ring[0][:half], forth), send(ring[1][half:], forth)]
+            ring[0] = send(ring[0][:half], forth)
+            ring[1] = send(after(ring[1], ring[0])[half:], forth)
         for c in chains:
-            pieces = [(4 * step - 2 + c, 0), (4 * step + c, 0)]
+            if c == 1 and step == 1:
+                delayed = [blocks[c], swapped[c]]
+                continue
             inputs = [after(blocks[c], earlier), swapped[c]]
-            if near is None:
-                kept, given, *near = half_expert(places, gates, pieces, inputs, gate_up, down_proj, load=True)
-            elif (step, c) != (far - 1, 1):
-                kept, given = half_expert(places, gates, pieces, inputs, *near)
+            if step == 1:
+                kept, given, *near = expert_rows(step, c, inputs, load=True)
             else:
-                last = pieces, [blocks[c], swapped[c]]
-                break
+                kept, given = expert_rows(step, c, inputs)
             results[step, c] = kept, send(given, cores)
             ring[c] = earlier = after(ring[c], kept)
-
-    base = 4 * far - 2
-    pieces = [(base, 0), (base + 1, half)]
-    (given,) = half_expert(places, gates, pieces, ring, *near, split=1)
+        if step == 1:
+            earlier = ring[1]
+
+    (given,) = half_expert(expert, gates[far], [(0, 0, 0), (0, 1, half)], ring, *near, split=1)
     swapped = [send(block, cores) for block in ring]
     swapped[0] = after(swapped[0], given)
     given = send(given, cores)
-    pieces = [(base + 2, 0), (base + 3, half)]
-    (kept,) = half_expert(places, gates, pieces, swapped, *near, split=1)
+    (kept,) = half_expert(expert, gates[far], [(0, 1, 0), (0, 0, half)], swapped, *near, split=1)
 
     first, second = slice(0, half), slice(half, rows)
     late = []
@@ -234,13 +231,8 @@
     for part in (second, first):
         earlier = rounded(total(after(kept[part], earlier), given[part]))
         late.append(send(earlier, back))
-    pieces, inputs = last
-    inputs[0] = after(inputs[0], earlier)
-    kept, given = half_expert(places, gates, pieces, inputs, *near, cost=1)
-    results[far - 1, 1] = kept, send(given, cores)
 
     sums = []
-    earlier = kept
     for c in chains:
         mine, theirs = results[far - 1, c]
         value = total(after(mine, earlier), theirs)
@@ -250,12 +242,15 @@
             value = jnp.concatenate([value[first] + total(late[c]), value[second]])
         earlier = rounded(value)
         sums.append(send(earlier, back))
+    kept, given = expert_rows(1, 1, [after(delayed[0], earlier), delayed[1]])
+    results[1, 1] = kept, send(given, cores)
+    earlier = kept
     for step in range(far - 2, 1, -1):
         for c in chains:
             mine, theirs = results[step, c]
             earlier = rounded(total(after(mine, earlier), theirs, sums[c]))
             sums[c] = send(earlier, back)
-    kept, given = half_expert(places, gates, [(0, 0), (1, 0)], [after(tokens, earlier), other], *near)
+    kept, given = half_expert(expert, gates[0], [(0, 0, 0), (0, 1, 0)], [after(tokens, earlier), other], *near)
     given = send(given, cores)
     earlier = kept
     for c, pairs in zip(chains, (back, across)):

time: 112 us -> 130 us (1.16)
  waiting for transfers between devices: 48.7 us -> 66.6 us
  starting transfers between devices: 23.7 us -> 30.6 us
  Pallas kernels: 31.5 us -> 26.6 us
    ppermute x33 -> x41, waiting for transfers between devices: 45.1 us -> 66.6 us  [send(): return lax.ppermute(value, 'blk', pairs)]
    ppermute x33 -> x41, starting transfers between devices: 17.9 us -> 30.6 us  [send(): return lax.ppermute(value, 'blk', pairs)]
    all_to_all x1 -> x0, starting transfers between devices: 5.8 us -> none  [by_tokens(): lax.all_to_all(jnp.repeat(weight, 2, axis=0), 'blk', split_axis=0, concat...]
    pallas_call x9, Pallas kernels: 31.3 us -> 26.4 us  [half_expert(): pl.pallas_call(functools.partial(half_expert_kernel, tuple(pieces), len(g...]
    all_to_all x1 -> x0, waiting for transfers between devices: 3.57 us -> none  [by_tokens(): lax.all_to_all(jnp.repeat(weight, 2, axis=0), 'blk', split_axis=0, concat...]
  transfers between devices with their start and end apart: 34 -> 41, of which waited for: 13 -> 20; matrix products, arithmetic and copies ran while one was open for 3% -> 2% of each run, Pallas kernels for 28% -> 21%
where the time goes in v6:
time: 130 us; the launch traced here: 129 us
  waiting for transfers between devices  66.6 us (51%)
  starting transfers between devices  30.6 us (24%)
  Pallas kernels  26.6 us (20%)
  other arithmetic  3.13 us (2%)
  local copies, waits for them, and re-layouts  2.03 us (2%)
    ppermute x41, waiting for transfers between devices, send(): return lax.ppermute(value, 'blk', pairs)  66.6 us
    ppermute x41, starting transfers between devices, send(): return lax.ppermute(value, 'blk', pairs)  30.6 us
    pallas_call x9, Pallas kernels, half_expert(): pl.pallas_call(functools.partial(half_expert_kernel, tuple(pieces), len(g...  26.4 us
  transfers between devices with their start and end apart: 41, of which 20 were waited for; matrix products, arithmetic and copies ran while one was open for 2% of the time, Pallas kernels for 21%

profile of v6, /device:TPU:0, one launch (start us, length us, event | category | flops | bytes accessed | tf_op | source)
XLA Modules:
  0.0 129.3 jit_solution(15350896676301588691)
XLA Ops:
  4.9 3.5 %collective-permute-start.8 = (f32[16,128]{1,0:T(8,128)S(1)}, f32[16,128]{1,0:T(8,128)S(1)}, u32[]{:S(2)}, u32[]{:S(2)}) collective-permute-start(f32[16,128]{1,0:T(8,128)S(1)} %pad_maximum_fusion.2.refs_0_), channel_id=1, source_target_pairs={{0,12},{1,11},{4,14},{5,7},{8,10},{9,3},{12,6},{13,1},{14,2},{15,5... | collective-permute-start | bytes 24584 | tf_op jit(solution)/shard_map/ppermute | solution.py:170
  11.3 6.9 %collective-permute-done.8.refs_0_ = f32[16,128]{1,0:T(8,128)S(1)} collective-permute-done((f32[16,128]{1,0:T(8,128)S(1)}, f32[16,128]{1,0:T(8,128)S(1)}, u32[]{:S(2)}, u32[]{:S(2)}) %collective-permute-start.8) | collective-permute-done | bytes 8224 | tf_op jit(solution)/shard_map/ppermute | solution.py:170
  18.5 2.8 %collective-permute-start.6 = (f32[16,128]{1,0:T(8,128)S(1)}, f32[16,128]{1,0:T(8,128)S(1)}, u32[]{:S(2)}, u32[]{:S(2)}) collective-permute-start(f32[16,128]{1,0:T(8,128)S(1)} %pad_maximum_fusion.2.refs_0_), channel_id=1, source_target_pairs={{0,4},{1,3},{4,8},{5,1},{8,12},{9,5},{12,14},{13,9},{14,10},{15,13... | collective-permute-start | bytes 24584 | tf_op jit(solution)/shard_map/ppermute | solution.py:170
  22.8 2.7 %collective-permute-start.10 = (f32[16,128]{1,0:T(8,128)S(1)}, f32[16,128]{1,0:T(8,128)S(1)}, u32[]{:S(2)}, u32[]{:S(2)}) collective-permute-start(f32[16,128]{1,0:T(8,128)S(1)} %pad_maximum_fusion.2.refs_0_), channel_id=1, source_target_pairs={{0,14},{1,15},{4,10},{5,11},{8,6},{9,7},{12,2},{13,3},{14,0},{15,1... | collective-permute-start | bytes 24584 | tf_op jit(solution)/shard_map/ppermute | solution.py:170
  25.4 3.7 %collective-permute-done.10.refs_0_ = f32[16,128]{1,0:T(8,128)S(1)} collective-permute-done((f32[16,128]{1,0:T(8,128)S(1)}, f32[16,128]{1,0:T(8,128)S(1)}, u32[]{:S(2)}, u32[]{:S(2)}) %collective-permute-start.10) | collective-permute-done | bytes 8224 | tf_op jit(solution)/shard_map/ppermute | solution.py:170
  32.9 4.9 %shard_map.55 = (bf16[128,2048]{1,0:T(8,128)(2,1)S(1)}, bf16[128,2048]{1,0:T(8,128)(2,1)S(1)}, bf16[2,768,2048]{2,1,0:T(8,128)(2,1)S(1)}, bf16[768,2048]{1,0:T(8,128)(2,1)S(1)}) custom-call(s32[1]{0:T(128)} %bitcast.mine_ref, f32[16,128]{1,0:T(8,128)S(1)} %collective-permute-done.6.refs_0_, f32[16,128]{1,0:T(8,128)S(1)} %collective-permute-done.7.refs_1_, ...), custom_call_target="tpu_custom_call" | custom-call | flops 805306368 | bytes 3145728 | tf_op jit(solution)/shard_map/pallas_call | solution.py:117
  39.6 4.4 %collective-permute-done.4.refs_2_ = bf16[128,2048]{1,0:T(8,128)(2,1)S(1)} collective-permute-done((bf16[128,2048]{1,0:T(8,128)(2,1)S(1)}, bf16[128,2048]{1,0:T(8,128)(2,1)S(1)}, u32[]{:S(2)}, u32[]{:S(2)}) %collective-permute-start.4) | collective-permute-done | bytes 524320 | tf_op jit(solution)/shard_map/ppermute | solution.py:170
  44.0 2.7 %shard_map.56 = (bf16[128,2048]{1,0:T(8,128)(2,1)S(1)}, bf16[128,2048]{1,0:T(8,128)(2,1)S(1)}) custom-call(s32[1]{0:T(128)} %bitcast.mine_ref, f32[16,128]{1,0:T(8,128)S(1)} %collective-permute-done.1.refs_0_, f32[16,128]{1,0:T(8,128)S(1)} %collective-permute-done.2.refs_1_, bf16[128,2048]{1,0:T(8,128)(2,1)S(1)} %collective-permute-done.11.refs_2_, ...), custom_call_target="tpu_custom_call" | custom-call | flops 805306368 | bytes 3145728 | tf_op jit(solution)/shard_map/pallas_call | solution.py:117
  46.7 2.9 %collective-permute-done.13.refs_2_ = bf16[128,2048]{1,0:T(8,128)(2,1)S(1)} collective-permute-done((bf16[128,2048]{1,0:T(8,128)(2,1)S(1)}, bf16[128,2048]{1,0:T(8,128)(2,1)S(1)}, u32[]{:S(2)}, u32[]{:S(2)}) %collective-permute-start.13) | collective-permute-done | bytes 524320 | tf_op jit(solution)/shard_map/ppermute | solution.py:170
  49.6 2.7 %shard_map.57 = (bf16[128,2048]{1,0:T(8,128)(2,1)S(1)}, bf16[128,2048]{1,0:T(8,128)(2,1)S(1)}) custom-call(s32[1]{0:T(128)} %bitcast.mine_ref, f32[16,128]{1,0:T(8,128)S(1)} %collective-permute-done.1.refs_0_, f32[16,128]{1,0:T(8,128)S(1)} %collective-permute-done.2.refs_1_, bf16[128,2048]{1,0:T(8,128)(2,1)S(1)} %collective-permute-done.4.refs_2_, ...), custom_call_target="tpu_custom_call" | custom-call | flops 805306368 | bytes 3145728 | tf_op jit(solution)/shard_map/pallas_call | solution.py:117
  52.3 2.9 %collective-permute-done.16.refs_2_ = bf16[128,2048]{1,0:T(8,128)(2,1)S(1)} collective-permute-done((bf16[128,2048]{1,0:T(8,128)(2,1)S(1)}, bf16[128,2048]{1,0:T(8,128)(2,1)S(1)}, u32[]{:S(2)}, u32[]{:S(2)}) %collective-permute-start.16) | collective-permute-done | bytes 524320 | tf_op jit(solution)/shard_map/ppermute | solution.py:170
  55.3 6.4 %collective-permute-done.17.refs_1_ = bf16[64,2048]{1,0:T(8,128)(2,1)S(1)} collective-permute-done((bf16[64,2048]{1,0:T(8,128)(2,1)S(1)}, bf16[64,2048]{1,0:T(8,128)(2,1)S(1)}, u32[]{:S(2)}, u32[]{:S(2)}) %collective-permute-start.17) | collective-permute-done | bytes 262176 | tf_op jit(solution)/shard_map/ppermute | solution.py:170
  61.9 2.7 %shard_map.58 = (bf16[128,2048]{1,0:T(8,128)(2,1)S(1)}, bf16[128,2048]{1,0:T(8,128)(2,1)S(1)}) custom-call(s32[1]{0:T(128)} %bitcast.mine_ref, f32[16,128]{1,0:T(8,128)S(1)} %collective-permute-done.8.refs_0_, f32[16,128]{1,0:T(8,128)S(1)} %collective-permute-done.9.refs_1_, bf16[128,2048]{1,0:T(8,128)(2,1)S(1)} %collective-permute-done.13.refs_2_, ...), custom_call_target="tpu_custom_call" | custom-call | flops 805306368 | bytes 3145728 | tf_op jit(solution)/shard_map/pallas_call | solution.py:117
  65.6 2.7 %shard_map.59 = (bf16[128,2048]{1,0:T(8,128)(2,1)S(1)}, bf16[128,2048]{1,0:T(8,128)(2,1)S(1)}) custom-call(s32[1]{0:T(128)} %bitcast.mine_ref, f32[16,128]{1,0:T(8,128)S(1)} %collective-permute-done.8.refs_0_, f32[16,128]{1,0:T(8,128)S(1)} %collective-permute-done.9.refs_1_, bf16[128,2048]{1,0:T(8,128)(2,1)S(1)} %collective-permute-done.16.refs_2_, ...), custom_call_target="tpu_custom_call" | custom-call | flops 805306368 | bytes 3145728 | tf_op jit(solution)/shard_map/pallas_call | solution.py:117
  68.4 2.7 %shard_map.60 = bf16[128,2048]{1,0:T(8,128)(2,1)S(1)} custom-call(s32[1]{0:T(128)} %bitcast.mine_ref, f32[16,128]{1,0:T(8,128)S(1)} %collective-permute-done.10.refs_0_, bf16[64,2048]{1,0:T(8,128)(2,1)S(1)} %collective-permute-done.17.refs_1_, bf16[64,2048]{1,0:T(8,128)(2,1)S(1)} %collective-permute-done.21.refs_2_, ...), custom_call_target="tpu_custom_call" | custom-call | flops 402653184 | bytes 3145728 | tf_op jit(solution)/shard_map/pallas_call | solution.py:117
  72.7 2.7 %shard_map.61 = bf16[128,2048]{1,0:T(8,128)(2,1)S(1)} custom-call(s32[1]{0:T(128)} %bitcast.mine_ref, f32[16,128]{1,0:T(8,128)S(1)} %collective-permute-done.10.refs_0_, bf16[64,2048]{1,0:T(8,128)(2,1)S(1)} %collective-permute-done.20.refs_1_, bf16[64,2048]{1,0:T(8,128)(2,1)S(1)} %collective-permute-done.22.refs_2_, ...), custom_call_target="tpu_custom_call" | custom-call | flops 402653184 | bytes 3145728 | tf_op jit(solution)/shard_map/pallas_call | solution.py:117
  79.1 4.7 %collective-permute-done.25 = bf16[64,2048]{1,0:T(8,128)(2,1)S(1)} collective-permute-done((bf16[64,2048]{1,0:T(8,128)(2,1)S(1)}, bf16[64,2048]{1,0:T(8,128)(2,1)S(1)}, u32[]{:S(2)}, u32[]{:S(2)}) %collective-permute-start.25) | collective-permute-done | bytes 262176 | tf_op jit(solution)/shard_map/ppermute | solution.py:170
  87.3 4.8 %collective-permute-done.27 = bf16[64,2048]{1,0:T(8,128)(2,1)S(1)} collective-permute-done((bf16[64,2048]{1,0:T(8,128)(2,1)S(1)}, bf16[64,2048]{1,0:T(8,128)(2,1)S(1)}, u32[]{:S(2)}, u32[]{:S(2)}) %collective-permute-start.27) | collective-permute-done | bytes 262176 | tf_op jit(solution)/shard_map/ppermute | solution.py:170
  97.8 3.4 %collective-permute-done.30 = bf16[128,2048]{1,0:T(8,128)(2,1)S(1)} collective-permute-done((bf16[128,2048]{1,0:T(8,128)(2,1)S(1)}, bf16[128,2048]{1,0:T(8,128)(2,1)S(1)}, u32[]{:S(2)}, u32[]{:S(2)}) %collective-permute-start.30) | collective-permute-done | bytes 524320 | tf_op jit(solution)/shard_map/ppermute | solution.py:170
  103.3 3.6 %collective-permute-done.32 = bf16[128,2048]{1,0:T(8,128)(2,1)S(1)} collective-permute-done((bf16[128,2048]{1,0:T(8,128)(2,1)S(1)}, bf16[128,2048]{1,0:T(8,128)(2,1)S(1)}, u32[]{:S(2)}, u32[]{:S(2)}) %collective-permute-start.32) | collective-permute-done | bytes 524320 | tf_op jit(solution)/shard_map/ppermute | solution.py:170
  108.7 2.7 %shard_map.63 = (bf16[128,2048]{1,0:T(8,128)(2,1)S(1)}, bf16[128,2048]{1,0:T(8,128)(2,1)S(1)}) custom-call(s32[1]{0:T(128)} %bitcast.mine_ref, f32[16,128]{1,0:T(8,128)S(1)} %pad_maximum_fusion.2.refs_0_, bf16[128,2048]{1,0:T(8,128)(2,1)S(1)} %copy-done.1, bf16[128,2048]{1,0:T(8,128)(2,1)S(1)} %collective-permute-done.33.refs_2_, ...), custom_call_target="tpu_custom_call" | custom-call | flops 805306368 | bytes 3145728 | tf_op jit(solution)/shard_map/pallas_call | solution.py:117
  114.3 3.8 %collective-permute-done.39 = bf16[128,2048]{1,0:T(8,128)(2,1)S(1)} collective-permute-done((bf16[128,2048]{1,0:T(8,128)(2,1)S(1)}, bf16[128,2048]{1,0:T(8,128)(2,1)S(1)}, u32[]{:S(2)}, u32[]{:S(2)}) %collective-permute-start.39) | collective-permute-done | bytes 524320 | tf_op jit(solution)/shard_map/ppermute | solution.py:170
  118.4 5.3 %collective-permute-done.37.refs_2_ = bf16[128,2048]{1,0:T(8,128)(2,1)S(1)} collective-permute-done((bf16[128,2048]{1,0:T(8,128)(2,1)S(1)}, bf16[128,2048]{1,0:T(8,128)(2,1)S(1)}, u32[]{:S(2)}, u32[]{:S(2)}) %collective-permute-start.37) | collective-permute-done | bytes 524320 | tf_op jit(solution)/shard_map/ppermute | solution.py:170
  124.0 4.4 %collective-permute-done.40 = bf16[128,2048]{1,0:T(8,128)(2,1)S(1)} collective-permute-done((bf16[128,2048]{1,0:T(8,128)(2,1)S(1)}, bf16[128,2048]{1,0:T(8,128)(2,1)S(1)}, u32[]{:S(2)}, u32[]{:S(2)}) %collective-permute-start.40) | collective-permute-done | bytes 524320 | tf_op jit(solution)/shard_map/ppermute | solution.py:170
  (92 shorter events, 39.1 us)
Async XLA Ops:
  0.0 29.1 %collective-permute-start.3 = (bf16[128,2048]{1,0:T(8,128)(2,1)}, bf16[128,2048]{1,0:T(8,128)(2,1)S(1)}, u32[]{:S(2)}, u32[]{:S(2)}) collective-permute-start(bf16[128,2048]{1,0:T(8,128)(2,1)} %refs_1_), channel_id=1, source_target_pairs={{0,3},{1,4},{4,1},{5,8},{8,5},{9,12},{12,9},{13,14},{14,13},{15,10... | collective-permute-start | bytes 1572872 | tf_op jit(solution)/shard_map/ppermute | solution.py:170
  2.4 26.7 %collective-permute-start.5 = (bf16[128,2048]{1,0:T(8,128)(2,1)}, bf16[128,2048]{1,0:T(8,128)(2,1)S(1)}, u32[]{:S(2)}, u32[]{:S(2)}) collective-permute-start(bf16[128,2048]{1,0:T(8,128)(2,1)} %refs_1_), channel_id=1, source_target_pairs={{0,4},{1,3},{4,8},{5,1},{8,12},{9,5},{12,14},{13,9},{14,10},{15,13... | collective-permute-start | bytes 1572872 | tf_op jit(solution)/shard_map/ppermute | solution.py:170
  4.9 13.3 %collective-permute-start.8 = (f32[16,128]{1,0:T(8,128)S(1)}, f32[16,128]{1,0:T(8,128)S(1)}, u32[]{:S(2)}, u32[]{:S(2)}) collective-permute-start(f32[16,128]{1,0:T(8,128)S(1)} %pad_maximum_fusion.2.refs_0_), channel_id=1, source_target_pairs={{0,12},{1,11},{4,14},{5,7},{8,10},{9,3},{12,6},{13,1},{14,2},{15,5... | collective-permute-start | bytes 24584 | tf_op jit(solution)/shard_map/ppermute | solution.py:170
  8.5 10.0 %collective-permute-start.9 = (f32[16,128]{1,0:T(8,128)S(1)}, f32[16,128]{1,0:T(8,128)S(1)}, u32[]{:S(2)}, u32[]{:S(2)}) collective-permute-start(f32[16,128]{1,0:T(8,128)S(1)} %pad_maximum_fusion.2.refs_0_), channel_id=1, source_target_pairs={{0,10},{1,13},{4,6},{5,15},{8,2},{9,11},{12,0},{13,7},{14,4},{15,3... | collective-permute-start | bytes 24584 | tf_op jit(solution)/shard_map/ppermute | solution.py:170
  8.8 12.5 %collective-permute-start.1 = (f32[16,128]{1,0:T(8,128)S(1)}, f32[16,128]{1,0:T(8,128)S(1)}, u32[]{:S(2)}, u32[]{:S(2)}) collective-permute-start(f32[16,128]{1,0:T(8,128)S(1)} %pad_maximum_fusion.2.refs_0_), channel_id=1, source_target_pairs={{0,8},{1,7},{4,12},{5,3},{8,14},{9,1},{12,10},{13,5},{14,6},{15,9}... | collective-permute-start | bytes 24584 | tf_op jit(solution)/shard_map/ppermute | solution.py:170
  29.1 9.2 %collective-permute-start.11 = (bf16[128,2048]{1,0:T(8,128)(2,1)S(1)}, bf16[128,2048]{1,0:T(8,128)(2,1)S(1)}, u32[]{:S(2)}, u32[]{:S(2)}) collective-permute-start(bf16[128,2048]{1,0:T(8,128)(2,1)S(1)} %collective-permute-done.5.refs_2_), channel_id=1, source_target_pairs={{0,4},{1,3},{4,8},{5,1},{8,12},{9,5},{12,14},{13,9},{14,10},{15,13... | collective-permute-start | bytes 1572872 | tf_op jit(solution)/shard_map/ppermute | solution.py:170
  29.2 14.8 %collective-permute-start.4 = (bf16[128,2048]{1,0:T(8,128)(2,1)S(1)}, bf16[128,2048]{1,0:T(8,128)(2,1)S(1)}, u32[]{:S(2)}, u32[]{:S(2)}) collective-permute-start(bf16[128,2048]{1,0:T(8,128)(2,1)S(1)} %collective-permute-done.3.refs_2_), channel_id=1, source_target_pairs={{0,4},{1,3},{4,8},{5,1},{8,12},{9,5},{12,14},{13,9},{14,10},{15,13... | collective-permute-start | bytes 1572872 | tf_op jit(solution)/shard_map/ppermute | solution.py:170
  38.4 11.2 %collective-permute-start.13 = (bf16[128,2048]{1,0:T(8,128)(2,1)S(1)}, bf16[128,2048]{1,0:T(8,128)(2,1)S(1)}, u32[]{:S(2)}, u32[]{:S(2)}) collective-permute-start(bf16[128,2048]{1,0:T(8,128)(2,1)S(1)} %collective-permute-done.11.refs_2_), channel_id=1, source_target_pairs={{0,4},{1,3},{4,8},{5,1},{8,12},{9,5},{12,14},{13,9},{14,10},{15,13... | collective-permute-start | bytes 1572872 | tf_op jit(solution)/shard_map/ppermute | solution.py:170
  44.0 11.2 %collective-permute-start.16 = (bf16[128,2048]{1,0:T(8,128)(2,1)S(1)}, bf16[128,2048]{1,0:T(8,128)(2,1)S(1)}, u32[]{:S(2)}, u32[]{:S(2)}) collective-permute-start(bf16[128,2048]{1,0:T(8,128)(2,1)S(1)} %collective-permute-done.4.refs_2_), channel_id=1, source_target_pairs={{0,4},{1,3},{4,8},{5,1},{8,12},{9,5},{12,14},{13,9},{14,10},{15,13... | collective-permute-start | bytes 1572872 | tf_op jit(solution)/shard_map/ppermute | solution.py:170
  49.6 12.3 %collective-permute-start.18 = (bf16[128,2048]{1,0:T(8,128)(2,1)S(1)}, bf16[128,2048]{1,0:T(8,128)(2,1)S(1)}, u32[]{:S(2)}, u32[]{:S(2)}) collective-permute-start(bf16[128,2048]{1,0:T(8,128)(2,1)S(1)} %collective-permute-done.13.refs_2_), channel_id=1, source_target_pairs={{0,1},{1,0},{4,5},{5,4},{8,9},{9,8},{12,13},{13,12},{14,15},{15,14... | collective-permute-start | bytes 1572872 | tf_op jit(solution)/shard_map/ppermute | solution.py:170
  55.2 10.4 %collective-permute-start.19 = (bf16[128,2048]{1,0:T(8,128)(2,1)S(1)}, bf16[128,2048]{1,0:T(8,128)(2,1)S(1)}, u32[]{:S(2)}, u32[]{:S(2)}) collective-permute-start(bf16[128,2048]{1,0:T(8,128)(2,1)S(1)} %collective-permute-done.16.refs_2_), channel_id=1, source_target_pairs={{0,1},{1,0},{4,5},{5,4},{8,9},{9,8},{12,13},{13,12},{14,15},{15,14... | collective-permute-start | bytes 1572872 | tf_op jit(solution)/shard_map/ppermute | solution.py:170
  64.6 7.6 %collective-permute-start.20 = (bf16[64,2048]{1,0:T(8,128)(2,1)S(1)}, bf16[64,2048]{1,0:T(8,128)(2,1)S(1)}, u32[]{:S(2)}, u32[]{:S(2)}) collective-permute-start(bf16[64,2048]{1,0:T(8,128)(2,1)S(1)} %collective-permute-done.17.refs_1_), channel_id=1, source_target_pairs={{0,1},{1,0},{4,5},{5,4},{8,9},{9,8},{12,13},{13,12},{14,15},{15,14... | collective-permute-start | bytes 786440 | tf_op jit(solution)/shard_map/ppermute | solution.py:170
  71.7 37.0 %collective-permute-start.33 = (bf16[128,2048]{1,0:T(8,128)(2,1)S(1)}, bf16[128,2048]{1,0:T(8,128)(2,1)S(1)}, u32[]{:S(2)}, u32[]{:S(2)}) collective-permute-start(bf16[128,2048]{1,0:T(8,128)(2,1)S(1)} %copy-done.1), channel_id=1, source_target_pairs={{0,1},{1,0},{4,5},{5,4},{8,9},{9,8},{12,13},{13,12},{14,15},{15,14... | collective-permute-start | bytes 1572872 | tf_op jit(solution)/shard_map/ppermute | solution.py:170
  71.7 21.9 %collective-permute-start.28 = (bf16[128,2048]{1,0:T(8,128)(2,1)S(1)}, bf16[128,2048]{1,0:T(8,128)(2,1)S(1)}, u32[]{:S(2)}, u32[]{:S(2)}) collective-permute-start(bf16[128,2048]{1,0:T(8,128)(2,1)S(1)} %collective-permute-done.3.refs_2_), channel_id=1, source_target_pairs={{0,1},{1,0},{4,5},{5,4},{8,9},{9,8},{12,13},{13,12},{14,15},{15,14... | collective-permute-start | bytes 1572872 | tf_op jit(solution)/shard_map/ppermute | solution.py:170
  72.2 29.3 %collective-permute-start.31 = (bf16[128,2048]{1,0:T(8,128)(2,1)S(1)}, bf16[128,2048]{1,0:T(8,128)(2,1)S(1)}, u32[]{:S(2)}, u32[]{:S(2)}) collective-permute-start(bf16[128,2048]{1,0:T(8,128)(2,1)S(1)} %get-tuple-element.75), channel_id=1, source_target_pairs={{0,1},{1,0},{4,5},{5,4},{8,9},{9,8},{12,13},{13,12},{14,15},{15,14... | collective-permute-start | bytes 1572872 | tf_op jit(solution)/shard_map/ppermute | solution.py:170
  72.3 25.5 %collective-permute-start.29 = (bf16[128,2048]{1,0:T(8,128)(2,1)S(1)}, bf16[128,2048]{1,0:T(8,128)(2,1)S(1)}, u32[]{:S(2)}, u32[]{:S(2)}) collective-permute-start(bf16[128,2048]{1,0:T(8,128)(2,1)S(1)} %get-tuple-element.73), channel_id=1, source_target_pairs={{0,1},{1,0},{4,5},{5,4},{8,9},{9,8},{12,13},{13,12},{14,15},{15,14... | collective-permute-start | bytes 1572872 | tf_op jit(solution)/shard_map/ppermute | solution.py:170
  92.1 9.2 %collective-permute-start.30 = (bf16[128,2048]{1,0:T(8,128)(2,1)S(1)}, bf16[128,2048]{1,0:T(8,128)(2,1)S(1)}, u32[]{:S(2)}, u32[]{:S(2)}) collective-permute-start(bf16[128,2048]{1,0:T(8,128)(2,1)S(1)} %pad_maximum_fusion), channel_id=1, source_target_pairs={{0,2},{1,5},{4,0},{5,9},{8,4},{9,13},{12,8},{13,15},{14,12},{15,11... | collective-permute-start | bytes 1572872 | tf_op jit(solution)/shard_map/ppermute | solution.py:170
  93.7 13.2 %collective-permute-start.32 = (bf16[128,2048]{1,0:T(8,128)(2,1)S(1)}, bf16[128,2048]{1,0:T(8,128)(2,1)S(1)}, u32[]{:S(2)}, u32[]{:S(2)}) collective-permute-start(bf16[128,2048]{1,0:T(8,128)(2,1)S(1)} %pad_maximum_fusion.1), channel_id=1, source_target_pairs={{0,2},{1,5},{4,0},{5,9},{8,4},{9,13},{12,8},{13,15},{14,12},{15,11... | collective-permute-start | bytes 1572872 | tf_op jit(solution)/shard_map/ppermute | solution.py:170
  97.8 13.7 %collective-permute-start.35 = (bf16[128,2048]{1,0:T(8,128)(2,1)S(1)}, bf16[128,2048]{1,0:T(8,128)(2,1)S(1)}, u32[]{:S(2)}, u32[]{:S(2)}) collective-permute-start(bf16[128,2048]{1,0:T(8,128)(2,1)S(1)} %get-tuple-element.80), channel_id=1, source_target_pairs={{0,1},{1,0},{4,5},{5,4},{8,9},{9,8},{12,13},{13,12},{14,15},{15,14... | collective-permute-start | bytes 1572872 | tf_op jit(solution)/shard_map/ppermute | solution.py:170
  101.3 13.0 %collective-permute-start.38 = (bf16[128,2048]{1,0:T(8,128)(2,1)S(1)}, bf16[128,2048]{1,0:T(8,128)(2,1)S(1)}, u32[]{:S(2)}, u32[]{:S(2)}) collective-permute-start(bf16[128,2048]{1,0:T(8,128)(2,1)S(1)} %get-tuple-element.82), channel_id=1, source_target_pairs={{0,1},{1,0},{4,5},{5,4},{8,9},{9,8},{12,13},{13,12},{14,15},{15,14... | collective-permute-start | bytes 1572872 | tf_op jit(solution)/shard_map/ppermute | solution.py:170
  101.5 11.0 %collective-permute-start.36 = (bf16[128,2048]{1,0:T(8,128)(2,1)S(1)}, bf16[128,2048]{1,0:T(8,128)(2,1)S(1)}, u32[]{:S(2)}, u32[]{:S(2)}) collective-permute-start(bf16[128,2048]{1,0:T(8,128)(2,1)S(1)} %add_convert_fusion.4), channel_id=1, source_target_pairs={{0,2},{1,5},{4,0},{5,9},{8,4},{9,13},{12,8},{13,15},{14,12},{15,11... | collective-permute-start | bytes 1572872 | tf_op jit(solution)/shard_map/ppermute | solution.py:170
  107.1 11.0 %collective-permute-start.39 = (bf16[128,2048]{1,0:T(8,128)(2,1)S(1)}, bf16[128,2048]{1,0:T(8,128)(2,1)S(1)}, u32[]{:S(2)}, u32[]{:S(2)}) collective-permute-start(bf16[128,2048]{1,0:T(8,128)(2,1)S(1)} %add_convert_fusion.3), channel_id=1, source_target_pairs={{0,2},{1,5},{4,0},{5,9},{8,4},{9,13},{12,8},{13,15},{14,12},{15,11... | collective-permute-start | bytes 1572872 | tf_op jit(solution)/shard_map/ppermute | solution.py:170
  112.7 11.0 %collective-permute-start.37 = (bf16[128,2048]{1,0:T(8,128)(2,1)S(1)}, bf16[128,2048]{1,0:T(8,128)(2,1)S(1)}, u32[]{:S(2)}, u32[]{:S(2)}) collective-permute-start(bf16[128,2048]{1,0:T(8,128)(2,1)S(1)} %add_convert_fusion.2), channel_id=1, source_target_pairs={{0,2},{1,5},{4,0},{5,9},{8,4},{9,13},{12,8},{13,15},{14,12},{15,11... | collective-permute-start | bytes 1572872 | tf_op jit(solution)/shard_map/ppermute | solution.py:170
  118.4 10.0 %collective-permute-start.40 = (bf16[128,2048]{1,0:T(8,128)(2,1)S(1)}, bf16[128,2048]{1,0:T(8,128)(2,1)S(1)}, u32[]{:S(2)}, u32[]{:S(2)}) collective-permute-start(bf16[128,2048]{1,0:T(8,128)(2,1)S(1)} %add_convert_fusion.1), channel_id=1, source_target_pairs={{0,3},{1,4},{4,1},{5,8},{8,5},{9,12},{12,9},{13,14},{14,13},{15,10... | collective-permute-start | bytes 1572872 | tf_op jit(solution)/shard_map/ppermute | solution.py:170
  (19 other events, 86.7 us)

commit v7 on v5

--- a/solution.py
+++ b/solution.py
@@ -65,13 +65,13 @@
     return table
 
 
-def half_expert_kernel(pieces, load, split, sources_ref, gates_ref, *refs):
+def half_expert_kernel(pieces, load, split, *refs):
     blocks, refs = refs[: len(pieces)], refs[len(pieces) :]
     if load:
-        (gate_up_far, down_far), refs = refs[:2], refs[2:]
-        outs, (gate_up_ref, down_ref, rows, hidden, arrived) = refs[:split], refs[split:]
+        (places, gates, gate_up_far, down_far), refs = refs[:4], refs[4:]
+        outs, (gate_up_ref, down_ref, columns, rows, hidden, lines, arrived) = refs[:split], refs[split:]
     else:
-        (gate_up_ref, down_ref), outs, (rows, hidden) = refs[:2], refs[2:-2], refs[-2:]
+        (gate_up_ref, down_ref, columns), outs, (rows, hidden) = refs[:3], refs[3:-2], refs[-2:]
     units, width = down_ref.shape
     tile = 256 if units % 256 == 0 else units
     tiles = units // tile
@@ -83,16 +83,18 @@
         copies.append(pltpu.make_async_copy(down_far, down_ref, arrived.at[tiles]))
         for copy in copies:
             copy.start()
-
+        lines[...] = jnp.zeros_like(lines)
+        for i in range(places.shape[0]):
+            lines[i : i + 1, :] = gates[pl.ds(places[i], 1), :]
+        columns[...] = lines[...].T
+
+    at = 0
     weights = []
-    at = 0
-    for block, (source, token) in zip(blocks, pieces):
+    for block, (column, token) in zip(blocks, pieces):
         count = block.shape[0]
         rows[at : at + count, :] = block[...]
         at += count
-        line = gates_ref[pl.ds(sources_ref[source], 1), :]
-        column = jnp.broadcast_to(line, (8, line.shape[1])).T[:, :1]
-        weights.append(column[token : token + count])
+        weights.append(columns[token : token + count, column : column + 1])
     weight = jnp.concatenate(weights)
 
     contract = (((1,), (1,)), ((), ()))
@@ -116,30 +118,35 @@
             out[:, low : low + tile] = product[i * share : (i + 1) * share]
 
 
-def half_expert(places, gates, pieces, blocks, gate_up, down_proj, load=False, cost=6, split=2):
+def half_expert(pieces, blocks, weights, load=False, cost=2, split=2):
     height = sum(block.shape[0] for block in blocks)
+    gate_up, down_proj = weights[2:] if load else weights[:2]
     units, width = down_proj.shape
     whole = pl.BlockSpec(memory_space=pltpu.VMEM)
+    far = pl.BlockSpec(memory_space=pltpu.HBM)
     outs = [jax.ShapeDtypeStruct((height // split, width), jnp.bfloat16)] * split
-    weights = [jax.ShapeDtypeStruct(array.shape, array.dtype) for array in (gate_up, down_proj)] if load else []
     scratch = [pltpu.VMEM((height, width), jnp.bfloat16), pltpu.VMEM((height, units), jnp.bfloat16)]
-    if load:
+    specs = [whole] * 3
+    if load:
+        tokens = weights[1].shape[1]
+        outs += [jax.ShapeDtypeStruct(array.shape, array.dtype) for array in (gate_up, down_proj)]
+        outs.append(jax.ShapeDtypeStruct((tokens, 128), jnp.float32))
+        scratch.append(pltpu.VMEM((128, tokens), jnp.float32))
         scratch.append(pltpu.SemaphoreType.DMA((units // 256 + 1 if units % 256 == 0 else 2,)))
+        specs = [pl.BlockSpec(memory_space=pltpu.SMEM), whole, far, far]
     return pl.pallas_call(
         functools.partial(half_expert_kernel, tuple(pieces), load, split),
-        out_shape=outs + weights,
-        in_specs=[pl.BlockSpec(memory_space=pltpu.SMEM)]
-        + [whole] * (len(blocks) + 1)
-        + [pl.BlockSpec(memory_space=pltpu.HBM) if load else whole] * 2,
-        out_specs=[whole] * (split + len(weights)),
+        out_shape=outs,
+        in_specs=[whole] * len(blocks) + specs,
+        out_specs=[whole] * len(outs),
         scratch_shapes=scratch,
         compiler_params=pltpu.CompilerParams(vmem_limit_bytes=(34 if load else 14) << 20),
         cost_estimate=pl.CostEstimate(
-            flops=cost * height * units * width,
-            bytes_accessed=cost * units * width,
-            transcendentals=height * units,
+            flops=int(cost * height * units * width),
+            bytes_accessed=int(cost * units * width),
+            transcendentals=0,
         ),
-    )(places, gates, *blocks, gate_up, down_proj)
+    )(*blocks, *weights)
 
 
 def sum_kernel(*refs):
@@ -166,15 +173,16 @@
     rows = tokens.shape[0]
     half = rows // 2
     chains = (0, 1)
-    forth, back, across, cores = [], [], [], []
-    for place in range(chips):
-        for core in (0, 1):
-            device = 2 * order[place] + core
-            ahead, behind = order[(place + 1 - 2 * core) % chips], order[(place - 1 + 2 * core) % chips]
-            forth.append((device, 2 * ahead + core))
-            back.append((device, 2 * behind + core))
-            across.append((device, 2 * behind + 1 - core))
-            cores.append((device, device ^ 1))
+
+    def moved(steps, swap=False):
+        pairs = []
+        for place in range(chips):
+            for core in (0, 1):
+                target = order[(place + steps * (1 - 2 * core)) % chips]
+                pairs.append((2 * order[place] + core, 2 * target + (1 - core if swap else core)))
+        return pairs
+
+    forth, back, across, cores = moved(1), moved(-1), moved(-1, True), moved(0, True)
 
     def send(value, pairs):
         return lax.ppermute(value, "blk", pairs)
@@ -189,44 +197,47 @@
         return lax.optimization_barrier((value, *earlier))[0]
 
     ring = [send(tokens, forth), send(tokens, across)]
-    other = send(tokens, cores)
 
     places = lax.dynamic_index_in_dim(jnp.asarray(sources(chips)), lax.axis_index("blk"), 0, keepdims=False)
     chosen = jnp.arange(chips, dtype=jnp.int32)[:, None, None] == expert_ids.T[None]
     weight = jnp.sum(jnp.where(chosen, route_gate.T[None], 0.0), axis=1)
     gates = lax.all_to_all(jnp.repeat(weight, 2, axis=0), "blk", split_axis=0, concat_axis=0, tiled=True)
     gates = gates.reshape(-1, rows)
-
-    results, near = {}, None
-    earlier = ring[1]
+    ring[1] = after(ring[1], gates)
+
+    def swapped_columns(step, c):
+        return [(4 * step - 2 + c, 0), (4 * step + c, 0)]
+
+    results = {}
+    near, delayed = None, None
     for step in range(1, far):
-        swapped = [send(block, cores) for block in ring]
+        swapped = [send(block, cores) for block in ring[: 1 if step == 1 else 2]]
         blocks = ring
         if step < far - 1:
             ring = [send(block, forth) for block in ring]
         else:
             ring = [send(ring[0][:half], forth), send(ring[1][half:], forth)]
-        for c in chains:
-            pieces = [(4 * step - 2 + c, 0), (4 * step + c, 0)]
-            inputs = [after(blocks[c], earlier), swapped[c]]
-            if near is None:
-                kept, given, *near = half_expert(places, gates, pieces, inputs, gate_up, down_proj, load=True)
-            elif (step, c) != (far - 1, 1):
-                kept, given = half_expert(places, gates, pieces, inputs, *near)
-            else:
-                last = pieces, [blocks[c], swapped[c]]
-                break
-            results[step, c] = kept, send(given, cores)
-            ring[c] = earlier = after(ring[c], kept)
+        if step == 1:
+            load = [places, gates, gate_up, down_proj]
+            kept, given, *near = half_expert(swapped_columns(1, 0), [blocks[0], swapped[0]], load, load=True)
+            results[1, 0] = kept, send(given, cores)
+            delayed = blocks[1]
+        else:
+            pieces = [(4 * step - 2 + i, 0) for i in range(4)]
+            kept, given = half_expert(pieces, blocks + swapped, near)
+            given = send(given, cores)
+            for c in chains:
+                results[step, c] = kept[c * rows : (c + 1) * rows], given[c * rows : (c + 1) * rows]
+        ring[0] = after(ring[0], kept)
+        if step == far - 1:
+            ring[1] = after(ring[1], kept)
 
     base = 4 * far - 2
-    pieces = [(base, 0), (base + 1, half)]
-    (given,) = half_expert(places, gates, pieces, ring, *near, split=1)
+    (given,) = half_expert([(base, 0), (base + 1, half)], ring, near, split=1)
     swapped = [send(block, cores) for block in ring]
     swapped[0] = after(swapped[0], given)
     given = send(given, cores)
-    pieces = [(base + 2, 0), (base + 3, half)]
-    (kept,) = half_expert(places, gates, pieces, swapped, *near, split=1)
+    (kept,) = half_expert([(base + 2, 0), (base + 3, half)], swapped, near, split=1)
 
     first, second = slice(0, half), slice(half, rows)
     late = []
@@ -234,13 +245,8 @@
     for part in (second, first):
         earlier = rounded(total(after(kept[part], earlier), given[part]))
         late.append(send(earlier, back))
-    pieces, inputs = last
-    inputs[0] = after(inputs[0], earlier)
-    kept, given = half_expert(places, gates, pieces, inputs, *near, cost=1)
-    results[far - 1, 1] = kept, send(given, cores)
-
-    sums = []
-    earlier = kept
+
+    late_value, sums = earlier, []
     for c in chains:
         mine, theirs = results[far - 1, c]
         value = total(after(mine, earlier), theirs)
@@ -250,12 +256,17 @@
             value = jnp.concatenate([value[first] + total(late[c]), value[second]])
         earlier = rounded(value)
         sums.append(send(earlier, back))
+    swapped = send(after(delayed, late_value), cores)
+    kept, given = half_expert(swapped_columns(1, 1), [after(delayed, earlier), swapped], near)
+    results[1, 1] = kept, send(given, cores)
+    other = send(after(tokens, earlier), cores)
+    earlier = kept
     for step in range(far - 2, 1, -1):
         for c in chains:
             mine, theirs = results[step, c]
             earlier = rounded(total(after(mine, earlier), theirs, sums[c]))
             sums[c] = send(earlier, back)
-    kept, given = half_expert(places, gates, [(0, 0), (1, 0)], [after(tokens, earlier), other], *near)
+    kept, given = half_expert([(0, 0), (1, 0)], [after(tokens, earlier), other], near)
     given = send(given, cores)
     earlier = kept
     for c, pairs in zip(chains, (back, across)):

time: 112 us -> 116 us (1.036)
  starting transfers between devices: 23.7 us -> 31.9 us
  Pallas kernels: 31.5 us -> 26.8 us
    ppermute x33 -> x31, starting transfers between devices: 17.9 us -> 24.2 us  [send(): return lax.ppermute(value, 'blk', pairs)]
    pallas_call x9 -> x7, Pallas kernels: 31.3 us -> 26.6 us  [half_expert(): pl.pallas_call(functools.partial(half_expert_kernel, tuple(pieces), load,...]
    all_to_all x1, starting transfers between devices: 5.8 us -> 7.73 us  [by_tokens(): lax.all_to_all(jnp.repeat(weight, 2, axis=0), 'blk', split_axis=0, concat...]
    ppermute x33 -> x31, waiting for transfers between devices: 45.1 us -> 44.7 us  [send(): return lax.ppermute(value, 'blk', pairs)]
  transfers between devices with their start and end apart: 34 -> 32, of which waited for: 13 -> 15; matrix products, arithmetic and copies ran while one was open for 3% -> 3% of each run, Pallas kernels for 28% -> 23%
where the time goes in v7:
time: 116 us; the launch traced here: 115 us
  waiting for transfers between devices  49.3 us (42%)
  starting transfers between devices  31.9 us (28%)
  Pallas kernels  26.8 us (23%)
  local copies, waits for them, and re-layouts  3.52 us (3%)
  other arithmetic  3.15 us (3%)
    ppermute x31, waiting for transfers between devices, send(): return lax.ppermute(value, 'blk', pairs)  44.7 us
    pallas_call x7, Pallas kernels, half_expert(): pl.pallas_call(functools.partial(half_expert_kernel, tuple(pieces), load,...  26.6 us
    ppermute x31, starting transfers between devices, send(): return lax.ppermute(value, 'blk', pairs)  24.2 us
    all_to_all x1, starting transfers between devices, by_tokens(): lax.all_to_all(jnp.repeat(weight, 2, axis=0), 'blk', split_axis=0, concat...  7.73 us
    all_to_all x1, waiting for transfers between devices, by_tokens(): lax.all_to_all(jnp.repeat(weight, 2, axis=0), 'blk', split_axis=0, concat...  4.58 us
  transfers between devices with their start and end apart: 32, of which 15 were waited for; matrix products, arithmetic and copies ran while one was open for 3% of the time, Pallas kernels for 23%

profile of v7, /device:TPU:0, one launch (start us, length us, event | category | flops | bytes accessed | tf_op | source)
XLA Modules:
  0.0 115.0 jit_solution(472408449779040541)
XLA Ops:
  0.0 3.0 %collective-permute-start = (bf16[128,2048]{1,0:T(8,128)(2,1)}, bf16[128,2048]{1,0:T(8,128)(2,1)S(1)}, u32[]{:S(2)}, u32[]{:S(2)}) collective-permute-start(bf16[128,2048]{1,0:T(8,128)(2,1)} %refs_0_), channel_id=1, source_target_pairs={{0,4},{1,3},{4,8},{5,1},{8,12},{9,5},{12,14},{13,9},{14,10},{15,13... | collective-permute-start | bytes 1572872 | tf_op jit(solution)/shard_map/ppermute | solution.py:188
  3.7 10.9 %collective-permute-done.refs_0_ = bf16[128,2048]{1,0:T(8,128)(2,1)S(1)} collective-permute-done((bf16[128,2048]{1,0:T(8,128)(2,1)}, bf16[128,2048]{1,0:T(8,128)(2,1)S(1)}, u32[]{:S(2)}, u32[]{:S(2)}) %collective-permute-start) | collective-permute-done | bytes 524320 | tf_op jit(solution)/shard_map/ppermute | solution.py:188
  16.0 7.7 %all-to-all-start = ((f32[16,1,128]{2,1,0:T(1,128)}), f32[16,1,128]{2,1,0:T(1,128)S(1)}, u32[]{:S(2)}, u32[]{:S(2)}) async-start(f32[16,1,128]{2,1,0:T(1,128)} %bitcast.3), calls=%async_computation | async-start | bytes 16384 | tf_op jit(solution)/shard_map/all_to_all | solution.py:204
  23.7 1.9 %collective-permute-start.1 = (bf16[128,2048]{1,0:T(8,128)(2,1)S(1)}, bf16[128,2048]{1,0:T(8,128)(2,1)S(1)}, u32[]{:S(2)}, u32[]{:S(2)}) collective-permute-start(bf16[128,2048]{1,0:T(8,128)(2,1)S(1)} %collective-permute-done.refs_0_), channel_id=1, source_target_pairs={{0,4},{1,3},{4,8},{5,1},{8,12},{9,5},{12,14},{13,9},{14,10},{15,13... | collective-permute-start | bytes 1572872 | tf_op jit(solution)/shard_map/ppermute | solution.py:188
  25.6 4.6 %all-to-all-done = f32[16,1,128]{2,1,0:T(1,128)S(1)} async-done(((f32[16,1,128]{2,1,0:T(1,128)}), f32[16,1,128]{2,1,0:T(1,128)S(1)}, u32[]{:S(2)}, u32[]{:S(2)}) %all-to-all-start) | async-done | bytes 8224 | tf_op jit(solution)/shard_map/all_to_all | solution.py:204
  31.3 1.9 %copy-done = bf16[768,2048]{1,0:T(8,128)(2,1)S(1)} copy-done((bf16[768,2048]{1,0:T(8,128)(2,1)S(1)}, bf16[768,2048]{1,0:T(8,128)(2,1)}, u32[]{:S(2)}) %copy-start) | copy-done | bytes 3145752
  33.1 5.5 %shard_map.64 = (bf16[128,2048]{1,0:T(8,128)(2,1)S(1)}, bf16[128,2048]{1,0:T(8,128)(2,1)S(1)}, bf16[2,768,2048]{2,1,0:T(8,128)(2,1)S(1)}, bf16[768,2048]{1,0:T(8,128)(2,1)S(1)}, f32[128,128]{1,0:T(8,128)S(1)}) custom-call(bf16[128,2048]{1,0:T(8,128)(2,1)S(1)} %collective-permute-done.refs_0_, bf16[128,2048]{1,0:T(8,128)(2,1)S(1)} %collective-permute-done.2.refs_1_, ...), custom_call_target="tpu_custom_call" | custom-call | flops 805306368 | bytes 3145728 | tf_op jit(solution)/shard_map/pallas_call | solution.py:137
  41.9 5.2 %shard_map.65 = (bf16[256,2048]{1,0:T(8,128)(2,1)S(1)}, bf16[256,2048]{1,0:T(8,128)(2,1)S(1)}) custom-call(bf16[128,2048]{1,0:T(8,128)(2,1)S(1)} %collective-permute-done.1.refs_0_, bf16[128,2048]{1,0:T(8,128)(2,1)S(1)} %collective-permute-done.4.refs_1_, bf16[128,2048]{1,0:T(8,128)(2,1)S(1)} %collective-permute-done.5.refs_2_, ...), custom_call_target="tpu_custom_call" | custom-call | flops 1610612736 | bytes 3145728 | tf_op jit(solution)/shard_map/pallas_call | solution.py:137
  48.6 5.6 %collective-permute-done.8.refs_1_ = bf16[128,2048]{1,0:T(8,128)(2,1)S(1)} collective-permute-done((bf16[128,2048]{1,0:T(8,128)(2,1)S(1)}, bf16[128,2048]{1,0:T(8,128)(2,1)S(1)}, u32[]{:S(2)}, u32[]{:S(2)}) %collective-permute-start.8) | collective-permute-done | bytes 524320 | tf_op jit(solution)/shard_map/ppermute | solution.py:188
  57.5 5.2 %shard_map.66 = (bf16[256,2048]{1,0:T(8,128)(2,1)S(1)}, bf16[256,2048]{1,0:T(8,128)(2,1)S(1)}) custom-call(bf16[128,2048]{1,0:T(8,128)(2,1)S(1)} %collective-permute-done.7.refs_0_, bf16[128,2048]{1,0:T(8,128)(2,1)S(1)} %collective-permute-done.8.refs_1_, bf16[128,2048]{1,0:T(8,128)(2,1)S(1)} %collective-permute-done.9.refs_2_, ...), custom_call_target="tpu_custom_call" | custom-call | flops 1610612736 | bytes 3145728 | tf_op jit(solution)/shard_map/pallas_call | solution.py:137
  64.0 2.7 %shard_map.67 = bf16[128,2048]{1,0:T(8,128)(2,1)S(1)} custom-call(bf16[64,2048]{1,0:T(8,128)(2,1)S(1)} %collective-permute-done.11.refs_0_, bf16[64,2048]{1,0:T(8,128)(2,1)S(1)} %collective-permute-done.13.refs_1_, bf16[2,768,2048]{2,1,0:T(8,128)(2,1)S(1)} %get-tuple-element.39.refs_4_.refs_2_, bf16[768,2048]{1,0:T(8,128)(2,1)S(1)} %get-tuple-element.40.refs_5_.refs_3_, ...), custom_call_target="tpu_custom_call" | custom-call | flops 402653184 | bytes 3145728 | tf_op jit(solution)/shard_map/pallas_call | solution.py:137
  68.4 2.7 %shard_map.68 = bf16[128,2048]{1,0:T(8,128)(2,1)S(1)} custom-call(bf16[64,2048]{1,0:T(8,128)(2,1)S(1)} %collective-permute-done.12.refs_0_, bf16[64,2048]{1,0:T(8,128)(2,1)S(1)} %collective-permute-done.14.refs_1_, bf16[2,768,2048]{2,1,0:T(8,128)(2,1)S(1)} %get-tuple-element.39.refs_4_.refs_2_, bf16[768,2048]{1,0:T(8,128)(2,1)S(1)} %get-tuple-element.40.refs_5_.refs_3_, ...), custom_call_target="tpu_custom_call" | custom-call | flops 402653184 | bytes 3145728 | tf_op jit(solution)/shard_map/pallas_call | solution.py:137
  71.2 1.6 %collective-permute-start.17 = (bf16[64,2048]{1,0:T(8,128)(2,1)S(1)}, bf16[64,2048]{1,0:T(8,128)(2,1)S(1)}, u32[]{:S(2)}, u32[]{:S(2)}) collective-permute-start(bf16[64,2048]{1,0:T(8,128)(2,1)S(1)} %add_convert_fusion.6), channel_id=1, source_target_pairs={{0,2},{1,5},{4,0},{5,9},{8,4},{9,13},{12,8},{13,15},{14,12},{15,11... | collective-permute-start | bytes 786440 | tf_op jit(solution)/shard_map/ppermute | solution.py:188
  74.1 3.5 %collective-permute-done.17 = bf16[64,2048]{1,0:T(8,128)(2,1)S(1)} collective-permute-done((bf16[64,2048]{1,0:T(8,128)(2,1)S(1)}, bf16[64,2048]{1,0:T(8,128)(2,1)S(1)}, u32[]{:S(2)}, u32[]{:S(2)}) %collective-permute-start.17) | collective-permute-done | bytes 262176 | tf_op jit(solution)/shard_map/ppermute | solution.py:188
  77.8 1.6 %collective-permute-start.21 = (bf16[128,2048]{1,0:T(8,128)(2,1)S(1)}, bf16[128,2048]{1,0:T(8,128)(2,1)S(1)}, u32[]{:S(2)}, u32[]{:S(2)}) collective-permute-start(bf16[128,2048]{1,0:T(8,128)(2,1)S(1)} %pad_maximum_fusion), channel_id=1, source_target_pairs={{0,2},{1,5},{4,0},{5,9},{8,4},{9,13},{12,8},{13,15},{14,12},{15,11... | collective-permute-start | bytes 1572872 | tf_op jit(solution)/shard_map/ppermute | solution.py:188
  80.6 1.6 %collective-permute-start.22 = (bf16[128,2048]{1,0:T(8,128)(2,1)S(1)}, bf16[128,2048]{1,0:T(8,128)(2,1)S(1)}, u32[]{:S(2)}, u32[]{:S(2)}) collective-permute-start(bf16[128,2048]{1,0:T(8,128)(2,1)S(1)} %pad_maximum_fusion.1), channel_id=1, source_target_pairs={{0,2},{1,5},{4,0},{5,9},{8,4},{9,13},{12,8},{13,15},{14,12},{15,11... | collective-permute-start | bytes 1572872 | tf_op jit(solution)/shard_map/ppermute | solution.py:188
  82.2 2.7 %shard_map.69 = (bf16[128,2048]{1,0:T(8,128)(2,1)S(1)}, bf16[128,2048]{1,0:T(8,128)(2,1)S(1)}) custom-call(bf16[128,2048]{1,0:T(8,128)(2,1)S(1)} %collective-permute-done.3.refs_0_, bf16[128,2048]{1,0:T(8,128)(2,1)S(1)} %collective-permute-done.19.refs_1_, bf16[2,768,2048]{2,1,0:T(8,128)(2,1)S(1)} %get-tuple-element.39.refs_4_.refs_2_, ...), custom_call_target="tpu_custom_call" | custom-call | flops 805306368 | bytes 3145728 | tf_op jit(solution)/shard_map/pallas_call | solution.py:137
  87.3 1.6 %collective-permute-start.26 = (bf16[128,2048]{1,0:T(8,128)(2,1)S(1)}, bf16[128,2048]{1,0:T(8,128)(2,1)S(1)}, u32[]{:S(2)}, u32[]{:S(2)}) collective-permute-start(bf16[128,2048]{1,0:T(8,128)(2,1)S(1)} %add_convert_fusion.4), channel_id=1, source_target_pairs={{0,2},{1,5},{4,0},{5,9},{8,4},{9,13},{12,8},{13,15},{14,12},{15,11... | collective-permute-start | bytes 1572872 | tf_op jit(solution)/shard_map/ppermute | solution.py:188
  88.8 3.8 %collective-permute-done.22 = bf16[128,2048]{1,0:T(8,128)(2,1)S(1)} collective-permute-done((bf16[128,2048]{1,0:T(8,128)(2,1)S(1)}, bf16[128,2048]{1,0:T(8,128)(2,1)S(1)}, u32[]{:S(2)}, u32[]{:S(2)}) %collective-permute-start.22) | collective-permute-done | bytes 524320 | tf_op jit(solution)/shard_map/ppermute | solution.py:188
  92.9 1.8 %collective-permute-start.29 = (bf16[128,2048]{1,0:T(8,128)(2,1)S(1)}, bf16[128,2048]{1,0:T(8,128)(2,1)S(1)}, u32[]{:S(2)}, u32[]{:S(2)}) collective-permute-start(bf16[128,2048]{1,0:T(8,128)(2,1)S(1)} %add_convert_fusion.3), channel_id=1, source_target_pairs={{0,2},{1,5},{4,0},{5,9},{8,4},{9,13},{12,8},{13,15},{14,12},{15,11... | collective-permute-start | bytes 1572872 | tf_op jit(solution)/shard_map/ppermute | solution.py:188
  94.6 2.7 %shard_map.70 = (bf16[128,2048]{1,0:T(8,128)(2,1)S(1)}, bf16[128,2048]{1,0:T(8,128)(2,1)S(1)}) custom-call(bf16[128,2048]{1,0:T(8,128)(2,1)S(1)} %copy-done.1, bf16[128,2048]{1,0:T(8,128)(2,1)S(1)} %collective-permute-done.23.refs_1_, bf16[2,768,2048]{2,1,0:T(8,128)(2,1)S(1)} %get-tuple-element.39.refs_4_.refs_2_, ...), custom_call_target="tpu_custom_call" | custom-call | flops 805306368 | bytes 3145728 | tf_op jit(solution)/shard_map/pallas_call | solution.py:137
  100.0 3.8 %collective-permute-done.29 = bf16[128,2048]{1,0:T(8,128)(2,1)S(1)} collective-permute-done((bf16[128,2048]{1,0:T(8,128)(2,1)S(1)}, bf16[128,2048]{1,0:T(8,128)(2,1)S(1)}, u32[]{:S(2)}, u32[]{:S(2)}) %collective-permute-start.29) | collective-permute-done | bytes 524320 | tf_op jit(solution)/shard_map/ppermute | solution.py:188
  104.2 5.3 %collective-permute-done.27.refs_2_ = bf16[128,2048]{1,0:T(8,128)(2,1)S(1)} collective-permute-done((bf16[128,2048]{1,0:T(8,128)(2,1)S(1)}, bf16[128,2048]{1,0:T(8,128)(2,1)S(1)}, u32[]{:S(2)}, u32[]{:S(2)}) %collective-permute-start.27) | collective-permute-done | bytes 524320 | tf_op jit(solution)/shard_map/ppermute | solution.py:188
  109.7 4.5 %collective-permute-done.30 = bf16[128,2048]{1,0:T(8,128)(2,1)S(1)} collective-permute-done((bf16[128,2048]{1,0:T(8,128)(2,1)S(1)}, bf16[128,2048]{1,0:T(8,128)(2,1)S(1)}, u32[]{:S(2)}, u32[]{:S(2)}) %collective-permute-start.30) | collective-permute-done | bytes 524320 | tf_op jit(solution)/shard_map/ppermute | solution.py:188
  (75 shorter events, 23.5 us)
Async XLA Ops:
  0.0 14.7 %collective-permute-start = (bf16[128,2048]{1,0:T(8,128)(2,1)}, bf16[128,2048]{1,0:T(8,128)(2,1)S(1)}, u32[]{:S(2)}, u32[]{:S(2)}) collective-permute-start(bf16[128,2048]{1,0:T(8,128)(2,1)} %refs_0_), channel_id=1, source_target_pairs={{0,4},{1,3},{4,8},{5,1},{8,12},{9,5},{12,14},{13,9},{14,10},{15,13... | collective-permute-start | bytes 1572872 | tf_op jit(solution)/shard_map/ppermute | solution.py:188
  3.0 27.2 %collective-permute-start.3 = (bf16[128,2048]{1,0:T(8,128)(2,1)}, bf16[128,2048]{1,0:T(8,128)(2,1)S(1)}, u32[]{:S(2)}, u32[]{:S(2)}) collective-permute-start(bf16[128,2048]{1,0:T(8,128)(2,1)} %refs_0_), channel_id=1, source_target_pairs={{0,3},{1,4},{4,1},{5,8},{8,5},{9,12},{12,9},{13,14},{14,13},{15,10... | collective-permute-start | bytes 1572872 | tf_op jit(solution)/shard_map/ppermute | solution.py:188
  14.7 16.6 %collective-permute-start.2 = (bf16[128,2048]{1,0:T(8,128)(2,1)S(1)}, bf16[128,2048]{1,0:T(8,128)(2,1)S(1)}, u32[]{:S(2)}, u32[]{:S(2)}) collective-permute-start(bf16[128,2048]{1,0:T(8,128)(2,1)S(1)} %collective-permute-done.refs_0_), channel_id=1, source_target_pairs={{0,1},{1,0},{4,5},{5,4},{8,9},{9,8},{12,13},{13,12},{14,15},{15,14... | collective-permute-start | bytes 1572872 | tf_op jit(solution)/shard_map/ppermute | solution.py:188
  16.0 14.2 %all-to-all-start = ((f32[16,1,128]{2,1,0:T(1,128)}), f32[16,1,128]{2,1,0:T(1,128)S(1)}, u32[]{:S(2)}, u32[]{:S(2)}) async-start(f32[16,1,128]{2,1,0:T(1,128)} %bitcast.3), calls=%async_computation | async-start | bytes 16384 | tf_op jit(solution)/shard_map/all_to_all | solution.py:204
  23.7 14.9 %collective-permute-start.1 = (bf16[128,2048]{1,0:T(8,128)(2,1)S(1)}, bf16[128,2048]{1,0:T(8,128)(2,1)S(1)}, u32[]{:S(2)}, u32[]{:S(2)}) collective-permute-start(bf16[128,2048]{1,0:T(8,128)(2,1)S(1)} %collective-permute-done.refs_0_), channel_id=1, source_target_pairs={{0,4},{1,3},{4,8},{5,1},{8,12},{9,5},{12,14},{13,9},{14,10},{15,13... | collective-permute-start | bytes 1572872 | tf_op jit(solution)/shard_map/ppermute | solution.py:188
  30.2 9.2 %collective-permute-start.4 = (bf16[128,2048]{1,0:T(8,128)(2,1)S(1)}, bf16[128,2048]{1,0:T(8,128)(2,1)S(1)}, u32[]{:S(2)}, u32[]{:S(2)}) collective-permute-start(bf16[128,2048]{1,0:T(8,128)(2,1)S(1)} %collective-permute-done.3.refs_0_), channel_id=1, source_target_pairs={{0,4},{1,3},{4,8},{5,1},{8,12},{9,5},{12,14},{13,9},{14,10},{15,13... | collective-permute-start | bytes 1572872 | tf_op jit(solution)/shard_map/ppermute | solution.py:188
  39.4 9.2 %collective-permute-start.7 = (bf16[128,2048]{1,0:T(8,128)(2,1)S(1)}, bf16[128,2048]{1,0:T(8,128)(2,1)S(1)}, u32[]{:S(2)}, u32[]{:S(2)}) collective-permute-start(bf16[128,2048]{1,0:T(8,128)(2,1)S(1)} %collective-permute-done.1.refs_0_), channel_id=1, source_target_pairs={{0,4},{1,3},{4,8},{5,1},{8,12},{9,5},{12,14},{13,9},{14,10},{15,13... | collective-permute-start | bytes 1572872 | tf_op jit(solution)/shard_map/ppermute | solution.py:188
  40.4 13.8 %collective-permute-start.8 = (bf16[128,2048]{1,0:T(8,128)(2,1)S(1)}, bf16[128,2048]{1,0:T(8,128)(2,1)S(1)}, u32[]{:S(2)}, u32[]{:S(2)}) collective-permute-start(bf16[128,2048]{1,0:T(8,128)(2,1)S(1)} %collective-permute-done.4.refs_1_), channel_id=1, source_target_pairs={{0,4},{1,3},{4,8},{5,1},{8,12},{9,5},{12,14},{13,9},{14,10},{15,13... | collective-permute-start | bytes 1572872 | tf_op jit(solution)/shard_map/ppermute | solution.py:188
  48.6 8.8 %collective-permute-start.9 = (bf16[128,2048]{1,0:T(8,128)(2,1)S(1)}, bf16[128,2048]{1,0:T(8,128)(2,1)S(1)}, u32[]{:S(2)}, u32[]{:S(2)}) collective-permute-start(bf16[128,2048]{1,0:T(8,128)(2,1)S(1)} %collective-permute-done.7.refs_0_), channel_id=1, source_target_pairs={{0,1},{1,0},{4,5},{5,4},{8,9},{9,8},{12,13},{13,12},{14,15},{15,14... | collective-permute-start | bytes 1572872 | tf_op jit(solution)/shard_map/ppermute | solution.py:188
  54.2 43.3 %collective-permute-start.25 = (bf16[128,2048]{1,0:T(8,128)(2,1)S(1)}, bf16[128,2048]{1,0:T(8,128)(2,1)S(1)}, u32[]{:S(2)}, u32[]{:S(2)}) collective-permute-start(bf16[128,2048]{1,0:T(8,128)(2,1)S(1)} %get-tuple-element.64), channel_id=1, source_target_pairs={{0,1},{1,0},{4,5},{5,4},{8,9},{9,8},{12,13},{13,12},{14,15},{15,14... | collective-permute-start | bytes 1572872 | tf_op jit(solution)/shard_map/ppermute | solution.py:188
  54.8 7.9 %collective-permute-start.13 = (bf16[64,2048]{1,0:T(8,128)(2,1)S(1)}, bf16[64,2048]{1,0:T(8,128)(2,1)S(1)}, u32[]{:S(2)}, u32[]{:S(2)}) collective-permute-start(bf16[64,2048]{1,0:T(8,128)(2,1)S(1)} %slice.74), channel_id=1, source_target_pairs={{0,4},{1,3},{4,8},{5,1},{8,12},{9,5},{12,14},{13,9},{14,10},{15,13... | collective-permute-start | bytes 786440 | tf_op jit(solution)/shard_map/ppermute | solution.py:188
  55.8 8.1 %collective-permute-start.11 = (bf16[64,2048]{1,0:T(8,128)(2,1)S(1)}, bf16[64,2048]{1,0:T(8,128)(2,1)S(1)}, u32[]{:S(2)}, u32[]{:S(2)}) collective-permute-start(bf16[64,2048]{1,0:T(8,128)(2,1)S(1)} %slice.60), channel_id=1, source_target_pairs={{0,4},{1,3},{4,8},{5,1},{8,12},{9,5},{12,14},{13,9},{14,10},{15,13... | collective-permute-start | bytes 786440 | tf_op jit(solution)/shard_map/ppermute | solution.py:188
  57.4 27.5 %collective-permute-start.20 = (bf16[256,2048]{1,0:T(8,128)(2,1)S(1)}, bf16[256,2048]{1,0:T(8,128)(2,1)S(1)}, u32[]{:S(2)}, u32[]{:S(2)}) collective-permute-start(bf16[256,2048]{1,0:T(8,128)(2,1)S(1)} %get-tuple-element.57), channel_id=1, source_target_pairs={{0,1},{1,0},{4,5},{5,4},{8,9},{9,8},{12,13},{13,12},{14,15},{15,14... | collective-permute-start | bytes 3145736 | tf_op jit(solution)/shard_map/ppermute | solution.py:188
  72.9 7.6 %collective-permute-start.18 = (bf16[64,2048]{1,0:T(8,128)(2,1)S(1)}, bf16[64,2048]{1,0:T(8,128)(2,1)S(1)}, u32[]{:S(2)}, u32[]{:S(2)}) collective-permute-start(bf16[64,2048]{1,0:T(8,128)(2,1)S(1)} %add_convert_fusion.5), channel_id=1, source_target_pairs={{0,2},{1,5},{4,0},{5,9},{8,4},{9,13},{12,8},{13,15},{14,12},{15,11... | collective-permute-start | bytes 786440 | tf_op jit(solution)/shard_map/ppermute | solution.py:188
  74.0 8.2 %collective-permute-start.19 = (bf16[128,2048]{1,0:T(8,128)(2,1)S(1)}, bf16[128,2048]{1,0:T(8,128)(2,1)S(1)}, u32[]{:S(2)}, u32[]{:S(2)}) collective-permute-start(bf16[128,2048]{1,0:T(8,128)(2,1)S(1)} %collective-permute-done.3.refs_0_), channel_id=1, source_target_pairs={{0,1},{1,0},{4,5},{5,4},{8,9},{9,8},{12,13},{13,12},{14,15},{15,14... | collective-permute-start | bytes 1572872 | tf_op jit(solution)/shard_map/ppermute | solution.py:188
  77.8 9.2 %collective-permute-start.21 = (bf16[128,2048]{1,0:T(8,128)(2,1)S(1)}, bf16[128,2048]{1,0:T(8,128)(2,1)S(1)}, u32[]{:S(2)}, u32[]{:S(2)}) collective-permute-start(bf16[128,2048]{1,0:T(8,128)(2,1)S(1)} %pad_maximum_fusion), channel_id=1, source_target_pairs={{0,2},{1,5},{4,0},{5,9},{8,4},{9,13},{12,8},{13,15},{14,12},{15,11... | collective-permute-start | bytes 1572872 | tf_op jit(solution)/shard_map/ppermute | solution.py:188
  80.6 12.0 %collective-permute-start.22 = (bf16[128,2048]{1,0:T(8,128)(2,1)S(1)}, bf16[128,2048]{1,0:T(8,128)(2,1)S(1)}, u32[]{:S(2)}, u32[]{:S(2)}) collective-permute-start(bf16[128,2048]{1,0:T(8,128)(2,1)S(1)} %pad_maximum_fusion.1), channel_id=1, source_target_pairs={{0,2},{1,5},{4,0},{5,9},{8,4},{9,13},{12,8},{13,15},{14,12},{15,11... | collective-permute-start | bytes 1572872 | tf_op jit(solution)/shard_map/ppermute | solution.py:188
  82.2 12.5 %collective-permute-start.23 = (bf16[128,2048]{1,0:T(8,128)(2,1)S(1)}, bf16[128,2048]{1,0:T(8,128)(2,1)S(1)}, u32[]{:S(2)}, u32[]{:S(2)}) collective-permute-start(bf16[128,2048]{1,0:T(8,128)(2,1)S(1)} %copy-done.1), channel_id=1, source_target_pairs={{0,1},{1,0},{4,5},{5,4},{8,9},{9,8},{12,13},{13,12},{14,15},{15,14... | collective-permute-start | bytes 1572872 | tf_op jit(solution)/shard_map/ppermute | solution.py:188
  84.9 15.1 %collective-permute-start.28 = (bf16[128,2048]{1,0:T(8,128)(2,1)S(1)}, bf16[128,2048]{1,0:T(8,128)(2,1)S(1)}, u32[]{:S(2)}, u32[]{:S(2)}) collective-permute-start(bf16[128,2048]{1,0:T(8,128)(2,1)S(1)} %get-tuple-element.66), channel_id=1, source_target_pairs={{0,1},{1,0},{4,5},{5,4},{8,9},{9,8},{12,13},{13,12},{14,15},{15,14... | collective-permute-start | bytes 1572872 | tf_op jit(solution)/shard_map/ppermute | solution.py:188
  87.3 11.0 %collective-permute-start.26 = (bf16[128,2048]{1,0:T(8,128)(2,1)S(1)}, bf16[128,2048]{1,0:T(8,128)(2,1)S(1)}, u32[]{:S(2)}, u32[]{:S(2)}) collective-permute-start(bf16[128,2048]{1,0:T(8,128)(2,1)S(1)} %add_convert_fusion.4), channel_id=1, source_target_pairs={{0,2},{1,5},{4,0},{5,9},{8,4},{9,13},{12,8},{13,15},{14,12},{15,11... | collective-permute-start | bytes 1572872 | tf_op jit(solution)/shard_map/ppermute | solution.py:188
  92.9 11.0 %collective-permute-start.29 = (bf16[128,2048]{1,0:T(8,128)(2,1)S(1)}, bf16[128,2048]{1,0:T(8,128)(2,1)S(1)}, u32[]{:S(2)}, u32[]{:S(2)}) collective-permute-start(bf16[128,2048]{1,0:T(8,128)(2,1)S(1)} %add_convert_fusion.3), channel_id=1, source_target_pairs={{0,2},{1,5},{4,0},{5,9},{8,4},{9,13},{12,8},{13,15},{14,12},{15,11... | collective-permute-start | bytes 1572872 | tf_op jit(solution)/shard_map/ppermute | solution.py:188
  97.4 6.8 %collective-permute-start.24 = (bf16[128,2048]{1,0:T(8,128)(2,1)S(1)}, bf16[128,2048]{1,0:T(8,128)(2,1)S(1)}, u32[]{:S(2)}, u32[]{:S(2)}) collective-permute-start(bf16[128,2048]{1,0:T(8,128)(2,1)S(1)} %get-tuple-element.62), channel_id=1, source_target_pairs={{0,1},{1,0},{4,5},{5,4},{8,9},{9,8},{12,13},{13,12},{14,15},{15,14... | collective-permute-start | bytes 1572872 | tf_op jit(solution)/shard_map/ppermute | solution.py:188
  98.5 11.0 %collective-permute-start.27 = (bf16[128,2048]{1,0:T(8,128)(2,1)S(1)}, bf16[128,2048]{1,0:T(8,128)(2,1)S(1)}, u32[]{:S(2)}, u32[]{:S(2)}) collective-permute-start(bf16[128,2048]{1,0:T(8,128)(2,1)S(1)} %add_convert_fusion.2), channel_id=1, source_target_pairs={{0,2},{1,5},{4,0},{5,9},{8,4},{9,13},{12,8},{13,15},{14,12},{15,11... | collective-permute-start | bytes 1572872 | tf_op jit(solution)/shard_map/ppermute | solution.py:188
  104.1 10.0 %collective-permute-start.30 = (bf16[128,2048]{1,0:T(8,128)(2,1)S(1)}, bf16[128,2048]{1,0:T(8,128)(2,1)S(1)}, u32[]{:S(2)}, u32[]{:S(2)}) collective-permute-start(bf16[128,2048]{1,0:T(8,128)(2,1)S(1)} %add_convert_fusion.1), channel_id=1, source_target_pairs={{0,3},{1,4},{4,1},{5,8},{8,5},{9,12},{12,9},{13,14},{14,13},{15,10... | collective-permute-start | bytes 1572872 | tf_op jit(solution)/shard_map/ppermute | solution.py:188
  (10 other events, 44.1 us)

commit v8 on v7

--- a/solution.py
+++ b/solution.py
@@ -7,6 +7,8 @@
 from jax.experimental import pallas as pl
 from jax.experimental.pallas import tpu as pltpu
 from jax.sharding import PartitionSpec as P
+
+GATE_ROWS, LANES = 8, 128
 
 
 def expert_half(slot_block, gate_up, down_proj):
@@ -52,26 +54,13 @@
     return list(range(0, chips, 2)) + list(range(chips - 1, 0, -2))
 
 
-def sources(chips):
-    order = snake(chips)
-    table = np.zeros((2 * chips, 2 + 2 * chips), np.int32)
-    for place in range(chips):
-        for core in (0, 1):
-            turn = 1 - 2 * core
-            row = [(0, core), (0, 1 - core)]
-            for step in range(1, chips // 2 + 1):
-                row += [(-step, core), (-step, 1 - core), (step, 1 - core), (step, core)]
-            table[2 * order[place] + core] = [2 * order[(place + turn * d) % chips] + c for d, c in row]
-    return table
-
-
-def half_expert_kernel(pieces, load, split, *refs):
-    blocks, refs = refs[: len(pieces)], refs[len(pieces) :]
-    if load:
-        (places, gates, gate_up_far, down_far), refs = refs[:4], refs[4:]
-        outs, (gate_up_ref, down_ref, columns, rows, hidden, lines, arrived) = refs[:split], refs[split:]
+def half_expert_kernel(first_tokens, load, split, expert_ref, *refs):
+    blocks, refs = refs[: len(first_tokens)], refs[len(first_tokens) :]
+    if load:
+        (gate_up_far, down_far), refs = refs[:2], refs[2:]
+        outs, (gate_up_ref, down_ref, rows, hidden, arrived) = refs[:split], refs[split:]
     else:
-        (gate_up_ref, down_ref, columns), outs, (rows, hidden) = refs[:3], refs[3:-2], refs[-2:]
+        (gate_up_ref, down_ref), outs, (rows, hidden) = refs[:2], refs[2:-2], refs[-2:]
     units, width = down_ref.shape
     tile = 256 if units % 256 == 0 else units
     tiles = units // tile
@@ -83,18 +72,17 @@
         copies.append(pltpu.make_async_copy(down_far, down_ref, arrived.at[tiles]))
         for copy in copies:
             copy.start()
-        lines[...] = jnp.zeros_like(lines)
-        for i in range(places.shape[0]):
-            lines[i : i + 1, :] = gates[pl.ds(places[i], 1), :]
-        columns[...] = lines[...].T
 
     at = 0
     weights = []
-    for block, (column, token) in zip(blocks, pieces):
-        count = block.shape[0]
-        rows[at : at + count, :] = block[...]
+    for block, token in zip(blocks, first_tokens):
+        count = block.shape[0] - GATE_ROWS
+        rows[at : at + count, :] = block[:count, :]
         at += count
-        weights.append(columns[token : token + count, column : column + 1])
+        high, low = (block[count:, i * LANES : (i + 1) * LANES].astype(jnp.float32) for i in (0, 1))
+        wanted = lax.broadcasted_iota(jnp.int32, high.shape, 0) == expert_ref[0]
+        line = jnp.sum(jnp.where(wanted, high + low, 0.0), axis=0, keepdims=True)
+        weights.append(jnp.broadcast_to(line, high.shape).T[token : token + count, :1])
     weight = jnp.concatenate(weights)
 
     contract = (((1,), (1,)), ((), ()))
@@ -118,26 +106,20 @@
             out[:, low : low + tile] = product[i * share : (i + 1) * share]
 
 
-def half_expert(pieces, blocks, weights, load=False, cost=2, split=2):
-    height = sum(block.shape[0] for block in blocks)
-    gate_up, down_proj = weights[2:] if load else weights[:2]
-    units, width = down_proj.shape
+def half_expert(first_tokens, blocks, expert, weights, load=False, cost=2, split=2):
+    height = sum(block.shape[0] - GATE_ROWS for block in blocks)
+    units, width = weights[1].shape
     whole = pl.BlockSpec(memory_space=pltpu.VMEM)
     far = pl.BlockSpec(memory_space=pltpu.HBM)
     outs = [jax.ShapeDtypeStruct((height // split, width), jnp.bfloat16)] * split
     scratch = [pltpu.VMEM((height, width), jnp.bfloat16), pltpu.VMEM((height, units), jnp.bfloat16)]
-    specs = [whole] * 3
-    if load:
-        tokens = weights[1].shape[1]
-        outs += [jax.ShapeDtypeStruct(array.shape, array.dtype) for array in (gate_up, down_proj)]
-        outs.append(jax.ShapeDtypeStruct((tokens, 128), jnp.float32))
-        scratch.append(pltpu.VMEM((128, tokens), jnp.float32))
+    if load:
+        outs += [jax.ShapeDtypeStruct(array.shape, array.dtype) for array in weights]
         scratch.append(pltpu.SemaphoreType.DMA((units // 256 + 1 if units % 256 == 0 else 2,)))
-        specs = [pl.BlockSpec(memory_space=pltpu.SMEM), whole, far, far]
     return pl.pallas_call(
-        functools.partial(half_expert_kernel, tuple(pieces), load, split),
+        functools.partial(half_expert_kernel, tuple(first_tokens), load, split),
         out_shape=outs,
-        in_specs=[whole] * len(blocks) + specs,
+        in_specs=[pl.BlockSpec(memory_space=pltpu.SMEM)] + [whole] * len(blocks) + [far if load else whole] * 2,
         out_specs=[whole] * len(outs),
         scratch_shapes=scratch,
         compiler_params=pltpu.CompilerParams(vmem_limit_bytes=(34 if load else 14) << 20),
@@ -146,7 +128,7 @@
             bytes_accessed=int(cost * units * width),
             transcendentals=0,
         ),
-    )(*blocks, *weights)
+    )(expert, *blocks, *weights)
 
 
 def sum_kernel(*refs):
@@ -196,18 +178,14 @@
     def after(value, *earlier):
         return lax.optimization_barrier((value, *earlier))[0]
 
-    ring = [send(tokens, forth), send(tokens, across)]
-
-    places = lax.dynamic_index_in_dim(jnp.asarray(sources(chips)), lax.axis_index("blk"), 0, keepdims=False)
-    chosen = jnp.arange(chips, dtype=jnp.int32)[:, None, None] == expert_ids.T[None]
+    expert = jnp.right_shift(lax.axis_index("blk"), 1).astype(jnp.int32).reshape(1)
+    chosen = jnp.arange(GATE_ROWS, dtype=jnp.int32)[:, None, None] == expert_ids.T[None]
     weight = jnp.sum(jnp.where(chosen, route_gate.T[None], 0.0), axis=1)
-    gates = lax.all_to_all(jnp.repeat(weight, 2, axis=0), "blk", split_axis=0, concat_axis=0, tiled=True)
-    gates = gates.reshape(-1, rows)
-    ring[1] = after(ring[1], gates)
-
-    def swapped_columns(step, c):
-        return [(4 * step - 2 + c, 0), (4 * step + c, 0)]
-
+    high = lax.reduce_precision(weight, 8, 7)
+    gates = jnp.concatenate([high, weight - high], axis=1).astype(jnp.bfloat16)
+    packed = jnp.concatenate([tokens, jnp.pad(gates, ((0, 0), (0, tokens.shape[1] - 2 * LANES)))])
+
+    ring = [send(packed, forth), send(packed, across)]
     results = {}
     near, delayed = None, None
     for step in range(1, far):
@@ -216,15 +194,13 @@
         if step < far - 1:
             ring = [send(block, forth) for block in ring]
         else:
-            ring = [send(ring[0][:half], forth), send(ring[1][half:], forth)]
+            ring = [send(jnp.concatenate([ring[0][:half], ring[0][rows:]]), forth), send(ring[1][half:], forth)]
         if step == 1:
-            load = [places, gates, gate_up, down_proj]
-            kept, given, *near = half_expert(swapped_columns(1, 0), [blocks[0], swapped[0]], load, load=True)
+            delayed = blocks[1]
+            kept, given, *near = half_expert([0, 0], [blocks[0], swapped[0]], expert, [gate_up, down_proj], load=True)
             results[1, 0] = kept, send(given, cores)
-            delayed = blocks[1]
         else:
-            pieces = [(4 * step - 2 + i, 0) for i in range(4)]
-            kept, given = half_expert(pieces, blocks + swapped, near)
+            kept, given = half_expert([0] * 4, blocks + swapped, expert, near)
             given = send(given, cores)
             for c in chains:
                 results[step, c] = kept[c * rows : (c + 1) * rows], given[c * rows : (c + 1) * rows]
@@ -232,12 +208,11 @@
         if step == far - 1:
             ring[1] = after(ring[1], kept)
 
-    base = 4 * far - 2
-    (given,) = half_expert([(base, 0), (base + 1, half)], ring, near, split=1)
+    (given,) = half_expert([0, half], ring, expert, near, split=1)
     swapped = [send(block, cores) for block in ring]
     swapped[0] = after(swapped[0], given)
     given = send(given, cores)
-    (kept,) = half_expert([(base + 2, 0), (base + 3, half)], swapped, near, split=1)
+    (kept,) = half_expert([0, half], swapped, expert, near, split=1)
 
     first, second = slice(0, half), slice(half, rows)
     late = []
@@ -257,16 +232,16 @@
         earlier = rounded(value)
         sums.append(send(earlier, back))
     swapped = send(after(delayed, late_value), cores)
-    kept, given = half_expert(swapped_columns(1, 1), [after(delayed, earlier), swapped], near)
+    kept, given = half_expert([0, 0], [after(delayed, earlier), swapped], expert, near)
     results[1, 1] = kept, send(given, cores)
-    other = send(after(tokens, earlier), cores)
+    other = send(after(packed, earlier), cores)
     earlier = kept
     for step in range(far - 2, 1, -1):
         for c in chains:
             mine, theirs = results[step, c]
             earlier = rounded(total(after(mine, earlier), theirs, sums[c]))
             sums[c] = send(earlier, back)
-    kept, given = half_expert([(0, 0), (1, 0)], [after(tokens, earlier), other], near)
+    kept, given = half_expert([0, 0], [after(packed, earlier), other], expert, near)
     given = send(given, cores)
     earlier = kept
     for c, pairs in zip(chains, (back, across)):
@@ -287,7 +262,8 @@
 
     def per_device(tokens, expert_ids, route_gate, gate_up, down_proj):
         experts = mesh.shape["blk"] // 2
-        body = by_tokens if experts <= 2 * expert_ids.shape[1] else by_slots
+        dense = experts <= min(GATE_ROWS, 2 * expert_ids.shape[1]) and tokens.shape[0] == LANES
+        body = by_tokens if dense else by_slots
         return body(tokens, expert_ids, route_gate, gate_up, down_proj)
 
     return jax.shard_map(

time: 116 us -> 111 us (0.957)
  waiting for transfers between devices: 49.3 us -> 46.2 us
  local copies, waits for them, and re-layouts: 3.52 us -> 2.23 us
    all_to_all x1 -> x0, starting transfers between devices: 7.73 us -> none  [by_tokens(): lax.all_to_all(jnp.repeat(weight, 2, axis=0), 'blk', split_axis=0, concat...]
    ppermute x31, starting transfers between devices: 24.2 us -> 31.8 us  [send(): return lax.ppermute(value, 'blk', pairs)]
    all_to_all x1 -> x0, waiting for transfers between devices: 4.58 us -> none  [by_tokens(): lax.all_to_all(jnp.repeat(weight, 2, axis=0), 'blk', split_axis=0, concat...]
    ppermute x31, waiting for transfers between devices: 44.7 us -> 46.2 us  [send(): return lax.ppermute(value, 'blk', pairs)]
  transfers between devices with their start and end apart: 32 -> 31, of which waited for: 15 -> 14; matrix products, arithmetic and copies ran while one was open for 3% -> 2% of each run, Pallas kernels for 23% -> 24%
where the time goes in v8:
time: 111 us
  waiting for transfers between devices  46.2 us (42%)
  starting transfers between devices  31.8 us (29%)
  Pallas kernels  26.1 us (24%)
  other arithmetic  4.28 us (4%)
  local copies, waits for them, and re-layouts  2.23 us (2%)
    ppermute x31, waiting for transfers between devices, send(): return lax.ppermute(value, 'blk', pairs)  46.2 us
    ppermute x31, starting transfers between devices, send(): return lax.ppermute(value, 'blk', pairs)  31.8 us
    pallas_call x7, Pallas kernels, half_expert(): pl.pallas_call(functools.partial(half_expert_kernel, tuple(first_tokens),...  26 us
  transfers between devices with their start and end apart: 31, of which 14 were waited for; matrix products, arithmetic and copies ran while one was open for 2% of the time, Pallas kernels for 24%

profile of v8, /device:TPU:0, one launch (start us, length us, event | category | flops | bytes accessed | tf_op | source)
XLA Modules:
  0.0 110.9 jit_solution(10076826241872144887)
XLA Ops:
  1.8 3.1 %collective-permute-start = (bf16[136,2048]{1,0:T(8,128)(2,1)S(1)}, bf16[136,2048]{1,0:T(8,128)(2,1)S(1)}, u32[]{:S(2)}, u32[]{:S(2)}) collective-permute-start(bf16[136,2048]{1,0:T(8,128)(2,1)S(1)} %pad_maximum_fusion.refs_0_), channel_id=1, source_target_pairs={{0,4},{1,3},{4,8},{5,1},{8,12},{9,5},{12,14},{13,9},{14,10},{15,13... | collective-permute-start | bytes 1671176 | tf_op jit(solution)/shard_map/ppermute | solution.py:170
  5.6 11.3 %collective-permute-done.refs_0_ = bf16[136,2048]{1,0:T(8,128)(2,1)S(1)} collective-permute-done((bf16[136,2048]{1,0:T(8,128)(2,1)S(1)}, bf16[136,2048]{1,0:T(8,128)(2,1)S(1)}, u32[]{:S(2)}, u32[]{:S(2)}) %collective-permute-start) | collective-permute-done | bytes 557088 | tf_op jit(solution)/shard_map/ppermute | solution.py:170
  16.9 2.5 %collective-permute-start.1 = (bf16[136,2048]{1,0:T(8,128)(2,1)S(1)}, bf16[136,2048]{1,0:T(8,128)(2,1)S(1)}, u32[]{:S(2)}, u32[]{:S(2)}) collective-permute-start(bf16[136,2048]{1,0:T(8,128)(2,1)S(1)} %collective-permute-done.refs_0_), channel_id=1, source_target_pairs={{0,4},{1,3},{4,8},{5,1},{8,12},{9,5},{12,14},{13,9},{14,10},{15,13... | collective-permute-start | bytes 1671176 | tf_op jit(solution)/shard_map/ppermute | solution.py:170
  21.0 1.9 %copy-done = bf16[768,2048]{1,0:T(8,128)(2,1)S(1)} copy-done((bf16[768,2048]{1,0:T(8,128)(2,1)S(1)}, bf16[768,2048]{1,0:T(8,128)(2,1)}, u32[]{:S(2)}) %copy-start) | copy-done | bytes 3145752
  22.9 4.9 %shard_map.55 = (bf16[128,2048]{1,0:T(8,128)(2,1)S(1)}, bf16[128,2048]{1,0:T(8,128)(2,1)S(1)}, bf16[2,768,2048]{2,1,0:T(8,128)(2,1)S(1)}, bf16[768,2048]{1,0:T(8,128)(2,1)S(1)}) custom-call(s32[1]{0:T(128)} %bitcast.expert_ref, bf16[136,2048]{1,0:T(8,128)(2,1)S(1)} %collective-permute-done.refs_0_, bf16[136,2048]{1,0:T(8,128)(2,1)S(1)} %collective-permute-done.2.refs_1_, ...), custom_call_target="tpu_custom_call" | custom-call | flops 805306368 | bytes 3145728 | tf_op jit(solution)/shard_map/pallas_call | solution.py:119
  28.8 5.0 %collective-permute-done.4.refs_1_ = bf16[136,2048]{1,0:T(8,128)(2,1)S(1)} collective-permute-done((bf16[136,2048]{1,0:T(8,128)(2,1)S(1)}, bf16[136,2048]{1,0:T(8,128)(2,1)S(1)}, u32[]{:S(2)}, u32[]{:S(2)}) %collective-permute-start.4) | collective-permute-done | bytes 557088 | tf_op jit(solution)/shard_map/ppermute | solution.py:170
  37.4 5.2 %shard_map.56 = (bf16[256,2048]{1,0:T(8,128)(2,1)S(1)}, bf16[256,2048]{1,0:T(8,128)(2,1)S(1)}) custom-call(s32[1]{0:T(128)} %bitcast.expert_ref, bf16[136,2048]{1,0:T(8,128)(2,1)S(1)} %collective-permute-done.1.refs_0_, bf16[136,2048]{1,0:T(8,128)(2,1)S(1)} %collective-permute-done.4.refs_1_, bf16[136,2048]{1,0:T(8,128)(2,1)S(1)} %collective-permute-done.5.refs_2_, ...), custom_call_target="tpu_custom_call" | custom-call | flops 1610612736 | bytes 3145728 | tf_op jit(solution)/shard_map/pallas_call | solution.py:119
  43.4 5.9 %collective-permute-done.8.refs_1_ = bf16[136,2048]{1,0:T(8,128)(2,1)S(1)} collective-permute-done((bf16[136,2048]{1,0:T(8,128)(2,1)S(1)}, bf16[136,2048]{1,0:T(8,128)(2,1)S(1)}, u32[]{:S(2)}, u32[]{:S(2)}) %collective-permute-start.8) | collective-permute-done | bytes 557088 | tf_op jit(solution)/shard_map/ppermute | solution.py:170
  52.5 5.1 %shard_map.57 = (bf16[256,2048]{1,0:T(8,128)(2,1)S(1)}, bf16[256,2048]{1,0:T(8,128)(2,1)S(1)}) custom-call(s32[1]{0:T(128)} %bitcast.expert_ref, bf16[136,2048]{1,0:T(8,128)(2,1)S(1)} %collective-permute-done.7.refs_0_, bf16[136,2048]{1,0:T(8,128)(2,1)S(1)} %collective-permute-done.8.refs_1_, bf16[136,2048]{1,0:T(8,128)(2,1)S(1)} %collective-permute-done.9.refs_2_, ...), custom_call_target="tpu_custom_call" | custom-call | flops 1610612736 | bytes 3145728 | tf_op jit(solution)/shard_map/pallas_call | solution.py:119
  59.3 2.7 %shard_map.58 = bf16[128,2048]{1,0:T(8,128)(2,1)S(1)} custom-call(s32[1]{0:T(128)} %bitcast.expert_ref, bf16[72,2048]{1,0:T(8,128)(2,1)S(1)} %collective-permute-done.11.refs_0_, bf16[72,2048]{1,0:T(8,128)(2,1)S(1)} %collective-permute-done.13.refs_1_, bf16[2,768,2048]{2,1,0:T(8,128)(2,1)S(1)} %get-tuple-element.36.refs_4_.refs_2_, ...), custom_call_target="tpu_custom_call" | custom-call | flops 402653184 | bytes 3145728 | tf_op jit(solution)/shard_map/pallas_call | solution.py:119
  63.8 2.7 %shard_map.59 = bf16[128,2048]{1,0:T(8,128)(2,1)S(1)} custom-call(s32[1]{0:T(128)} %bitcast.expert_ref, bf16[72,2048]{1,0:T(8,128)(2,1)S(1)} %collective-permute-done.12.refs_0_, bf16[72,2048]{1,0:T(8,128)(2,1)S(1)} %collective-permute-done.14.refs_1_, bf16[2,768,2048]{2,1,0:T(8,128)(2,1)S(1)} %get-tuple-element.36.refs_4_.refs_2_, ...), custom_call_target="tpu_custom_call" | custom-call | flops 402653184 | bytes 3145728 | tf_op jit(solution)/shard_map/pallas_call | solution.py:119
  66.6 2.1 %collective-permute-start.17 = (bf16[64,2048]{1,0:T(8,128)(2,1)S(1)}, bf16[64,2048]{1,0:T(8,128)(2,1)S(1)}, u32[]{:S(2)}, u32[]{:S(2)}) collective-permute-start(bf16[64,2048]{1,0:T(8,128)(2,1)S(1)} %add_convert_fusion.6), channel_id=1, source_target_pairs={{0,2},{1,5},{4,0},{5,9},{8,4},{9,13},{12,8},{13,15},{14,12},{15,11... | collective-permute-start | bytes 786440 | tf_op jit(solution)/shard_map/ppermute | solution.py:170
  70.5 2.5 %collective-permute-done.17 = bf16[64,2048]{1,0:T(8,128)(2,1)S(1)} collective-permute-done((bf16[64,2048]{1,0:T(8,128)(2,1)S(1)}, bf16[64,2048]{1,0:T(8,128)(2,1)S(1)}, u32[]{:S(2)}, u32[]{:S(2)}) %collective-permute-start.17) | collective-permute-done | bytes 262176 | tf_op jit(solution)/shard_map/ppermute | solution.py:170
  73.1 2.1 %collective-permute-start.21 = (bf16[128,2048]{1,0:T(8,128)(2,1)S(1)}, bf16[128,2048]{1,0:T(8,128)(2,1)S(1)}, u32[]{:S(2)}, u32[]{:S(2)}) collective-permute-start(bf16[128,2048]{1,0:T(8,128)(2,1)S(1)} %pad_maximum_fusion.1), channel_id=1, source_target_pairs={{0,2},{1,5},{4,0},{5,9},{8,4},{9,13},{12,8},{13,15},{14,12},{15,11... | collective-permute-start | bytes 1572872 | tf_op jit(solution)/shard_map/ppermute | solution.py:170
  76.0 2.1 %collective-permute-start.22 = (bf16[128,2048]{1,0:T(8,128)(2,1)S(1)}, bf16[128,2048]{1,0:T(8,128)(2,1)S(1)}, u32[]{:S(2)}, u32[]{:S(2)}) collective-permute-start(bf16[128,2048]{1,0:T(8,128)(2,1)S(1)} %pad_maximum_fusion.2), channel_id=1, source_target_pairs={{0,2},{1,5},{4,0},{5,9},{8,4},{9,13},{12,8},{13,15},{14,12},{15,11... | collective-permute-start | bytes 1572872 | tf_op jit(solution)/shard_map/ppermute | solution.py:170
  78.0 2.7 %shard_map.60 = (bf16[128,2048]{1,0:T(8,128)(2,1)S(1)}, bf16[128,2048]{1,0:T(8,128)(2,1)S(1)}) custom-call(s32[1]{0:T(128)} %bitcast.expert_ref, bf16[136,2048]{1,0:T(8,128)(2,1)S(1)} %collective-permute-done.3.refs_0_, bf16[136,2048]{1,0:T(8,128)(2,1)S(1)} %collective-permute-done.19.refs_1_, bf16[2,768,2048]{2,1,0:T(8,128)(2,1)S(1)} %get-tuple-element.36.refs_4_.refs_2_, ...), custom_call_target="tpu_custom_call" | custom-call | flops 805306368 | bytes 3145728 | tf_op jit(solution)/shard_map/pallas_call | solution.py:119
  82.6 2.1 %collective-permute-start.26 = (bf16[128,2048]{1,0:T(8,128)(2,1)S(1)}, bf16[128,2048]{1,0:T(8,128)(2,1)S(1)}, u32[]{:S(2)}, u32[]{:S(2)}) collective-permute-start(bf16[128,2048]{1,0:T(8,128)(2,1)S(1)} %add_convert_fusion.4), channel_id=1, source_target_pairs={{0,2},{1,5},{4,0},{5,9},{8,4},{9,13},{12,8},{13,15},{14,12},{15,11... | collective-permute-start | bytes 1572872 | tf_op jit(solution)/shard_map/ppermute | solution.py:170
  84.7 3.3 %collective-permute-done.22 = bf16[128,2048]{1,0:T(8,128)(2,1)S(1)} collective-permute-done((bf16[128,2048]{1,0:T(8,128)(2,1)S(1)}, bf16[128,2048]{1,0:T(8,128)(2,1)S(1)}, u32[]{:S(2)}, u32[]{:S(2)}) %collective-permute-start.22) | collective-permute-done | bytes 524320 | tf_op jit(solution)/shard_map/ppermute | solution.py:170
  88.2 2.3 %collective-permute-start.29 = (bf16[128,2048]{1,0:T(8,128)(2,1)S(1)}, bf16[128,2048]{1,0:T(8,128)(2,1)S(1)}, u32[]{:S(2)}, u32[]{:S(2)}) collective-permute-start(bf16[128,2048]{1,0:T(8,128)(2,1)S(1)} %add_convert_fusion.3), channel_id=1, source_target_pairs={{0,2},{1,5},{4,0},{5,9},{8,4},{9,13},{12,8},{13,15},{14,12},{15,11... | collective-permute-start | bytes 1572872 | tf_op jit(solution)/shard_map/ppermute | solution.py:170
  90.5 2.7 %shard_map.61 = (bf16[128,2048]{1,0:T(8,128)(2,1)S(1)}, bf16[128,2048]{1,0:T(8,128)(2,1)S(1)}) custom-call(s32[1]{0:T(128)} %bitcast.expert_ref, bf16[136,2048]{1,0:T(8,128)(2,1)S(1)} %pad_maximum_fusion.refs_0_, bf16[136,2048]{1,0:T(8,128)(2,1)S(1)} %collective-permute-done.23.refs_1_, bf16[2,768,2048]{2,1,0:T(8,128)(2,1)S(1)} %get-tuple-element.36.refs_4_.refs_2_, ...), custom_call_target="tpu_custom_call" | custom-call | flops 805306368 | bytes 3145728 | tf_op jit(solution)/shard_map/pallas_call | solution.py:119
  93.8 2.1 %collective-permute-start.27 = (bf16[128,2048]{1,0:T(8,128)(2,1)S(1)}, bf16[128,2048]{1,0:T(8,128)(2,1)S(1)}, u32[]{:S(2)}, u32[]{:S(2)}) collective-permute-start(bf16[128,2048]{1,0:T(8,128)(2,1)S(1)} %add_convert_fusion.2), channel_id=1, source_target_pairs={{0,2},{1,5},{4,0},{5,9},{8,4},{9,13},{12,8},{13,15},{14,12},{15,11... | collective-permute-start | bytes 1572872 | tf_op jit(solution)/shard_map/ppermute | solution.py:170
  95.9 3.3 %collective-permute-done.29 = bf16[128,2048]{1,0:T(8,128)(2,1)S(1)} collective-permute-done((bf16[128,2048]{1,0:T(8,128)(2,1)S(1)}, bf16[128,2048]{1,0:T(8,128)(2,1)S(1)}, u32[]{:S(2)}, u32[]{:S(2)}) %collective-permute-start.29) | collective-permute-done | bytes 524320 | tf_op jit(solution)/shard_map/ppermute | solution.py:170
  99.8 5.0 %collective-permute-done.27.refs_2_ = bf16[128,2048]{1,0:T(8,128)(2,1)S(1)} collective-permute-done((bf16[128,2048]{1,0:T(8,128)(2,1)S(1)}, bf16[128,2048]{1,0:T(8,128)(2,1)S(1)}, u32[]{:S(2)}, u32[]{:S(2)}) %collective-permute-start.27) | collective-permute-done | bytes 524320 | tf_op jit(solution)/shard_map/ppermute | solution.py:170
  105.0 5.0 %collective-permute-done.30 = bf16[128,2048]{1,0:T(8,128)(2,1)S(1)} collective-permute-done((bf16[128,2048]{1,0:T(8,128)(2,1)S(1)}, bf16[128,2048]{1,0:T(8,128)(2,1)S(1)}, u32[]{:S(2)}, u32[]{:S(2)}) %collective-permute-start.30) | collective-permute-done | bytes 524320 | tf_op jit(solution)/shard_map/ppermute | solution.py:170
  (74 shorter events, 23.2 us)
Async XLA Ops:
  1.8 15.1 %collective-permute-start = (bf16[136,2048]{1,0:T(8,128)(2,1)S(1)}, bf16[136,2048]{1,0:T(8,128)(2,1)S(1)}, u32[]{:S(2)}, u32[]{:S(2)}) collective-permute-start(bf16[136,2048]{1,0:T(8,128)(2,1)S(1)} %pad_maximum_fusion.refs_0_), channel_id=1, source_target_pairs={{0,4},{1,3},{4,8},{5,1},{8,12},{9,5},{12,14},{13,9},{14,10},{15,13... | collective-permute-start | bytes 1671176 | tf_op jit(solution)/shard_map/ppermute | solution.py:170
  4.9 14.5 %collective-permute-start.3 = (bf16[136,2048]{1,0:T(8,128)(2,1)S(1)}, bf16[136,2048]{1,0:T(8,128)(2,1)S(1)}, u32[]{:S(2)}, u32[]{:S(2)}) collective-permute-start(bf16[136,2048]{1,0:T(8,128)(2,1)S(1)} %pad_maximum_fusion.refs_0_), channel_id=1, source_target_pairs={{0,3},{1,4},{4,1},{5,8},{8,5},{9,12},{12,9},{13,14},{14,13},{15,10... | collective-permute-start | bytes 1671176 | tf_op jit(solution)/shard_map/ppermute | solution.py:170
  16.9 10.9 %collective-permute-start.1 = (bf16[136,2048]{1,0:T(8,128)(2,1)S(1)}, bf16[136,2048]{1,0:T(8,128)(2,1)S(1)}, u32[]{:S(2)}, u32[]{:S(2)}) collective-permute-start(bf16[136,2048]{1,0:T(8,128)(2,1)S(1)} %collective-permute-done.refs_0_), channel_id=1, source_target_pairs={{0,4},{1,3},{4,8},{5,1},{8,12},{9,5},{12,14},{13,9},{14,10},{15,13... | collective-permute-start | bytes 1671176 | tf_op jit(solution)/shard_map/ppermute | solution.py:170
  19.4 14.4 %collective-permute-start.4 = (bf16[136,2048]{1,0:T(8,128)(2,1)S(1)}, bf16[136,2048]{1,0:T(8,128)(2,1)S(1)}, u32[]{:S(2)}, u32[]{:S(2)}) collective-permute-start(bf16[136,2048]{1,0:T(8,128)(2,1)S(1)} %collective-permute-done.3.refs_0_), channel_id=1, source_target_pairs={{0,4},{1,3},{4,8},{5,1},{8,12},{9,5},{12,14},{13,9},{14,10},{15,13... | collective-permute-start | bytes 1671176 | tf_op jit(solution)/shard_map/ppermute | solution.py:170
  27.8 9.5 %collective-permute-start.5 = (bf16[136,2048]{1,0:T(8,128)(2,1)S(1)}, bf16[136,2048]{1,0:T(8,128)(2,1)S(1)}, u32[]{:S(2)}, u32[]{:S(2)}) collective-permute-start(bf16[136,2048]{1,0:T(8,128)(2,1)S(1)} %collective-permute-done.1.refs_0_), channel_id=1, source_target_pairs={{0,1},{1,0},{4,5},{5,4},{8,9},{9,8},{12,13},{13,12},{14,15},{15,14... | collective-permute-start | bytes 1671176 | tf_op jit(solution)/shard_map/ppermute | solution.py:170
  33.8 9.5 %collective-permute-start.7 = (bf16[136,2048]{1,0:T(8,128)(2,1)S(1)}, bf16[136,2048]{1,0:T(8,128)(2,1)S(1)}, u32[]{:S(2)}, u32[]{:S(2)}) collective-permute-start(bf16[136,2048]{1,0:T(8,128)(2,1)S(1)} %collective-permute-done.1.refs_0_), channel_id=1, source_target_pairs={{0,4},{1,3},{4,8},{5,1},{8,12},{9,5},{12,14},{13,9},{14,10},{15,13... | collective-permute-start | bytes 1671176 | tf_op jit(solution)/shard_map/ppermute | solution.py:170
  34.9 14.4 %collective-permute-start.8 = (bf16[136,2048]{1,0:T(8,128)(2,1)S(1)}, bf16[136,2048]{1,0:T(8,128)(2,1)S(1)}, u32[]{:S(2)}, u32[]{:S(2)}) collective-permute-start(bf16[136,2048]{1,0:T(8,128)(2,1)S(1)} %collective-permute-done.4.refs_1_), channel_id=1, source_target_pairs={{0,4},{1,3},{4,8},{5,1},{8,12},{9,5},{12,14},{13,9},{14,10},{15,13... | collective-permute-start | bytes 1671176 | tf_op jit(solution)/shard_map/ppermute | solution.py:170
  36.5 56.8 %collective-permute-start.25 = (bf16[128,2048]{1,0:T(8,128)(2,1)S(1)}, bf16[128,2048]{1,0:T(8,128)(2,1)S(1)}, u32[]{:S(2)}, u32[]{:S(2)}) collective-permute-start(bf16[128,2048]{1,0:T(8,128)(2,1)S(1)} %get-tuple-element.60), channel_id=1, source_target_pairs={{0,1},{1,0},{4,5},{5,4},{8,9},{9,8},{12,13},{13,12},{14,15},{15,14... | collective-permute-start | bytes 1572872 | tf_op jit(solution)/shard_map/ppermute | solution.py:170
  43.3 9.1 %collective-permute-start.9 = (bf16[136,2048]{1,0:T(8,128)(2,1)S(1)}, bf16[136,2048]{1,0:T(8,128)(2,1)S(1)}, u32[]{:S(2)}, u32[]{:S(2)}) collective-permute-start(bf16[136,2048]{1,0:T(8,128)(2,1)S(1)} %collective-permute-done.7.refs_0_), channel_id=1, source_target_pairs={{0,1},{1,0},{4,5},{5,4},{8,9},{9,8},{12,13},{13,12},{14,15},{15,14... | collective-permute-start | bytes 1671176 | tf_op jit(solution)/shard_map/ppermute | solution.py:170
  49.3 8.3 %collective-permute-start.13 = (bf16[72,2048]{1,0:T(8,128)(2,1)S(1)}, bf16[72,2048]{1,0:T(8,128)(2,1)S(1)}, u32[]{:S(2)}, u32[]{:S(2)}) collective-permute-start(bf16[72,2048]{1,0:T(8,128)(2,1)S(1)} %slice.78), channel_id=1, source_target_pairs={{0,4},{1,3},{4,8},{5,1},{8,12},{9,5},{12,14},{13,9},{14,10},{15,13... | collective-permute-start | bytes 884744 | tf_op jit(solution)/shard_map/ppermute | solution.py:170
  50.8 8.5 %collective-permute-start.11 = (bf16[72,2048]{1,0:T(8,128)(2,1)S(1)}, bf16[72,2048]{1,0:T(8,128)(2,1)S(1)}, u32[]{:S(2)}, u32[]{:S(2)}) collective-permute-start(bf16[72,2048]{1,0:T(8,128)(2,1)S(1)} %pad_maximum_fusion.3), channel_id=1, source_target_pairs={{0,4},{1,3},{4,8},{5,1},{8,12},{9,5},{12,14},{13,9},{14,10},{15,13... | collective-permute-start | bytes 884744 | tf_op jit(solution)/shard_map/ppermute | solution.py:170
  52.4 28.3 %collective-permute-start.20 = (bf16[256,2048]{1,0:T(8,128)(2,1)S(1)}, bf16[256,2048]{1,0:T(8,128)(2,1)S(1)}, u32[]{:S(2)}, u32[]{:S(2)}) collective-permute-start(bf16[256,2048]{1,0:T(8,128)(2,1)S(1)} %get-tuple-element.53), channel_id=1, source_target_pairs={{0,1},{1,0},{4,5},{5,4},{8,9},{9,8},{12,13},{13,12},{14,15},{15,14... | collective-permute-start | bytes 3145736 | tf_op jit(solution)/shard_map/ppermute | solution.py:170
  62.7 7.6 %collective-permute-start.16 = (bf16[256,2048]{1,0:T(8,128)(2,1)S(1)}, bf16[256,2048]{1,0:T(8,128)(2,1)S(1)}, u32[]{:S(2)}, u32[]{:S(2)}) collective-permute-start(bf16[256,2048]{1,0:T(8,128)(2,1)S(1)} %get-tuple-element.47), channel_id=1, source_target_pairs={{0,1},{1,0},{4,5},{5,4},{8,9},{9,8},{12,13},{13,12},{14,15},{15,14... | collective-permute-start | bytes 3145736 | tf_op jit(solution)/shard_map/ppermute | solution.py:170
  68.7 7.1 %collective-permute-start.18 = (bf16[64,2048]{1,0:T(8,128)(2,1)S(1)}, bf16[64,2048]{1,0:T(8,128)(2,1)S(1)}, u32[]{:S(2)}, u32[]{:S(2)}) collective-permute-start(bf16[64,2048]{1,0:T(8,128)(2,1)S(1)} %add_convert_fusion.5), channel_id=1, source_target_pairs={{0,2},{1,5},{4,0},{5,9},{8,4},{9,13},{12,8},{13,15},{14,12},{15,11... | collective-permute-start | bytes 786440 | tf_op jit(solution)/shard_map/ppermute | solution.py:170
  70.4 7.7 %collective-permute-start.19 = (bf16[136,2048]{1,0:T(8,128)(2,1)S(1)}, bf16[136,2048]{1,0:T(8,128)(2,1)S(1)}, u32[]{:S(2)}, u32[]{:S(2)}) collective-permute-start(bf16[136,2048]{1,0:T(8,128)(2,1)S(1)} %collective-permute-done.3.refs_0_), channel_id=1, source_target_pairs={{0,1},{1,0},{4,5},{5,4},{8,9},{9,8},{12,13},{13,12},{14,15},{15,14... | collective-permute-start | bytes 1671176 | tf_op jit(solution)/shard_map/ppermute | solution.py:170
  73.1 9.2 %collective-permute-start.21 = (bf16[128,2048]{1,0:T(8,128)(2,1)S(1)}, bf16[128,2048]{1,0:T(8,128)(2,1)S(1)}, u32[]{:S(2)}, u32[]{:S(2)}) collective-permute-start(bf16[128,2048]{1,0:T(8,128)(2,1)S(1)} %pad_maximum_fusion.1), channel_id=1, source_target_pairs={{0,2},{1,5},{4,0},{5,9},{8,4},{9,13},{12,8},{13,15},{14,12},{15,11... | collective-permute-start | bytes 1572872 | tf_op jit(solution)/shard_map/ppermute | solution.py:170
  76.0 12.0 %collective-permute-start.22 = (bf16[128,2048]{1,0:T(8,128)(2,1)S(1)}, bf16[128,2048]{1,0:T(8,128)(2,1)S(1)}, u32[]{:S(2)}, u32[]{:S(2)}) collective-permute-start(bf16[128,2048]{1,0:T(8,128)(2,1)S(1)} %pad_maximum_fusion.2), channel_id=1, source_target_pairs={{0,2},{1,5},{4,0},{5,9},{8,4},{9,13},{12,8},{13,15},{14,12},{15,11... | collective-permute-start | bytes 1572872 | tf_op jit(solution)/shard_map/ppermute | solution.py:170
  78.0 12.5 %collective-permute-start.23 = (bf16[136,2048]{1,0:T(8,128)(2,1)S(1)}, bf16[136,2048]{1,0:T(8,128)(2,1)S(1)}, u32[]{:S(2)}, u32[]{:S(2)}) collective-permute-start(bf16[136,2048]{1,0:T(8,128)(2,1)S(1)} %pad_maximum_fusion.refs_0_), channel_id=1, source_target_pairs={{0,1},{1,0},{4,5},{5,4},{8,9},{9,8},{12,13},{13,12},{14,15},{15,14... | collective-permute-start | bytes 1671176 | tf_op jit(solution)/shard_map/ppermute | solution.py:170
  80.7 15.2 %collective-permute-start.28 = (bf16[128,2048]{1,0:T(8,128)(2,1)S(1)}, bf16[128,2048]{1,0:T(8,128)(2,1)S(1)}, u32[]{:S(2)}, u32[]{:S(2)}) collective-permute-start(bf16[128,2048]{1,0:T(8,128)(2,1)S(1)} %get-tuple-element.62), channel_id=1, source_target_pairs={{0,1},{1,0},{4,5},{5,4},{8,9},{9,8},{12,13},{13,12},{14,15},{15,14... | collective-permute-start | bytes 1572872 | tf_op jit(solution)/shard_map/ppermute | solution.py:170
  82.6 11.0 %collective-permute-start.26 = (bf16[128,2048]{1,0:T(8,128)(2,1)S(1)}, bf16[128,2048]{1,0:T(8,128)(2,1)S(1)}, u32[]{:S(2)}, u32[]{:S(2)}) collective-permute-start(bf16[128,2048]{1,0:T(8,128)(2,1)S(1)} %add_convert_fusion.4), channel_id=1, source_target_pairs={{0,2},{1,5},{4,0},{5,9},{8,4},{9,13},{12,8},{13,15},{14,12},{15,11... | collective-permute-start | bytes 1572872 | tf_op jit(solution)/shard_map/ppermute | solution.py:170
  88.2 11.0 %collective-permute-start.29 = (bf16[128,2048]{1,0:T(8,128)(2,1)S(1)}, bf16[128,2048]{1,0:T(8,128)(2,1)S(1)}, u32[]{:S(2)}, u32[]{:S(2)}) collective-permute-start(bf16[128,2048]{1,0:T(8,128)(2,1)S(1)} %add_convert_fusion.3), channel_id=1, source_target_pairs={{0,2},{1,5},{4,0},{5,9},{8,4},{9,13},{12,8},{13,15},{14,12},{15,11... | collective-permute-start | bytes 1572872 | tf_op jit(solution)/shard_map/ppermute | solution.py:170
  93.2 6.6 %collective-permute-start.24 = (bf16[128,2048]{1,0:T(8,128)(2,1)S(1)}, bf16[128,2048]{1,0:T(8,128)(2,1)S(1)}, u32[]{:S(2)}, u32[]{:S(2)}) collective-permute-start(bf16[128,2048]{1,0:T(8,128)(2,1)S(1)} %get-tuple-element.58), channel_id=1, source_target_pairs={{0,1},{1,0},{4,5},{5,4},{8,9},{9,8},{12,13},{13,12},{14,15},{15,14... | collective-permute-start | bytes 1572872 | tf_op jit(solution)/shard_map/ppermute | solution.py:170
  93.8 11.0 %collective-permute-start.27 = (bf16[128,2048]{1,0:T(8,128)(2,1)S(1)}, bf16[128,2048]{1,0:T(8,128)(2,1)S(1)}, u32[]{:S(2)}, u32[]{:S(2)}) collective-permute-start(bf16[128,2048]{1,0:T(8,128)(2,1)S(1)} %add_convert_fusion.2), channel_id=1, source_target_pairs={{0,2},{1,5},{4,0},{5,9},{8,4},{9,13},{12,8},{13,15},{14,12},{15,11... | collective-permute-start | bytes 1572872 | tf_op jit(solution)/shard_map/ppermute | solution.py:170
  99.5 10.5 %collective-permute-start.30 = (bf16[128,2048]{1,0:T(8,128)(2,1)S(1)}, bf16[128,2048]{1,0:T(8,128)(2,1)S(1)}, u32[]{:S(2)}, u32[]{:S(2)}) collective-permute-start(bf16[128,2048]{1,0:T(8,128)(2,1)S(1)} %add_convert_fusion.1), channel_id=1, source_target_pairs={{0,3},{1,4},{4,1},{5,8},{8,5},{9,12},{12,9},{13,14},{14,13},{15,10... | collective-permute-start | bytes 1572872 | tf_op jit(solution)/shard_map/ppermute | solution.py:170
  (8 other events, 27.2 us)

commit v9 on v8

--- a/solution.py
+++ b/solution.py
@@ -166,8 +166,9 @@
 
     forth, back, across, cores = moved(1), moved(-1), moved(-1, True), moved(0, True)
 
-    def send(value, pairs):
-        return lax.ppermute(value, "blk", pairs)
+    def send(value, pairs, name):
+        with jax.named_scope(name):
+            return lax.ppermute(value, "blk", pairs)
 
     def total(*terms):
         return sum(term.astype(jnp.float32) for term in terms)
@@ -185,43 +186,66 @@
     gates = jnp.concatenate([high, weight - high], axis=1).astype(jnp.bfloat16)
     packed = jnp.concatenate([tokens, jnp.pad(gates, ((0, 0), (0, tokens.shape[1] - 2 * LANES)))])
 
-    ring = [send(packed, forth), send(packed, across)]
+    ring = [send(packed, forth, "ring_1_0"), send(packed, across, "ring_1_1")]
+
+    def expert_rows(step, c, inputs, **options):
+        with jax.named_scope(f"expert_{step}_{c}"):
+            kept, given = half_expert([0, 0], inputs, expert, near, **options)
+        results[step, c] = kept, given
+        if step == far - 1 or (step, c) == (1, 1):
+            give(step, c)
+        return kept
+
+    def give(step, c, *earlier):
+        kept, given = results[step, c]
+        results[step, c] = kept, send(after(given, *earlier) if earlier else given, cores, f"give_{step}_{c}")
+
     results = {}
-    near, delayed = None, None
+    with jax.named_scope("expert_0"):
+        own, given, *near = half_expert([0, 0], [packed, send(packed, cores, "swap_0")], expert, [gate_up, down_proj], load=True)
+    results[0, 0] = own, given
+    ring[0] = after(ring[0], own)
+    delayed = None
+    earlier = ring[1]
     for step in range(1, far):
-        swapped = [send(block, cores) for block in ring[: 1 if step == 1 else 2]]
-        blocks = ring
+        swapped = [send(block, cores, f"swap_{step}_{c}") for c, block in enumerate(ring[: 1 if step == 1 else 2])]
+        blocks = list(ring)
         if step < far - 1:
-            ring = [send(block, forth) for block in ring]
+            ring = [send(block, forth, f"ring_{step + 1}_{c}") for c, block in enumerate(ring)]
         else:
-            ring = [send(jnp.concatenate([ring[0][:half], ring[0][rows:]]), forth), send(ring[1][half:], forth)]
-        if step == 1:
-            delayed = blocks[1]
-            kept, given, *near = half_expert([0, 0], [blocks[0], swapped[0]], expert, [gate_up, down_proj], load=True)
-            results[1, 0] = kept, send(given, cores)
-        else:
-            kept, given = half_expert([0] * 4, blocks + swapped, expert, near)
-            given = send(given, cores)
-            for c in chains:
-                results[step, c] = kept[c * rows : (c + 1) * rows], given[c * rows : (c + 1) * rows]
-        ring[0] = after(ring[0], kept)
-        if step == far - 1:
-            ring[1] = after(ring[1], kept)
-
-    (given,) = half_expert([0, half], ring, expert, near, split=1)
-    swapped = [send(block, cores) for block in ring]
+            ring[0] = send(jnp.concatenate([ring[0][:half], ring[0][rows:]]), forth, f"ring_{far}_0")
+            ring[1] = send(ring[1][half:], forth, f"ring_{far}_1")
+        for c in chains:
+            if (step, c) == (1, 1):
+                delayed = blocks[1]
+                earlier = ring[1]
+                continue
+            if (step, c) == (far - 1, 1):
+                last = blocks[1], swapped[1]
+                continue
+            kept = expert_rows(step, c, [after(blocks[c], earlier), swapped[c]])
+            ring[c] = after(ring[c], kept)
+            earlier = ring[c]
+
+    with jax.named_scope("expert_far_ring"):
+        (given,) = half_expert([0, half], ring, expert, near, split=1)
+    swapped = [send(block, cores, f"swap_{far}_{c}") for c, block in enumerate(ring)]
     swapped[0] = after(swapped[0], given)
-    given = send(given, cores)
-    (kept,) = half_expert([0, half], swapped, expert, near, split=1)
+    given = send(given, cores, "give_far")
+    with jax.named_scope("expert_far_swapped"):
+        (kept,) = half_expert([0, half], swapped, expert, near, split=1)
 
     first, second = slice(0, half), slice(half, rows)
     late = []
     earlier = kept
-    for part in (second, first):
+    for c, part in enumerate((second, first)):
         earlier = rounded(total(after(kept[part], earlier), given[part]))
-        late.append(send(earlier, back))
-
+        late.append(send(earlier, back, f"back_{far}_{c}"))
+    earlier = expert_rows(far - 1, 1, [after(last[0], earlier), last[1]], cost=0.2)
     late_value, sums = earlier, []
+    for step in range(far - 2, 1, -1):
+        for c in chains:
+            give(step, c, late_value)
     for c in chains:
         mine, theirs = results[far - 1, c]
         value = total(after(mine, earlier), theirs)
@@ -230,25 +254,21 @@
         else:
             value = jnp.concatenate([value[first] + total(late[c]), value[second]])
         earlier = rounded(value)
-        sums.append(send(earlier, back))
-    swapped = send(after(delayed, late_value), cores)
-    kept, given = half_expert([0, 0], [after(delayed, earlier), swapped], expert, near)
-    results[1, 1] = kept, send(given, cores)
-    other = send(after(packed, earlier), cores)
-    earlier = kept
+        sums.append(send(earlier, back, f"back_{far - 1}_{c}"))
+    swapped = send(after(delayed, late_value), cores, "swap_1_1")
+    give(1, 0, earlier)
+    give(0, 0, earlier)
+    earlier = expert_rows(1, 1, [after(delayed, earlier), swapped])
     for step in range(far - 2, 1, -1):
         for c in chains:
             mine, theirs = results[step, c]
             earlier = rounded(total(after(mine, earlier), theirs, sums[c]))
-            sums[c] = send(earlier, back)
-    kept, given = half_expert([0, 0], [after(packed, earlier), other], expert, near)
-    given = send(given, cores)
-    earlier = kept
+            sums[c] = send(earlier, back, f"back_{step}_{c}")
     for c, pairs in zip(chains, (back, across)):
         mine, theirs = results[1, c]
         earlier = rounded(total(after(mine, earlier), theirs, sums[c]))
-        sums[c] = send(earlier, pairs)
-    return rounded(total(summed(kept, given, sums[0]), sums[1]))
+        sums[c] = send(earlier, pairs, f"back_1_{c}")
+    return rounded(total(summed(*results[0, 0], sums[0]), sums[1]))
 
 
 def solution(mesh):

time: 111 us -> 105 us (0.946)
  waiting for transfers between devices: 46.2 us -> 39.9 us
    ppermute x31 -> x33, waiting for transfers between devices: 46.2 us -> 39.9 us  [send(): return lax.ppermute(value, 'blk', pairs)]
    pallas_call x7 -> x9, Pallas kernels: 26 us -> 26.4 us  [half_expert(): pl.pallas_call(functools.partial(half_expert_kernel, tuple(first_tokens),...]
    ppermute x31 -> x33, starting transfers between devices: 31.8 us -> 32 us  [send(): return lax.ppermute(value, 'blk', pairs)]
  transfers between devices with their start and end apart: 31 -> 33, of which waited for: 14 -> 13; matrix products, arithmetic and copies ran while one was open for 2% -> 2% of each run, Pallas kernels for 24% -> 25%
where the time goes in v9:
time: 105 us
  waiting for transfers between devices  39.9 us (38%)
  starting transfers between devices  32 us (30%)
  Pallas kernels  26.5 us (25%)
  other arithmetic  4.24 us (4%)
  local copies, waits for them, and re-layouts  2.03 us (2%)
    ppermute x33, waiting for transfers between devices, send(): return lax.ppermute(value, 'blk', pairs)  39.9 us
    ppermute x33, starting transfers between devices, send(): return lax.ppermute(value, 'blk', pairs)  32 us
    pallas_call x9, Pallas kernels, half_expert(): pl.pallas_call(functools.partial(half_expert_kernel, tuple(first_tokens),...  26.4 us
  transfers between devices with their start and end apart: 33, of which 13 were waited for; matrix products, arithmetic and copies ran while one was open for 2% of the time, Pallas kernels for 25%

profile of v9, /device:TPU:0, one launch (start us, length us, event | category | flops | bytes accessed | tf_op | source)
XLA Modules:
  0.0 105.0 jit_solution(14070690198399721519)
XLA Ops:
  2.3 2.6 %collective-permute-start.4 = (bf16[136,2048]{1,0:T(8,128)(2,1)S(1)}, bf16[136,2048]{1,0:T(8,128)(2,1)S(1)}, u32[]{:S(2)}, u32[]{:S(2)}) collective-permute-start(bf16[136,2048]{1,0:T(8,128)(2,1)S(1)} %pad_maximum_fusion.refs_0_), channel_id=1, source_target_pairs={{0,4},{1,3},{4,8},{5,1},{8,12},{9,5},{12,14},{13,9},{14,10},{15,13... | collective-permute-start | bytes 1671176 | tf_op jit(solution)/shard_map/ring_1_0/ppermute | solution.py:171
  8.1 4.9 %expert_0.1 = (bf16[128,2048]{1,0:T(8,128)(2,1)S(1)}, bf16[128,2048]{1,0:T(8,128)(2,1)S(1)}, bf16[2,768,2048]{2,1,0:T(8,128)(2,1)S(1)}, bf16[768,2048]{1,0:T(8,128)(2,1)S(1)}) custom-call(s32[1]{0:T(128)} %bitcast.expert_ref, bf16[136,2048]{1,0:T(8,128)(2,1)S(1)} %pad_maximum_fusion.refs_0_, bf16[136,2048]{1,0:T(8,128)(2,1)S(1)} %collective-permute-done.refs_1_, ...), custom_call_target="tpu_custom_call" | custom-call | flops 805306368 | bytes 3145728 | tf_op jit(solution)/shard_map/expert_0/pallas_call | solution.py:119
  13.1 3.9 %collective-permute-done.4.refs_0_ = bf16[136,2048]{1,0:T(8,128)(2,1)S(1)} collective-permute-done((bf16[136,2048]{1,0:T(8,128)(2,1)S(1)}, bf16[136,2048]{1,0:T(8,128)(2,1)S(1)}, u32[]{:S(2)}, u32[]{:S(2)}) %collective-permute-start.4) | collective-permute-done | bytes 557088 | tf_op jit(solution)/shard_map/ring_1_0/ppermute | solution.py:171
  17.0 2.5 %collective-permute-start.5 = (bf16[136,2048]{1,0:T(8,128)(2,1)S(1)}, bf16[136,2048]{1,0:T(8,128)(2,1)S(1)}, u32[]{:S(2)}, u32[]{:S(2)}) collective-permute-start(bf16[136,2048]{1,0:T(8,128)(2,1)S(1)} %collective-permute-done.4.refs_0_), channel_id=1, source_target_pairs={{0,4},{1,3},{4,8},{5,1},{8,12},{9,5},{12,14},{13,9},{14,10},{15,13... | collective-permute-start | bytes 1671176 | tf_op jit(solution)/shard_map/ring_2_0/ppermute | solution.py:171
  21.1 2.7 %expert_1_0.1 = (bf16[128,2048]{1,0:T(8,128)(2,1)S(1)}, bf16[128,2048]{1,0:T(8,128)(2,1)S(1)}) custom-call(s32[1]{0:T(128)} %bitcast.expert_ref, bf16[136,2048]{1,0:T(8,128)(2,1)S(1)} %collective-permute-done.4.refs_0_, bf16[136,2048]{1,0:T(8,128)(2,1)S(1)} %collective-permute-done.6.refs_1_, bf16[2,768,2048]{2,1,0:T(8,128)(2,1)S(1)} %get-tuple-element.50.refs_2_, ...), custom_call_target="tpu_custom_call" | custom-call | flops 805306368 | bytes 3145728 | tf_op jit(solution)/shard_map/expert_1_0/pallas_call | solution.py:119
  23.7 3.6 %collective-permute-done.5.refs_0_ = bf16[136,2048]{1,0:T(8,128)(2,1)S(1)} collective-permute-done((bf16[136,2048]{1,0:T(8,128)(2,1)S(1)}, bf16[136,2048]{1,0:T(8,128)(2,1)S(1)}, u32[]{:S(2)}, u32[]{:S(2)}) %collective-permute-start.5) | collective-permute-done | bytes 557088 | tf_op jit(solution)/shard_map/ring_2_0/ppermute | solution.py:171
  29.0 4.3 %collective-permute-done.2.refs_0_ = bf16[136,2048]{1,0:T(8,128)(2,1)S(1)} collective-permute-done((bf16[136,2048]{1,0:T(8,128)(2,1)S(1)}, bf16[136,2048]{1,0:T(8,128)(2,1)S(1)}, u32[]{:S(2)}, u32[]{:S(2)}) %collective-permute-start.2) | collective-permute-done | bytes 557088 | tf_op jit(solution)/shard_map/ring_2_1/ppermute | solution.py:171
  35.0 2.7 %expert_2_0.1 = (bf16[128,2048]{1,0:T(8,128)(2,1)S(1)}, bf16[128,2048]{1,0:T(8,128)(2,1)S(1)}) custom-call(s32[1]{0:T(128)} %bitcast.expert_ref, bf16[136,2048]{1,0:T(8,128)(2,1)S(1)} %collective-permute-done.5.refs_0_, bf16[136,2048]{1,0:T(8,128)(2,1)S(1)} %collective-permute-done.8.refs_1_, bf16[2,768,2048]{2,1,0:T(8,128)(2,1)S(1)} %get-tuple-element.50.refs_2_, ...), custom_call_target="tpu_custom_call" | custom-call | flops 805306368 | bytes 3145728 | tf_op jit(solution)/shard_map/expert_2_0/pallas_call | solution.py:119
  41.0 2.7 %expert_2_1.1 = (bf16[128,2048]{1,0:T(8,128)(2,1)S(1)}, bf16[128,2048]{1,0:T(8,128)(2,1)S(1)}) custom-call(s32[1]{0:T(128)} %bitcast.expert_ref, bf16[136,2048]{1,0:T(8,128)(2,1)S(1)} %collective-permute-done.2.refs_0_, bf16[136,2048]{1,0:T(8,128)(2,1)S(1)} %collective-permute-done.9.refs_1_, bf16[2,768,2048]{2,1,0:T(8,128)(2,1)S(1)} %get-tuple-element.50.refs_2_, ...), custom_call_target="tpu_custom_call" | custom-call | flops 805306368 | bytes 3145728 | tf_op jit(solution)/shard_map/expert_2_1/pallas_call | solution.py:119
  47.2 2.7 %expert_3_0.1 = (bf16[128,2048]{1,0:T(8,128)(2,1)S(1)}, bf16[128,2048]{1,0:T(8,128)(2,1)S(1)}) custom-call(s32[1]{0:T(128)} %bitcast.expert_ref, bf16[136,2048]{1,0:T(8,128)(2,1)S(1)} %collective-permute-done.7.refs_0_, bf16[136,2048]{1,0:T(8,128)(2,1)S(1)} %collective-permute-done.11.refs_1_, bf16[2,768,2048]{2,1,0:T(8,128)(2,1)S(1)} %get-tuple-element.50.refs_2_, ...), custom_call_target="tpu_custom_call" | custom-call | flops 805306368 | bytes 3145728 | tf_op jit(solution)/shard_map/expert_3_0/pallas_call | solution.py:119
  49.9 2.3 %collective-permute-done.13.refs_1_ = bf16[72,2048]{1,0:T(8,128)(2,1)S(1)} collective-permute-done((bf16[72,2048]{1,0:T(8,128)(2,1)S(1)}, bf16[72,2048]{1,0:T(8,128)(2,1)S(1)}, u32[]{:S(2)}, u32[]{:S(2)}) %collective-permute-start.13) | collective-permute-done | bytes 294944 | tf_op jit(solution)/shard_map/ring_4_1/ppermute | solution.py:171
  52.3 2.7 %expert_far_ring.1 = bf16[128,2048]{1,0:T(8,128)(2,1)S(1)} custom-call(s32[1]{0:T(128)} %bitcast.expert_ref, bf16[72,2048]{1,0:T(8,128)(2,1)S(1)} %collective-permute-done.10.refs_0_, bf16[72,2048]{1,0:T(8,128)(2,1)S(1)} %collective-permute-done.13.refs_1_, bf16[2,768,2048]{2,1,0:T(8,128)(2,1)S(1)} %get-tuple-element.50.refs_2_, ...), custom_call_target="tpu_custom_call" | custom-call | flops 402653184 | bytes 3145728 | tf_op jit(solution)/shard_map/expert_far_ring/pallas_call | solution.py:119
  56.1 2.7 %expert_far_swapped.1 = bf16[128,2048]{1,0:T(8,128)(2,1)S(1)} custom-call(s32[1]{0:T(128)} %bitcast.expert_ref, bf16[72,2048]{1,0:T(8,128)(2,1)S(1)} %collective-permute-done.12.refs_0_, bf16[72,2048]{1,0:T(8,128)(2,1)S(1)} %collective-permute-done.14.refs_1_, bf16[2,768,2048]{2,1,0:T(8,128)(2,1)S(1)} %get-tuple-element.50.refs_2_, ...), custom_call_target="tpu_custom_call" | custom-call | flops 402653184 | bytes 3145728 | tf_op jit(solution)/shard_map/expert_far_swapped/pallas_call | solution.py:119
  58.9 2.1 %collective-permute-start.18 = (bf16[64,2048]{1,0:T(8,128)(2,1)S(1)}, bf16[64,2048]{1,0:T(8,128)(2,1)S(1)}, u32[]{:S(2)}, u32[]{:S(2)}) collective-permute-start(bf16[64,2048]{1,0:T(8,128)(2,1)S(1)} %add_convert_fusion.6), channel_id=1, source_target_pairs={{0,2},{1,5},{4,0},{5,9},{8,4},{9,13},{12,8},{13,15},{14,12},{15,11... | collective-permute-start | bytes 786440 | tf_op jit(solution)/shard_map/back_4_0/ppermute | solution.py:171
  62.7 2.7 %expert_3_1.1 = (bf16[128,2048]{1,0:T(8,128)(2,1)S(1)}, bf16[128,2048]{1,0:T(8,128)(2,1)S(1)}) custom-call(s32[1]{0:T(128)} %bitcast.expert_ref, bf16[136,2048]{1,0:T(8,128)(2,1)S(1)} %collective-permute-done.3.refs_0_, bf16[136,2048]{1,0:T(8,128)(2,1)S(1)} %collective-permute-done.16.refs_1_, bf16[2,768,2048]{2,1,0:T(8,128)(2,1)S(1)} %get-tuple-element.50.refs_2_, ...), custom_call_target="tpu_custom_call" | custom-call | flops 80530640 | bytes 314572 | tf_op jit(solution)/shard_map/expert_3_1/pallas_call | solution.py:119
  71.2 2.7 %expert_1_1.1 = (bf16[128,2048]{1,0:T(8,128)(2,1)S(1)}, bf16[128,2048]{1,0:T(8,128)(2,1)S(1)}) custom-call(s32[1]{0:T(128)} %bitcast.expert_ref, bf16[136,2048]{1,0:T(8,128)(2,1)S(1)} %collective-permute-done.1.refs_0_, bf16[136,2048]{1,0:T(8,128)(2,1)S(1)} %collective-permute-done.22.refs_1_, bf16[2,768,2048]{2,1,0:T(8,128)(2,1)S(1)} %get-tuple-element.50.refs_2_, ...), custom_call_target="tpu_custom_call" | custom-call | flops 805306368 | bytes 3145728 | tf_op jit(solution)/shard_map/expert_1_1/pallas_call | solution.py:119
  73.9 2.6 %collective-permute-done.24 = bf16[128,2048]{1,0:T(8,128)(2,1)S(1)} collective-permute-done((bf16[128,2048]{1,0:T(8,128)(2,1)S(1)}, bf16[128,2048]{1,0:T(8,128)(2,1)S(1)}, u32[]{:S(2)}, u32[]{:S(2)}) %collective-permute-start.24) | collective-permute-done | bytes 524320 | tf_op jit(solution)/shard_map/back_3_0/ppermute | solution.py:171
  76.7 2.0 %collective-permute-start.28 = (bf16[128,2048]{1,0:T(8,128)(2,1)S(1)}, bf16[128,2048]{1,0:T(8,128)(2,1)S(1)}, u32[]{:S(2)}, u32[]{:S(2)}) collective-permute-start(bf16[128,2048]{1,0:T(8,128)(2,1)S(1)} %add_convert_fusion.4), channel_id=1, source_target_pairs={{0,2},{1,5},{4,0},{5,9},{8,4},{9,13},{12,8},{13,15},{14,12},{15,11... | collective-permute-start | bytes 1572872 | tf_op jit(solution)/shard_map/back_2_0/ppermute | solution.py:171
  78.8 3.3 %collective-permute-done.26 = bf16[128,2048]{1,0:T(8,128)(2,1)S(1)} collective-permute-done((bf16[128,2048]{1,0:T(8,128)(2,1)S(1)}, bf16[128,2048]{1,0:T(8,128)(2,1)S(1)}, u32[]{:S(2)}, u32[]{:S(2)}) %collective-permute-start.26) | collective-permute-done | bytes 524320 | tf_op jit(solution)/shard_map/back_3_1/ppermute | solution.py:171
  84.4 3.3 %collective-permute-done.28 = bf16[128,2048]{1,0:T(8,128)(2,1)S(1)} collective-permute-done((bf16[128,2048]{1,0:T(8,128)(2,1)S(1)}, bf16[128,2048]{1,0:T(8,128)(2,1)S(1)}, u32[]{:S(2)}, u32[]{:S(2)}) %collective-permute-start.28) | collective-permute-done | bytes 524320 | tf_op jit(solution)/shard_map/back_2_0/ppermute | solution.py:171
  88.0 2.0 %collective-permute-start.29 = (bf16[128,2048]{1,0:T(8,128)(2,1)S(1)}, bf16[128,2048]{1,0:T(8,128)(2,1)S(1)}, u32[]{:S(2)}, u32[]{:S(2)}) collective-permute-start(bf16[128,2048]{1,0:T(8,128)(2,1)S(1)} %add_convert_fusion.2), channel_id=1, source_target_pairs={{0,2},{1,5},{4,0},{5,9},{8,4},{9,13},{12,8},{13,15},{14,12},{15,11... | collective-permute-start | bytes 1572872 | tf_op jit(solution)/shard_map/back_1_0/ppermute | solution.py:171
  90.0 3.3 %collective-permute-done.31 = bf16[128,2048]{1,0:T(8,128)(2,1)S(1)} collective-permute-done((bf16[128,2048]{1,0:T(8,128)(2,1)S(1)}, bf16[128,2048]{1,0:T(8,128)(2,1)S(1)}, u32[]{:S(2)}, u32[]{:S(2)}) %collective-permute-start.31) | collective-permute-done | bytes 524320 | tf_op jit(solution)/shard_map/back_2_1/ppermute | solution.py:171
  94.5 4.4 %collective-permute-done.29.refs_2_ = bf16[128,2048]{1,0:T(8,128)(2,1)S(1)} collective-permute-done((bf16[128,2048]{1,0:T(8,128)(2,1)S(1)}, bf16[128,2048]{1,0:T(8,128)(2,1)S(1)}, u32[]{:S(2)}, u32[]{:S(2)}) %collective-permute-start.29) | collective-permute-done | bytes 524320 | tf_op jit(solution)/shard_map/back_1_0/ppermute | solution.py:171
  99.1 5.0 %collective-permute-done.32 = bf16[128,2048]{1,0:T(8,128)(2,1)S(1)} collective-permute-done((bf16[128,2048]{1,0:T(8,128)(2,1)S(1)}, bf16[128,2048]{1,0:T(8,128)(2,1)S(1)}, u32[]{:S(2)}, u32[]{:S(2)}) %collective-permute-start.32) | collective-permute-done | bytes 524320 | tf_op jit(solution)/shard_map/back_1_1/ppermute | solution.py:171
  (78 shorter events, 31.0 us)
Async XLA Ops:
  2.3 14.7 %collective-permute-start.4 = (bf16[136,2048]{1,0:T(8,128)(2,1)S(1)}, bf16[136,2048]{1,0:T(8,128)(2,1)S(1)}, u32[]{:S(2)}, u32[]{:S(2)}) collective-permute-start(bf16[136,2048]{1,0:T(8,128)(2,1)S(1)} %pad_maximum_fusion.refs_0_), channel_id=1, source_target_pairs={{0,4},{1,3},{4,8},{5,1},{8,12},{9,5},{12,14},{13,9},{14,10},{15,13... | collective-permute-start | bytes 1671176 | tf_op jit(solution)/shard_map/ring_1_0/ppermute | solution.py:171
  5.0 14.5 %collective-permute-start.1 = (bf16[136,2048]{1,0:T(8,128)(2,1)S(1)}, bf16[136,2048]{1,0:T(8,128)(2,1)S(1)}, u32[]{:S(2)}, u32[]{:S(2)}) collective-permute-start(bf16[136,2048]{1,0:T(8,128)(2,1)S(1)} %pad_maximum_fusion.refs_0_), channel_id=1, source_target_pairs={{0,3},{1,4},{4,1},{5,8},{8,5},{9,12},{12,9},{13,14},{14,13},{15,10... | collective-permute-start | bytes 1671176 | tf_op jit(solution)/shard_map/ring_1_1/ppermute | solution.py:171
  17.0 10.4 %collective-permute-start.5 = (bf16[136,2048]{1,0:T(8,128)(2,1)S(1)}, bf16[136,2048]{1,0:T(8,128)(2,1)S(1)}, u32[]{:S(2)}, u32[]{:S(2)}) collective-permute-start(bf16[136,2048]{1,0:T(8,128)(2,1)S(1)} %collective-permute-done.4.refs_0_), channel_id=1, source_target_pairs={{0,4},{1,3},{4,8},{5,1},{8,12},{9,5},{12,14},{13,9},{14,10},{15,13... | collective-permute-start | bytes 1671176 | tf_op jit(solution)/shard_map/ring_2_0/ppermute | solution.py:171
  19.5 13.9 %collective-permute-start.2 = (bf16[136,2048]{1,0:T(8,128)(2,1)S(1)}, bf16[136,2048]{1,0:T(8,128)(2,1)S(1)}, u32[]{:S(2)}, u32[]{:S(2)}) collective-permute-start(bf16[136,2048]{1,0:T(8,128)(2,1)S(1)} %collective-permute-done.1.refs_0_), channel_id=1, source_target_pairs={{0,4},{1,3},{4,8},{5,1},{8,12},{9,5},{12,14},{13,9},{14,10},{15,13... | collective-permute-start | bytes 1671176 | tf_op jit(solution)/shard_map/ring_2_1/ppermute | solution.py:171
  27.4 7.6 %collective-permute-start.8 = (bf16[136,2048]{1,0:T(8,128)(2,1)S(1)}, bf16[136,2048]{1,0:T(8,128)(2,1)S(1)}, u32[]{:S(2)}, u32[]{:S(2)}) collective-permute-start(bf16[136,2048]{1,0:T(8,128)(2,1)S(1)} %collective-permute-done.5.refs_0_), channel_id=1, source_target_pairs={{0,1},{1,0},{4,5},{5,4},{8,9},{9,8},{12,13},{13,12},{14,15},{15,14... | collective-permute-start | bytes 1671176 | tf_op jit(solution)/shard_map/swap_2_0/ppermute | solution.py:171
  27.4 11.9 %collective-permute-start.7 = (bf16[136,2048]{1,0:T(8,128)(2,1)S(1)}, bf16[136,2048]{1,0:T(8,128)(2,1)S(1)}, u32[]{:S(2)}, u32[]{:S(2)}) collective-permute-start(bf16[136,2048]{1,0:T(8,128)(2,1)S(1)} %collective-permute-done.5.refs_0_), channel_id=1, source_target_pairs={{0,4},{1,3},{4,8},{5,1},{8,12},{9,5},{12,14},{13,9},{14,10},{15,13... | collective-permute-start | bytes 1671176 | tf_op jit(solution)/shard_map/ring_3_0/ppermute | solution.py:171
  33.3 7.7 %collective-permute-start.9 = (bf16[136,2048]{1,0:T(8,128)(2,1)S(1)}, bf16[136,2048]{1,0:T(8,128)(2,1)S(1)}, u32[]{:S(2)}, u32[]{:S(2)}) collective-permute-start(bf16[136,2048]{1,0:T(8,128)(2,1)S(1)} %collective-permute-done.2.refs_0_), channel_id=1, source_target_pairs={{0,1},{1,0},{4,5},{5,4},{8,9},{9,8},{12,13},{13,12},{14,15},{15,14... | collective-permute-start | bytes 1671176 | tf_op jit(solution)/shard_map/swap_2_1/ppermute | solution.py:171
  33.3 11.9 %collective-permute-start.3 = (bf16[136,2048]{1,0:T(8,128)(2,1)S(1)}, bf16[136,2048]{1,0:T(8,128)(2,1)S(1)}, u32[]{:S(2)}, u32[]{:S(2)}) collective-permute-start(bf16[136,2048]{1,0:T(8,128)(2,1)S(1)} %collective-permute-done.2.refs_0_), channel_id=1, source_target_pairs={{0,4},{1,3},{4,8},{5,1},{8,12},{9,5},{12,14},{13,9},{14,10},{15,13... | collective-permute-start | bytes 1671176 | tf_op jit(solution)/shard_map/ring_3_1/ppermute | solution.py:171
  39.3 7.9 %collective-permute-start.11 = (bf16[136,2048]{1,0:T(8,128)(2,1)S(1)}, bf16[136,2048]{1,0:T(8,128)(2,1)S(1)}, u32[]{:S(2)}, u32[]{:S(2)}) collective-permute-start(bf16[136,2048]{1,0:T(8,128)(2,1)S(1)} %collective-permute-done.7.refs_0_), channel_id=1, source_target_pairs={{0,1},{1,0},{4,5},{5,4},{8,9},{9,8},{12,13},{13,12},{14,15},{15,14... | collective-permute-start | bytes 1671176 | tf_op jit(solution)/shard_map/swap_3_0/ppermute | solution.py:171
  39.4 10.5 %collective-permute-start.10 = (bf16[72,2048]{1,0:T(8,128)(2,1)S(1)}, bf16[72,2048]{1,0:T(8,128)(2,1)S(1)}, u32[]{:S(2)}, u32[]{:S(2)}) collective-permute-start(bf16[72,2048]{1,0:T(8,128)(2,1)S(1)} %pad_maximum_fusion.3), channel_id=1, source_target_pairs={{0,4},{1,3},{4,8},{5,1},{8,12},{9,5},{12,14},{13,9},{14,10},{15,13... | collective-permute-start | bytes 884744 | tf_op jit(solution)/shard_map/ring_4_0/ppermute | solution.py:171
  55.6 9.8 %collective-permute-start.17 = (bf16[128,2048]{1,0:T(8,128)(2,1)S(1)}, bf16[128,2048]{1,0:T(8,128)(2,1)S(1)}, u32[]{:S(2)}, u32[]{:S(2)}) collective-permute-start(bf16[128,2048]{1,0:T(8,128)(2,1)S(1)} %get-tuple-element.69), channel_id=1, source_target_pairs={{0,1},{1,0},{4,5},{5,4},{8,9},{9,8},{12,13},{13,12},{14,15},{15,14... | collective-permute-start | bytes 1572872 | tf_op jit(solution)/shard_map/give_3_0/ppermute | solution.py:171
  58.9 7.4 %collective-permute-start.18 = (bf16[64,2048]{1,0:T(8,128)(2,1)S(1)}, bf16[64,2048]{1,0:T(8,128)(2,1)S(1)}, u32[]{:S(2)}, u32[]{:S(2)}) collective-permute-start(bf16[64,2048]{1,0:T(8,128)(2,1)S(1)} %add_convert_fusion.6), channel_id=1, source_target_pairs={{0,2},{1,5},{4,0},{5,9},{8,4},{9,13},{12,8},{13,15},{14,12},{15,11... | collective-permute-start | bytes 786440 | tf_op jit(solution)/shard_map/back_4_0/ppermute | solution.py:171
  61.0 8.4 %collective-permute-start.20 = (bf16[64,2048]{1,0:T(8,128)(2,1)S(1)}, bf16[64,2048]{1,0:T(8,128)(2,1)S(1)}, u32[]{:S(2)}, u32[]{:S(2)}) collective-permute-start(bf16[64,2048]{1,0:T(8,128)(2,1)S(1)} %add_convert_fusion.5), channel_id=1, source_target_pairs={{0,2},{1,5},{4,0},{5,9},{8,4},{9,13},{12,8},{13,15},{14,12},{15,11... | collective-permute-start | bytes 786440 | tf_op jit(solution)/shard_map/back_4_1/ppermute | solution.py:171
  65.6 8.3 %collective-permute-start.23 = (bf16[128,2048]{1,0:T(8,128)(2,1)S(1)}, bf16[128,2048]{1,0:T(8,128)(2,1)S(1)}, u32[]{:S(2)}, u32[]{:S(2)}) collective-permute-start(bf16[128,2048]{1,0:T(8,128)(2,1)S(1)} %get-tuple-element.78), channel_id=1, source_target_pairs={{0,1},{1,0},{4,5},{5,4},{8,9},{9,8},{12,13},{13,12},{14,15},{15,14... | collective-permute-start | bytes 1572872 | tf_op jit(solution)/shard_map/give_2_0/ppermute | solution.py:171
  66.2 12.6 %collective-permute-start.25 = (bf16[128,2048]{1,0:T(8,128)(2,1)S(1)}, bf16[128,2048]{1,0:T(8,128)(2,1)S(1)}, u32[]{:S(2)}, u32[]{:S(2)}) collective-permute-start(bf16[128,2048]{1,0:T(8,128)(2,1)S(1)} %get-tuple-element.81), channel_id=1, source_target_pairs={{0,1},{1,0},{4,5},{5,4},{8,9},{9,8},{12,13},{13,12},{14,15},{15,14... | collective-permute-start | bytes 1572872 | tf_op jit(solution)/shard_map/give_2_1/ppermute | solution.py:171
  67.3 9.2 %collective-permute-start.24 = (bf16[128,2048]{1,0:T(8,128)(2,1)S(1)}, bf16[128,2048]{1,0:T(8,128)(2,1)S(1)}, u32[]{:S(2)}, u32[]{:S(2)}) collective-permute-start(bf16[128,2048]{1,0:T(8,128)(2,1)S(1)} %pad_maximum_fusion.1), channel_id=1, source_target_pairs={{0,2},{1,5},{4,0},{5,9},{8,4},{9,13},{12,8},{13,15},{14,12},{15,11... | collective-permute-start | bytes 1572872 | tf_op jit(solution)/shard_map/back_3_0/ppermute | solution.py:171
  69.6 12.5 %collective-permute-start.26 = (bf16[128,2048]{1,0:T(8,128)(2,1)S(1)}, bf16[128,2048]{1,0:T(8,128)(2,1)S(1)}, u32[]{:S(2)}, u32[]{:S(2)}) collective-permute-start(bf16[128,2048]{1,0:T(8,128)(2,1)S(1)} %pad_maximum_fusion.2), channel_id=1, source_target_pairs={{0,2},{1,5},{4,0},{5,9},{8,4},{9,13},{12,8},{13,15},{14,12},{15,11... | collective-permute-start | bytes 1572872 | tf_op jit(solution)/shard_map/back_3_1/ppermute | solution.py:171
  71.2 13.2 %collective-permute-start.27 = (bf16[128,2048]{1,0:T(8,128)(2,1)S(1)}, bf16[128,2048]{1,0:T(8,128)(2,1)S(1)}, u32[]{:S(2)}, u32[]{:S(2)}) collective-permute-start(bf16[128,2048]{1,0:T(8,128)(2,1)S(1)} %get-tuple-element.84), channel_id=1, source_target_pairs={{0,1},{1,0},{4,5},{5,4},{8,9},{9,8},{12,13},{13,12},{14,15},{15,14... | collective-permute-start | bytes 1572872 | tf_op jit(solution)/shard_map/give_1_0/ppermute | solution.py:171
  76.7 11.0 %collective-permute-start.28 = (bf16[128,2048]{1,0:T(8,128)(2,1)S(1)}, bf16[128,2048]{1,0:T(8,128)(2,1)S(1)}, u32[]{:S(2)}, u32[]{:S(2)}) collective-permute-start(bf16[128,2048]{1,0:T(8,128)(2,1)S(1)} %add_convert_fusion.4), channel_id=1, source_target_pairs={{0,2},{1,5},{4,0},{5,9},{8,4},{9,13},{12,8},{13,15},{14,12},{15,11... | collective-permute-start | bytes 1572872 | tf_op jit(solution)/shard_map/back_2_0/ppermute | solution.py:171
  78.8 11.2 %collective-permute-start.30 = (bf16[128,2048]{1,0:T(8,128)(2,1)S(1)}, bf16[128,2048]{1,0:T(8,128)(2,1)S(1)}, u32[]{:S(2)}, u32[]{:S(2)}) collective-permute-start(bf16[128,2048]{1,0:T(8,128)(2,1)S(1)} %get-tuple-element.86), channel_id=1, source_target_pairs={{0,1},{1,0},{4,5},{5,4},{8,9},{9,8},{12,13},{13,12},{14,15},{15,14... | collective-permute-start | bytes 1572872 | tf_op jit(solution)/shard_map/give_1_1/ppermute | solution.py:171
  82.4 11.0 %collective-permute-start.31 = (bf16[128,2048]{1,0:T(8,128)(2,1)S(1)}, bf16[128,2048]{1,0:T(8,128)(2,1)S(1)}, u32[]{:S(2)}, u32[]{:S(2)}) collective-permute-start(bf16[128,2048]{1,0:T(8,128)(2,1)S(1)} %add_convert_fusion.3), channel_id=1, source_target_pairs={{0,2},{1,5},{4,0},{5,9},{8,4},{9,13},{12,8},{13,15},{14,12},{15,11... | collective-permute-start | bytes 1572872 | tf_op jit(solution)/shard_map/back_2_1/ppermute | solution.py:171
  84.4 10.1 %collective-permute-start.21 = (bf16[128,2048]{1,0:T(8,128)(2,1)S(1)}, bf16[128,2048]{1,0:T(8,128)(2,1)S(1)}, u32[]{:S(2)}, u32[]{:S(2)}) collective-permute-start(bf16[128,2048]{1,0:T(8,128)(2,1)S(1)} %get-tuple-element.72), channel_id=1, source_target_pairs={{0,1},{1,0},{4,5},{5,4},{8,9},{9,8},{12,13},{13,12},{14,15},{15,14... | collective-permute-start | bytes 1572872 | tf_op jit(solution)/shard_map/give_0_0/ppermute | solution.py:171
  88.0 11.0 %collective-permute-start.29 = (bf16[128,2048]{1,0:T(8,128)(2,1)S(1)}, bf16[128,2048]{1,0:T(8,128)(2,1)S(1)}, u32[]{:S(2)}, u32[]{:S(2)}) collective-permute-start(bf16[128,2048]{1,0:T(8,128)(2,1)S(1)} %add_convert_fusion.2), channel_id=1, source_target_pairs={{0,2},{1,5},{4,0},{5,9},{8,4},{9,13},{12,8},{13,15},{14,12},{15,11... | collective-permute-start | bytes 1572872 | tf_op jit(solution)/shard_map/back_1_0/ppermute | solution.py:171
  93.6 10.5 %collective-permute-start.32 = (bf16[128,2048]{1,0:T(8,128)(2,1)S(1)}, bf16[128,2048]{1,0:T(8,128)(2,1)S(1)}, u32[]{:S(2)}, u32[]{:S(2)}) collective-permute-start(bf16[128,2048]{1,0:T(8,128)(2,1)S(1)} %add_convert_fusion.1), channel_id=1, source_target_pairs={{0,3},{1,4},{4,1},{5,8},{8,5},{9,12},{12,9},{13,14},{14,13},{15,10... | collective-permute-start | bytes 1572872 | tf_op jit(solution)/shard_map/back_1_1/ppermute | solution.py:171
  (10 other events, 45.4 us)

commit v10 on v9

--- a/solution.py
+++ b/solution.py
@@ -131,21 +131,24 @@
     )(expert, *blocks, *weights)
 
 
-def sum_kernel(*refs):
-    *terms, out = refs
-    out[...] = sum(term[...].astype(jnp.float32) for term in terms)
-
-
-def summed(*terms):
+def sum_kernel(low, *refs):
+    *terms, part, out = refs
+    value = sum(term[...].astype(jnp.float32) for term in terms)
+    out[...] = value.astype(out.dtype)
+    near = slice(low, low + part.shape[0])
+    out[near, :] = (value[near] + part[...].astype(jnp.float32)).astype(out.dtype)
+
+
+def summed(*terms, low=0, dtype=jnp.bfloat16, cost=1):
     whole = pl.BlockSpec(memory_space=pltpu.VMEM)
     size = terms[0].size
     return pl.pallas_call(
-        sum_kernel,
-        out_shape=jax.ShapeDtypeStruct(terms[0].shape, jnp.float32),
+        functools.partial(sum_kernel, low),
+        out_shape=jax.ShapeDtypeStruct(terms[0].shape, dtype),
         in_specs=[whole] * len(terms),
         out_specs=whole,
         compiler_params=pltpu.CompilerParams(vmem_limit_bytes=8 << 20),
-        cost_estimate=pl.CostEstimate(flops=size * 20000, bytes_accessed=size * 100, transcendentals=0),
+        cost_estimate=pl.CostEstimate(flops=size * cost, bytes_accessed=size, transcendentals=0),
     )(*terms)
 
 
@@ -186,7 +189,8 @@
     gates = jnp.concatenate([high, weight - high], axis=1).astype(jnp.bfloat16)
     packed = jnp.concatenate([tokens, jnp.pad(gates, ((0, 0), (0, tokens.shape[1] - 2 * LANES)))])
 
-    ring = [send(packed, forth, "ring_1_0"), send(packed, across, "ring_1_1")]
+    other = send(packed, cores, "swap_0")
+    ring = [send(packed, forth, "ring_1_0"), send(other, forth, "ring_1_1")]
 
     def expert_rows(step, c, inputs, **options):
         with jax.named_scope(f"expert_{step}_{c}"):
@@ -202,7 +206,7 @@
 
     results = {}
     with jax.named_scope("expert_0"):
-        own, given, *near = half_expert([0, 0], [packed, send(packed, cores, "swap_0")], expert, [gate_up, down_proj], load=True)
+        own, given, *near = half_expert([0, 0], [packed, other], expert, [gate_up, down_proj], load=True)
     results[0, 0] = own, given
     ring[0] = after(ring[0], own)
     delayed = None
@@ -242,10 +246,7 @@
         earlier = rounded(total(after(kept[part], earlier), given[part]))
         late.append(send(earlier, back, f"back_{far}_{c}"))
     earlier = expert_rows(far - 1, 1, [after(last[0], earlier), last[1]], cost=0.2)
-    late_value, sums = earlier, []
-    for step in range(far - 2, 1, -1):
-        for c in chains:
-            give(step, c, late_value)
+    sums = []
     for c in chains:
         mine, theirs = results[far - 1, c]
         value = total(after(mine, earlier), theirs)
@@ -255,7 +256,11 @@
             value = jnp.concatenate([value[first] + total(late[c]), value[second]])
         earlier = rounded(value)
         sums.append(send(earlier, back, f"back_{far - 1}_{c}"))
-    swapped = send(after(delayed, late_value), cores, "swap_1_1")
+        if c == 0:
+            swapped = send(after(delayed, earlier), cores, "swap_1_1")
+            for step in range(far - 2, 1, -1):
+                for c2 in chains:
+                    give(step, c2, earlier)
     give(1, 0, earlier)
     give(0, 0, earlier)
     earlier = expert_rows(1, 1, [after(delayed, earlier), swapped])
@@ -268,7 +273,7 @@
         mine, theirs = results[1, c]
         earlier = rounded(total(after(mine, earlier), theirs, sums[c]))
         sums[c] = send(earlier, pairs, f"back_1_{c}")
-    return rounded(total(summed(*results[0, 0], sums[0]), sums[1]))
+    return rounded(total(summed(*results[0, 0], sums[0], dtype=jnp.float32, cost=20000), sums[1]))
 
 
 def solution(mesh):

time: 105 us -> 101 us (0.962)
  waiting for transfers between devices: 39.9 us -> 34.5 us
    ppermute x33, waiting for transfers between devices: 39.9 us -> 34.5 us  [send(): return lax.ppermute(value, 'blk', pairs)]
  transfers between devices with their start and end apart: 33 -> 33, of which waited for: 13 -> 12; matrix products, arithmetic and copies ran while one was open for 2% -> 2% of each run, Pallas kernels for 25% -> 26%
where the time goes in v10:
time: 101 us; the launch traced here: 100 us
  waiting for transfers between devices  34.5 us (34%)
  starting transfers between devices  32.8 us (32%)
  Pallas kernels  26.5 us (26%)
  other arithmetic  4.26 us (4%)
  local copies, waits for them, and re-layouts  2.03 us (2%)
    ppermute x33, waiting for transfers between devices, send(): return lax.ppermute(value, 'blk', pairs)  34.5 us
    ppermute x33, starting transfers between devices, send(): return lax.ppermute(value, 'blk', pairs)  32.8 us
    pallas_call x9, Pallas kernels, half_expert(): pl.pallas_call(functools.partial(half_expert_kernel, tuple(first_tokens),...  26.4 us
  transfers between devices with their start and end apart: 33, of which 12 were waited for; matrix products, arithmetic and copies ran while one was open for 2% of the time, Pallas kernels for 26%

profile of v10, /device:TPU:0, one launch (start us, length us, event | category | flops | bytes accessed | tf_op | source)
XLA Modules:
  0.0 100.5 jit_solution(6162867565859856330)
XLA Ops:
  2.3 2.6 %collective-permute-start.4 = (bf16[136,2048]{1,0:T(8,128)(2,1)S(1)}, bf16[136,2048]{1,0:T(8,128)(2,1)S(1)}, u32[]{:S(2)}, u32[]{:S(2)}) collective-permute-start(bf16[136,2048]{1,0:T(8,128)(2,1)S(1)} %pad_maximum_fusion.refs_0_), channel_id=1, source_target_pairs={{0,4},{1,3},{4,8},{5,1},{8,12},{9,5},{12,14},{13,9},{14,10},{15,13... | collective-permute-start | bytes 1671176 | tf_op jit(solution)/shard_map/ring_1_0/ppermute | solution.py:174
  8.7 4.9 %expert_0.1 = (bf16[128,2048]{1,0:T(8,128)(2,1)S(1)}, bf16[128,2048]{1,0:T(8,128)(2,1)S(1)}, bf16[2,768,2048]{2,1,0:T(8,128)(2,1)S(1)}, bf16[768,2048]{1,0:T(8,128)(2,1)S(1)}) custom-call(s32[1]{0:T(128)} %bitcast.expert_ref, bf16[136,2048]{1,0:T(8,128)(2,1)S(1)} %pad_maximum_fusion.refs_0_, bf16[136,2048]{1,0:T(8,128)(2,1)S(1)} %collective-permute-done.refs_1_, ...), custom_call_target="tpu_custom_call" | custom-call | flops 805306368 | bytes 3145728 | tf_op jit(solution)/shard_map/expert_0/pallas_call | solution.py:119
  15.4 3.0 %collective-permute-done.1.refs_0_ = bf16[136,2048]{1,0:T(8,128)(2,1)S(1)} collective-permute-done((bf16[136,2048]{1,0:T(8,128)(2,1)S(1)}, bf16[136,2048]{1,0:T(8,128)(2,1)S(1)}, u32[]{:S(2)}, u32[]{:S(2)}) %collective-permute-start.1) | collective-permute-done | bytes 557088 | tf_op jit(solution)/shard_map/ring_1_1/ppermute | solution.py:174
  18.4 2.1 %collective-permute-start.2 = (bf16[136,2048]{1,0:T(8,128)(2,1)S(1)}, bf16[136,2048]{1,0:T(8,128)(2,1)S(1)}, u32[]{:S(2)}, u32[]{:S(2)}) collective-permute-start(bf16[136,2048]{1,0:T(8,128)(2,1)S(1)} %collective-permute-done.1.refs_0_), channel_id=1, source_target_pairs={{0,4},{1,3},{4,8},{5,1},{8,12},{9,5},{12,14},{13,9},{14,10},{15,13... | collective-permute-start | bytes 1671176 | tf_op jit(solution)/shard_map/ring_2_1/ppermute | solution.py:174
  20.5 2.7 %expert_1_0.1 = (bf16[128,2048]{1,0:T(8,128)(2,1)S(1)}, bf16[128,2048]{1,0:T(8,128)(2,1)S(1)}) custom-call(s32[1]{0:T(128)} %bitcast.expert_ref, bf16[136,2048]{1,0:T(8,128)(2,1)S(1)} %collective-permute-done.4.refs_0_, bf16[136,2048]{1,0:T(8,128)(2,1)S(1)} %collective-permute-done.6.refs_1_, bf16[2,768,2048]{2,1,0:T(8,128)(2,1)S(1)} %get-tuple-element.50.refs_2_, ...), custom_call_target="tpu_custom_call" | custom-call | flops 805306368 | bytes 3145728 | tf_op jit(solution)/shard_map/expert_1_0/pallas_call | solution.py:119
  24.4 2.1 %collective-permute-start.7 = (bf16[136,2048]{1,0:T(8,128)(2,1)S(1)}, bf16[136,2048]{1,0:T(8,128)(2,1)S(1)}, u32[]{:S(2)}, u32[]{:S(2)}) collective-permute-start(bf16[136,2048]{1,0:T(8,128)(2,1)S(1)} %collective-permute-done.5.refs_0_), channel_id=1, source_target_pairs={{0,4},{1,3},{4,8},{5,1},{8,12},{9,5},{12,14},{13,9},{14,10},{15,13... | collective-permute-start | bytes 1671176 | tf_op jit(solution)/shard_map/ring_3_0/ppermute | solution.py:174
  26.4 3.9 %collective-permute-done.2.refs_0_ = bf16[136,2048]{1,0:T(8,128)(2,1)S(1)} collective-permute-done((bf16[136,2048]{1,0:T(8,128)(2,1)S(1)}, bf16[136,2048]{1,0:T(8,128)(2,1)S(1)}, u32[]{:S(2)}, u32[]{:S(2)}) %collective-permute-start.2) | collective-permute-done | bytes 557088 | tf_op jit(solution)/shard_map/ring_2_1/ppermute | solution.py:174
  30.3 2.1 %collective-permute-start.3 = (bf16[136,2048]{1,0:T(8,128)(2,1)S(1)}, bf16[136,2048]{1,0:T(8,128)(2,1)S(1)}, u32[]{:S(2)}, u32[]{:S(2)}) collective-permute-start(bf16[136,2048]{1,0:T(8,128)(2,1)S(1)} %collective-permute-done.2.refs_0_), channel_id=1, source_target_pairs={{0,4},{1,3},{4,8},{5,1},{8,12},{9,5},{12,14},{13,9},{14,10},{15,13... | collective-permute-start | bytes 1671176 | tf_op jit(solution)/shard_map/ring_3_1/ppermute | solution.py:174
  32.4 2.7 %expert_2_0.1 = (bf16[128,2048]{1,0:T(8,128)(2,1)S(1)}, bf16[128,2048]{1,0:T(8,128)(2,1)S(1)}) custom-call(s32[1]{0:T(128)} %bitcast.expert_ref, bf16[136,2048]{1,0:T(8,128)(2,1)S(1)} %collective-permute-done.5.refs_0_, bf16[136,2048]{1,0:T(8,128)(2,1)S(1)} %collective-permute-done.8.refs_1_, bf16[2,768,2048]{2,1,0:T(8,128)(2,1)S(1)} %get-tuple-element.50.refs_2_, ...), custom_call_target="tpu_custom_call" | custom-call | flops 805306368 | bytes 3145728 | tf_op jit(solution)/shard_map/expert_2_0/pallas_call | solution.py:119
  36.4 2.1 %collective-permute-start.10 = (bf16[72,2048]{1,0:T(8,128)(2,1)S(1)}, bf16[72,2048]{1,0:T(8,128)(2,1)S(1)}, u32[]{:S(2)}, u32[]{:S(2)}) collective-permute-start(bf16[72,2048]{1,0:T(8,128)(2,1)S(1)} %pad_maximum_fusion.3), channel_id=1, source_target_pairs={{0,4},{1,3},{4,8},{5,1},{8,12},{9,5},{12,14},{13,9},{14,10},{15,13... | collective-permute-start | bytes 884744 | tf_op jit(solution)/shard_map/ring_4_0/ppermute | solution.py:174
  38.5 2.7 %expert_2_1.1 = (bf16[128,2048]{1,0:T(8,128)(2,1)S(1)}, bf16[128,2048]{1,0:T(8,128)(2,1)S(1)}) custom-call(s32[1]{0:T(128)} %bitcast.expert_ref, bf16[136,2048]{1,0:T(8,128)(2,1)S(1)} %collective-permute-done.2.refs_0_, bf16[136,2048]{1,0:T(8,128)(2,1)S(1)} %collective-permute-done.9.refs_1_, bf16[2,768,2048]{2,1,0:T(8,128)(2,1)S(1)} %get-tuple-element.50.refs_2_, ...), custom_call_target="tpu_custom_call" | custom-call | flops 805306368 | bytes 3145728 | tf_op jit(solution)/shard_map/expert_2_1/pallas_call | solution.py:119
  42.3 2.3 %collective-permute-start.13 = (bf16[72,2048]{1,0:T(8,128)(2,1)S(1)}, bf16[72,2048]{1,0:T(8,128)(2,1)S(1)}, u32[]{:S(2)}, u32[]{:S(2)}) collective-permute-start(bf16[72,2048]{1,0:T(8,128)(2,1)S(1)} %slice.37), channel_id=1, source_target_pairs={{0,4},{1,3},{4,8},{5,1},{8,12},{9,5},{12,14},{13,9},{14,10},{15,13... | collective-permute-start | bytes 884744 | tf_op jit(solution)/shard_map/ring_4_1/ppermute | solution.py:174
  44.6 2.7 %expert_3_0.1 = (bf16[128,2048]{1,0:T(8,128)(2,1)S(1)}, bf16[128,2048]{1,0:T(8,128)(2,1)S(1)}) custom-call(s32[1]{0:T(128)} %bitcast.expert_ref, bf16[136,2048]{1,0:T(8,128)(2,1)S(1)} %collective-permute-done.7.refs_0_, bf16[136,2048]{1,0:T(8,128)(2,1)S(1)} %collective-permute-done.11.refs_1_, bf16[2,768,2048]{2,1,0:T(8,128)(2,1)S(1)} %get-tuple-element.50.refs_2_, ...), custom_call_target="tpu_custom_call" | custom-call | flops 805306368 | bytes 3145728 | tf_op jit(solution)/shard_map/expert_3_0/pallas_call | solution.py:119
  49.2 2.7 %expert_far_ring.1 = bf16[128,2048]{1,0:T(8,128)(2,1)S(1)} custom-call(s32[1]{0:T(128)} %bitcast.expert_ref, bf16[72,2048]{1,0:T(8,128)(2,1)S(1)} %collective-permute-done.10.refs_0_, bf16[72,2048]{1,0:T(8,128)(2,1)S(1)} %collective-permute-done.13.refs_1_, bf16[2,768,2048]{2,1,0:T(8,128)(2,1)S(1)} %get-tuple-element.50.refs_2_, ...), custom_call_target="tpu_custom_call" | custom-call | flops 402653184 | bytes 3145728 | tf_op jit(solution)/shard_map/expert_far_ring/pallas_call | solution.py:119
  53.0 2.7 %expert_far_swapped.1 = bf16[128,2048]{1,0:T(8,128)(2,1)S(1)} custom-call(s32[1]{0:T(128)} %bitcast.expert_ref, bf16[72,2048]{1,0:T(8,128)(2,1)S(1)} %collective-permute-done.12.refs_0_, bf16[72,2048]{1,0:T(8,128)(2,1)S(1)} %collective-permute-done.14.refs_1_, bf16[2,768,2048]{2,1,0:T(8,128)(2,1)S(1)} %get-tuple-element.50.refs_2_, ...), custom_call_target="tpu_custom_call" | custom-call | flops 402653184 | bytes 3145728 | tf_op jit(solution)/shard_map/expert_far_swapped/pallas_call | solution.py:119
  55.9 2.1 %collective-permute-start.18 = (bf16[64,2048]{1,0:T(8,128)(2,1)S(1)}, bf16[64,2048]{1,0:T(8,128)(2,1)S(1)}, u32[]{:S(2)}, u32[]{:S(2)}) collective-permute-start(bf16[64,2048]{1,0:T(8,128)(2,1)S(1)} %add_convert_fusion.6), channel_id=1, source_target_pairs={{0,2},{1,5},{4,0},{5,9},{8,4},{9,13},{12,8},{13,15},{14,12},{15,11... | collective-permute-start | bytes 786440 | tf_op jit(solution)/shard_map/back_4_0/ppermute | solution.py:174
  59.6 2.7 %expert_3_1.1 = (bf16[128,2048]{1,0:T(8,128)(2,1)S(1)}, bf16[128,2048]{1,0:T(8,128)(2,1)S(1)}) custom-call(s32[1]{0:T(128)} %bitcast.expert_ref, bf16[136,2048]{1,0:T(8,128)(2,1)S(1)} %collective-permute-done.3.refs_0_, bf16[136,2048]{1,0:T(8,128)(2,1)S(1)} %collective-permute-done.16.refs_1_, bf16[2,768,2048]{2,1,0:T(8,128)(2,1)S(1)} %get-tuple-element.50.refs_2_, ...), custom_call_target="tpu_custom_call" | custom-call | flops 80530640 | bytes 314572 | tf_op jit(solution)/shard_map/expert_3_1/pallas_call | solution.py:119
  65.3 2.0 %collective-permute-start.26 = (bf16[128,2048]{1,0:T(8,128)(2,1)S(1)}, bf16[128,2048]{1,0:T(8,128)(2,1)S(1)}, u32[]{:S(2)}, u32[]{:S(2)}) collective-permute-start(bf16[128,2048]{1,0:T(8,128)(2,1)S(1)} %pad_maximum_fusion.2), channel_id=1, source_target_pairs={{0,2},{1,5},{4,0},{5,9},{8,4},{9,13},{12,8},{13,15},{14,12},{15,11... | collective-permute-start | bytes 1572872 | tf_op jit(solution)/shard_map/back_3_1/ppermute | solution.py:174
  67.3 2.7 %expert_1_1.1 = (bf16[128,2048]{1,0:T(8,128)(2,1)S(1)}, bf16[128,2048]{1,0:T(8,128)(2,1)S(1)}) custom-call(s32[1]{0:T(128)} %bitcast.expert_ref, bf16[136,2048]{1,0:T(8,128)(2,1)S(1)} %collective-permute-done.1.refs_0_, bf16[136,2048]{1,0:T(8,128)(2,1)S(1)} %collective-permute-done.22.refs_1_, bf16[2,768,2048]{2,1,0:T(8,128)(2,1)S(1)} %get-tuple-element.50.refs_2_, ...), custom_call_target="tpu_custom_call" | custom-call | flops 805306368 | bytes 3145728 | tf_op jit(solution)/shard_map/expert_1_1/pallas_call | solution.py:119
  74.0 3.6 %collective-permute-done.26 = bf16[128,2048]{1,0:T(8,128)(2,1)S(1)} collective-permute-done((bf16[128,2048]{1,0:T(8,128)(2,1)S(1)}, bf16[128,2048]{1,0:T(8,128)(2,1)S(1)}, u32[]{:S(2)}, u32[]{:S(2)}) %collective-permute-start.26) | collective-permute-done | bytes 524320 | tf_op jit(solution)/shard_map/back_3_1/ppermute | solution.py:174
  79.6 3.6 %collective-permute-done.28 = bf16[128,2048]{1,0:T(8,128)(2,1)S(1)} collective-permute-done((bf16[128,2048]{1,0:T(8,128)(2,1)S(1)}, bf16[128,2048]{1,0:T(8,128)(2,1)S(1)}, u32[]{:S(2)}, u32[]{:S(2)}) %collective-permute-start.28) | collective-permute-done | bytes 524320 | tf_op jit(solution)/shard_map/back_2_0/ppermute | solution.py:174
  85.2 3.6 %collective-permute-done.31 = bf16[128,2048]{1,0:T(8,128)(2,1)S(1)} collective-permute-done((bf16[128,2048]{1,0:T(8,128)(2,1)S(1)}, bf16[128,2048]{1,0:T(8,128)(2,1)S(1)}, u32[]{:S(2)}, u32[]{:S(2)}) %collective-permute-start.31) | collective-permute-done | bytes 524320 | tf_op jit(solution)/shard_map/back_2_1/ppermute | solution.py:174
  89.9 4.5 %collective-permute-done.29.refs_2_ = bf16[128,2048]{1,0:T(8,128)(2,1)S(1)} collective-permute-done((bf16[128,2048]{1,0:T(8,128)(2,1)S(1)}, bf16[128,2048]{1,0:T(8,128)(2,1)S(1)}, u32[]{:S(2)}, u32[]{:S(2)}) %collective-permute-start.29) | collective-permute-done | bytes 524320 | tf_op jit(solution)/shard_map/back_1_0/ppermute | solution.py:174
  94.6 5.0 %collective-permute-done.32 = bf16[128,2048]{1,0:T(8,128)(2,1)S(1)} collective-permute-done((bf16[128,2048]{1,0:T(8,128)(2,1)S(1)}, bf16[128,2048]{1,0:T(8,128)(2,1)S(1)}, u32[]{:S(2)}, u32[]{:S(2)}) %collective-permute-start.32) | collective-permute-done | bytes 524320 | tf_op jit(solution)/shard_map/back_1_1/ppermute | solution.py:174
  (78 shorter events, 29.3 us)
Async XLA Ops:
  2.3 11.4 %collective-permute-start.4 = (bf16[136,2048]{1,0:T(8,128)(2,1)S(1)}, bf16[136,2048]{1,0:T(8,128)(2,1)S(1)}, u32[]{:S(2)}, u32[]{:S(2)}) collective-permute-start(bf16[136,2048]{1,0:T(8,128)(2,1)S(1)} %pad_maximum_fusion.refs_0_), channel_id=1, source_target_pairs={{0,4},{1,3},{4,8},{5,1},{8,12},{9,5},{12,14},{13,9},{14,10},{15,13... | collective-permute-start | bytes 1671176 | tf_op jit(solution)/shard_map/ring_1_0/ppermute | solution.py:174
  5.0 13.4 %collective-permute-start.1 = (bf16[136,2048]{1,0:T(8,128)(2,1)S(1)}, bf16[136,2048]{1,0:T(8,128)(2,1)S(1)}, u32[]{:S(2)}, u32[]{:S(2)}) collective-permute-start(bf16[136,2048]{1,0:T(8,128)(2,1)S(1)} %collective-permute-done.refs_1_), channel_id=1, source_target_pairs={{0,4},{1,3},{4,8},{5,1},{8,12},{9,5},{12,14},{13,9},{14,10},{15,13... | collective-permute-start | bytes 1671176 | tf_op jit(solution)/shard_map/ring_1_1/ppermute | solution.py:174
  13.8 10.6 %collective-permute-start.5 = (bf16[136,2048]{1,0:T(8,128)(2,1)S(1)}, bf16[136,2048]{1,0:T(8,128)(2,1)S(1)}, u32[]{:S(2)}, u32[]{:S(2)}) collective-permute-start(bf16[136,2048]{1,0:T(8,128)(2,1)S(1)} %collective-permute-done.4.refs_0_), channel_id=1, source_target_pairs={{0,4},{1,3},{4,8},{5,1},{8,12},{9,5},{12,14},{13,9},{14,10},{15,13... | collective-permute-start | bytes 1671176 | tf_op jit(solution)/shard_map/ring_2_0/ppermute | solution.py:174
  18.4 11.9 %collective-permute-start.2 = (bf16[136,2048]{1,0:T(8,128)(2,1)S(1)}, bf16[136,2048]{1,0:T(8,128)(2,1)S(1)}, u32[]{:S(2)}, u32[]{:S(2)}) collective-permute-start(bf16[136,2048]{1,0:T(8,128)(2,1)S(1)} %collective-permute-done.1.refs_0_), channel_id=1, source_target_pairs={{0,4},{1,3},{4,8},{5,1},{8,12},{9,5},{12,14},{13,9},{14,10},{15,13... | collective-permute-start | bytes 1671176 | tf_op jit(solution)/shard_map/ring_2_1/ppermute | solution.py:174
  24.4 8.1 %collective-permute-start.8 = (bf16[136,2048]{1,0:T(8,128)(2,1)S(1)}, bf16[136,2048]{1,0:T(8,128)(2,1)S(1)}, u32[]{:S(2)}, u32[]{:S(2)}) collective-permute-start(bf16[136,2048]{1,0:T(8,128)(2,1)S(1)} %collective-permute-done.5.refs_0_), channel_id=1, source_target_pairs={{0,1},{1,0},{4,5},{5,4},{8,9},{9,8},{12,13},{13,12},{14,15},{15,14... | collective-permute-start | bytes 1671176 | tf_op jit(solution)/shard_map/swap_2_0/ppermute | solution.py:174
  24.4 11.9 %collective-permute-start.7 = (bf16[136,2048]{1,0:T(8,128)(2,1)S(1)}, bf16[136,2048]{1,0:T(8,128)(2,1)S(1)}, u32[]{:S(2)}, u32[]{:S(2)}) collective-permute-start(bf16[136,2048]{1,0:T(8,128)(2,1)S(1)} %collective-permute-done.5.refs_0_), channel_id=1, source_target_pairs={{0,4},{1,3},{4,8},{5,1},{8,12},{9,5},{12,14},{13,9},{14,10},{15,13... | collective-permute-start | bytes 1671176 | tf_op jit(solution)/shard_map/ring_3_0/ppermute | solution.py:174
  30.3 8.2 %collective-permute-start.9 = (bf16[136,2048]{1,0:T(8,128)(2,1)S(1)}, bf16[136,2048]{1,0:T(8,128)(2,1)S(1)}, u32[]{:S(2)}, u32[]{:S(2)}) collective-permute-start(bf16[136,2048]{1,0:T(8,128)(2,1)S(1)} %collective-permute-done.2.refs_0_), channel_id=1, source_target_pairs={{0,1},{1,0},{4,5},{5,4},{8,9},{9,8},{12,13},{13,12},{14,15},{15,14... | collective-permute-start | bytes 1671176 | tf_op jit(solution)/shard_map/swap_2_1/ppermute | solution.py:174
  30.3 11.9 %collective-permute-start.3 = (bf16[136,2048]{1,0:T(8,128)(2,1)S(1)}, bf16[136,2048]{1,0:T(8,128)(2,1)S(1)}, u32[]{:S(2)}, u32[]{:S(2)}) collective-permute-start(bf16[136,2048]{1,0:T(8,128)(2,1)S(1)} %collective-permute-done.2.refs_0_), channel_id=1, source_target_pairs={{0,4},{1,3},{4,8},{5,1},{8,12},{9,5},{12,14},{13,9},{14,10},{15,13... | collective-permute-start | bytes 1671176 | tf_op jit(solution)/shard_map/ring_3_1/ppermute | solution.py:174
  36.3 8.3 %collective-permute-start.11 = (bf16[136,2048]{1,0:T(8,128)(2,1)S(1)}, bf16[136,2048]{1,0:T(8,128)(2,1)S(1)}, u32[]{:S(2)}, u32[]{:S(2)}) collective-permute-start(bf16[136,2048]{1,0:T(8,128)(2,1)S(1)} %collective-permute-done.7.refs_0_), channel_id=1, source_target_pairs={{0,1},{1,0},{4,5},{5,4},{8,9},{9,8},{12,13},{13,12},{14,15},{15,14... | collective-permute-start | bytes 1671176 | tf_op jit(solution)/shard_map/swap_3_0/ppermute | solution.py:174
  36.4 10.9 %collective-permute-start.10 = (bf16[72,2048]{1,0:T(8,128)(2,1)S(1)}, bf16[72,2048]{1,0:T(8,128)(2,1)S(1)}, u32[]{:S(2)}, u32[]{:S(2)}) collective-permute-start(bf16[72,2048]{1,0:T(8,128)(2,1)S(1)} %pad_maximum_fusion.3), channel_id=1, source_target_pairs={{0,4},{1,3},{4,8},{5,1},{8,12},{9,5},{12,14},{13,9},{14,10},{15,13... | collective-permute-start | bytes 884744 | tf_op jit(solution)/shard_map/ring_4_0/ppermute | solution.py:174
  52.5 7.1 %collective-permute-start.16 = (bf16[136,2048]{1,0:T(8,128)(2,1)S(1)}, bf16[136,2048]{1,0:T(8,128)(2,1)S(1)}, u32[]{:S(2)}, u32[]{:S(2)}) collective-permute-start(bf16[136,2048]{1,0:T(8,128)(2,1)S(1)} %collective-permute-done.3.refs_0_), channel_id=1, source_target_pairs={{0,1},{1,0},{4,5},{5,4},{8,9},{9,8},{12,13},{13,12},{14,15},{15,14... | collective-permute-start | bytes 1671176 | tf_op jit(solution)/shard_map/swap_3_1/ppermute | solution.py:174
  52.6 9.8 %collective-permute-start.17 = (bf16[128,2048]{1,0:T(8,128)(2,1)S(1)}, bf16[128,2048]{1,0:T(8,128)(2,1)S(1)}, u32[]{:S(2)}, u32[]{:S(2)}) collective-permute-start(bf16[128,2048]{1,0:T(8,128)(2,1)S(1)} %get-tuple-element.69), channel_id=1, source_target_pairs={{0,1},{1,0},{4,5},{5,4},{8,9},{9,8},{12,13},{13,12},{14,15},{15,14... | collective-permute-start | bytes 1572872 | tf_op jit(solution)/shard_map/give_3_0/ppermute | solution.py:174
  58.0 7.1 %collective-permute-start.20 = (bf16[64,2048]{1,0:T(8,128)(2,1)S(1)}, bf16[64,2048]{1,0:T(8,128)(2,1)S(1)}, u32[]{:S(2)}, u32[]{:S(2)}) collective-permute-start(bf16[64,2048]{1,0:T(8,128)(2,1)S(1)} %add_convert_fusion.5), channel_id=1, source_target_pairs={{0,2},{1,5},{4,0},{5,9},{8,4},{9,13},{12,8},{13,15},{14,12},{15,11... | collective-permute-start | bytes 786440 | tf_op jit(solution)/shard_map/back_4_1/ppermute | solution.py:174
  62.7 9.2 %collective-permute-start.24 = (bf16[128,2048]{1,0:T(8,128)(2,1)S(1)}, bf16[128,2048]{1,0:T(8,128)(2,1)S(1)}, u32[]{:S(2)}, u32[]{:S(2)}) collective-permute-start(bf16[128,2048]{1,0:T(8,128)(2,1)S(1)} %pad_maximum_fusion.1), channel_id=1, source_target_pairs={{0,2},{1,5},{4,0},{5,9},{8,4},{9,13},{12,8},{13,15},{14,12},{15,11... | collective-permute-start | bytes 1572872 | tf_op jit(solution)/shard_map/back_3_0/ppermute | solution.py:174
  64.5 7.5 %collective-permute-start.23 = (bf16[128,2048]{1,0:T(8,128)(2,1)S(1)}, bf16[128,2048]{1,0:T(8,128)(2,1)S(1)}, u32[]{:S(2)}, u32[]{:S(2)}) collective-permute-start(bf16[128,2048]{1,0:T(8,128)(2,1)S(1)} %get-tuple-element.78), channel_id=1, source_target_pairs={{0,1},{1,0},{4,5},{5,4},{8,9},{9,8},{12,13},{13,12},{14,15},{15,14... | collective-permute-start | bytes 1572872 | tf_op jit(solution)/shard_map/give_2_0/ppermute | solution.py:174
  65.0 9.0 %collective-permute-start.25 = (bf16[128,2048]{1,0:T(8,128)(2,1)S(1)}, bf16[128,2048]{1,0:T(8,128)(2,1)S(1)}, u32[]{:S(2)}, u32[]{:S(2)}) collective-permute-start(bf16[128,2048]{1,0:T(8,128)(2,1)S(1)} %get-tuple-element.81), channel_id=1, source_target_pairs={{0,1},{1,0},{4,5},{5,4},{8,9},{9,8},{12,13},{13,12},{14,15},{15,14... | collective-permute-start | bytes 1572872 | tf_op jit(solution)/shard_map/give_2_1/ppermute | solution.py:174
  65.3 12.3 %collective-permute-start.26 = (bf16[128,2048]{1,0:T(8,128)(2,1)S(1)}, bf16[128,2048]{1,0:T(8,128)(2,1)S(1)}, u32[]{:S(2)}, u32[]{:S(2)}) collective-permute-start(bf16[128,2048]{1,0:T(8,128)(2,1)S(1)} %pad_maximum_fusion.2), channel_id=1, source_target_pairs={{0,2},{1,5},{4,0},{5,9},{8,4},{9,13},{12,8},{13,15},{14,12},{15,11... | collective-permute-start | bytes 1572872 | tf_op jit(solution)/shard_map/back_3_1/ppermute | solution.py:174
  67.3 12.3 %collective-permute-start.27 = (bf16[128,2048]{1,0:T(8,128)(2,1)S(1)}, bf16[128,2048]{1,0:T(8,128)(2,1)S(1)}, u32[]{:S(2)}, u32[]{:S(2)}) collective-permute-start(bf16[128,2048]{1,0:T(8,128)(2,1)S(1)} %get-tuple-element.84), channel_id=1, source_target_pairs={{0,1},{1,0},{4,5},{5,4},{8,9},{9,8},{12,13},{13,12},{14,15},{15,14... | collective-permute-start | bytes 1572872 | tf_op jit(solution)/shard_map/give_1_0/ppermute | solution.py:174
  72.2 11.0 %collective-permute-start.28 = (bf16[128,2048]{1,0:T(8,128)(2,1)S(1)}, bf16[128,2048]{1,0:T(8,128)(2,1)S(1)}, u32[]{:S(2)}, u32[]{:S(2)}) collective-permute-start(bf16[128,2048]{1,0:T(8,128)(2,1)S(1)} %add_convert_fusion.4), channel_id=1, source_target_pairs={{0,2},{1,5},{4,0},{5,9},{8,4},{9,13},{12,8},{13,15},{14,12},{15,11... | collective-permute-start | bytes 1572872 | tf_op jit(solution)/shard_map/back_2_0/ppermute | solution.py:174
  74.0 11.2 %collective-permute-start.30 = (bf16[128,2048]{1,0:T(8,128)(2,1)S(1)}, bf16[128,2048]{1,0:T(8,128)(2,1)S(1)}, u32[]{:S(2)}, u32[]{:S(2)}) collective-permute-start(bf16[128,2048]{1,0:T(8,128)(2,1)S(1)} %get-tuple-element.86), channel_id=1, source_target_pairs={{0,1},{1,0},{4,5},{5,4},{8,9},{9,8},{12,13},{13,12},{14,15},{15,14... | collective-permute-start | bytes 1572872 | tf_op jit(solution)/shard_map/give_1_1/ppermute | solution.py:174
  77.8 11.0 %collective-permute-start.31 = (bf16[128,2048]{1,0:T(8,128)(2,1)S(1)}, bf16[128,2048]{1,0:T(8,128)(2,1)S(1)}, u32[]{:S(2)}, u32[]{:S(2)}) collective-permute-start(bf16[128,2048]{1,0:T(8,128)(2,1)S(1)} %add_convert_fusion.3), channel_id=1, source_target_pairs={{0,2},{1,5},{4,0},{5,9},{8,4},{9,13},{12,8},{13,15},{14,12},{15,11... | collective-permute-start | bytes 1572872 | tf_op jit(solution)/shard_map/back_2_1/ppermute | solution.py:174
  79.6 10.4 %collective-permute-start.21 = (bf16[128,2048]{1,0:T(8,128)(2,1)S(1)}, bf16[128,2048]{1,0:T(8,128)(2,1)S(1)}, u32[]{:S(2)}, u32[]{:S(2)}) collective-permute-start(bf16[128,2048]{1,0:T(8,128)(2,1)S(1)} %get-tuple-element.72), channel_id=1, source_target_pairs={{0,1},{1,0},{4,5},{5,4},{8,9},{9,8},{12,13},{13,12},{14,15},{15,14... | collective-permute-start | bytes 1572872 | tf_op jit(solution)/shard_map/give_0_0/ppermute | solution.py:174
  83.4 11.0 %collective-permute-start.29 = (bf16[128,2048]{1,0:T(8,128)(2,1)S(1)}, bf16[128,2048]{1,0:T(8,128)(2,1)S(1)}, u32[]{:S(2)}, u32[]{:S(2)}) collective-permute-start(bf16[128,2048]{1,0:T(8,128)(2,1)S(1)} %add_convert_fusion.2), channel_id=1, source_target_pairs={{0,2},{1,5},{4,0},{5,9},{8,4},{9,13},{12,8},{13,15},{14,12},{15,11... | collective-permute-start | bytes 1572872 | tf_op jit(solution)/shard_map/back_1_0/ppermute | solution.py:174
  89.0 10.5 %collective-permute-start.32 = (bf16[128,2048]{1,0:T(8,128)(2,1)S(1)}, bf16[128,2048]{1,0:T(8,128)(2,1)S(1)}, u32[]{:S(2)}, u32[]{:S(2)}) collective-permute-start(bf16[128,2048]{1,0:T(8,128)(2,1)S(1)} %add_convert_fusion.1), channel_id=1, source_target_pairs={{0,3},{1,4},{4,1},{5,8},{8,5},{9,12},{12,9},{13,14},{14,13},{15,10... | collective-permute-start | bytes 1572872 | tf_op jit(solution)/shard_map/back_1_1/ppermute | solution.py:174
  (10 other events, 44.3 us)

commit v11 on v10

--- a/solution.py
+++ b/solution.py
@@ -54,8 +54,8 @@
     return list(range(0, chips, 2)) + list(range(chips - 1, 0, -2))
 
 
-def half_expert_kernel(first_tokens, load, split, expert_ref, *refs):
-    blocks, refs = refs[: len(first_tokens)], refs[len(first_tokens) :]
+def half_expert_kernel(heights, load, split, *refs):
+    blocks, refs = refs[: len(heights)], refs[len(heights) :]
     if load:
         (gate_up_far, down_far), refs = refs[:2], refs[2:]
         outs, (gate_up_ref, down_ref, rows, hidden, arrived) = refs[:split], refs[split:]
@@ -74,16 +74,9 @@
             copy.start()
 
     at = 0
-    weights = []
-    for block, token in zip(blocks, first_tokens):
-        count = block.shape[0] - GATE_ROWS
-        rows[at : at + count, :] = block[:count, :]
-        at += count
-        high, low = (block[count:, i * LANES : (i + 1) * LANES].astype(jnp.float32) for i in (0, 1))
-        wanted = lax.broadcasted_iota(jnp.int32, high.shape, 0) == expert_ref[0]
-        line = jnp.sum(jnp.where(wanted, high + low, 0.0), axis=0, keepdims=True)
-        weights.append(jnp.broadcast_to(line, high.shape).T[token : token + count, :1])
-    weight = jnp.concatenate(weights)
+    for block, height in zip(blocks, heights):
+        rows[at : at + height, :] = block[:height, :]
+        at += height
 
     contract = (((1,), (1,)), ((), ()))
     taken = rows[...]
@@ -100,14 +93,14 @@
     share = outs[0].shape[0]
     tile = 512 if width % 512 == 0 else width
     for low in range(0, width, tile):
-        product = jnp.dot(inner, down_ref[:, low : low + tile], preferred_element_type=jnp.float32) * weight
+        product = jnp.dot(inner, down_ref[:, low : low + tile], preferred_element_type=jnp.float32)
         product = product.astype(jnp.bfloat16)
         for i, out in enumerate(outs):
             out[:, low : low + tile] = product[i * share : (i + 1) * share]
 
 
-def half_expert(first_tokens, blocks, expert, weights, load=False, cost=2, split=2):
-    height = sum(block.shape[0] - GATE_ROWS for block in blocks)
+def half_expert(heights, blocks, weights, load=False, cost=2, split=2):
+    height = sum(heights)
     units, width = weights[1].shape
     whole = pl.BlockSpec(memory_space=pltpu.VMEM)
     far = pl.BlockSpec(memory_space=pltpu.HBM)
@@ -117,9 +110,9 @@
         outs += [jax.ShapeDtypeStruct(array.shape, array.dtype) for array in weights]
         scratch.append(pltpu.SemaphoreType.DMA((units // 256 + 1 if units % 256 == 0 else 2,)))
     return pl.pallas_call(
-        functools.partial(half_expert_kernel, tuple(first_tokens), load, split),
+        functools.partial(half_expert_kernel, tuple(heights), load, split),
         out_shape=outs,
-        in_specs=[pl.BlockSpec(memory_space=pltpu.SMEM)] + [whole] * len(blocks) + [far if load else whole] * 2,
+        in_specs=[whole] * len(blocks) + [far if load else whole] * 2,
         out_specs=[whole] * len(outs),
         scratch_shapes=scratch,
         compiler_params=pltpu.CompilerParams(vmem_limit_bytes=(34 if load else 14) << 20),
@@ -128,28 +121,37 @@
             bytes_accessed=int(cost * units * width),
             transcendentals=0,
         ),
-    )(expert, *blocks, *weights)
-
-
-def sum_kernel(low, *refs):
-    *terms, part, out = refs
-    value = sum(term[...].astype(jnp.float32) for term in terms)
-    out[...] = value.astype(out.dtype)
-    near = slice(low, low + part.shape[0])
-    out[near, :] = (value[near] + part[...].astype(jnp.float32)).astype(out.dtype)
-
-
-def summed(*terms, low=0, dtype=jnp.bfloat16, cost=1):
+    )(*blocks, *weights)
+
+
+def weighted_kernel(kind, token, low, part_rows, expert_ref, holder, mine, theirs, *refs):
+    *arrived, out = refs
+    height = mine.shape[0]
+    last = holder.shape[0] - GATE_ROWS
+    near, far = (holder[last:, (2 * kind + i) * LANES : (2 * kind + i + 1) * LANES].astype(jnp.float32) for i in (0, 1))
+    wanted = lax.broadcasted_iota(jnp.int32, near.shape, 0) == expert_ref[0]
+    line = jnp.sum(jnp.where(wanted, near + far, 0.0), axis=0, keepdims=True)
+    weight = jnp.broadcast_to(line, near.shape).T[token : token + height, :1]
+    value = weight * (mine[...].astype(jnp.float32) + theirs[...].astype(jnp.float32))
+    out[:height, :] = value.astype(out.dtype)
+    if height < out.shape[0]:
+        out[height:, :] = jnp.zeros((out.shape[0] - height, out.shape[1]), out.dtype)
+    if arrived:
+        part = slice(low, low + part_rows)
+        out[part, :] = (value[part] + arrived[0][:part_rows, :].astype(jnp.float32)).astype(out.dtype)
+
+
+def weighted(expert, holder, kind, mine, theirs, *arrived, token=0, low=0, part=None, more=0, dtype=jnp.bfloat16):
     whole = pl.BlockSpec(memory_space=pltpu.VMEM)
-    size = terms[0].size
+    size = mine.size
     return pl.pallas_call(
-        functools.partial(sum_kernel, low),
-        out_shape=jax.ShapeDtypeStruct(terms[0].shape, dtype),
-        in_specs=[whole] * len(terms),
+        functools.partial(weighted_kernel, kind, token, low, part or mine.shape[0]),
+        out_shape=jax.ShapeDtypeStruct((mine.shape[0] + more, mine.shape[1]), dtype),
+        in_specs=[pl.BlockSpec(memory_space=pltpu.SMEM)] + [whole] * (3 + len(arrived)),
         out_specs=whole,
-        compiler_params=pltpu.CompilerParams(vmem_limit_bytes=8 << 20),
-        cost_estimate=pl.CostEstimate(flops=size * cost, bytes_accessed=size, transcendentals=0),
-    )(*terms)
+        compiler_params=pltpu.CompilerParams(vmem_limit_bytes=10 << 20),
+        cost_estimate=pl.CostEstimate(flops=size * 20000, bytes_accessed=size, transcendentals=0),
+    )(expert, holder, mine, theirs, *arrived)
 
 
 def by_tokens(tokens, expert_ids, route_gate, gate_up, down_proj):
@@ -183,42 +185,45 @@
         return lax.optimization_barrier((value, *earlier))[0]
 
     expert = jnp.right_shift(lax.axis_index("blk"), 1).astype(jnp.int32).reshape(1)
+    ring = [send(tokens, forth, "ring_1_0"), None]
+    others = send(tokens, cores, "swap_0_0")
     chosen = jnp.arange(GATE_ROWS, dtype=jnp.int32)[:, None, None] == expert_ids.T[None]
     weight = jnp.sum(jnp.where(chosen, route_gate.T[None], 0.0), axis=1)
     high = lax.reduce_precision(weight, 8, 7)
     gates = jnp.concatenate([high, weight - high], axis=1).astype(jnp.bfloat16)
-    packed = jnp.concatenate([tokens, jnp.pad(gates, ((0, 0), (0, tokens.shape[1] - 2 * LANES)))])
-
-    other = send(packed, cores, "swap_0")
-    ring = [send(packed, forth, "ring_1_0"), send(other, forth, "ring_1_1")]
+    gates = jnp.concatenate([gates, send(gates, cores, "swap_0_1")], axis=1)
+    packed = jnp.concatenate([others, jnp.pad(gates, ((0, 0), (0, tokens.shape[1] - 4 * LANES)))])
+    ring[1] = send(packed, forth, "ring_1_1")
+
+    results, holders = {}, {0: packed}
+    with jax.named_scope("expert_0"):
+        inputs = [after(tokens, ring[0]), packed]
+        own, given, *near = half_expert([rows] * 2, inputs, [gate_up, down_proj], load=True)
+    results[0, 0] = own, given
+    ring[1] = after(ring[1], own)
 
     def expert_rows(step, c, inputs, **options):
         with jax.named_scope(f"expert_{step}_{c}"):
-            kept, given = half_expert([0, 0], inputs, expert, near, **options)
-        results[step, c] = kept, given
+            results[step, c] = half_expert([rows] * 2, inputs, near, **options)
         if step == far - 1 or (step, c) == (1, 1):
             give(step, c)
-        return kept
+        return results[step, c][0]
 
     def give(step, c, *earlier):
         kept, given = results[step, c]
         results[step, c] = kept, send(after(given, *earlier) if earlier else given, cores, f"give_{step}_{c}")
 
-    results = {}
-    with jax.named_scope("expert_0"):
-        own, given, *near = half_expert([0, 0], [packed, other], expert, [gate_up, down_proj], load=True)
-    results[0, 0] = own, given
-    ring[0] = after(ring[0], own)
-    delayed = None
     earlier = ring[1]
     for step in range(1, far):
-        swapped = [send(block, cores, f"swap_{step}_{c}") for c, block in enumerate(ring[: 1 if step == 1 else 2])]
+        holders[step] = ring[1]
+        swapped = [
+            send(block[:rows], cores, f"swap_{step}_{c}") for c, block in enumerate(ring[: 1 if step == 1 else 2])
+        ]
         blocks = list(ring)
         if step < far - 1:
             ring = [send(block, forth, f"ring_{step + 1}_{c}") for c, block in enumerate(ring)]
         else:
-            ring[0] = send(jnp.concatenate([ring[0][:half], ring[0][rows:]]), forth, f"ring_{far}_0")
-            ring[1] = send(ring[1][half:], forth, f"ring_{far}_1")
+            ring = [send(ring[0][: half + GATE_ROWS], forth, f"ring_{far}_0"), send(ring[1][half:], forth, f"ring_{far}_1")]
         for c in chains:
             if (step, c) == (1, 1):
                 delayed = blocks[1]
@@ -232,48 +237,41 @@
             earlier = ring[c]
 
     with jax.named_scope("expert_far_ring"):
-        (given,) = half_expert([0, half], ring, expert, near, split=1)
-    swapped = [send(block, cores, f"swap_{far}_{c}") for c, block in enumerate(ring)]
+        (given,) = half_expert([half] * 2, ring, near, split=1)
+    swapped = [send(block[:half], cores, f"swap_{far}_{c}") for c, block in enumerate(ring)]
     swapped[0] = after(swapped[0], given)
     given = send(given, cores, "give_far")
     with jax.named_scope("expert_far_swapped"):
-        (kept,) = half_expert([0, half], swapped, expert, near, split=1)
-
-    first, second = slice(0, half), slice(half, rows)
+        (kept,) = half_expert([half] * 2, swapped, near, split=1)
+
     late = []
     earlier = kept
-    for c, part in enumerate((second, first)):
-        earlier = rounded(total(after(kept[part], earlier), given[part]))
+    for c, part in enumerate((slice(half, rows), slice(0, half))):
+        mine = after(kept[part], earlier)
+        earlier = weighted(expert, ring[1], c, mine, given[part], token=half if c == 0 else 0, more=GATE_ROWS)
         late.append(send(earlier, back, f"back_{far}_{c}"))
     earlier = expert_rows(far - 1, 1, [after(last[0], earlier), last[1]], cost=0.2)
     sums = []
     for c in chains:
         mine, theirs = results[far - 1, c]
-        value = total(after(mine, earlier), theirs)
-        if c == 0:
-            value = jnp.concatenate([value[first], value[second] + total(late[c])])
-        else:
-            value = jnp.concatenate([value[first] + total(late[c]), value[second]])
-        earlier = rounded(value)
+        low = half if c == 0 else 0
+        earlier = weighted(expert, holders[far - 1], c, after(mine, earlier), theirs, late[c], low=low, part=half)
         sums.append(send(earlier, back, f"back_{far - 1}_{c}"))
         if c == 0:
-            swapped = send(after(delayed, earlier), cores, "swap_1_1")
             for step in range(far - 2, 1, -1):
                 for c2 in chains:
                     give(step, c2, earlier)
+    swapped = send(after(delayed, earlier)[:rows], cores, "swap_1_1")
     give(1, 0, earlier)
     give(0, 0, earlier)
     earlier = expert_rows(1, 1, [after(delayed, earlier), swapped])
-    for step in range(far - 2, 1, -1):
+    for step in range(far - 2, 0, -1):
         for c in chains:
             mine, theirs = results[step, c]
-            earlier = rounded(total(after(mine, earlier), theirs, sums[c]))
-            sums[c] = send(earlier, back, f"back_{step}_{c}")
-    for c, pairs in zip(chains, (back, across)):
-        mine, theirs = results[1, c]
-        earlier = rounded(total(after(mine, earlier), theirs, sums[c]))
-        sums[c] = send(earlier, pairs, f"back_1_{c}")
-    return rounded(total(summed(*results[0, 0], sums[0], dtype=jnp.float32, cost=20000), sums[1]))
+            earlier = weighted(expert, holders[step], c, after(mine, earlier), theirs, sums[c])
+            sums[c] = send(earlier, across if (step, c) == (1, 1) else back, f"back_{step}_{c}")
+    own = weighted(expert, packed, 0, *results[0, 0], sums[0], dtype=jnp.float32)
+    return rounded(total(own, sums[1]))
 
 
 def solution(mesh):

time: 101 us -> 115 us (1.14)
  waiting for transfers between devices: 34.5 us -> 45.6 us
  local copies, waits for them, and re-layouts: 2.03 us -> 11.3 us
  starting transfers between devices: 32.8 us -> 24.5 us
  Pallas kernels: 26.5 us -> 30.4 us
  other arithmetic: 4.26 us -> 1.67 us
    ppermute x33 -> x34, waiting for transfers between devices: 34.5 us -> 45.6 us  [send(): return lax.ppermute(value, 'blk', pairs)]
    ppermute x33 -> x34, starting transfers between devices: 32.8 us -> 24.5 us  [send(): return lax.ppermute(value, 'blk', pairs)]
    unnamed x2 -> x62, local copies, waits for them, and re-layouts: 1.89 us -> 7.5 us
    pallas_call x10 -> x18, Pallas kernels: 26.5 us -> 30.4 us  [the longest x9 27.9 us: half_expert(): pl.pallas_call(functools.partial(half_expert_kernel, tuple(heights), load...]
    slice x6 -> x9, local copies, waits for them, and re-layouts: 0.14 us -> 3.84 us  [the longest x2 1.53 us: by_tokens(): block[:half]]
  transfers between devices with their start and end apart: 33 -> 34, of which waited for: 12 -> 13; matrix products, arithmetic and copies ran while one was open for 2% -> 4% of each run, Pallas kernels for 26% -> 26%
where the time goes in v11:
time: 115 us; the launch traced here: 114 us
  waiting for transfers between devices  45.6 us (40%)
  Pallas kernels  30.4 us (26%)
  starting transfers between devices  24.5 us (21%)
  local copies, waits for them, and re-layouts  11.3 us (10%)
  other arithmetic  1.67 us (1%)
    ppermute x34, waiting for transfers between devices, send(): return lax.ppermute(value, 'blk', pairs)  45.6 us
    pallas_call x9, Pallas kernels, half_expert(): pl.pallas_call(functools.partial(half_expert_kernel, tuple(heights), load...  27.9 us
    ppermute x34, starting transfers between devices, send(): return lax.ppermute(value, 'blk', pairs)  24.5 us
    unnamed x62, local copies, waits for them, and re-layouts  7.5 us
    pallas_call x9, Pallas kernels, weighted(): pl.pallas_call(functools.partial(weighted_kernel, kind, token, low, part...  2.44 us
  transfers between devices with their start and end apart: 34, of which 13 were waited for; matrix products, arithmetic and copies ran while one was open for 4% of the time, Pallas kernels for 26%

profile of v11, /device:TPU:0, one launch (start us, length us, event | category | flops | bytes accessed | tf_op | source)
XLA Modules:
  0.0 114.1 jit_solution(7820386089198418384)
XLA Ops:
  1.3 3.0 %collective-permute-start.2 = (bf16[128,2048]{1,0:T(8,128)(2,1)}, bf16[128,2048]{1,0:T(8,128)(2,1)S(1)}, u32[]{:S(2)}, u32[]{:S(2)}) collective-permute-start(bf16[128,2048]{1,0:T(8,128)(2,1)} %refs_0_), channel_id=1, source_target_pairs={{0,4},{1,3},{4,8},{5,1},{8,12},{9,5},{12,14},{13,9},{14,10},{15,13... | collective-permute-start | bytes 1572872 | tf_op jit(solution)/shard_map/ring_1_0/ppermute | solution.py:176
  6.0 5.6 %collective-permute-done.2.refs_0_ = bf16[128,2048]{1,0:T(8,128)(2,1)S(1)} collective-permute-done((bf16[128,2048]{1,0:T(8,128)(2,1)}, bf16[128,2048]{1,0:T(8,128)(2,1)S(1)}, u32[]{:S(2)}, u32[]{:S(2)}) %collective-permute-start.2) | collective-permute-done | bytes 524320 | tf_op jit(solution)/shard_map/ring_1_0/ppermute | solution.py:176
  11.6 2.1 %collective-permute-start.6 = (bf16[128,2048]{1,0:T(8,128)(2,1)S(1)}, bf16[128,2048]{1,0:T(8,128)(2,1)S(1)}, u32[]{:S(2)}, u32[]{:S(2)}) collective-permute-start(bf16[128,2048]{1,0:T(8,128)(2,1)S(1)} %collective-permute-done.2.refs_0_), channel_id=1, source_target_pairs={{0,4},{1,3},{4,8},{5,1},{8,12},{9,5},{12,14},{13,9},{14,10},{15,13... | collective-permute-start | bytes 1572872 | tf_op jit(solution)/shard_map/ring_2_0/ppermute | solution.py:176
  13.7 1.9 %copy-done.4 = bf16[768,2048]{1,0:T(8,128)(2,1)S(1)} copy-done((bf16[768,2048]{1,0:T(8,128)(2,1)S(1)}, bf16[768,2048]{1,0:T(8,128)(2,1)}, u32[]{:S(2)}) %copy-start.4) | copy-done | bytes 3145752
  16.7 4.9 %expert_0.1 = (bf16[128,2048]{1,0:T(8,128)(2,1)S(1)}, bf16[128,2048]{1,0:T(8,128)(2,1)S(1)}, bf16[2,768,2048]{2,1,0:T(8,128)(2,1)S(1)}, bf16[768,2048]{1,0:T(8,128)(2,1)S(1)}) custom-call(bf16[128,2048]{1,0:T(8,128)(2,1)S(1)} %copy-done.11, bf16[136,2048]{1,0:T(8,128)(2,1)S(1)} %pad_maximum_fusion.refs_1_.holder, bf16[2,768,2048]{2,1,0:T(8,128)(2,1)} %refs_2_.1, ...), custom_call_target="tpu_custom_call" | custom-call | flops 805306368 | bytes 3145728 | tf_op jit(solution)/shard_map/expert_0/pallas_call | solution.py:112
  23.2 2.6 %expert_1_0.1 = (bf16[128,2048]{1,0:T(8,128)(2,1)S(1)}, bf16[128,2048]{1,0:T(8,128)(2,1)S(1)}) custom-call(bf16[128,2048]{1,0:T(8,128)(2,1)S(1)} %collective-permute-done.2.refs_0_, bf16[128,2048]{1,0:T(8,128)(2,1)S(1)} %collective-permute-done.7.refs_1_, bf16[2,768,2048]{2,1,0:T(8,128)(2,1)S(1)} %get-tuple-element.51.refs_2_, ...), custom_call_target="tpu_custom_call" | custom-call | flops 805306368 | bytes 3145728 | tf_op jit(solution)/shard_map/expert_1_0/pallas_call | solution.py:112
  26.0 1.6 %collective-permute-start.8 = (bf16[128,2048]{1,0:T(8,128)(2,1)S(1)}, bf16[128,2048]{1,0:T(8,128)(2,1)S(1)}, u32[]{:S(2)}, u32[]{:S(2)}) collective-permute-start(bf16[128,2048]{1,0:T(8,128)(2,1)S(1)} %collective-permute-done.6.refs_0_), channel_id=1, source_target_pairs={{0,4},{1,3},{4,8},{5,1},{8,12},{9,5},{12,14},{13,9},{14,10},{15,13... | collective-permute-start | bytes 1572872 | tf_op jit(solution)/shard_map/ring_3_0/ppermute | solution.py:176
  27.7 3.5 %collective-permute-done.4.refs_0_.holder = bf16[136,2048]{1,0:T(8,128)(2,1)S(1)} collective-permute-done((bf16[136,2048]{1,0:T(8,128)(2,1)S(1)}, bf16[136,2048]{1,0:T(8,128)(2,1)S(1)}, u32[]{:S(2)}, u32[]{:S(2)}) %collective-permute-start.4) | collective-permute-done | bytes 557088 | tf_op jit(solution)/shard_map/ring_2_1/ppermute | solution.py:176
  33.0 2.6 %expert_2_0.1 = (bf16[128,2048]{1,0:T(8,128)(2,1)S(1)}, bf16[128,2048]{1,0:T(8,128)(2,1)S(1)}) custom-call(bf16[128,2048]{1,0:T(8,128)(2,1)S(1)} %collective-permute-done.6.refs_0_, bf16[128,2048]{1,0:T(8,128)(2,1)S(1)} %collective-permute-done.9.refs_1_, bf16[2,768,2048]{2,1,0:T(8,128)(2,1)S(1)} %get-tuple-element.51.refs_2_, ...), custom_call_target="tpu_custom_call" | custom-call | flops 805306368 | bytes 3145728 | tf_op jit(solution)/shard_map/expert_2_0/pallas_call | solution.py:112
  38.5 2.7 %expert_2_1.1 = (bf16[128,2048]{1,0:T(8,128)(2,1)S(1)}, bf16[128,2048]{1,0:T(8,128)(2,1)S(1)}) custom-call(bf16[136,2048]{1,0:T(8,128)(2,1)S(1)} %collective-permute-done.4.refs_0_.holder, bf16[128,2048]{1,0:T(8,128)(2,1)S(1)} %collective-permute-done.10.refs_1_, bf16[2,768,2048]{2,1,0:T(8,128)(2,1)S(1)} %get-tuple-element.51.refs_2_, ...), custom_call_target="tpu_custom_call" | custom-call | flops 805306368 | bytes 3145728 | tf_op jit(solution)/shard_map/expert_2_1/pallas_call | solution.py:112
  42.8 1.8 %collective-permute-start.11 = (bf16[72,2048]{1,0:T(8,128)(2,1)S(1)}, bf16[72,2048]{1,0:T(8,128)(2,1)S(1)}, u32[]{:S(2)}, u32[]{:S(2)}) collective-permute-start(bf16[72,2048]{1,0:T(8,128)(2,1)S(1)} %slice.34), channel_id=1, source_target_pairs={{0,4},{1,3},{4,8},{5,1},{8,12},{9,5},{12,14},{13,9},{14,10},{15,13... | collective-permute-start | bytes 884744 | tf_op jit(solution)/shard_map/ring_4_1/ppermute | solution.py:176
  44.6 2.6 %expert_3_0.1 = (bf16[128,2048]{1,0:T(8,128)(2,1)S(1)}, bf16[128,2048]{1,0:T(8,128)(2,1)S(1)}) custom-call(bf16[128,2048]{1,0:T(8,128)(2,1)S(1)} %collective-permute-done.8.refs_0_, bf16[128,2048]{1,0:T(8,128)(2,1)S(1)} %collective-permute-done.13.refs_1_, bf16[2,768,2048]{2,1,0:T(8,128)(2,1)S(1)} %get-tuple-element.51.refs_2_, ...), custom_call_target="tpu_custom_call" | custom-call | flops 805306368 | bytes 3145728 | tf_op jit(solution)/shard_map/expert_3_0/pallas_call | solution.py:112
  50.5 3.5 %expert_far_ring.1 = bf16[128,2048]{1,0:T(8,128)(2,1)} custom-call(bf16[72,2048]{1,0:T(8,128)(2,1)S(1)} %collective-permute-done.12.refs_0_, bf16[72,2048]{1,0:T(8,128)(2,1)S(1)} %collective-permute-done.11.refs_1_.holder, bf16[2,768,2048]{2,1,0:T(8,128)(2,1)S(1)} %get-tuple-element.51.refs_2_, bf16[768,2048]{1,0:T(8,128)(2,1)S(1)} %get-tuple-element.52.refs_3_), custom_call_target="tpu_custom_call" | custom-call | flops 402653184 | bytes 3145728 | tf_op jit(solution)/shard_map/expert_far_ring/pallas_call | solution.py:112
  56.1 2.8 %copy-done.1 = bf16[2,768,2048]{2,1,0:T(8,128)(2,1)S(1)} copy-done((bf16[2,768,2048]{2,1,0:T(8,128)(2,1)S(1)}, bf16[2,768,2048]{2,1,0:T(8,128)(2,1)}, u32[]{:S(2)}) %copy-start.1) | copy-done | bytes 6291480
  58.9 3.7 %expert_far_swapped.1 = bf16[128,2048]{1,0:T(8,128)(2,1)S(1)} custom-call(bf16[64,2048]{1,0:T(8,128)(2,1)} %collective-permute-done.14.refs_0_, bf16[64,2048]{1,0:T(8,128)(2,1)} %collective-permute-done.15.refs_1_, bf16[2,768,2048]{2,1,0:T(8,128)(2,1)S(1)} %copy-done.1, bf16[768,2048]{1,0:T(8,128)(2,1)S(1)} %get-tuple-element.52.refs_3_), custom_call_target="tpu_custom_call" | custom-call | flops 402653184 | bytes 3145728 | tf_op jit(solution)/shard_map/expert_far_swapped/pallas_call | solution.py:112
  65.1 2.6 %expert_3_1.1 = (bf16[128,2048]{1,0:T(8,128)(2,1)S(1)}, bf16[128,2048]{1,0:T(8,128)(2,1)S(1)}) custom-call(bf16[136,2048]{1,0:T(8,128)(2,1)S(1)} %copy-done.3, bf16[128,2048]{1,0:T(8,128)(2,1)S(1)} %collective-permute-done.17.refs_1_, bf16[2,768,2048]{2,1,0:T(8,128)(2,1)S(1)} %copy-done.1, bf16[768,2048]{1,0:T(8,128)(2,1)S(1)} %get-tuple-element.52.refs_3_), custom_call_target="tpu_custom_call" | custom-call | flops 80530640 | bytes 314572 | tf_op jit(solution)/shard_map/expert_3_1/pallas_call | solution.py:112
  71.0 4.8 %collective-permute-done.21.refs_0_ = bf16[72,2048]{1,0:T(8,128)(2,1)S(1)} collective-permute-done((bf16[72,2048]{1,0:T(8,128)(2,1)S(1)}, bf16[72,2048]{1,0:T(8,128)(2,1)S(1)}, u32[]{:S(2)}, u32[]{:S(2)}) %collective-permute-start.21) | collective-permute-done | bytes 294944 | tf_op jit(solution)/shard_map/back_4_1/ppermute | solution.py:176
  79.5 2.6 %expert_1_1.1 = (bf16[128,2048]{1,0:T(8,128)(2,1)S(1)}, bf16[128,2048]{1,0:T(8,128)(2,1)S(1)}) custom-call(bf16[136,2048]{1,0:T(8,128)(2,1)S(1)} %copy-done.8, bf16[128,2048]{1,0:T(8,128)(2,1)S(1)} %collective-permute-done.23.refs_1_, bf16[2,768,2048]{2,1,0:T(8,128)(2,1)S(1)} %copy-done.1, bf16[768,2048]{1,0:T(8,128)(2,1)S(1)} %get-tuple-element.52.refs_3_), custom_call_target="tpu_custom_call" | custom-call | flops 805306368 | bytes 3145728 | tf_op jit(solution)/shard_map/expert_1_1/pallas_call | solution.py:112
  82.2 3.8 %collective-permute-done.25.refs_0_ = bf16[128,2048]{1,0:T(8,128)(2,1)S(1)} collective-permute-done((bf16[128,2048]{1,0:T(8,128)(2,1)S(1)}, bf16[128,2048]{1,0:T(8,128)(2,1)S(1)}, u32[]{:S(2)}, u32[]{:S(2)}) %collective-permute-start.25) | collective-permute-done | bytes 524320 | tf_op jit(solution)/shard_map/back_3_0/ppermute | solution.py:176
  87.0 4.6 %collective-permute-done.27.refs_0_ = bf16[128,2048]{1,0:T(8,128)(2,1)S(1)} collective-permute-done((bf16[128,2048]{1,0:T(8,128)(2,1)S(1)}, bf16[128,2048]{1,0:T(8,128)(2,1)S(1)}, u32[]{:S(2)}, u32[]{:S(2)}) %collective-permute-start.27) | collective-permute-done | bytes 524320 | tf_op jit(solution)/shard_map/back_3_1/ppermute | solution.py:176
  92.6 4.6 %collective-permute-done.29.refs_0_ = bf16[128,2048]{1,0:T(8,128)(2,1)S(1)} collective-permute-done((bf16[128,2048]{1,0:T(8,128)(2,1)S(1)}, bf16[128,2048]{1,0:T(8,128)(2,1)S(1)}, u32[]{:S(2)}, u32[]{:S(2)}) %collective-permute-start.29) | collective-permute-done | bytes 524320 | tf_op jit(solution)/shard_map/back_2_0/ppermute | solution.py:176
  98.3 4.6 %collective-permute-done.32.refs_0_ = bf16[128,2048]{1,0:T(8,128)(2,1)S(1)} collective-permute-done((bf16[128,2048]{1,0:T(8,128)(2,1)S(1)}, bf16[128,2048]{1,0:T(8,128)(2,1)S(1)}, u32[]{:S(2)}, u32[]{:S(2)}) %collective-permute-start.32) | collective-permute-done | bytes 524320 | tf_op jit(solution)/shard_map/back_2_1/ppermute | solution.py:176
  103.2 5.2 %collective-permute-done.30.refs_0_ = bf16[128,2048]{1,0:T(8,128)(2,1)S(1)} collective-permute-done((bf16[128,2048]{1,0:T(8,128)(2,1)S(1)}, bf16[128,2048]{1,0:T(8,128)(2,1)S(1)}, u32[]{:S(2)}, u32[]{:S(2)}) %collective-permute-start.30) | collective-permute-done | bytes 524320 | tf_op jit(solution)/shard_map/back_1_0/ppermute | solution.py:176
  108.8 4.4 %collective-permute-done.33 = bf16[128,2048]{1,0:T(8,128)(2,1)S(1)} collective-permute-done((bf16[128,2048]{1,0:T(8,128)(2,1)S(1)}, bf16[128,2048]{1,0:T(8,128)(2,1)S(1)}, u32[]{:S(2)}, u32[]{:S(2)}) %collective-permute-start.33) | collective-permute-done | bytes 524320 | tf_op jit(solution)/shard_map/back_1_1/ppermute | solution.py:176
  (139 shorter events, 31.3 us)
Async XLA Ops:
  1.3 10.3 %collective-permute-start.2 = (bf16[128,2048]{1,0:T(8,128)(2,1)}, bf16[128,2048]{1,0:T(8,128)(2,1)S(1)}, u32[]{:S(2)}, u32[]{:S(2)}) collective-permute-start(bf16[128,2048]{1,0:T(8,128)(2,1)} %refs_0_), channel_id=1, source_target_pairs={{0,4},{1,3},{4,8},{5,1},{8,12},{9,5},{12,14},{13,9},{14,10},{15,13... | collective-permute-start | bytes 1572872 | tf_op jit(solution)/shard_map/ring_1_0/ppermute | solution.py:176
  4.4 17.2 %collective-permute-start.3 = (bf16[136,2048]{1,0:T(8,128)(2,1)S(1)}, bf16[136,2048]{1,0:T(8,128)(2,1)S(1)}, u32[]{:S(2)}, u32[]{:S(2)}) collective-permute-start(bf16[136,2048]{1,0:T(8,128)(2,1)S(1)} %pad_maximum_fusion.refs_1_.holder), channel_id=1, source_target_pairs={{0,4},{1,3},{4,8},{5,1},{8,12},{9,5},{12,14},{13,9},{14,10},{15,13... | collective-permute-start | bytes 1671176 | tf_op jit(solution)/shard_map/ring_1_1/ppermute | solution.py:176
  11.6 11.6 %collective-permute-start.7 = (bf16[128,2048]{1,0:T(8,128)(2,1)S(1)}, bf16[128,2048]{1,0:T(8,128)(2,1)S(1)}, u32[]{:S(2)}, u32[]{:S(2)}) collective-permute-start(bf16[128,2048]{1,0:T(8,128)(2,1)S(1)} %collective-permute-done.2.refs_0_), channel_id=1, source_target_pairs={{0,1},{1,0},{4,5},{5,4},{8,9},{9,8},{12,13},{13,12},{14,15},{15,14... | collective-permute-start | bytes 1572872 | tf_op jit(solution)/shard_map/swap_1_0/ppermute | solution.py:176
  11.6 14.3 %collective-permute-start.6 = (bf16[128,2048]{1,0:T(8,128)(2,1)S(1)}, bf16[128,2048]{1,0:T(8,128)(2,1)S(1)}, u32[]{:S(2)}, u32[]{:S(2)}) collective-permute-start(bf16[128,2048]{1,0:T(8,128)(2,1)S(1)} %collective-permute-done.2.refs_0_), channel_id=1, source_target_pairs={{0,4},{1,3},{4,8},{5,1},{8,12},{9,5},{12,14},{13,9},{14,10},{15,13... | collective-permute-start | bytes 1572872 | tf_op jit(solution)/shard_map/ring_2_0/ppermute | solution.py:176
  21.6 9.6 %collective-permute-start.4 = (bf16[136,2048]{1,0:T(8,128)(2,1)S(1)}, bf16[136,2048]{1,0:T(8,128)(2,1)S(1)}, u32[]{:S(2)}, u32[]{:S(2)}) collective-permute-start(bf16[136,2048]{1,0:T(8,128)(2,1)S(1)} %collective-permute-done.3.refs_0_.holder), channel_id=1, source_target_pairs={{0,4},{1,3},{4,8},{5,1},{8,12},{9,5},{12,14},{13,9},{14,10},{15,13... | collective-permute-start | bytes 1671176 | tf_op jit(solution)/shard_map/ring_2_1/ppermute | solution.py:176
  26.0 10.8 %collective-permute-start.8 = (bf16[128,2048]{1,0:T(8,128)(2,1)S(1)}, bf16[128,2048]{1,0:T(8,128)(2,1)S(1)}, u32[]{:S(2)}, u32[]{:S(2)}) collective-permute-start(bf16[128,2048]{1,0:T(8,128)(2,1)S(1)} %collective-permute-done.6.refs_0_), channel_id=1, source_target_pairs={{0,4},{1,3},{4,8},{5,1},{8,12},{9,5},{12,14},{13,9},{14,10},{15,13... | collective-permute-start | bytes 1572872 | tf_op jit(solution)/shard_map/ring_3_0/ppermute | solution.py:176
  31.3 11.5 %collective-permute-start.5 = (bf16[136,2048]{1,0:T(8,128)(2,1)S(1)}, bf16[136,2048]{1,0:T(8,128)(2,1)S(1)}, u32[]{:S(2)}, u32[]{:S(2)}) collective-permute-start(bf16[136,2048]{1,0:T(8,128)(2,1)S(1)} %collective-permute-done.4.refs_0_.holder), channel_id=1, source_target_pairs={{0,4},{1,3},{4,8},{5,1},{8,12},{9,5},{12,14},{13,9},{14,10},{15,13... | collective-permute-start | bytes 1671176 | tf_op jit(solution)/shard_map/ring_3_1/ppermute | solution.py:176
  36.8 7.8 %collective-permute-start.13 = (bf16[128,2048]{1,0:T(8,128)(2,1)S(1)}, bf16[128,2048]{1,0:T(8,128)(2,1)S(1)}, u32[]{:S(2)}, u32[]{:S(2)}) collective-permute-start(bf16[128,2048]{1,0:T(8,128)(2,1)S(1)} %collective-permute-done.8.refs_0_), channel_id=1, source_target_pairs={{0,1},{1,0},{4,5},{5,4},{8,9},{9,8},{12,13},{13,12},{14,15},{15,14... | collective-permute-start | bytes 1572872 | tf_op jit(solution)/shard_map/swap_3_0/ppermute | solution.py:176
  36.8 10.5 %collective-permute-start.12 = (bf16[72,2048]{1,0:T(8,128)(2,1)S(1)}, bf16[72,2048]{1,0:T(8,128)(2,1)S(1)}, u32[]{:S(2)}, u32[]{:S(2)}) collective-permute-start(bf16[72,2048]{1,0:T(8,128)(2,1)S(1)} %slice.35), channel_id=1, source_target_pairs={{0,4},{1,3},{4,8},{5,1},{8,12},{9,5},{12,14},{13,9},{14,10},{15,13... | collective-permute-start | bytes 884744 | tf_op jit(solution)/shard_map/ring_4_0/ppermute | solution.py:176
  48.1 8.0 %collective-permute-start.14 = (bf16[64,2048]{1,0:T(8,128)(2,1)}, bf16[64,2048]{1,0:T(8,128)(2,1)}, u32[]{:S(2)}, u32[]{:S(2)}) collective-permute-start(bf16[64,2048]{1,0:T(8,128)(2,1)} %slice.36), channel_id=1, source_target_pairs={{0,1},{1,0},{4,5},{5,4},{8,9},{9,8},{12,13},{13,12},{14,15},{15,14... | collective-permute-start | bytes 786440 | tf_op jit(solution)/shard_map/swap_4_0/ppermute | solution.py:176
  54.0 8.7 %collective-permute-start.16 = (bf16[128,2048]{1,0:T(8,128)(2,1)}, bf16[128,2048]{1,0:T(8,128)(2,1)}, u32[]{:S(2)}, u32[]{:S(2)}) collective-permute-start(bf16[128,2048]{1,0:T(8,128)(2,1)} %expert_far_ring.1), channel_id=1, source_target_pairs={{0,1},{1,0},{4,5},{5,4},{8,9},{9,8},{12,13},{13,12},{14,15},{15,14... | collective-permute-start | bytes 1572872 | tf_op jit(solution)/shard_map/give_far/ppermute | solution.py:176
  55.6 8.7 %collective-permute-start.17 = (bf16[128,2048]{1,0:T(8,128)(2,1)S(1)}, bf16[128,2048]{1,0:T(8,128)(2,1)S(1)}, u32[]{:S(2)}, u32[]{:S(2)}) collective-permute-start(bf16[128,2048]{1,0:T(8,128)(2,1)S(1)} %slice.42), channel_id=1, source_target_pairs={{0,1},{1,0},{4,5},{5,4},{8,9},{9,8},{12,13},{13,12},{14,15},{15,14... | collective-permute-start | bytes 1572872 | tf_op jit(solution)/shard_map/swap_3_1/ppermute | solution.py:176
  55.6 14.2 %collective-permute-start.18 = (bf16[128,2048]{1,0:T(8,128)(2,1)}, bf16[128,2048]{1,0:T(8,128)(2,1)S(1)}, u32[]{:S(2)}, u32[]{:S(2)}) collective-permute-start(bf16[128,2048]{1,0:T(8,128)(2,1)} %copy-done.30), channel_id=1, source_target_pairs={{0,1},{1,0},{4,5},{5,4},{8,9},{9,8},{12,13},{13,12},{14,15},{15,14... | collective-permute-start | bytes 1572872 | tf_op jit(solution)/shard_map/give_3_0/ppermute | solution.py:176
  67.7 8.1 %collective-permute-start.20 = (bf16[128,2048]{1,0:T(8,128)(2,1)S(1)}, bf16[128,2048]{1,0:T(8,128)(2,1)S(1)}, u32[]{:S(2)}, u32[]{:S(2)}) collective-permute-start(bf16[128,2048]{1,0:T(8,128)(2,1)S(1)} %get-tuple-element.72), channel_id=1, source_target_pairs={{0,1},{1,0},{4,5},{5,4},{8,9},{9,8},{12,13},{13,12},{14,15},{15,14... | collective-permute-start | bytes 1572872 | tf_op jit(solution)/shard_map/give_3_1/ppermute | solution.py:176
  76.8 9.2 %collective-permute-start.25 = (bf16[128,2048]{1,0:T(8,128)(2,1)S(1)}, bf16[128,2048]{1,0:T(8,128)(2,1)S(1)}, u32[]{:S(2)}, u32[]{:S(2)}) collective-permute-start(bf16[128,2048]{1,0:T(8,128)(2,1)S(1)} %shard_map.57), channel_id=1, source_target_pairs={{0,2},{1,5},{4,0},{5,9},{8,4},{9,13},{12,8},{13,15},{14,12},{15,11... | collective-permute-start | bytes 1572872 | tf_op jit(solution)/shard_map/back_3_0/ppermute | solution.py:176
  77.5 9.6 %collective-permute-start.26 = (bf16[128,2048]{1,0:T(8,128)(2,1)S(1)}, bf16[128,2048]{1,0:T(8,128)(2,1)S(1)}, u32[]{:S(2)}, u32[]{:S(2)}) collective-permute-start(bf16[128,2048]{1,0:T(8,128)(2,1)S(1)} %copy-done.27), channel_id=1, source_target_pairs={{0,1},{1,0},{4,5},{5,4},{8,9},{9,8},{12,13},{13,12},{14,15},{15,14... | collective-permute-start | bytes 1572872 | tf_op jit(solution)/shard_map/give_2_1/ppermute | solution.py:176
  78.2 13.4 %collective-permute-start.27 = (bf16[128,2048]{1,0:T(8,128)(2,1)S(1)}, bf16[128,2048]{1,0:T(8,128)(2,1)S(1)}, u32[]{:S(2)}, u32[]{:S(2)}) collective-permute-start(bf16[128,2048]{1,0:T(8,128)(2,1)S(1)} %shard_map.58), channel_id=1, source_target_pairs={{0,2},{1,5},{4,0},{5,9},{8,4},{9,13},{12,8},{13,15},{14,12},{15,11... | collective-permute-start | bytes 1572872 | tf_op jit(solution)/shard_map/back_3_1/ppermute | solution.py:176
  79.1 13.6 %collective-permute-start.28 = (bf16[128,2048]{1,0:T(8,128)(2,1)S(1)}, bf16[128,2048]{1,0:T(8,128)(2,1)S(1)}, u32[]{:S(2)}, u32[]{:S(2)}) collective-permute-start(bf16[128,2048]{1,0:T(8,128)(2,1)S(1)} %copy-done.19), channel_id=1, source_target_pairs={{0,1},{1,0},{4,5},{5,4},{8,9},{9,8},{12,13},{13,12},{14,15},{15,14... | collective-permute-start | bytes 1572872 | tf_op jit(solution)/shard_map/give_1_0/ppermute | solution.py:176
  86.3 10.9 %collective-permute-start.29 = (bf16[128,2048]{1,0:T(8,128)(2,1)S(1)}, bf16[128,2048]{1,0:T(8,128)(2,1)S(1)}, u32[]{:S(2)}, u32[]{:S(2)}) collective-permute-start(bf16[128,2048]{1,0:T(8,128)(2,1)S(1)} %shard_map.59), channel_id=1, source_target_pairs={{0,2},{1,5},{4,0},{5,9},{8,4},{9,13},{12,8},{13,15},{14,12},{15,11... | collective-permute-start | bytes 1572872 | tf_op jit(solution)/shard_map/back_2_0/ppermute | solution.py:176
  87.0 11.3 %collective-permute-start.31 = (bf16[128,2048]{1,0:T(8,128)(2,1)S(1)}, bf16[128,2048]{1,0:T(8,128)(2,1)S(1)}, u32[]{:S(2)}, u32[]{:S(2)}) collective-permute-start(bf16[128,2048]{1,0:T(8,128)(2,1)S(1)} %get-tuple-element.86), channel_id=1, source_target_pairs={{0,1},{1,0},{4,5},{5,4},{8,9},{9,8},{12,13},{13,12},{14,15},{15,14... | collective-permute-start | bytes 1572872 | tf_op jit(solution)/shard_map/give_1_1/ppermute | solution.py:176
  91.9 10.9 %collective-permute-start.32 = (bf16[128,2048]{1,0:T(8,128)(2,1)S(1)}, bf16[128,2048]{1,0:T(8,128)(2,1)S(1)}, u32[]{:S(2)}, u32[]{:S(2)}) collective-permute-start(bf16[128,2048]{1,0:T(8,128)(2,1)S(1)} %shard_map.60), channel_id=1, source_target_pairs={{0,2},{1,5},{4,0},{5,9},{8,4},{9,13},{12,8},{13,15},{14,12},{15,11... | collective-permute-start | bytes 1572872 | tf_op jit(solution)/shard_map/back_2_1/ppermute | solution.py:176
  92.6 10.6 %collective-permute-start.22 = (bf16[128,2048]{1,0:T(8,128)(2,1)S(1)}, bf16[128,2048]{1,0:T(8,128)(2,1)S(1)}, u32[]{:S(2)}, u32[]{:S(2)}) collective-permute-start(bf16[128,2048]{1,0:T(8,128)(2,1)S(1)} %copy-done.15), channel_id=1, source_target_pairs={{0,1},{1,0},{4,5},{5,4},{8,9},{9,8},{12,13},{13,12},{14,15},{15,14... | collective-permute-start | bytes 1572872 | tf_op jit(solution)/shard_map/give_0_0/ppermute | solution.py:176
  97.6 10.9 %collective-permute-start.30 = (bf16[128,2048]{1,0:T(8,128)(2,1)S(1)}, bf16[128,2048]{1,0:T(8,128)(2,1)S(1)}, u32[]{:S(2)}, u32[]{:S(2)}) collective-permute-start(bf16[128,2048]{1,0:T(8,128)(2,1)S(1)} %shard_map.61), channel_id=1, source_target_pairs={{0,2},{1,5},{4,0},{5,9},{8,4},{9,13},{12,8},{13,15},{14,12},{15,11... | collective-permute-start | bytes 1572872 | tf_op jit(solution)/shard_map/back_1_0/ppermute | solution.py:176
  103.1 10.0 %collective-permute-start.33 = (bf16[128,2048]{1,0:T(8,128)(2,1)S(1)}, bf16[128,2048]{1,0:T(8,128)(2,1)S(1)}, u32[]{:S(2)}, u32[]{:S(2)}) collective-permute-start(bf16[128,2048]{1,0:T(8,128)(2,1)S(1)} %shard_map.63), channel_id=1, source_target_pairs={{0,3},{1,4},{4,1},{5,8},{8,5},{9,12},{12,9},{13,14},{14,13},{15,10... | collective-permute-start | bytes 1572872 | tf_op jit(solution)/shard_map/back_1_1/ppermute | solution.py:176
  (41 other events, 269.5 us)

commit v12 on v11

--- a/solution.py
+++ b/solution.py
@@ -124,15 +124,15 @@
     )(*blocks, *weights)
 
 
-def weighted_kernel(kind, token, low, part_rows, expert_ref, holder, mine, theirs, *refs):
+def weighted_kernel(kind, first, height, low, part_rows, expert_ref, holder, mine, theirs, *refs):
     *arrived, out = refs
-    height = mine.shape[0]
     last = holder.shape[0] - GATE_ROWS
     near, far = (holder[last:, (2 * kind + i) * LANES : (2 * kind + i + 1) * LANES].astype(jnp.float32) for i in (0, 1))
     wanted = lax.broadcasted_iota(jnp.int32, near.shape, 0) == expert_ref[0]
     line = jnp.sum(jnp.where(wanted, near + far, 0.0), axis=0, keepdims=True)
-    weight = jnp.broadcast_to(line, near.shape).T[token : token + height, :1]
-    value = weight * (mine[...].astype(jnp.float32) + theirs[...].astype(jnp.float32))
+    weight = jnp.broadcast_to(line, near.shape).T[first : first + height, :1]
+    value = mine[...].astype(jnp.float32) + theirs[first : first + height, :].astype(jnp.float32)
+    value = weight * value
     out[:height, :] = value.astype(out.dtype)
     if height < out.shape[0]:
         out[height:, :] = jnp.zeros((out.shape[0] - height, out.shape[1]), out.dtype)
@@ -141,12 +141,13 @@
         out[part, :] = (value[part] + arrived[0][:part_rows, :].astype(jnp.float32)).astype(out.dtype)
 
 
-def weighted(expert, holder, kind, mine, theirs, *arrived, token=0, low=0, part=None, more=0, dtype=jnp.bfloat16):
+def weighted(expert, holder, kind, mine, theirs, *arrived, first=0, low=0, part=None, more=0, dtype=jnp.bfloat16):
     whole = pl.BlockSpec(memory_space=pltpu.VMEM)
-    size = mine.size
+    height = mine.shape[0]
+    size = height * mine.shape[1]
     return pl.pallas_call(
-        functools.partial(weighted_kernel, kind, token, low, part or mine.shape[0]),
-        out_shape=jax.ShapeDtypeStruct((mine.shape[0] + more, mine.shape[1]), dtype),
+        functools.partial(weighted_kernel, kind, first, height, low, part or height),
+        out_shape=jax.ShapeDtypeStruct((height + more, mine.shape[1]), dtype),
         in_specs=[pl.BlockSpec(memory_space=pltpu.SMEM)] + [whole] * (3 + len(arrived)),
         out_specs=whole,
         compiler_params=pltpu.CompilerParams(vmem_limit_bytes=10 << 20),
@@ -197,10 +198,10 @@
 
     results, holders = {}, {0: packed}
     with jax.named_scope("expert_0"):
-        inputs = [after(tokens, ring[0]), packed]
+        inputs = [tokens, packed]
         own, given, *near = half_expert([rows] * 2, inputs, [gate_up, down_proj], load=True)
     results[0, 0] = own, given
-    ring[1] = after(ring[1], own)
+    ring[0] = after(ring[0], own)
 
     def expert_rows(step, c, inputs, **options):
         with jax.named_scope(f"expert_{step}_{c}"):
@@ -217,7 +218,7 @@
     for step in range(1, far):
         holders[step] = ring[1]
         swapped = [
-            send(block[:rows], cores, f"swap_{step}_{c}") for c, block in enumerate(ring[: 1 if step == 1 else 2])
+            send(block, cores, f"swap_{step}_{c}") for c, block in enumerate(ring[: 1 if step == 1 else 2])
         ]
         blocks = list(ring)
         if step < far - 1:
@@ -238,7 +239,7 @@
 
     with jax.named_scope("expert_far_ring"):
         (given,) = half_expert([half] * 2, ring, near, split=1)
-    swapped = [send(block[:half], cores, f"swap_{far}_{c}") for c, block in enumerate(ring)]
+    swapped = [send(block, cores, f"swap_{far}_{c}") for c, block in enumerate(ring)]
     swapped[0] = after(swapped[0], given)
     given = send(given, cores, "give_far")
     with jax.named_scope("expert_far_swapped"):
@@ -246,9 +247,10 @@
 
     late = []
     earlier = kept
-    for c, part in enumerate((slice(half, rows), slice(0, half))):
-        mine = after(kept[part], earlier)
-        earlier = weighted(expert, ring[1], c, mine, given[part], token=half if c == 0 else 0, more=GATE_ROWS)
+    for c in chains:
+        first = (1 - c) * half
+        mine = after(kept[first : first + half], earlier)
+        earlier = weighted(expert, ring[1], c, mine, given, first=first, more=GATE_ROWS)
         late.append(send(earlier, back, f"back_{far}_{c}"))
     earlier = expert_rows(far - 1, 1, [after(last[0], earlier), last[1]], cost=0.2)
     sums = []
@@ -258,10 +260,10 @@
         earlier = weighted(expert, holders[far - 1], c, after(mine, earlier), theirs, late[c], low=low, part=half)
         sums.append(send(earlier, back, f"back_{far - 1}_{c}"))
         if c == 0:
+            swapped = send(after(delayed, earlier), cores, "swap_1_1")
             for step in range(far - 2, 1, -1):
                 for c2 in chains:
                     give(step, c2, earlier)
-    swapped = send(after(delayed, earlier)[:rows], cores, "swap_1_1")
     give(1, 0, earlier)
     give(0, 0, earlier)
     earlier = expert_rows(1, 1, [after(delayed, earlier), swapped])

time: 115 us -> 108 us (0.939)
  waiting for transfers between devices: 45.6 us -> 31.4 us
  starting transfers between devices: 24.5 us -> 32.3 us
  local copies, waits for them, and re-layouts: 11.3 us -> 8.14 us
  Pallas kernels: 30.4 us -> 33.5 us
    ppermute x34, waiting for transfers between devices: 45.6 us -> 31.4 us  [send(): return lax.ppermute(value, 'blk', pairs)]
    ppermute x34, starting transfers between devices: 24.5 us -> 32.3 us  [send(): return lax.ppermute(value, 'blk', pairs)]
    slice x7 -> x1, local copies, waits for them, and re-layouts: 3.8 us -> 0.04 us  [by_tokens(): mine = after(kept[first:first + half], earlier)]
    pallas_call x9, Pallas kernels: 2.44 us -> 4.58 us  [weighted(): pl.pallas_call(functools.partial(weighted_kernel, kind, first, height, lo...]
  transfers between devices with their start and end apart: 34 -> 34, of which waited for: 13 -> 12; matrix products, arithmetic and copies ran while one was open for 4% -> 1% of each run, Pallas kernels for 26% -> 31%
where the time goes in v12:
time: 108 us; the launch traced here: 107 us
  Pallas kernels  33.5 us (31%)
  starting transfers between devices  32.3 us (30%)
  waiting for transfers between devices  31.4 us (29%)
  local copies, waits for them, and re-layouts  8.14 us (8%)
  other arithmetic  1.67 us (2%)
    ppermute x34, starting transfers between devices, send(): return lax.ppermute(value, 'blk', pairs)  32.3 us
    ppermute x34, waiting for transfers between devices, send(): return lax.ppermute(value, 'blk', pairs)  31.4 us
    pallas_call x9, Pallas kernels, half_expert(): pl.pallas_call(functools.partial(half_expert_kernel, tuple(heights), load...  28.9 us
    unnamed x62, local copies, waits for them, and re-layouts  8.06 us
    pallas_call x9, Pallas kernels, weighted(): pl.pallas_call(functools.partial(weighted_kernel, kind, first, height, lo...  4.58 us
  transfers between devices with their start and end apart: 34, of which 12 were waited for; matrix products, arithmetic and copies ran while one was open for 1% of the time, Pallas kernels for 31%

profile of v12, /device:TPU:0, one launch (start us, length us, event | category | flops | bytes accessed | tf_op | source)
XLA Modules:
  0.0 107.4 jit_solution(8972987486101212826)
XLA Ops:
  1.3 3.0 %collective-permute-start.5 = (bf16[128,2048]{1,0:T(8,128)(2,1)}, bf16[128,2048]{1,0:T(8,128)(2,1)S(1)}, u32[]{:S(2)}, u32[]{:S(2)}) collective-permute-start(bf16[128,2048]{1,0:T(8,128)(2,1)} %refs_0_.1), channel_id=1, source_target_pairs={{0,4},{1,3},{4,8},{5,1},{8,12},{9,5},{12,14},{13,9},{14,10},{15,13... | collective-permute-start | bytes 1572872 | tf_op jit(solution)/shard_map/ring_1_0/ppermute | solution.py:177
  9.0 4.9 %expert_0.1 = (bf16[128,2048]{1,0:T(8,128)(2,1)S(1)}, bf16[128,2048]{1,0:T(8,128)(2,1)S(1)}, bf16[2,768,2048]{2,1,0:T(8,128)(2,1)S(1)}, bf16[768,2048]{1,0:T(8,128)(2,1)S(1)}) custom-call(bf16[128,2048]{1,0:T(8,128)(2,1)S(1)} %copy-done.11, bf16[136,2048]{1,0:T(8,128)(2,1)S(1)} %pad_maximum_fusion.refs_1_.holder, bf16[2,768,2048]{2,1,0:T(8,128)(2,1)} %refs_2_.1, ...), custom_call_target="tpu_custom_call" | custom-call | flops 805306368 | bytes 3145728 | tf_op jit(solution)/shard_map/expert_0/pallas_call | solution.py:112
  17.6 2.1 %collective-permute-start.3 = (bf16[136,2048]{1,0:T(8,128)(2,1)S(1)}, bf16[136,2048]{1,0:T(8,128)(2,1)S(1)}, u32[]{:S(2)}, u32[]{:S(2)}) collective-permute-start(bf16[136,2048]{1,0:T(8,128)(2,1)S(1)} %collective-permute-done.2.refs_0_.holder), channel_id=1, source_target_pairs={{0,4},{1,3},{4,8},{5,1},{8,12},{9,5},{12,14},{13,9},{14,10},{15,13... | collective-permute-start | bytes 1671176 | tf_op jit(solution)/shard_map/ring_2_1/ppermute | solution.py:177
  19.7 2.6 %expert_1_0.1 = (bf16[128,2048]{1,0:T(8,128)(2,1)S(1)}, bf16[128,2048]{1,0:T(8,128)(2,1)S(1)}) custom-call(bf16[128,2048]{1,0:T(8,128)(2,1)S(1)} %collective-permute-done.5.refs_0_, bf16[128,2048]{1,0:T(8,128)(2,1)S(1)} %collective-permute-done.7.refs_1_, bf16[2,768,2048]{2,1,0:T(8,128)(2,1)S(1)} %get-tuple-element.50.refs_2_, ...), custom_call_target="tpu_custom_call" | custom-call | flops 805306368 | bytes 3145728 | tf_op jit(solution)/shard_map/expert_1_0/pallas_call | solution.py:112
  23.2 2.1 %collective-permute-start.8 = (bf16[128,2048]{1,0:T(8,128)(2,1)S(1)}, bf16[128,2048]{1,0:T(8,128)(2,1)S(1)}, u32[]{:S(2)}, u32[]{:S(2)}) collective-permute-start(bf16[128,2048]{1,0:T(8,128)(2,1)S(1)} %collective-permute-done.6.refs_0_), channel_id=1, source_target_pairs={{0,4},{1,3},{4,8},{5,1},{8,12},{9,5},{12,14},{13,9},{14,10},{15,13... | collective-permute-start | bytes 1572872 | tf_op jit(solution)/shard_map/ring_3_0/ppermute | solution.py:177
  25.3 3.9 %collective-permute-done.3.refs_0_.holder = bf16[136,2048]{1,0:T(8,128)(2,1)S(1)} collective-permute-done((bf16[136,2048]{1,0:T(8,128)(2,1)S(1)}, bf16[136,2048]{1,0:T(8,128)(2,1)S(1)}, u32[]{:S(2)}, u32[]{:S(2)}) %collective-permute-start.3) | collective-permute-done | bytes 557088 | tf_op jit(solution)/shard_map/ring_2_1/ppermute | solution.py:177
  29.2 2.1 %collective-permute-start.4 = (bf16[136,2048]{1,0:T(8,128)(2,1)S(1)}, bf16[136,2048]{1,0:T(8,128)(2,1)S(1)}, u32[]{:S(2)}, u32[]{:S(2)}) collective-permute-start(bf16[136,2048]{1,0:T(8,128)(2,1)S(1)} %collective-permute-done.3.refs_0_.holder), channel_id=1, source_target_pairs={{0,4},{1,3},{4,8},{5,1},{8,12},{9,5},{12,14},{13,9},{14,10},{15,13... | collective-permute-start | bytes 1671176 | tf_op jit(solution)/shard_map/ring_3_1/ppermute | solution.py:177
  31.3 2.6 %expert_2_0.1 = (bf16[128,2048]{1,0:T(8,128)(2,1)S(1)}, bf16[128,2048]{1,0:T(8,128)(2,1)S(1)}) custom-call(bf16[128,2048]{1,0:T(8,128)(2,1)S(1)} %collective-permute-done.6.refs_0_, bf16[128,2048]{1,0:T(8,128)(2,1)S(1)} %collective-permute-done.9.refs_1_, bf16[2,768,2048]{2,1,0:T(8,128)(2,1)S(1)} %get-tuple-element.50.refs_2_, ...), custom_call_target="tpu_custom_call" | custom-call | flops 805306368 | bytes 3145728 | tf_op jit(solution)/shard_map/expert_2_0/pallas_call | solution.py:112
  35.0 2.0 %collective-permute-start.12 = (bf16[72,2048]{1,0:T(8,128)(2,1)S(1)}, bf16[72,2048]{1,0:T(8,128)(2,1)}, u32[]{:S(2)}, u32[]{:S(2)}) collective-permute-start(bf16[72,2048]{1,0:T(8,128)(2,1)S(1)} %slice.13), channel_id=1, source_target_pairs={{0,4},{1,3},{4,8},{5,1},{8,12},{9,5},{12,14},{13,9},{14,10},{15,13... | collective-permute-start | bytes 884744 | tf_op jit(solution)/shard_map/ring_4_0/ppermute | solution.py:177
  37.0 2.7 %expert_2_1.1 = (bf16[128,2048]{1,0:T(8,128)(2,1)S(1)}, bf16[128,2048]{1,0:T(8,128)(2,1)S(1)}) custom-call(bf16[136,2048]{1,0:T(8,128)(2,1)S(1)} %collective-permute-done.3.refs_0_.holder, bf16[136,2048]{1,0:T(8,128)(2,1)S(1)} %collective-permute-done.10.refs_1_, bf16[2,768,2048]{2,1,0:T(8,128)(2,1)S(1)} %get-tuple-element.50.refs_2_, ...), custom_call_target="tpu_custom_call" | custom-call | flops 805306368 | bytes 3145728 | tf_op jit(solution)/shard_map/expert_2_1/pallas_call | solution.py:112
  40.8 2.3 %collective-permute-start.11 = (bf16[72,2048]{1,0:T(8,128)(2,1)S(1)}, bf16[72,2048]{1,0:T(8,128)(2,1)S(1)}, u32[]{:S(2)}, u32[]{:S(2)}) collective-permute-start(bf16[72,2048]{1,0:T(8,128)(2,1)S(1)} %slice.12), channel_id=1, source_target_pairs={{0,4},{1,3},{4,8},{5,1},{8,12},{9,5},{12,14},{13,9},{14,10},{15,13... | collective-permute-start | bytes 884744 | tf_op jit(solution)/shard_map/ring_4_1/ppermute | solution.py:177
  43.1 2.6 %expert_3_0.1 = (bf16[128,2048]{1,0:T(8,128)(2,1)S(1)}, bf16[128,2048]{1,0:T(8,128)(2,1)S(1)}) custom-call(bf16[128,2048]{1,0:T(8,128)(2,1)S(1)} %collective-permute-done.8.refs_0_, bf16[128,2048]{1,0:T(8,128)(2,1)S(1)} %collective-permute-done.13.refs_1_, bf16[2,768,2048]{2,1,0:T(8,128)(2,1)S(1)} %get-tuple-element.50.refs_2_, ...), custom_call_target="tpu_custom_call" | custom-call | flops 805306368 | bytes 3145728 | tf_op jit(solution)/shard_map/expert_3_0/pallas_call | solution.py:112
  47.8 4.4 %expert_far_ring.1 = bf16[128,2048]{1,0:T(8,128)(2,1)} custom-call(bf16[72,2048]{1,0:T(8,128)(2,1)} %collective-permute-done.12.refs_0_, bf16[72,2048]{1,0:T(8,128)(2,1)S(1)} %collective-permute-done.11.refs_1_.holder, bf16[2,768,2048]{2,1,0:T(8,128)(2,1)S(1)} %get-tuple-element.50.refs_2_, bf16[768,2048]{1,0:T(8,128)(2,1)S(1)} %get-tuple-element.51.refs_3_), custom_call_target="tpu_custom_call" | custom-call | flops 402653184 | bytes 3145728 | tf_op jit(solution)/shard_map/expert_far_ring/pallas_call | solution.py:112
  53.2 2.8 %copy-done.1 = bf16[2,768,2048]{2,1,0:T(8,128)(2,1)S(1)} copy-done((bf16[2,768,2048]{2,1,0:T(8,128)(2,1)S(1)}, bf16[2,768,2048]{2,1,0:T(8,128)(2,1)}, u32[]{:S(2)}) %copy-start.1) | copy-done | bytes 6291480
  56.0 3.7 %expert_far_swapped.1 = bf16[128,2048]{1,0:T(8,128)(2,1)S(1)} custom-call(bf16[72,2048]{1,0:T(8,128)(2,1)} %collective-permute-done.14.refs_0_, bf16[72,2048]{1,0:T(8,128)(2,1)} %collective-permute-done.15.refs_1_, bf16[2,768,2048]{2,1,0:T(8,128)(2,1)S(1)} %copy-done.1, bf16[768,2048]{1,0:T(8,128)(2,1)S(1)} %get-tuple-element.51.refs_3_), custom_call_target="tpu_custom_call" | custom-call | flops 402653184 | bytes 3145728 | tf_op jit(solution)/shard_map/expert_far_swapped/pallas_call | solution.py:112
  61.0 2.1 %collective-permute-start.19 = (bf16[72,2048]{1,0:T(8,128)(2,1)S(1)}, bf16[72,2048]{1,0:T(8,128)(2,1)S(1)}, u32[]{:S(2)}, u32[]{:S(2)}) collective-permute-start(bf16[72,2048]{1,0:T(8,128)(2,1)S(1)} %shard_map.55), channel_id=1, source_target_pairs={{0,2},{1,5},{4,0},{5,9},{8,4},{9,13},{12,8},{13,15},{14,12},{15,11... | collective-permute-start | bytes 884744 | tf_op jit(solution)/shard_map/back_4_0/ppermute | solution.py:177
  66.0 2.6 %expert_3_1.1 = (bf16[128,2048]{1,0:T(8,128)(2,1)S(1)}, bf16[128,2048]{1,0:T(8,128)(2,1)S(1)}) custom-call(bf16[136,2048]{1,0:T(8,128)(2,1)S(1)} %copy-done.6, bf16[136,2048]{1,0:T(8,128)(2,1)S(1)} %collective-permute-done.17.refs_1_, bf16[2,768,2048]{2,1,0:T(8,128)(2,1)S(1)} %copy-done.1, bf16[768,2048]{1,0:T(8,128)(2,1)S(1)} %get-tuple-element.51.refs_3_), custom_call_target="tpu_custom_call" | custom-call | flops 80530640 | bytes 314572 | tf_op jit(solution)/shard_map/expert_3_1/pallas_call | solution.py:112
  74.1 2.7 %expert_1_1.1 = (bf16[128,2048]{1,0:T(8,128)(2,1)S(1)}, bf16[128,2048]{1,0:T(8,128)(2,1)S(1)}) custom-call(bf16[136,2048]{1,0:T(8,128)(2,1)S(1)} %copy-done.8, bf16[136,2048]{1,0:T(8,128)(2,1)S(1)} %collective-permute-done.23.refs_1_, bf16[2,768,2048]{2,1,0:T(8,128)(2,1)S(1)} %copy-done.1, bf16[768,2048]{1,0:T(8,128)(2,1)S(1)} %get-tuple-element.51.refs_3_), custom_call_target="tpu_custom_call" | custom-call | flops 805306368 | bytes 3145728 | tf_op jit(solution)/shard_map/expert_1_1/pallas_call | solution.py:112
  76.8 2.2 %collective-permute-done.25.refs_0_ = bf16[128,2048]{1,0:T(8,128)(2,1)S(1)} collective-permute-done((bf16[128,2048]{1,0:T(8,128)(2,1)S(1)}, bf16[128,2048]{1,0:T(8,128)(2,1)S(1)}, u32[]{:S(2)}, u32[]{:S(2)}) %collective-permute-start.25) | collective-permute-done | bytes 524320 | tf_op jit(solution)/shard_map/back_3_0/ppermute | solution.py:177
  80.9 3.7 %collective-permute-done.27.refs_0_ = bf16[128,2048]{1,0:T(8,128)(2,1)S(1)} collective-permute-done((bf16[128,2048]{1,0:T(8,128)(2,1)S(1)}, bf16[128,2048]{1,0:T(8,128)(2,1)S(1)}, u32[]{:S(2)}, u32[]{:S(2)}) %collective-permute-start.27) | collective-permute-done | bytes 524320 | tf_op jit(solution)/shard_map/back_3_1/ppermute | solution.py:177
  86.5 3.7 %collective-permute-done.29.refs_0_ = bf16[128,2048]{1,0:T(8,128)(2,1)S(1)} collective-permute-done((bf16[128,2048]{1,0:T(8,128)(2,1)S(1)}, bf16[128,2048]{1,0:T(8,128)(2,1)S(1)}, u32[]{:S(2)}, u32[]{:S(2)}) %collective-permute-start.29) | collective-permute-done | bytes 524320 | tf_op jit(solution)/shard_map/back_2_0/ppermute | solution.py:177
  92.1 3.6 %collective-permute-done.32.refs_0_ = bf16[128,2048]{1,0:T(8,128)(2,1)S(1)} collective-permute-done((bf16[128,2048]{1,0:T(8,128)(2,1)S(1)}, bf16[128,2048]{1,0:T(8,128)(2,1)S(1)}, u32[]{:S(2)}, u32[]{:S(2)}) %collective-permute-start.32) | collective-permute-done | bytes 524320 | tf_op jit(solution)/shard_map/back_2_1/ppermute | solution.py:177
  97.0 4.4 %collective-permute-done.30.refs_0_ = bf16[128,2048]{1,0:T(8,128)(2,1)S(1)} collective-permute-done((bf16[128,2048]{1,0:T(8,128)(2,1)S(1)}, bf16[128,2048]{1,0:T(8,128)(2,1)S(1)}, u32[]{:S(2)}, u32[]{:S(2)}) %collective-permute-start.30) | collective-permute-done | bytes 524320 | tf_op jit(solution)/shard_map/back_1_0/ppermute | solution.py:177
  101.7 4.8 %collective-permute-done.33 = bf16[128,2048]{1,0:T(8,128)(2,1)S(1)} collective-permute-done((bf16[128,2048]{1,0:T(8,128)(2,1)S(1)}, bf16[128,2048]{1,0:T(8,128)(2,1)S(1)}, u32[]{:S(2)}, u32[]{:S(2)}) %collective-permute-start.33) | collective-permute-done | bytes 524320 | tf_op jit(solution)/shard_map/back_1_1/ppermute | solution.py:177
  (133 shorter events, 33.3 us)
Async XLA Ops:
  1.3 12.6 %collective-permute-start.5 = (bf16[128,2048]{1,0:T(8,128)(2,1)}, bf16[128,2048]{1,0:T(8,128)(2,1)S(1)}, u32[]{:S(2)}, u32[]{:S(2)}) collective-permute-start(bf16[128,2048]{1,0:T(8,128)(2,1)} %refs_0_.1), channel_id=1, source_target_pairs={{0,4},{1,3},{4,8},{5,1},{8,12},{9,5},{12,14},{13,9},{14,10},{15,13... | collective-permute-start | bytes 1572872 | tf_op jit(solution)/shard_map/ring_1_0/ppermute | solution.py:177
  4.4 13.2 %collective-permute-start.2 = (bf16[136,2048]{1,0:T(8,128)(2,1)S(1)}, bf16[136,2048]{1,0:T(8,128)(2,1)S(1)}, u32[]{:S(2)}, u32[]{:S(2)}) collective-permute-start(bf16[136,2048]{1,0:T(8,128)(2,1)S(1)} %pad_maximum_fusion.refs_1_.holder), channel_id=1, source_target_pairs={{0,4},{1,3},{4,8},{5,1},{8,12},{9,5},{12,14},{13,9},{14,10},{15,13... | collective-permute-start | bytes 1671176 | tf_op jit(solution)/shard_map/ring_1_1/ppermute | solution.py:177
  14.0 9.2 %collective-permute-start.6 = (bf16[128,2048]{1,0:T(8,128)(2,1)S(1)}, bf16[128,2048]{1,0:T(8,128)(2,1)S(1)}, u32[]{:S(2)}, u32[]{:S(2)}) collective-permute-start(bf16[128,2048]{1,0:T(8,128)(2,1)S(1)} %collective-permute-done.5.refs_0_), channel_id=1, source_target_pairs={{0,4},{1,3},{4,8},{5,1},{8,12},{9,5},{12,14},{13,9},{14,10},{15,13... | collective-permute-start | bytes 1572872 | tf_op jit(solution)/shard_map/ring_2_0/ppermute | solution.py:177
  17.6 11.6 %collective-permute-start.3 = (bf16[136,2048]{1,0:T(8,128)(2,1)S(1)}, bf16[136,2048]{1,0:T(8,128)(2,1)S(1)}, u32[]{:S(2)}, u32[]{:S(2)}) collective-permute-start(bf16[136,2048]{1,0:T(8,128)(2,1)S(1)} %collective-permute-done.2.refs_0_.holder), channel_id=1, source_target_pairs={{0,4},{1,3},{4,8},{5,1},{8,12},{9,5},{12,14},{13,9},{14,10},{15,13... | collective-permute-start | bytes 1671176 | tf_op jit(solution)/shard_map/ring_2_1/ppermute | solution.py:177
  23.2 8.1 %collective-permute-start.9 = (bf16[128,2048]{1,0:T(8,128)(2,1)S(1)}, bf16[128,2048]{1,0:T(8,128)(2,1)S(1)}, u32[]{:S(2)}, u32[]{:S(2)}) collective-permute-start(bf16[128,2048]{1,0:T(8,128)(2,1)S(1)} %collective-permute-done.6.refs_0_), channel_id=1, source_target_pairs={{0,1},{1,0},{4,5},{5,4},{8,9},{9,8},{12,13},{13,12},{14,15},{15,14... | collective-permute-start | bytes 1572872 | tf_op jit(solution)/shard_map/swap_2_0/ppermute | solution.py:177
  23.2 11.6 %collective-permute-start.8 = (bf16[128,2048]{1,0:T(8,128)(2,1)S(1)}, bf16[128,2048]{1,0:T(8,128)(2,1)S(1)}, u32[]{:S(2)}, u32[]{:S(2)}) collective-permute-start(bf16[128,2048]{1,0:T(8,128)(2,1)S(1)} %collective-permute-done.6.refs_0_), channel_id=1, source_target_pairs={{0,4},{1,3},{4,8},{5,1},{8,12},{9,5},{12,14},{13,9},{14,10},{15,13... | collective-permute-start | bytes 1572872 | tf_op jit(solution)/shard_map/ring_3_0/ppermute | solution.py:177
  29.2 7.8 %collective-permute-start.10 = (bf16[136,2048]{1,0:T(8,128)(2,1)S(1)}, bf16[136,2048]{1,0:T(8,128)(2,1)S(1)}, u32[]{:S(2)}, u32[]{:S(2)}) collective-permute-start(bf16[136,2048]{1,0:T(8,128)(2,1)S(1)} %collective-permute-done.3.refs_0_.holder), channel_id=1, source_target_pairs={{0,1},{1,0},{4,5},{5,4},{8,9},{9,8},{12,13},{13,12},{14,15},{15,14... | collective-permute-start | bytes 1671176 | tf_op jit(solution)/shard_map/swap_2_1/ppermute | solution.py:177
  29.2 11.6 %collective-permute-start.4 = (bf16[136,2048]{1,0:T(8,128)(2,1)S(1)}, bf16[136,2048]{1,0:T(8,128)(2,1)S(1)}, u32[]{:S(2)}, u32[]{:S(2)}) collective-permute-start(bf16[136,2048]{1,0:T(8,128)(2,1)S(1)} %collective-permute-done.3.refs_0_.holder), channel_id=1, source_target_pairs={{0,4},{1,3},{4,8},{5,1},{8,12},{9,5},{12,14},{13,9},{14,10},{15,13... | collective-permute-start | bytes 1671176 | tf_op jit(solution)/shard_map/ring_3_1/ppermute | solution.py:177
  34.8 8.3 %collective-permute-start.13 = (bf16[128,2048]{1,0:T(8,128)(2,1)S(1)}, bf16[128,2048]{1,0:T(8,128)(2,1)S(1)}, u32[]{:S(2)}, u32[]{:S(2)}) collective-permute-start(bf16[128,2048]{1,0:T(8,128)(2,1)S(1)} %collective-permute-done.8.refs_0_), channel_id=1, source_target_pairs={{0,1},{1,0},{4,5},{5,4},{8,9},{9,8},{12,13},{13,12},{14,15},{15,14... | collective-permute-start | bytes 1572872 | tf_op jit(solution)/shard_map/swap_3_0/ppermute | solution.py:177
  35.0 10.9 %collective-permute-start.12 = (bf16[72,2048]{1,0:T(8,128)(2,1)S(1)}, bf16[72,2048]{1,0:T(8,128)(2,1)}, u32[]{:S(2)}, u32[]{:S(2)}) collective-permute-start(bf16[72,2048]{1,0:T(8,128)(2,1)S(1)} %slice.13), channel_id=1, source_target_pairs={{0,4},{1,3},{4,8},{5,1},{8,12},{9,5},{12,14},{13,9},{14,10},{15,13... | collective-permute-start | bytes 884744 | tf_op jit(solution)/shard_map/ring_4_0/ppermute | solution.py:177
  52.2 7.6 %collective-permute-start.16 = (bf16[128,2048]{1,0:T(8,128)(2,1)}, bf16[128,2048]{1,0:T(8,128)(2,1)}, u32[]{:S(2)}, u32[]{:S(2)}) collective-permute-start(bf16[128,2048]{1,0:T(8,128)(2,1)} %expert_far_ring.1), channel_id=1, source_target_pairs={{0,1},{1,0},{4,5},{5,4},{8,9},{9,8},{12,13},{13,12},{14,15},{15,14... | collective-permute-start | bytes 1572872 | tf_op jit(solution)/shard_map/give_far/ppermute | solution.py:177
  52.7 13.3 %collective-permute-start.17 = (bf16[136,2048]{1,0:T(8,128)(2,1)}, bf16[136,2048]{1,0:T(8,128)(2,1)S(1)}, u32[]{:S(2)}, u32[]{:S(2)}) collective-permute-start(bf16[136,2048]{1,0:T(8,128)(2,1)} %copy-done.5), channel_id=1, source_target_pairs={{0,1},{1,0},{4,5},{5,4},{8,9},{9,8},{12,13},{13,12},{14,15},{15,14... | collective-permute-start | bytes 1671176 | tf_op jit(solution)/shard_map/swap_3_1/ppermute | solution.py:177
  52.8 16.0 %collective-permute-start.18 = (bf16[128,2048]{1,0:T(8,128)(2,1)}, bf16[128,2048]{1,0:T(8,128)(2,1)S(1)}, u32[]{:S(2)}, u32[]{:S(2)}) collective-permute-start(bf16[128,2048]{1,0:T(8,128)(2,1)} %copy-done.30), channel_id=1, source_target_pairs={{0,1},{1,0},{4,5},{5,4},{8,9},{9,8},{12,13},{13,12},{14,15},{15,14... | collective-permute-start | bytes 1572872 | tf_op jit(solution)/shard_map/give_3_0/ppermute | solution.py:177
  61.0 7.8 %collective-permute-start.19 = (bf16[72,2048]{1,0:T(8,128)(2,1)S(1)}, bf16[72,2048]{1,0:T(8,128)(2,1)S(1)}, u32[]{:S(2)}, u32[]{:S(2)}) collective-permute-start(bf16[72,2048]{1,0:T(8,128)(2,1)S(1)} %shard_map.55), channel_id=1, source_target_pairs={{0,2},{1,5},{4,0},{5,9},{8,4},{9,13},{12,8},{13,15},{14,12},{15,11... | collective-permute-start | bytes 884744 | tf_op jit(solution)/shard_map/back_4_0/ppermute | solution.py:177
  69.7 9.2 %collective-permute-start.25 = (bf16[128,2048]{1,0:T(8,128)(2,1)S(1)}, bf16[128,2048]{1,0:T(8,128)(2,1)S(1)}, u32[]{:S(2)}, u32[]{:S(2)}) collective-permute-start(bf16[128,2048]{1,0:T(8,128)(2,1)S(1)} %shard_map.57), channel_id=1, source_target_pairs={{0,2},{1,5},{4,0},{5,9},{8,4},{9,13},{12,8},{13,15},{14,12},{15,11... | collective-permute-start | bytes 1572872 | tf_op jit(solution)/shard_map/back_3_0/ppermute | solution.py:177
  71.3 9.5 %collective-permute-start.26 = (bf16[128,2048]{1,0:T(8,128)(2,1)S(1)}, bf16[128,2048]{1,0:T(8,128)(2,1)S(1)}, u32[]{:S(2)}, u32[]{:S(2)}) collective-permute-start(bf16[128,2048]{1,0:T(8,128)(2,1)S(1)} %copy-done.25), channel_id=1, source_target_pairs={{0,1},{1,0},{4,5},{5,4},{8,9},{9,8},{12,13},{13,12},{14,15},{15,14... | collective-permute-start | bytes 1572872 | tf_op jit(solution)/shard_map/give_2_1/ppermute | solution.py:177
  72.1 12.4 %collective-permute-start.27 = (bf16[128,2048]{1,0:T(8,128)(2,1)S(1)}, bf16[128,2048]{1,0:T(8,128)(2,1)S(1)}, u32[]{:S(2)}, u32[]{:S(2)}) collective-permute-start(bf16[128,2048]{1,0:T(8,128)(2,1)S(1)} %shard_map.58), channel_id=1, source_target_pairs={{0,2},{1,5},{4,0},{5,9},{8,4},{9,13},{12,8},{13,15},{14,12},{15,11... | collective-permute-start | bytes 1572872 | tf_op jit(solution)/shard_map/back_3_1/ppermute | solution.py:177
  74.0 12.5 %collective-permute-start.28 = (bf16[128,2048]{1,0:T(8,128)(2,1)S(1)}, bf16[128,2048]{1,0:T(8,128)(2,1)S(1)}, u32[]{:S(2)}, u32[]{:S(2)}) collective-permute-start(bf16[128,2048]{1,0:T(8,128)(2,1)S(1)} %copy-done.19), channel_id=1, source_target_pairs={{0,1},{1,0},{4,5},{5,4},{8,9},{9,8},{12,13},{13,12},{14,15},{15,14... | collective-permute-start | bytes 1572872 | tf_op jit(solution)/shard_map/give_1_0/ppermute | solution.py:177
  79.2 10.9 %collective-permute-start.29 = (bf16[128,2048]{1,0:T(8,128)(2,1)S(1)}, bf16[128,2048]{1,0:T(8,128)(2,1)S(1)}, u32[]{:S(2)}, u32[]{:S(2)}) collective-permute-start(bf16[128,2048]{1,0:T(8,128)(2,1)S(1)} %shard_map.59), channel_id=1, source_target_pairs={{0,2},{1,5},{4,0},{5,9},{8,4},{9,13},{12,8},{13,15},{14,12},{15,11... | collective-permute-start | bytes 1572872 | tf_op jit(solution)/shard_map/back_2_0/ppermute | solution.py:177
  80.9 11.3 %collective-permute-start.31 = (bf16[128,2048]{1,0:T(8,128)(2,1)S(1)}, bf16[128,2048]{1,0:T(8,128)(2,1)S(1)}, u32[]{:S(2)}, u32[]{:S(2)}) collective-permute-start(bf16[128,2048]{1,0:T(8,128)(2,1)S(1)} %get-tuple-element.86), channel_id=1, source_target_pairs={{0,1},{1,0},{4,5},{5,4},{8,9},{9,8},{12,13},{13,12},{14,15},{15,14... | collective-permute-start | bytes 1572872 | tf_op jit(solution)/shard_map/give_1_1/ppermute | solution.py:177
  84.9 10.9 %collective-permute-start.32 = (bf16[128,2048]{1,0:T(8,128)(2,1)S(1)}, bf16[128,2048]{1,0:T(8,128)(2,1)S(1)}, u32[]{:S(2)}, u32[]{:S(2)}) collective-permute-start(bf16[128,2048]{1,0:T(8,128)(2,1)S(1)} %shard_map.60), channel_id=1, source_target_pairs={{0,2},{1,5},{4,0},{5,9},{8,4},{9,13},{12,8},{13,15},{14,12},{15,11... | collective-permute-start | bytes 1572872 | tf_op jit(solution)/shard_map/back_2_1/ppermute | solution.py:177
  86.5 10.5 %collective-permute-start.22 = (bf16[128,2048]{1,0:T(8,128)(2,1)S(1)}, bf16[128,2048]{1,0:T(8,128)(2,1)S(1)}, u32[]{:S(2)}, u32[]{:S(2)}) collective-permute-start(bf16[128,2048]{1,0:T(8,128)(2,1)S(1)} %copy-done.15), channel_id=1, source_target_pairs={{0,1},{1,0},{4,5},{5,4},{8,9},{9,8},{12,13},{13,12},{14,15},{15,14... | collective-permute-start | bytes 1572872 | tf_op jit(solution)/shard_map/give_0_0/ppermute | solution.py:177
  90.5 10.9 %collective-permute-start.30 = (bf16[128,2048]{1,0:T(8,128)(2,1)S(1)}, bf16[128,2048]{1,0:T(8,128)(2,1)S(1)}, u32[]{:S(2)}, u32[]{:S(2)}) collective-permute-start(bf16[128,2048]{1,0:T(8,128)(2,1)S(1)} %shard_map.61), channel_id=1, source_target_pairs={{0,2},{1,5},{4,0},{5,9},{8,4},{9,13},{12,8},{13,15},{14,12},{15,11... | collective-permute-start | bytes 1572872 | tf_op jit(solution)/shard_map/back_1_0/ppermute | solution.py:177
  96.1 10.5 %collective-permute-start.33 = (bf16[128,2048]{1,0:T(8,128)(2,1)S(1)}, bf16[128,2048]{1,0:T(8,128)(2,1)S(1)}, u32[]{:S(2)}, u32[]{:S(2)}) collective-permute-start(bf16[128,2048]{1,0:T(8,128)(2,1)S(1)} %shard_map.63), channel_id=1, source_target_pairs={{0,3},{1,4},{4,1},{5,8},{8,5},{9,12},{12,9},{13,14},{14,13},{15,10... | collective-permute-start | bytes 1572872 | tf_op jit(solution)/shard_map/back_1_1/ppermute | solution.py:177
  (41 other events, 254.9 us)

commit v13 on v12

--- a/solution.py
+++ b/solution.py
@@ -198,7 +198,7 @@
 
     results, holders = {}, {0: packed}
     with jax.named_scope("expert_0"):
-        inputs = [tokens, packed]
+        inputs = [after(tokens, expert), packed]
         own, given, *near = half_expert([rows] * 2, inputs, [gate_up, down_proj], load=True)
     results[0, 0] = own, given
     ring[0] = after(ring[0], own)

time: 108 us -> 99.8 us (0.924)
  local copies, waits for them, and re-layouts: 8.14 us -> 3.01 us
  Pallas kernels: 33.5 us -> 28.6 us
  starting transfers between devices: 32.3 us -> 33.5 us
  waiting for transfers between devices: 31.4 us -> 32.6 us
    unnamed x62 -> x4, local copies, waits for them, and re-layouts: 8.06 us -> 2.93 us
    pallas_call x9, Pallas kernels: 28.9 us -> 26.1 us  [half_expert(): pl.pallas_call(functools.partial(half_expert_kernel, tuple(heights), load...]
    pallas_call x9, Pallas kernels: 4.58 us -> 2.43 us  [weighted(): pl.pallas_call(functools.partial(weighted_kernel, kind, first, height, lo...]
    ppermute x34, waiting for transfers between devices: 31.4 us -> 32.6 us  [send(): return lax.ppermute(value, 'blk', pairs)]
    ppermute x34, starting transfers between devices: 32.3 us -> 33.5 us  [send(): return lax.ppermute(value, 'blk', pairs)]
  transfers between devices with their start and end apart: 34 -> 34, of which waited for: 12 -> 14; matrix products, arithmetic and copies ran while one was open for 1% -> 1% of each run, Pallas kernels for 31% -> 29%
where the time goes in v13:
time: 99.8 us; the launch traced here: 99.6 us
  starting transfers between devices  33.5 us (34%)
  waiting for transfers between devices  32.6 us (33%)
  Pallas kernels  28.6 us (29%)
  local copies, waits for them, and re-layouts  3.01 us (3%)
  other arithmetic  1.67 us (2%)
    ppermute x34, starting transfers between devices, send(): return lax.ppermute(value, 'blk', pairs)  33.5 us
    ppermute x34, waiting for transfers between devices, send(): return lax.ppermute(value, 'blk', pairs)  32.6 us
    pallas_call x9, Pallas kernels, half_expert(): pl.pallas_call(functools.partial(half_expert_kernel, tuple(heights), load...  26.1 us
    unnamed x4, local copies, waits for them, and re-layouts  2.93 us
    pallas_call x9, Pallas kernels, weighted(): pl.pallas_call(functools.partial(weighted_kernel, kind, first, height, lo...  2.43 us
  transfers between devices with their start and end apart: 34, of which 14 were waited for; matrix products, arithmetic and copies ran while one was open for 1% of the time, Pallas kernels for 29%

profile of v13, /device:TPU:0, one launch (start us, length us, event | category | flops | bytes accessed | tf_op | source)
XLA Modules:
  0.0 99.6 jit_solution(9803970763729499068)
XLA Ops:
  1.3 3.0 %collective-permute-start.5 = (bf16[128,2048]{1,0:T(8,128)(2,1)}, bf16[128,2048]{1,0:T(8,128)(2,1)S(1)}, u32[]{:S(2)}, u32[]{:S(2)}) collective-permute-start(bf16[128,2048]{1,0:T(8,128)(2,1)} %refs_0_), channel_id=1, source_target_pairs={{0,4},{1,3},{4,8},{5,1},{8,12},{9,5},{12,14},{13,9},{14,10},{15,13... | collective-permute-start | bytes 1572872 | tf_op jit(solution)/shard_map/ring_1_0/ppermute | solution.py:177
  9.0 4.9 %expert_0.1 = (bf16[128,2048]{1,0:T(8,128)(2,1)S(1)}, bf16[128,2048]{1,0:T(8,128)(2,1)S(1)}, bf16[2,768,2048]{2,1,0:T(8,128)(2,1)S(1)}, bf16[768,2048]{1,0:T(8,128)(2,1)S(1)}) custom-call(bf16[128,2048]{1,0:T(8,128)(2,1)S(1)} %copy-done.1, bf16[136,2048]{1,0:T(8,128)(2,1)S(1)} %pad_maximum_fusion.refs_1_.holder, bf16[2,768,2048]{2,1,0:T(8,128)(2,1)} %refs_2_.1, ...), custom_call_target="tpu_custom_call" | custom-call | flops 805306368 | bytes 3145728 | tf_op jit(solution)/shard_map/expert_0/pallas_call | solution.py:112
  15.6 2.0 %collective-permute-done.2.refs_0_.holder = bf16[136,2048]{1,0:T(8,128)(2,1)S(1)} collective-permute-done((bf16[136,2048]{1,0:T(8,128)(2,1)S(1)}, bf16[136,2048]{1,0:T(8,128)(2,1)S(1)}, u32[]{:S(2)}, u32[]{:S(2)}) %collective-permute-start.2) | collective-permute-done | bytes 557088 | tf_op jit(solution)/shard_map/ring_1_1/ppermute | solution.py:177
  17.6 2.1 %collective-permute-start.3 = (bf16[136,2048]{1,0:T(8,128)(2,1)S(1)}, bf16[136,2048]{1,0:T(8,128)(2,1)S(1)}, u32[]{:S(2)}, u32[]{:S(2)}) collective-permute-start(bf16[136,2048]{1,0:T(8,128)(2,1)S(1)} %collective-permute-done.2.refs_0_.holder), channel_id=1, source_target_pairs={{0,4},{1,3},{4,8},{5,1},{8,12},{9,5},{12,14},{13,9},{14,10},{15,13... | collective-permute-start | bytes 1671176 | tf_op jit(solution)/shard_map/ring_2_1/ppermute | solution.py:177
  19.7 2.6 %expert_1_0.1 = (bf16[128,2048]{1,0:T(8,128)(2,1)S(1)}, bf16[128,2048]{1,0:T(8,128)(2,1)S(1)}) custom-call(bf16[128,2048]{1,0:T(8,128)(2,1)S(1)} %collective-permute-done.5.refs_0_, bf16[128,2048]{1,0:T(8,128)(2,1)S(1)} %collective-permute-done.7.refs_1_, bf16[2,768,2048]{2,1,0:T(8,128)(2,1)S(1)} %get-tuple-element.52.refs_2_, ...), custom_call_target="tpu_custom_call" | custom-call | flops 805306368 | bytes 3145728 | tf_op jit(solution)/shard_map/expert_1_0/pallas_call | solution.py:112
  23.2 2.1 %collective-permute-start.8 = (bf16[128,2048]{1,0:T(8,128)(2,1)S(1)}, bf16[128,2048]{1,0:T(8,128)(2,1)S(1)}, u32[]{:S(2)}, u32[]{:S(2)}) collective-permute-start(bf16[128,2048]{1,0:T(8,128)(2,1)S(1)} %collective-permute-done.6.refs_0_), channel_id=1, source_target_pairs={{0,4},{1,3},{4,8},{5,1},{8,12},{9,5},{12,14},{13,9},{14,10},{15,13... | collective-permute-start | bytes 1572872 | tf_op jit(solution)/shard_map/ring_3_0/ppermute | solution.py:177
  25.3 3.9 %collective-permute-done.3.refs_0_.holder = bf16[136,2048]{1,0:T(8,128)(2,1)S(1)} collective-permute-done((bf16[136,2048]{1,0:T(8,128)(2,1)S(1)}, bf16[136,2048]{1,0:T(8,128)(2,1)S(1)}, u32[]{:S(2)}, u32[]{:S(2)}) %collective-permute-start.3) | collective-permute-done | bytes 557088 | tf_op jit(solution)/shard_map/ring_2_1/ppermute | solution.py:177
  29.2 2.1 %collective-permute-start.4 = (bf16[136,2048]{1,0:T(8,128)(2,1)S(1)}, bf16[136,2048]{1,0:T(8,128)(2,1)S(1)}, u32[]{:S(2)}, u32[]{:S(2)}) collective-permute-start(bf16[136,2048]{1,0:T(8,128)(2,1)S(1)} %collective-permute-done.3.refs_0_.holder), channel_id=1, source_target_pairs={{0,4},{1,3},{4,8},{5,1},{8,12},{9,5},{12,14},{13,9},{14,10},{15,13... | collective-permute-start | bytes 1671176 | tf_op jit(solution)/shard_map/ring_3_1/ppermute | solution.py:177
  31.3 2.6 %expert_2_0.1 = (bf16[128,2048]{1,0:T(8,128)(2,1)S(1)}, bf16[128,2048]{1,0:T(8,128)(2,1)S(1)}) custom-call(bf16[128,2048]{1,0:T(8,128)(2,1)S(1)} %collective-permute-done.6.refs_0_, bf16[128,2048]{1,0:T(8,128)(2,1)S(1)} %collective-permute-done.9.refs_1_, bf16[2,768,2048]{2,1,0:T(8,128)(2,1)S(1)} %get-tuple-element.52.refs_2_, ...), custom_call_target="tpu_custom_call" | custom-call | flops 805306368 | bytes 3145728 | tf_op jit(solution)/shard_map/expert_2_0/pallas_call | solution.py:112
  34.8 2.1 %collective-permute-start.12 = (bf16[72,2048]{1,0:T(8,128)(2,1)S(1)}, bf16[72,2048]{1,0:T(8,128)(2,1)S(1)}, u32[]{:S(2)}, u32[]{:S(2)}) collective-permute-start(bf16[72,2048]{1,0:T(8,128)(2,1)S(1)} %slice.13), channel_id=1, source_target_pairs={{0,4},{1,3},{4,8},{5,1},{8,12},{9,5},{12,14},{13,9},{14,10},{15,13... | collective-permute-start | bytes 884744 | tf_op jit(solution)/shard_map/ring_4_0/ppermute | solution.py:177
  37.0 2.6 %expert_2_1.1 = (bf16[128,2048]{1,0:T(8,128)(2,1)S(1)}, bf16[128,2048]{1,0:T(8,128)(2,1)S(1)}) custom-call(bf16[136,2048]{1,0:T(8,128)(2,1)S(1)} %collective-permute-done.3.refs_0_.holder, bf16[136,2048]{1,0:T(8,128)(2,1)S(1)} %collective-permute-done.10.refs_1_, bf16[2,768,2048]{2,1,0:T(8,128)(2,1)S(1)} %get-tuple-element.52.refs_2_, ...), custom_call_target="tpu_custom_call" | custom-call | flops 805306368 | bytes 3145728 | tf_op jit(solution)/shard_map/expert_2_1/pallas_call | solution.py:112
  40.8 2.3 %collective-permute-start.11 = (bf16[72,2048]{1,0:T(8,128)(2,1)S(1)}, bf16[72,2048]{1,0:T(8,128)(2,1)S(1)}, u32[]{:S(2)}, u32[]{:S(2)}) collective-permute-start(bf16[72,2048]{1,0:T(8,128)(2,1)S(1)} %slice.12), channel_id=1, source_target_pairs={{0,4},{1,3},{4,8},{5,1},{8,12},{9,5},{12,14},{13,9},{14,10},{15,13... | collective-permute-start | bytes 884744 | tf_op jit(solution)/shard_map/ring_4_1/ppermute | solution.py:177
  43.1 2.6 %expert_3_0.1 = (bf16[128,2048]{1,0:T(8,128)(2,1)S(1)}, bf16[128,2048]{1,0:T(8,128)(2,1)S(1)}) custom-call(bf16[128,2048]{1,0:T(8,128)(2,1)S(1)} %collective-permute-done.8.refs_0_, bf16[128,2048]{1,0:T(8,128)(2,1)S(1)} %collective-permute-done.13.refs_1_, bf16[2,768,2048]{2,1,0:T(8,128)(2,1)S(1)} %get-tuple-element.52.refs_2_, ...), custom_call_target="tpu_custom_call" | custom-call | flops 805306368 | bytes 3145728 | tf_op jit(solution)/shard_map/expert_3_0/pallas_call | solution.py:112
  47.8 2.7 %expert_far_ring.1 = bf16[128,2048]{1,0:T(8,128)(2,1)S(1)} custom-call(bf16[72,2048]{1,0:T(8,128)(2,1)S(1)} %collective-permute-done.12.refs_0_, bf16[72,2048]{1,0:T(8,128)(2,1)S(1)} %collective-permute-done.11.refs_1_.holder, bf16[2,768,2048]{2,1,0:T(8,128)(2,1)S(1)} %get-tuple-element.52.refs_2_, bf16[768,2048]{1,0:T(8,128)(2,1)S(1)} %get-tuple-element.53.refs_3_), custom_call_target="tpu_custom_call" | custom-call | flops 402653184 | bytes 3145728 | tf_op jit(solution)/shard_map/expert_far_ring/pallas_call | solution.py:112
  51.5 2.7 %expert_far_swapped.1 = bf16[128,2048]{1,0:T(8,128)(2,1)S(1)} custom-call(bf16[72,2048]{1,0:T(8,128)(2,1)S(1)} %collective-permute-done.14.refs_0_, bf16[72,2048]{1,0:T(8,128)(2,1)S(1)} %collective-permute-done.15.refs_1_, bf16[2,768,2048]{2,1,0:T(8,128)(2,1)S(1)} %get-tuple-element.52.refs_2_, bf16[768,2048]{1,0:T(8,128)(2,1)S(1)} %get-tuple-element.53.refs_3_), custom_call_target="tpu_custom_call" | custom-call | flops 402653184 | bytes 3145728 | tf_op jit(solution)/shard_map/expert_far_swapped/pallas_call | solution.py:112
  54.4 2.1 %collective-permute-start.19 = (bf16[72,2048]{1,0:T(8,128)(2,1)S(1)}, bf16[72,2048]{1,0:T(8,128)(2,1)S(1)}, u32[]{:S(2)}, u32[]{:S(2)}) collective-permute-start(bf16[72,2048]{1,0:T(8,128)(2,1)S(1)} %shard_map.55), channel_id=1, source_target_pairs={{0,2},{1,5},{4,0},{5,9},{8,4},{9,13},{12,8},{13,15},{14,12},{15,11... | collective-permute-start | bytes 884744 | tf_op jit(solution)/shard_map/back_4_0/ppermute | solution.py:177
  58.4 2.7 %expert_3_1.1 = (bf16[128,2048]{1,0:T(8,128)(2,1)S(1)}, bf16[128,2048]{1,0:T(8,128)(2,1)S(1)}) custom-call(bf16[136,2048]{1,0:T(8,128)(2,1)S(1)} %collective-permute-done.4.refs_0_.holder, bf16[136,2048]{1,0:T(8,128)(2,1)S(1)} %collective-permute-done.17.refs_1_, bf16[2,768,2048]{2,1,0:T(8,128)(2,1)S(1)} %get-tuple-element.52.refs_2_, ...), custom_call_target="tpu_custom_call" | custom-call | flops 80530640 | bytes 314572 | tf_op jit(solution)/shard_map/expert_3_1/pallas_call | solution.py:112
  64.7 2.0 %collective-permute-start.27 = (bf16[128,2048]{1,0:T(8,128)(2,1)S(1)}, bf16[128,2048]{1,0:T(8,128)(2,1)S(1)}, u32[]{:S(2)}, u32[]{:S(2)}) collective-permute-start(bf16[128,2048]{1,0:T(8,128)(2,1)S(1)} %shard_map.58), channel_id=1, source_target_pairs={{0,2},{1,5},{4,0},{5,9},{8,4},{9,13},{12,8},{13,15},{14,12},{15,11... | collective-permute-start | bytes 1572872 | tf_op jit(solution)/shard_map/back_3_1/ppermute | solution.py:177
  67.0 2.6 %expert_1_1.1 = (bf16[128,2048]{1,0:T(8,128)(2,1)S(1)}, bf16[128,2048]{1,0:T(8,128)(2,1)S(1)}) custom-call(bf16[136,2048]{1,0:T(8,128)(2,1)S(1)} %collective-permute-done.2.refs_0_.holder, bf16[136,2048]{1,0:T(8,128)(2,1)S(1)} %collective-permute-done.23.refs_1_, bf16[2,768,2048]{2,1,0:T(8,128)(2,1)S(1)} %get-tuple-element.52.refs_2_, ...), custom_call_target="tpu_custom_call" | custom-call | flops 805306368 | bytes 3145728 | tf_op jit(solution)/shard_map/expert_1_1/pallas_call | solution.py:112
  73.2 3.5 %collective-permute-done.27.refs_0_ = bf16[128,2048]{1,0:T(8,128)(2,1)S(1)} collective-permute-done((bf16[128,2048]{1,0:T(8,128)(2,1)S(1)}, bf16[128,2048]{1,0:T(8,128)(2,1)S(1)}, u32[]{:S(2)}, u32[]{:S(2)}) %collective-permute-start.27) | collective-permute-done | bytes 524320 | tf_op jit(solution)/shard_map/back_3_1/ppermute | solution.py:177
  78.8 3.5 %collective-permute-done.29.refs_0_ = bf16[128,2048]{1,0:T(8,128)(2,1)S(1)} collective-permute-done((bf16[128,2048]{1,0:T(8,128)(2,1)S(1)}, bf16[128,2048]{1,0:T(8,128)(2,1)S(1)}, u32[]{:S(2)}, u32[]{:S(2)}) %collective-permute-start.29) | collective-permute-done | bytes 524320 | tf_op jit(solution)/shard_map/back_2_0/ppermute | solution.py:177
  84.4 3.5 %collective-permute-done.32.refs_0_ = bf16[128,2048]{1,0:T(8,128)(2,1)S(1)} collective-permute-done((bf16[128,2048]{1,0:T(8,128)(2,1)S(1)}, bf16[128,2048]{1,0:T(8,128)(2,1)S(1)}, u32[]{:S(2)}, u32[]{:S(2)}) %collective-permute-start.32) | collective-permute-done | bytes 524320 | tf_op jit(solution)/shard_map/back_2_1/ppermute | solution.py:177
  89.3 4.3 %collective-permute-done.30.refs_0_ = bf16[128,2048]{1,0:T(8,128)(2,1)S(1)} collective-permute-done((bf16[128,2048]{1,0:T(8,128)(2,1)S(1)}, bf16[128,2048]{1,0:T(8,128)(2,1)S(1)}, u32[]{:S(2)}, u32[]{:S(2)}) %collective-permute-start.30) | collective-permute-done | bytes 524320 | tf_op jit(solution)/shard_map/back_1_0/ppermute | solution.py:177
  93.9 4.8 %collective-permute-done.33 = bf16[128,2048]{1,0:T(8,128)(2,1)S(1)} collective-permute-done((bf16[128,2048]{1,0:T(8,128)(2,1)S(1)}, bf16[128,2048]{1,0:T(8,128)(2,1)S(1)}, u32[]{:S(2)}, u32[]{:S(2)}) %collective-permute-start.33) | collective-permute-done | bytes 524320 | tf_op jit(solution)/shard_map/back_1_1/ppermute | solution.py:177
  (75 shorter events, 29.8 us)
Async XLA Ops:
  1.3 12.6 %collective-permute-start.5 = (bf16[128,2048]{1,0:T(8,128)(2,1)}, bf16[128,2048]{1,0:T(8,128)(2,1)S(1)}, u32[]{:S(2)}, u32[]{:S(2)}) collective-permute-start(bf16[128,2048]{1,0:T(8,128)(2,1)} %refs_0_), channel_id=1, source_target_pairs={{0,4},{1,3},{4,8},{5,1},{8,12},{9,5},{12,14},{13,9},{14,10},{15,13... | collective-permute-start | bytes 1572872 | tf_op jit(solution)/shard_map/ring_1_0/ppermute | solution.py:177
  4.4 13.2 %collective-permute-start.2 = (bf16[136,2048]{1,0:T(8,128)(2,1)S(1)}, bf16[136,2048]{1,0:T(8,128)(2,1)S(1)}, u32[]{:S(2)}, u32[]{:S(2)}) collective-permute-start(bf16[136,2048]{1,0:T(8,128)(2,1)S(1)} %pad_maximum_fusion.refs_1_.holder), channel_id=1, source_target_pairs={{0,4},{1,3},{4,8},{5,1},{8,12},{9,5},{12,14},{13,9},{14,10},{15,13... | collective-permute-start | bytes 1671176 | tf_op jit(solution)/shard_map/ring_1_1/ppermute | solution.py:177
  13.9 9.3 %collective-permute-start.6 = (bf16[128,2048]{1,0:T(8,128)(2,1)S(1)}, bf16[128,2048]{1,0:T(8,128)(2,1)S(1)}, u32[]{:S(2)}, u32[]{:S(2)}) collective-permute-start(bf16[128,2048]{1,0:T(8,128)(2,1)S(1)} %collective-permute-done.5.refs_0_), channel_id=1, source_target_pairs={{0,4},{1,3},{4,8},{5,1},{8,12},{9,5},{12,14},{13,9},{14,10},{15,13... | collective-permute-start | bytes 1572872 | tf_op jit(solution)/shard_map/ring_2_0/ppermute | solution.py:177
  17.6 11.6 %collective-permute-start.3 = (bf16[136,2048]{1,0:T(8,128)(2,1)S(1)}, bf16[136,2048]{1,0:T(8,128)(2,1)S(1)}, u32[]{:S(2)}, u32[]{:S(2)}) collective-permute-start(bf16[136,2048]{1,0:T(8,128)(2,1)S(1)} %collective-permute-done.2.refs_0_.holder), channel_id=1, source_target_pairs={{0,4},{1,3},{4,8},{5,1},{8,12},{9,5},{12,14},{13,9},{14,10},{15,13... | collective-permute-start | bytes 1671176 | tf_op jit(solution)/shard_map/ring_2_1/ppermute | solution.py:177
  23.2 8.1 %collective-permute-start.9 = (bf16[128,2048]{1,0:T(8,128)(2,1)S(1)}, bf16[128,2048]{1,0:T(8,128)(2,1)S(1)}, u32[]{:S(2)}, u32[]{:S(2)}) collective-permute-start(bf16[128,2048]{1,0:T(8,128)(2,1)S(1)} %collective-permute-done.6.refs_0_), channel_id=1, source_target_pairs={{0,1},{1,0},{4,5},{5,4},{8,9},{9,8},{12,13},{13,12},{14,15},{15,14... | collective-permute-start | bytes 1572872 | tf_op jit(solution)/shard_map/swap_2_0/ppermute | solution.py:177
  23.2 11.6 %collective-permute-start.8 = (bf16[128,2048]{1,0:T(8,128)(2,1)S(1)}, bf16[128,2048]{1,0:T(8,128)(2,1)S(1)}, u32[]{:S(2)}, u32[]{:S(2)}) collective-permute-start(bf16[128,2048]{1,0:T(8,128)(2,1)S(1)} %collective-permute-done.6.refs_0_), channel_id=1, source_target_pairs={{0,4},{1,3},{4,8},{5,1},{8,12},{9,5},{12,14},{13,9},{14,10},{15,13... | collective-permute-start | bytes 1572872 | tf_op jit(solution)/shard_map/ring_3_0/ppermute | solution.py:177
  29.2 7.8 %collective-permute-start.10 = (bf16[136,2048]{1,0:T(8,128)(2,1)S(1)}, bf16[136,2048]{1,0:T(8,128)(2,1)S(1)}, u32[]{:S(2)}, u32[]{:S(2)}) collective-permute-start(bf16[136,2048]{1,0:T(8,128)(2,1)S(1)} %collective-permute-done.3.refs_0_.holder), channel_id=1, source_target_pairs={{0,1},{1,0},{4,5},{5,4},{8,9},{9,8},{12,13},{13,12},{14,15},{15,14... | collective-permute-start | bytes 1671176 | tf_op jit(solution)/shard_map/swap_2_1/ppermute | solution.py:177
  29.2 11.6 %collective-permute-start.4 = (bf16[136,2048]{1,0:T(8,128)(2,1)S(1)}, bf16[136,2048]{1,0:T(8,128)(2,1)S(1)}, u32[]{:S(2)}, u32[]{:S(2)}) collective-permute-start(bf16[136,2048]{1,0:T(8,128)(2,1)S(1)} %collective-permute-done.3.refs_0_.holder), channel_id=1, source_target_pairs={{0,4},{1,3},{4,8},{5,1},{8,12},{9,5},{12,14},{13,9},{14,10},{15,13... | collective-permute-start | bytes 1671176 | tf_op jit(solution)/shard_map/ring_3_1/ppermute | solution.py:177
  34.8 8.3 %collective-permute-start.13 = (bf16[128,2048]{1,0:T(8,128)(2,1)S(1)}, bf16[128,2048]{1,0:T(8,128)(2,1)S(1)}, u32[]{:S(2)}, u32[]{:S(2)}) collective-permute-start(bf16[128,2048]{1,0:T(8,128)(2,1)S(1)} %collective-permute-done.8.refs_0_), channel_id=1, source_target_pairs={{0,1},{1,0},{4,5},{5,4},{8,9},{9,8},{12,13},{13,12},{14,15},{15,14... | collective-permute-start | bytes 1572872 | tf_op jit(solution)/shard_map/swap_3_0/ppermute | solution.py:177
  34.8 10.9 %collective-permute-start.12 = (bf16[72,2048]{1,0:T(8,128)(2,1)S(1)}, bf16[72,2048]{1,0:T(8,128)(2,1)S(1)}, u32[]{:S(2)}, u32[]{:S(2)}) collective-permute-start(bf16[72,2048]{1,0:T(8,128)(2,1)S(1)} %slice.13), channel_id=1, source_target_pairs={{0,4},{1,3},{4,8},{5,1},{8,12},{9,5},{12,14},{13,9},{14,10},{15,13... | collective-permute-start | bytes 884744 | tf_op jit(solution)/shard_map/ring_4_0/ppermute | solution.py:177
  40.8 7.0 %collective-permute-start.11 = (bf16[72,2048]{1,0:T(8,128)(2,1)S(1)}, bf16[72,2048]{1,0:T(8,128)(2,1)S(1)}, u32[]{:S(2)}, u32[]{:S(2)}) collective-permute-start(bf16[72,2048]{1,0:T(8,128)(2,1)S(1)} %slice.12), channel_id=1, source_target_pairs={{0,4},{1,3},{4,8},{5,1},{8,12},{9,5},{12,14},{13,9},{14,10},{15,13... | collective-permute-start | bytes 884744 | tf_op jit(solution)/shard_map/ring_4_1/ppermute | solution.py:177
  51.0 7.3 %collective-permute-start.17 = (bf16[136,2048]{1,0:T(8,128)(2,1)S(1)}, bf16[136,2048]{1,0:T(8,128)(2,1)S(1)}, u32[]{:S(2)}, u32[]{:S(2)}) collective-permute-start(bf16[136,2048]{1,0:T(8,128)(2,1)S(1)} %collective-permute-done.4.refs_0_.holder), channel_id=1, source_target_pairs={{0,1},{1,0},{4,5},{5,4},{8,9},{9,8},{12,13},{13,12},{14,15},{15,14... | collective-permute-start | bytes 1671176 | tf_op jit(solution)/shard_map/swap_3_1/ppermute | solution.py:177
  51.1 10.0 %collective-permute-start.18 = (bf16[128,2048]{1,0:T(8,128)(2,1)S(1)}, bf16[128,2048]{1,0:T(8,128)(2,1)S(1)}, u32[]{:S(2)}, u32[]{:S(2)}) collective-permute-start(bf16[128,2048]{1,0:T(8,128)(2,1)S(1)} %get-tuple-element.71), channel_id=1, source_target_pairs={{0,1},{1,0},{4,5},{5,4},{8,9},{9,8},{12,13},{13,12},{14,15},{15,14... | collective-permute-start | bytes 1572872 | tf_op jit(solution)/shard_map/give_3_0/ppermute | solution.py:177
  56.7 7.7 %collective-permute-start.21 = (bf16[72,2048]{1,0:T(8,128)(2,1)S(1)}, bf16[72,2048]{1,0:T(8,128)(2,1)S(1)}, u32[]{:S(2)}, u32[]{:S(2)}) collective-permute-start(bf16[72,2048]{1,0:T(8,128)(2,1)S(1)} %shard_map.56), channel_id=1, source_target_pairs={{0,2},{1,5},{4,0},{5,9},{8,4},{9,13},{12,8},{13,15},{14,12},{15,11... | collective-permute-start | bytes 884744 | tf_op jit(solution)/shard_map/back_4_1/ppermute | solution.py:177
  61.9 9.2 %collective-permute-start.25 = (bf16[128,2048]{1,0:T(8,128)(2,1)S(1)}, bf16[128,2048]{1,0:T(8,128)(2,1)S(1)}, u32[]{:S(2)}, u32[]{:S(2)}) collective-permute-start(bf16[128,2048]{1,0:T(8,128)(2,1)S(1)} %shard_map.57), channel_id=1, source_target_pairs={{0,2},{1,5},{4,0},{5,9},{8,4},{9,13},{12,8},{13,15},{14,12},{15,11... | collective-permute-start | bytes 1572872 | tf_op jit(solution)/shard_map/back_3_0/ppermute | solution.py:177
  64.4 8.8 %collective-permute-start.26 = (bf16[128,2048]{1,0:T(8,128)(2,1)S(1)}, bf16[128,2048]{1,0:T(8,128)(2,1)S(1)}, u32[]{:S(2)}, u32[]{:S(2)}) collective-permute-start(bf16[128,2048]{1,0:T(8,128)(2,1)S(1)} %get-tuple-element.83), channel_id=1, source_target_pairs={{0,1},{1,0},{4,5},{5,4},{8,9},{9,8},{12,13},{13,12},{14,15},{15,14... | collective-permute-start | bytes 1572872 | tf_op jit(solution)/shard_map/give_2_1/ppermute | solution.py:177
  64.7 12.0 %collective-permute-start.27 = (bf16[128,2048]{1,0:T(8,128)(2,1)S(1)}, bf16[128,2048]{1,0:T(8,128)(2,1)S(1)}, u32[]{:S(2)}, u32[]{:S(2)}) collective-permute-start(bf16[128,2048]{1,0:T(8,128)(2,1)S(1)} %shard_map.58), channel_id=1, source_target_pairs={{0,2},{1,5},{4,0},{5,9},{8,4},{9,13},{12,8},{13,15},{14,12},{15,11... | collective-permute-start | bytes 1572872 | tf_op jit(solution)/shard_map/back_3_1/ppermute | solution.py:177
  66.8 12.1 %collective-permute-start.28 = (bf16[128,2048]{1,0:T(8,128)(2,1)S(1)}, bf16[128,2048]{1,0:T(8,128)(2,1)S(1)}, u32[]{:S(2)}, u32[]{:S(2)}) collective-permute-start(bf16[128,2048]{1,0:T(8,128)(2,1)S(1)} %get-tuple-element.86), channel_id=1, source_target_pairs={{0,1},{1,0},{4,5},{5,4},{8,9},{9,8},{12,13},{13,12},{14,15},{15,14... | collective-permute-start | bytes 1572872 | tf_op jit(solution)/shard_map/give_1_0/ppermute | solution.py:177
  71.4 10.9 %collective-permute-start.29 = (bf16[128,2048]{1,0:T(8,128)(2,1)S(1)}, bf16[128,2048]{1,0:T(8,128)(2,1)S(1)}, u32[]{:S(2)}, u32[]{:S(2)}) collective-permute-start(bf16[128,2048]{1,0:T(8,128)(2,1)S(1)} %shard_map.59), channel_id=1, source_target_pairs={{0,2},{1,5},{4,0},{5,9},{8,4},{9,13},{12,8},{13,15},{14,12},{15,11... | collective-permute-start | bytes 1572872 | tf_op jit(solution)/shard_map/back_2_0/ppermute | solution.py:177
  73.2 11.2 %collective-permute-start.31 = (bf16[128,2048]{1,0:T(8,128)(2,1)S(1)}, bf16[128,2048]{1,0:T(8,128)(2,1)S(1)}, u32[]{:S(2)}, u32[]{:S(2)}) collective-permute-start(bf16[128,2048]{1,0:T(8,128)(2,1)S(1)} %get-tuple-element.88), channel_id=1, source_target_pairs={{0,1},{1,0},{4,5},{5,4},{8,9},{9,8},{12,13},{13,12},{14,15},{15,14... | collective-permute-start | bytes 1572872 | tf_op jit(solution)/shard_map/give_1_1/ppermute | solution.py:177
  77.1 10.9 %collective-permute-start.32 = (bf16[128,2048]{1,0:T(8,128)(2,1)S(1)}, bf16[128,2048]{1,0:T(8,128)(2,1)S(1)}, u32[]{:S(2)}, u32[]{:S(2)}) collective-permute-start(bf16[128,2048]{1,0:T(8,128)(2,1)S(1)} %shard_map.60), channel_id=1, source_target_pairs={{0,2},{1,5},{4,0},{5,9},{8,4},{9,13},{12,8},{13,15},{14,12},{15,11... | collective-permute-start | bytes 1572872 | tf_op jit(solution)/shard_map/back_2_1/ppermute | solution.py:177
  78.8 10.4 %collective-permute-start.22 = (bf16[128,2048]{1,0:T(8,128)(2,1)S(1)}, bf16[128,2048]{1,0:T(8,128)(2,1)S(1)}, u32[]{:S(2)}, u32[]{:S(2)}) collective-permute-start(bf16[128,2048]{1,0:T(8,128)(2,1)S(1)} %get-tuple-element.74), channel_id=1, source_target_pairs={{0,1},{1,0},{4,5},{5,4},{8,9},{9,8},{12,13},{13,12},{14,15},{15,14... | collective-permute-start | bytes 1572872 | tf_op jit(solution)/shard_map/give_0_0/ppermute | solution.py:177
  82.7 10.9 %collective-permute-start.30 = (bf16[128,2048]{1,0:T(8,128)(2,1)S(1)}, bf16[128,2048]{1,0:T(8,128)(2,1)S(1)}, u32[]{:S(2)}, u32[]{:S(2)}) collective-permute-start(bf16[128,2048]{1,0:T(8,128)(2,1)S(1)} %shard_map.61), channel_id=1, source_target_pairs={{0,2},{1,5},{4,0},{5,9},{8,4},{9,13},{12,8},{13,15},{14,12},{15,11... | collective-permute-start | bytes 1572872 | tf_op jit(solution)/shard_map/back_1_0/ppermute | solution.py:177
  88.3 10.4 %collective-permute-start.33 = (bf16[128,2048]{1,0:T(8,128)(2,1)S(1)}, bf16[128,2048]{1,0:T(8,128)(2,1)S(1)}, u32[]{:S(2)}, u32[]{:S(2)}) collective-permute-start(bf16[128,2048]{1,0:T(8,128)(2,1)S(1)} %shard_map.63), channel_id=1, source_target_pairs={{0,3},{1,4},{4,1},{5,8},{8,5},{9,12},{12,9},{13,14},{14,13},{15,10... | collective-permute-start | bytes 1572872 | tf_op jit(solution)/shard_map/back_1_1/ppermute | solution.py:177
  (12 other events, 51.0 us)

commit v14 on v13

--- a/solution.py
+++ b/solution.py
@@ -99,6 +99,44 @@
             out[:, low : low + tile] = product[i * share : (i + 1) * share]
 
 
+def load_kernel(*refs):
+    copies = [pltpu.make_async_copy(far, near, refs[4].at[i]) for i, (far, near) in enumerate(zip(refs[:2], refs[2:4]))]
+    for copy in copies:
+        copy.start()
+    for copy in copies:
+        copy.wait()
+
+
+def loaded(*weights):
+    return pl.pallas_call(
+        load_kernel,
+        out_shape=[jax.ShapeDtypeStruct(array.shape, array.dtype) for array in weights],
+        in_specs=[pl.BlockSpec(memory_space=pltpu.HBM)] * 2,
+        out_specs=[pl.BlockSpec(memory_space=pltpu.VMEM)] * 2,
+        scratch_shapes=[pltpu.SemaphoreType.DMA((2,))],
+        compiler_params=pltpu.CompilerParams(vmem_limit_bytes=38 << 20),
+        cost_estimate=pl.CostEstimate(flops=1 << 28, bytes_accessed=1 << 20, transcendentals=0),
+    )(*weights)
+
+
+def widen_kernel(gates, out):
+    out[...] = jnp.concatenate([gates[...], jnp.zeros((GATE_ROWS, out.shape[1] - gates.shape[1]), out.dtype)], axis=1)
+
+
+def widened(own, other, width):
+    whole = pl.BlockSpec(memory_space=pltpu.VMEM)
+    wide = pl.pallas_call(
+        widen_kernel,
+        out_shape=jax.ShapeDtypeStruct((GATE_ROWS, width), own.dtype),
+        in_specs=[whole],
+        out_specs=whole,
+        compiler_params=pltpu.CompilerParams(vmem_limit_bytes=8 << 20),
+        cost_estimate=pl.CostEstimate(flops=1 << 28, bytes_accessed=1 << 20, transcendentals=0),
+    )(own)
+    size = own.shape[1]
+    return jnp.concatenate([wide[:, :size], other, wide[:, 2 * size :]], axis=1)
+
+
 def half_expert(heights, blocks, weights, load=False, cost=2, split=2):
     height = sum(heights)
     units, width = weights[1].shape
@@ -192,16 +230,16 @@
     weight = jnp.sum(jnp.where(chosen, route_gate.T[None], 0.0), axis=1)
     high = lax.reduce_precision(weight, 8, 7)
     gates = jnp.concatenate([high, weight - high], axis=1).astype(jnp.bfloat16)
-    gates = jnp.concatenate([gates, send(gates, cores, "swap_0_1")], axis=1)
-    packed = jnp.concatenate([others, jnp.pad(gates, ((0, 0), (0, tokens.shape[1] - 4 * LANES)))])
+    packed = jnp.concatenate([others, widened(gates, send(gates, cores, "swap_0_1"), tokens.shape[1])])
     ring[1] = send(packed, forth, "ring_1_1")
 
+    near = loaded(after(gate_up, expert), down_proj)
+    ring[0] = after(ring[0], near[1])
     results, holders = {}, {0: packed}
     with jax.named_scope("expert_0"):
-        inputs = [after(tokens, expert), packed]
-        own, given, *near = half_expert([rows] * 2, inputs, [gate_up, down_proj], load=True)
+        own, given = half_expert([rows] * 2, [after(tokens, ring[0]), packed], near)
     results[0, 0] = own, given
-    ring[0] = after(ring[0], own)
+    ring[1] = after(ring[1], own)
 
     def expert_rows(step, c, inputs, **options):
         with jax.named_scope(f"expert_{step}_{c}"):

time: 99.8 us -> 98.4 us (0.986)
  local copies, waits for them, and re-layouts: 3.01 us -> 1.97 us
    pallas_call x0 -> x2, Pallas kernels: none -> 2.87 us  [the longest x1 2.86 us: loaded(): pl.pallas_call(load_kernel, out_shape=[jax.ShapeDtypeStruct(array.shape,...]
    pallas_call x9, Pallas kernels: 26.1 us -> 23.9 us  [half_expert(): pl.pallas_call(functools.partial(half_expert_kernel, tuple(heights), load...]
    unnamed x4, local copies, waits for them, and re-layouts: 2.93 us -> 1.89 us
  transfers between devices with their start and end apart: 34 -> 34, of which waited for: 14 -> 15; matrix products, arithmetic and copies ran while one was open for 1% -> 1% of each run, Pallas kernels for 29% -> 30%
where the time goes in v14:
time: 98.4 us; the launch traced here: 98.3 us
  starting transfers between devices  33.2 us (34%)
  waiting for transfers between devices  32 us (33%)
  Pallas kernels  29.2 us (30%)
  local copies, waits for them, and re-layouts  1.97 us (2%)
  other arithmetic  1.67 us (2%)
    ppermute x34, starting transfers between devices, send(): return lax.ppermute(value, 'blk', pairs)  33.2 us
    ppermute x34, waiting for transfers between devices, send(): return lax.ppermute(value, 'blk', pairs)  32 us
    pallas_call x9, Pallas kernels, half_expert(): pl.pallas_call(functools.partial(half_expert_kernel, tuple(heights), load...  23.9 us
    pallas_call x1, Pallas kernels, loaded(): pl.pallas_call(load_kernel, out_shape=[jax.ShapeDtypeStruct(array.shape,...  2.86 us
    pallas_call x9, Pallas kernels, weighted(): pl.pallas_call(functools.partial(weighted_kernel, kind, first, height, lo...  2.43 us
  transfers between devices with their start and end apart: 34, of which 15 were waited for; matrix products, arithmetic and copies ran while one was open for 1% of the time, Pallas kernels for 30%

profile of v14, /device:TPU:0, one launch (start us, length us, event | category | flops | bytes accessed | tf_op | source)
XLA Modules:
  0.0 98.3 jit_solution(13086810721240286493)
XLA Ops:
  0.5 2.6 %collective-permute-start.2 = (bf16[128,2048]{1,0:T(8,128)(2,1)}, bf16[128,2048]{1,0:T(8,128)(2,1)S(1)}, u32[]{:S(2)}, u32[]{:S(2)}) collective-permute-start(bf16[128,2048]{1,0:T(8,128)(2,1)} %refs_0_.1), channel_id=1, source_target_pairs={{0,4},{1,3},{4,8},{5,1},{8,12},{9,5},{12,14},{13,9},{14,10},{15,13... | collective-permute-start | bytes 1572872 | tf_op jit(solution)/shard_map/ring_1_0/ppermute | solution.py:215
  8.6 2.9 %shard_map.56 = (bf16[2,768,2048]{2,1,0:T(8,128)(2,1)S(1)}, bf16[768,2048]{1,0:T(8,128)(2,1)S(1)}) custom-call(bf16[2,768,2048]{2,1,0:T(8,128)(2,1)} %refs_0_, bf16[768,2048]{1,0:T(8,128)(2,1)S(1)} %copy-done), custom_call_target="tpu_custom_call" | custom-call | flops 268435456 | bytes 1048576 | tf_op jit(solution)/shard_map/pallas_call | solution.py:111
  13.2 2.6 %expert_0.1 = (bf16[128,2048]{1,0:T(8,128)(2,1)S(1)}, bf16[128,2048]{1,0:T(8,128)(2,1)S(1)}) custom-call(bf16[128,2048]{1,0:T(8,128)(2,1)S(1)} %copy-done.1, bf16[136,2048]{1,0:T(8,128)(2,1)S(1)} %maximum_maximum_fusion.refs_1_.holder, bf16[2,768,2048]{2,1,0:T(8,128)(2,1)S(1)} %get-tuple-element.53.refs_2_, bf16[768,2048]{1,0:T(8,128)(2,1)S(1)} %get-tuple-element.50.refs_3_), custom_call_target="tpu_custom_call" | custom-call | flops 805306368 | bytes 3145728 | tf_op jit(solution)/shard_map/expert_0/pallas_call | solution.py:150
  16.3 2.1 %collective-permute-start.4 = (bf16[136,2048]{1,0:T(8,128)(2,1)S(1)}, bf16[136,2048]{1,0:T(8,128)(2,1)S(1)}, u32[]{:S(2)}, u32[]{:S(2)}) collective-permute-start(bf16[136,2048]{1,0:T(8,128)(2,1)S(1)} %collective-permute-done.3.refs_0_.holder), channel_id=1, source_target_pairs={{0,4},{1,3},{4,8},{5,1},{8,12},{9,5},{12,14},{13,9},{14,10},{15,13... | collective-permute-start | bytes 1671176 | tf_op jit(solution)/shard_map/ring_2_1/ppermute | solution.py:215
  18.4 2.7 %expert_1_0.1 = (bf16[128,2048]{1,0:T(8,128)(2,1)S(1)}, bf16[128,2048]{1,0:T(8,128)(2,1)S(1)}) custom-call(bf16[128,2048]{1,0:T(8,128)(2,1)S(1)} %collective-permute-done.2.refs_0_, bf16[128,2048]{1,0:T(8,128)(2,1)S(1)} %collective-permute-done.7.refs_1_, bf16[2,768,2048]{2,1,0:T(8,128)(2,1)S(1)} %get-tuple-element.53.refs_2_, ...), custom_call_target="tpu_custom_call" | custom-call | flops 805306368 | bytes 3145728 | tf_op jit(solution)/shard_map/expert_1_0/pallas_call | solution.py:150
  21.9 2.1 %collective-permute-start.8 = (bf16[128,2048]{1,0:T(8,128)(2,1)S(1)}, bf16[128,2048]{1,0:T(8,128)(2,1)S(1)}, u32[]{:S(2)}, u32[]{:S(2)}) collective-permute-start(bf16[128,2048]{1,0:T(8,128)(2,1)S(1)} %collective-permute-done.6.refs_0_), channel_id=1, source_target_pairs={{0,4},{1,3},{4,8},{5,1},{8,12},{9,5},{12,14},{13,9},{14,10},{15,13... | collective-permute-start | bytes 1572872 | tf_op jit(solution)/shard_map/ring_3_0/ppermute | solution.py:215
  24.0 3.9 %collective-permute-done.4.refs_0_.holder = bf16[136,2048]{1,0:T(8,128)(2,1)S(1)} collective-permute-done((bf16[136,2048]{1,0:T(8,128)(2,1)S(1)}, bf16[136,2048]{1,0:T(8,128)(2,1)S(1)}, u32[]{:S(2)}, u32[]{:S(2)}) %collective-permute-start.4) | collective-permute-done | bytes 557088 | tf_op jit(solution)/shard_map/ring_2_1/ppermute | solution.py:215
  27.9 2.1 %collective-permute-start.5 = (bf16[136,2048]{1,0:T(8,128)(2,1)S(1)}, bf16[136,2048]{1,0:T(8,128)(2,1)S(1)}, u32[]{:S(2)}, u32[]{:S(2)}) collective-permute-start(bf16[136,2048]{1,0:T(8,128)(2,1)S(1)} %collective-permute-done.4.refs_0_.holder), channel_id=1, source_target_pairs={{0,4},{1,3},{4,8},{5,1},{8,12},{9,5},{12,14},{13,9},{14,10},{15,13... | collective-permute-start | bytes 1671176 | tf_op jit(solution)/shard_map/ring_3_1/ppermute | solution.py:215
  30.0 2.6 %expert_2_0.1 = (bf16[128,2048]{1,0:T(8,128)(2,1)S(1)}, bf16[128,2048]{1,0:T(8,128)(2,1)S(1)}) custom-call(bf16[128,2048]{1,0:T(8,128)(2,1)S(1)} %collective-permute-done.6.refs_0_, bf16[128,2048]{1,0:T(8,128)(2,1)S(1)} %collective-permute-done.9.refs_1_, bf16[2,768,2048]{2,1,0:T(8,128)(2,1)S(1)} %get-tuple-element.53.refs_2_, ...), custom_call_target="tpu_custom_call" | custom-call | flops 805306368 | bytes 3145728 | tf_op jit(solution)/shard_map/expert_2_0/pallas_call | solution.py:150
  33.5 2.1 %collective-permute-start.12 = (bf16[72,2048]{1,0:T(8,128)(2,1)S(1)}, bf16[72,2048]{1,0:T(8,128)(2,1)S(1)}, u32[]{:S(2)}, u32[]{:S(2)}) collective-permute-start(bf16[72,2048]{1,0:T(8,128)(2,1)S(1)} %slice.21), channel_id=1, source_target_pairs={{0,4},{1,3},{4,8},{5,1},{8,12},{9,5},{12,14},{13,9},{14,10},{15,13... | collective-permute-start | bytes 884744 | tf_op jit(solution)/shard_map/ring_4_0/ppermute | solution.py:215
  35.7 2.6 %expert_2_1.1 = (bf16[128,2048]{1,0:T(8,128)(2,1)S(1)}, bf16[128,2048]{1,0:T(8,128)(2,1)S(1)}) custom-call(bf16[136,2048]{1,0:T(8,128)(2,1)S(1)} %collective-permute-done.4.refs_0_.holder, bf16[136,2048]{1,0:T(8,128)(2,1)S(1)} %collective-permute-done.10.refs_1_, bf16[2,768,2048]{2,1,0:T(8,128)(2,1)S(1)} %get-tuple-element.53.refs_2_, ...), custom_call_target="tpu_custom_call" | custom-call | flops 805306368 | bytes 3145728 | tf_op jit(solution)/shard_map/expert_2_1/pallas_call | solution.py:150
  39.5 2.3 %collective-permute-start.11 = (bf16[72,2048]{1,0:T(8,128)(2,1)S(1)}, bf16[72,2048]{1,0:T(8,128)(2,1)S(1)}, u32[]{:S(2)}, u32[]{:S(2)}) collective-permute-start(bf16[72,2048]{1,0:T(8,128)(2,1)S(1)} %slice.20), channel_id=1, source_target_pairs={{0,4},{1,3},{4,8},{5,1},{8,12},{9,5},{12,14},{13,9},{14,10},{15,13... | collective-permute-start | bytes 884744 | tf_op jit(solution)/shard_map/ring_4_1/ppermute | solution.py:215
  41.8 2.6 %expert_3_0.1 = (bf16[128,2048]{1,0:T(8,128)(2,1)S(1)}, bf16[128,2048]{1,0:T(8,128)(2,1)S(1)}) custom-call(bf16[128,2048]{1,0:T(8,128)(2,1)S(1)} %collective-permute-done.8.refs_0_, bf16[128,2048]{1,0:T(8,128)(2,1)S(1)} %collective-permute-done.13.refs_1_, bf16[2,768,2048]{2,1,0:T(8,128)(2,1)S(1)} %get-tuple-element.53.refs_2_, ...), custom_call_target="tpu_custom_call" | custom-call | flops 805306368 | bytes 3145728 | tf_op jit(solution)/shard_map/expert_3_0/pallas_call | solution.py:150
  46.5 2.7 %expert_far_ring.1 = bf16[128,2048]{1,0:T(8,128)(2,1)S(1)} custom-call(bf16[72,2048]{1,0:T(8,128)(2,1)S(1)} %collective-permute-done.12.refs_0_, bf16[72,2048]{1,0:T(8,128)(2,1)S(1)} %collective-permute-done.11.refs_1_.holder, bf16[2,768,2048]{2,1,0:T(8,128)(2,1)S(1)} %get-tuple-element.53.refs_2_, bf16[768,2048]{1,0:T(8,128)(2,1)S(1)} %get-tuple-element.50.refs_3_), custom_call_target="tpu_custom_call" | custom-call | flops 402653184 | bytes 3145728 | tf_op jit(solution)/shard_map/expert_far_ring/pallas_call | solution.py:150
  50.2 2.7 %expert_far_swapped.1 = bf16[128,2048]{1,0:T(8,128)(2,1)S(1)} custom-call(bf16[72,2048]{1,0:T(8,128)(2,1)S(1)} %collective-permute-done.14.refs_0_, bf16[72,2048]{1,0:T(8,128)(2,1)S(1)} %collective-permute-done.15.refs_1_, bf16[2,768,2048]{2,1,0:T(8,128)(2,1)S(1)} %get-tuple-element.53.refs_2_, bf16[768,2048]{1,0:T(8,128)(2,1)S(1)} %get-tuple-element.50.refs_3_), custom_call_target="tpu_custom_call" | custom-call | flops 402653184 | bytes 3145728 | tf_op jit(solution)/shard_map/expert_far_swapped/pallas_call | solution.py:150
  53.2 2.1 %collective-permute-start.19 = (bf16[72,2048]{1,0:T(8,128)(2,1)S(1)}, bf16[72,2048]{1,0:T(8,128)(2,1)S(1)}, u32[]{:S(2)}, u32[]{:S(2)}) collective-permute-start(bf16[72,2048]{1,0:T(8,128)(2,1)S(1)} %shard_map.57), channel_id=1, source_target_pairs={{0,2},{1,5},{4,0},{5,9},{8,4},{9,13},{12,8},{13,15},{14,12},{15,11... | collective-permute-start | bytes 884744 | tf_op jit(solution)/shard_map/back_4_0/ppermute | solution.py:215
  57.0 2.6 %expert_3_1.1 = (bf16[128,2048]{1,0:T(8,128)(2,1)S(1)}, bf16[128,2048]{1,0:T(8,128)(2,1)S(1)}) custom-call(bf16[136,2048]{1,0:T(8,128)(2,1)S(1)} %collective-permute-done.5.refs_0_.holder, bf16[136,2048]{1,0:T(8,128)(2,1)S(1)} %collective-permute-done.17.refs_1_, bf16[2,768,2048]{2,1,0:T(8,128)(2,1)S(1)} %get-tuple-element.53.refs_2_, ...), custom_call_target="tpu_custom_call" | custom-call | flops 80530640 | bytes 314572 | tf_op jit(solution)/shard_map/expert_3_1/pallas_call | solution.py:150
  63.4 2.0 %collective-permute-start.27 = (bf16[128,2048]{1,0:T(8,128)(2,1)S(1)}, bf16[128,2048]{1,0:T(8,128)(2,1)S(1)}, u32[]{:S(2)}, u32[]{:S(2)}) collective-permute-start(bf16[128,2048]{1,0:T(8,128)(2,1)S(1)} %shard_map.60), channel_id=1, source_target_pairs={{0,2},{1,5},{4,0},{5,9},{8,4},{9,13},{12,8},{13,15},{14,12},{15,11... | collective-permute-start | bytes 1572872 | tf_op jit(solution)/shard_map/back_3_1/ppermute | solution.py:215
  65.7 2.6 %expert_1_1.1 = (bf16[128,2048]{1,0:T(8,128)(2,1)S(1)}, bf16[128,2048]{1,0:T(8,128)(2,1)S(1)}) custom-call(bf16[136,2048]{1,0:T(8,128)(2,1)S(1)} %collective-permute-done.3.refs_0_.holder, bf16[136,2048]{1,0:T(8,128)(2,1)S(1)} %collective-permute-done.23.refs_1_, bf16[2,768,2048]{2,1,0:T(8,128)(2,1)S(1)} %get-tuple-element.53.refs_2_, ...), custom_call_target="tpu_custom_call" | custom-call | flops 805306368 | bytes 3145728 | tf_op jit(solution)/shard_map/expert_1_1/pallas_call | solution.py:150
  71.9 3.5 %collective-permute-done.27.refs_0_ = bf16[128,2048]{1,0:T(8,128)(2,1)S(1)} collective-permute-done((bf16[128,2048]{1,0:T(8,128)(2,1)S(1)}, bf16[128,2048]{1,0:T(8,128)(2,1)S(1)}, u32[]{:S(2)}, u32[]{:S(2)}) %collective-permute-start.27) | collective-permute-done | bytes 524320 | tf_op jit(solution)/shard_map/back_3_1/ppermute | solution.py:215
  77.5 3.5 %collective-permute-done.29.refs_0_ = bf16[128,2048]{1,0:T(8,128)(2,1)S(1)} collective-permute-done((bf16[128,2048]{1,0:T(8,128)(2,1)S(1)}, bf16[128,2048]{1,0:T(8,128)(2,1)S(1)}, u32[]{:S(2)}, u32[]{:S(2)}) %collective-permute-start.29) | collective-permute-done | bytes 524320 | tf_op jit(solution)/shard_map/back_2_0/ppermute | solution.py:215
  83.1 3.5 %collective-permute-done.32.refs_0_ = bf16[128,2048]{1,0:T(8,128)(2,1)S(1)} collective-permute-done((bf16[128,2048]{1,0:T(8,128)(2,1)S(1)}, bf16[128,2048]{1,0:T(8,128)(2,1)S(1)}, u32[]{:S(2)}, u32[]{:S(2)}) %collective-permute-start.32) | collective-permute-done | bytes 524320 | tf_op jit(solution)/shard_map/back_2_1/ppermute | solution.py:215
  88.0 4.3 %collective-permute-done.30.refs_0_ = bf16[128,2048]{1,0:T(8,128)(2,1)S(1)} collective-permute-done((bf16[128,2048]{1,0:T(8,128)(2,1)S(1)}, bf16[128,2048]{1,0:T(8,128)(2,1)S(1)}, u32[]{:S(2)}, u32[]{:S(2)}) %collective-permute-start.30) | collective-permute-done | bytes 524320 | tf_op jit(solution)/shard_map/back_1_0/ppermute | solution.py:215
  92.6 4.8 %collective-permute-done.33 = bf16[128,2048]{1,0:T(8,128)(2,1)S(1)} collective-permute-done((bf16[128,2048]{1,0:T(8,128)(2,1)S(1)}, bf16[128,2048]{1,0:T(8,128)(2,1)S(1)}, u32[]{:S(2)}, u32[]{:S(2)}) %collective-permute-start.33) | collective-permute-done | bytes 524320 | tf_op jit(solution)/shard_map/back_1_1/ppermute | solution.py:215
  (78 shorter events, 30.4 us)
Async XLA Ops:
  0.5 11.0 %collective-permute-start.2 = (bf16[128,2048]{1,0:T(8,128)(2,1)}, bf16[128,2048]{1,0:T(8,128)(2,1)S(1)}, u32[]{:S(2)}, u32[]{:S(2)}) collective-permute-start(bf16[128,2048]{1,0:T(8,128)(2,1)} %refs_0_.1), channel_id=1, source_target_pairs={{0,4},{1,3},{4,8},{5,1},{8,12},{9,5},{12,14},{13,9},{14,10},{15,13... | collective-permute-start | bytes 1572872 | tf_op jit(solution)/shard_map/ring_1_0/ppermute | solution.py:215
  5.0 11.3 %collective-permute-start.3 = (bf16[136,2048]{1,0:T(8,128)(2,1)S(1)}, bf16[136,2048]{1,0:T(8,128)(2,1)S(1)}, u32[]{:S(2)}, u32[]{:S(2)}) collective-permute-start(bf16[136,2048]{1,0:T(8,128)(2,1)S(1)} %maximum_maximum_fusion.refs_1_.holder), channel_id=1, source_target_pairs={{0,4},{1,3},{4,8},{5,1},{8,12},{9,5},{12,14},{13,9},{14,10},{15,13... | collective-permute-start | bytes 1671176 | tf_op jit(solution)/shard_map/ring_1_1/ppermute | solution.py:215
  11.5 10.4 %collective-permute-start.6 = (bf16[128,2048]{1,0:T(8,128)(2,1)S(1)}, bf16[128,2048]{1,0:T(8,128)(2,1)S(1)}, u32[]{:S(2)}, u32[]{:S(2)}) collective-permute-start(bf16[128,2048]{1,0:T(8,128)(2,1)S(1)} %collective-permute-done.2.refs_0_), channel_id=1, source_target_pairs={{0,4},{1,3},{4,8},{5,1},{8,12},{9,5},{12,14},{13,9},{14,10},{15,13... | collective-permute-start | bytes 1572872 | tf_op jit(solution)/shard_map/ring_2_0/ppermute | solution.py:215
  16.3 11.6 %collective-permute-start.4 = (bf16[136,2048]{1,0:T(8,128)(2,1)S(1)}, bf16[136,2048]{1,0:T(8,128)(2,1)S(1)}, u32[]{:S(2)}, u32[]{:S(2)}) collective-permute-start(bf16[136,2048]{1,0:T(8,128)(2,1)S(1)} %collective-permute-done.3.refs_0_.holder), channel_id=1, source_target_pairs={{0,4},{1,3},{4,8},{5,1},{8,12},{9,5},{12,14},{13,9},{14,10},{15,13... | collective-permute-start | bytes 1671176 | tf_op jit(solution)/shard_map/ring_2_1/ppermute | solution.py:215
  21.9 8.1 %collective-permute-start.9 = (bf16[128,2048]{1,0:T(8,128)(2,1)S(1)}, bf16[128,2048]{1,0:T(8,128)(2,1)S(1)}, u32[]{:S(2)}, u32[]{:S(2)}) collective-permute-start(bf16[128,2048]{1,0:T(8,128)(2,1)S(1)} %collective-permute-done.6.refs_0_), channel_id=1, source_target_pairs={{0,1},{1,0},{4,5},{5,4},{8,9},{9,8},{12,13},{13,12},{14,15},{15,14... | collective-permute-start | bytes 1572872 | tf_op jit(solution)/shard_map/swap_2_0/ppermute | solution.py:215
  21.9 11.6 %collective-permute-start.8 = (bf16[128,2048]{1,0:T(8,128)(2,1)S(1)}, bf16[128,2048]{1,0:T(8,128)(2,1)S(1)}, u32[]{:S(2)}, u32[]{:S(2)}) collective-permute-start(bf16[128,2048]{1,0:T(8,128)(2,1)S(1)} %collective-permute-done.6.refs_0_), channel_id=1, source_target_pairs={{0,4},{1,3},{4,8},{5,1},{8,12},{9,5},{12,14},{13,9},{14,10},{15,13... | collective-permute-start | bytes 1572872 | tf_op jit(solution)/shard_map/ring_3_0/ppermute | solution.py:215
  27.9 7.8 %collective-permute-start.10 = (bf16[136,2048]{1,0:T(8,128)(2,1)S(1)}, bf16[136,2048]{1,0:T(8,128)(2,1)S(1)}, u32[]{:S(2)}, u32[]{:S(2)}) collective-permute-start(bf16[136,2048]{1,0:T(8,128)(2,1)S(1)} %collective-permute-done.4.refs_0_.holder), channel_id=1, source_target_pairs={{0,1},{1,0},{4,5},{5,4},{8,9},{9,8},{12,13},{13,12},{14,15},{15,14... | collective-permute-start | bytes 1671176 | tf_op jit(solution)/shard_map/swap_2_1/ppermute | solution.py:215
  27.9 11.6 %collective-permute-start.5 = (bf16[136,2048]{1,0:T(8,128)(2,1)S(1)}, bf16[136,2048]{1,0:T(8,128)(2,1)S(1)}, u32[]{:S(2)}, u32[]{:S(2)}) collective-permute-start(bf16[136,2048]{1,0:T(8,128)(2,1)S(1)} %collective-permute-done.4.refs_0_.holder), channel_id=1, source_target_pairs={{0,4},{1,3},{4,8},{5,1},{8,12},{9,5},{12,14},{13,9},{14,10},{15,13... | collective-permute-start | bytes 1671176 | tf_op jit(solution)/shard_map/ring_3_1/ppermute | solution.py:215
  33.5 8.3 %collective-permute-start.13 = (bf16[128,2048]{1,0:T(8,128)(2,1)S(1)}, bf16[128,2048]{1,0:T(8,128)(2,1)S(1)}, u32[]{:S(2)}, u32[]{:S(2)}) collective-permute-start(bf16[128,2048]{1,0:T(8,128)(2,1)S(1)} %collective-permute-done.8.refs_0_), channel_id=1, source_target_pairs={{0,1},{1,0},{4,5},{5,4},{8,9},{9,8},{12,13},{13,12},{14,15},{15,14... | collective-permute-start | bytes 1572872 | tf_op jit(solution)/shard_map/swap_3_0/ppermute | solution.py:215
  33.5 10.9 %collective-permute-start.12 = (bf16[72,2048]{1,0:T(8,128)(2,1)S(1)}, bf16[72,2048]{1,0:T(8,128)(2,1)S(1)}, u32[]{:S(2)}, u32[]{:S(2)}) collective-permute-start(bf16[72,2048]{1,0:T(8,128)(2,1)S(1)} %slice.21), channel_id=1, source_target_pairs={{0,4},{1,3},{4,8},{5,1},{8,12},{9,5},{12,14},{13,9},{14,10},{15,13... | collective-permute-start | bytes 884744 | tf_op jit(solution)/shard_map/ring_4_0/ppermute | solution.py:215
  39.5 7.0 %collective-permute-start.11 = (bf16[72,2048]{1,0:T(8,128)(2,1)S(1)}, bf16[72,2048]{1,0:T(8,128)(2,1)S(1)}, u32[]{:S(2)}, u32[]{:S(2)}) collective-permute-start(bf16[72,2048]{1,0:T(8,128)(2,1)S(1)} %slice.20), channel_id=1, source_target_pairs={{0,4},{1,3},{4,8},{5,1},{8,12},{9,5},{12,14},{13,9},{14,10},{15,13... | collective-permute-start | bytes 884744 | tf_op jit(solution)/shard_map/ring_4_1/ppermute | solution.py:215
  49.7 7.3 %collective-permute-start.17 = (bf16[136,2048]{1,0:T(8,128)(2,1)S(1)}, bf16[136,2048]{1,0:T(8,128)(2,1)S(1)}, u32[]{:S(2)}, u32[]{:S(2)}) collective-permute-start(bf16[136,2048]{1,0:T(8,128)(2,1)S(1)} %collective-permute-done.5.refs_0_.holder), channel_id=1, source_target_pairs={{0,1},{1,0},{4,5},{5,4},{8,9},{9,8},{12,13},{13,12},{14,15},{15,14... | collective-permute-start | bytes 1671176 | tf_op jit(solution)/shard_map/swap_3_1/ppermute | solution.py:215
  49.8 10.0 %collective-permute-start.18 = (bf16[128,2048]{1,0:T(8,128)(2,1)S(1)}, bf16[128,2048]{1,0:T(8,128)(2,1)S(1)}, u32[]{:S(2)}, u32[]{:S(2)}) collective-permute-start(bf16[128,2048]{1,0:T(8,128)(2,1)S(1)} %get-tuple-element.75), channel_id=1, source_target_pairs={{0,1},{1,0},{4,5},{5,4},{8,9},{9,8},{12,13},{13,12},{14,15},{15,14... | collective-permute-start | bytes 1572872 | tf_op jit(solution)/shard_map/give_3_0/ppermute | solution.py:215
  55.4 7.7 %collective-permute-start.21 = (bf16[72,2048]{1,0:T(8,128)(2,1)S(1)}, bf16[72,2048]{1,0:T(8,128)(2,1)S(1)}, u32[]{:S(2)}, u32[]{:S(2)}) collective-permute-start(bf16[72,2048]{1,0:T(8,128)(2,1)S(1)} %shard_map.58), channel_id=1, source_target_pairs={{0,2},{1,5},{4,0},{5,9},{8,4},{9,13},{12,8},{13,15},{14,12},{15,11... | collective-permute-start | bytes 884744 | tf_op jit(solution)/shard_map/back_4_1/ppermute | solution.py:215
  60.6 9.2 %collective-permute-start.25 = (bf16[128,2048]{1,0:T(8,128)(2,1)S(1)}, bf16[128,2048]{1,0:T(8,128)(2,1)S(1)}, u32[]{:S(2)}, u32[]{:S(2)}) collective-permute-start(bf16[128,2048]{1,0:T(8,128)(2,1)S(1)} %shard_map.59), channel_id=1, source_target_pairs={{0,2},{1,5},{4,0},{5,9},{8,4},{9,13},{12,8},{13,15},{14,12},{15,11... | collective-permute-start | bytes 1572872 | tf_op jit(solution)/shard_map/back_3_0/ppermute | solution.py:215
  63.1 8.8 %collective-permute-start.26 = (bf16[128,2048]{1,0:T(8,128)(2,1)S(1)}, bf16[128,2048]{1,0:T(8,128)(2,1)S(1)}, u32[]{:S(2)}, u32[]{:S(2)}) collective-permute-start(bf16[128,2048]{1,0:T(8,128)(2,1)S(1)} %get-tuple-element.87), channel_id=1, source_target_pairs={{0,1},{1,0},{4,5},{5,4},{8,9},{9,8},{12,13},{13,12},{14,15},{15,14... | collective-permute-start | bytes 1572872 | tf_op jit(solution)/shard_map/give_2_1/ppermute | solution.py:215
  63.4 12.0 %collective-permute-start.27 = (bf16[128,2048]{1,0:T(8,128)(2,1)S(1)}, bf16[128,2048]{1,0:T(8,128)(2,1)S(1)}, u32[]{:S(2)}, u32[]{:S(2)}) collective-permute-start(bf16[128,2048]{1,0:T(8,128)(2,1)S(1)} %shard_map.60), channel_id=1, source_target_pairs={{0,2},{1,5},{4,0},{5,9},{8,4},{9,13},{12,8},{13,15},{14,12},{15,11... | collective-permute-start | bytes 1572872 | tf_op jit(solution)/shard_map/back_3_1/ppermute | solution.py:215
  65.5 12.1 %collective-permute-start.28 = (bf16[128,2048]{1,0:T(8,128)(2,1)S(1)}, bf16[128,2048]{1,0:T(8,128)(2,1)S(1)}, u32[]{:S(2)}, u32[]{:S(2)}) collective-permute-start(bf16[128,2048]{1,0:T(8,128)(2,1)S(1)} %get-tuple-element.90), channel_id=1, source_target_pairs={{0,1},{1,0},{4,5},{5,4},{8,9},{9,8},{12,13},{13,12},{14,15},{15,14... | collective-permute-start | bytes 1572872 | tf_op jit(solution)/shard_map/give_1_0/ppermute | solution.py:215
  70.1 10.9 %collective-permute-start.29 = (bf16[128,2048]{1,0:T(8,128)(2,1)S(1)}, bf16[128,2048]{1,0:T(8,128)(2,1)S(1)}, u32[]{:S(2)}, u32[]{:S(2)}) collective-permute-start(bf16[128,2048]{1,0:T(8,128)(2,1)S(1)} %shard_map.61), channel_id=1, source_target_pairs={{0,2},{1,5},{4,0},{5,9},{8,4},{9,13},{12,8},{13,15},{14,12},{15,11... | collective-permute-start | bytes 1572872 | tf_op jit(solution)/shard_map/back_2_0/ppermute | solution.py:215
  71.9 11.2 %collective-permute-start.31 = (bf16[128,2048]{1,0:T(8,128)(2,1)S(1)}, bf16[128,2048]{1,0:T(8,128)(2,1)S(1)}, u32[]{:S(2)}, u32[]{:S(2)}) collective-permute-start(bf16[128,2048]{1,0:T(8,128)(2,1)S(1)} %get-tuple-element.92), channel_id=1, source_target_pairs={{0,1},{1,0},{4,5},{5,4},{8,9},{9,8},{12,13},{13,12},{14,15},{15,14... | collective-permute-start | bytes 1572872 | tf_op jit(solution)/shard_map/give_1_1/ppermute | solution.py:215
  75.7 10.9 %collective-permute-start.32 = (bf16[128,2048]{1,0:T(8,128)(2,1)S(1)}, bf16[128,2048]{1,0:T(8,128)(2,1)S(1)}, u32[]{:S(2)}, u32[]{:S(2)}) collective-permute-start(bf16[128,2048]{1,0:T(8,128)(2,1)S(1)} %shard_map.62), channel_id=1, source_target_pairs={{0,2},{1,5},{4,0},{5,9},{8,4},{9,13},{12,8},{13,15},{14,12},{15,11... | collective-permute-start | bytes 1572872 | tf_op jit(solution)/shard_map/back_2_1/ppermute | solution.py:215
  77.5 10.4 %collective-permute-start.22 = (bf16[128,2048]{1,0:T(8,128)(2,1)S(1)}, bf16[128,2048]{1,0:T(8,128)(2,1)S(1)}, u32[]{:S(2)}, u32[]{:S(2)}) collective-permute-start(bf16[128,2048]{1,0:T(8,128)(2,1)S(1)} %get-tuple-element.78), channel_id=1, source_target_pairs={{0,1},{1,0},{4,5},{5,4},{8,9},{9,8},{12,13},{13,12},{14,15},{15,14... | collective-permute-start | bytes 1572872 | tf_op jit(solution)/shard_map/give_0_0/ppermute | solution.py:215
  81.4 10.9 %collective-permute-start.30 = (bf16[128,2048]{1,0:T(8,128)(2,1)S(1)}, bf16[128,2048]{1,0:T(8,128)(2,1)S(1)}, u32[]{:S(2)}, u32[]{:S(2)}) collective-permute-start(bf16[128,2048]{1,0:T(8,128)(2,1)S(1)} %shard_map.63), channel_id=1, source_target_pairs={{0,2},{1,5},{4,0},{5,9},{8,4},{9,13},{12,8},{13,15},{14,12},{15,11... | collective-permute-start | bytes 1572872 | tf_op jit(solution)/shard_map/back_1_0/ppermute | solution.py:215
  87.0 10.4 %collective-permute-start.33 = (bf16[128,2048]{1,0:T(8,128)(2,1)S(1)}, bf16[128,2048]{1,0:T(8,128)(2,1)S(1)}, u32[]{:S(2)}, u32[]{:S(2)}) collective-permute-start(bf16[128,2048]{1,0:T(8,128)(2,1)S(1)} %shard_map.65), channel_id=1, source_target_pairs={{0,3},{1,4},{4,1},{5,8},{8,5},{9,12},{12,9},{13,14},{14,13},{15,10... | collective-permute-start | bytes 1572872 | tf_op jit(solution)/shard_map/back_1_1/ppermute | solution.py:215
  (12 other events, 54.5 us)

commit v15 on v14

--- a/solution.py
+++ b/solution.py
@@ -162,35 +162,40 @@
     )(*blocks, *weights)
 
 
-def weighted_kernel(kind, first, height, low, part_rows, expert_ref, holder, mine, theirs, *refs):
-    *arrived, out = refs
+def weighted_kernel(kind, own, distant, experts_ref, holder, *refs):
+    *terms, out = refs
+    rows = out.shape[0]
     last = holder.shape[0] - GATE_ROWS
     near, far = (holder[last:, (2 * kind + i) * LANES : (2 * kind + i + 1) * LANES].astype(jnp.float32) for i in (0, 1))
-    wanted = lax.broadcasted_iota(jnp.int32, near.shape, 0) == expert_ref[0]
-    line = jnp.sum(jnp.where(wanted, near + far, 0.0), axis=0, keepdims=True)
-    weight = jnp.broadcast_to(line, near.shape).T[first : first + height, :1]
-    value = mine[...].astype(jnp.float32) + theirs[first : first + height, :].astype(jnp.float32)
-    value = weight * value
-    out[:height, :] = value.astype(out.dtype)
-    if height < out.shape[0]:
-        out[height:, :] = jnp.zeros((out.shape[0] - height, out.shape[1]), out.dtype)
-    if arrived:
-        part = slice(low, low + part_rows)
-        out[part, :] = (value[part] + arrived[0][:part_rows, :].astype(jnp.float32)).astype(out.dtype)
-
-
-def weighted(expert, holder, kind, mine, theirs, *arrived, first=0, low=0, part=None, more=0, dtype=jnp.bfloat16):
+
+    def weight(place):
+        wanted = lax.broadcasted_iota(jnp.int32, near.shape, 0) == experts_ref[place]
+        line = jnp.sum(jnp.where(wanted, near + far, 0.0), axis=0, keepdims=True)
+        return jnp.broadcast_to(line, near.shape).T[:rows, :1]
+
+    def total(blocks):
+        return sum(block[...].astype(jnp.float32) for block in blocks)
+
+    value = weight(0) * total(terms[:own])
+    if distant:
+        value += weight(1) * total(terms[own : own + distant])
+    if own + distant < len(terms):
+        value += total(terms[own + distant :])
+    out[...] = value.astype(out.dtype)
+
+
+def weighted(experts, holder, kind, own, distant=(), plain=(), dtype=jnp.bfloat16):
     whole = pl.BlockSpec(memory_space=pltpu.VMEM)
-    height = mine.shape[0]
-    size = height * mine.shape[1]
+    terms = [*own, *distant, *plain]
+    size = own[0].size
     return pl.pallas_call(
-        functools.partial(weighted_kernel, kind, first, height, low, part or height),
-        out_shape=jax.ShapeDtypeStruct((height + more, mine.shape[1]), dtype),
-        in_specs=[pl.BlockSpec(memory_space=pltpu.SMEM)] + [whole] * (3 + len(arrived)),
+        functools.partial(weighted_kernel, kind, len(own), len(distant)),
+        out_shape=jax.ShapeDtypeStruct(own[0].shape, dtype),
+        in_specs=[pl.BlockSpec(memory_space=pltpu.SMEM)] + [whole] * (1 + len(terms)),
         out_specs=whole,
         compiler_params=pltpu.CompilerParams(vmem_limit_bytes=10 << 20),
         cost_estimate=pl.CostEstimate(flops=size * 20000, bytes_accessed=size, transcendentals=0),
-    )(expert, holder, mine, theirs, *arrived)
+    )(experts, holder, *terms)
 
 
 def by_tokens(tokens, expert_ids, route_gate, gate_up, down_proj):
@@ -223,7 +228,11 @@
     def after(value, *earlier):
         return lax.optimization_barrier((value, *earlier))[0]
 
-    expert = jnp.right_shift(lax.axis_index("blk"), 1).astype(jnp.int32).reshape(1)
+    table = np.zeros((2 * chips, 2), np.int32)
+    for place in range(chips):
+        for core in (0, 1):
+            table[2 * order[place] + core] = order[place], order[(place + 1 - 2 * core) % chips]
+    expert = lax.dynamic_index_in_dim(jnp.asarray(table), lax.axis_index("blk"), 0, keepdims=False)
     ring = [send(tokens, forth, "ring_1_0"), None]
     others = send(tokens, cores, "swap_0_0")
     chosen = jnp.arange(GATE_ROWS, dtype=jnp.int32)[:, None, None] == expert_ids.T[None]
@@ -262,7 +271,7 @@
         if step < far - 1:
             ring = [send(block, forth, f"ring_{step + 1}_{c}") for c, block in enumerate(ring)]
         else:
-            ring = [send(ring[0][: half + GATE_ROWS], forth, f"ring_{far}_0"), send(ring[1][half:], forth, f"ring_{far}_1")]
+            ring = [send(ring[0], forth, f"ring_{far}_0")]
         for c in chains:
             if (step, c) == (1, 1):
                 delayed = blocks[1]
@@ -272,45 +281,46 @@
                 last = blocks[1], swapped[1]
                 continue
             kept = expert_rows(step, c, [after(blocks[c], earlier), swapped[c]])
-            ring[c] = after(ring[c], kept)
-            earlier = ring[c]
+            place = c if step < far - 1 else 0
+            ring[place] = after(ring[place], kept)
+            earlier = ring[place]
 
     with jax.named_scope("expert_far_ring"):
-        (given,) = half_expert([half] * 2, ring, near, split=1)
-    swapped = [send(block, cores, f"swap_{far}_{c}") for c, block in enumerate(ring)]
-    swapped[0] = after(swapped[0], given)
+        (given,) = half_expert([rows], ring, near, split=1)
+    swapped = send(ring[0], cores, f"swap_{far}")
+    mine, theirs = results[far - 1, 0]
+    earlier = weighted(expert, holders[far - 1], 0, [after(mine, given), theirs])
+    sums = [send(earlier, back, f"back_{far - 1}_0")]
+    swapped = after(swapped, earlier)
     given = send(given, cores, "give_far")
     with jax.named_scope("expert_far_swapped"):
-        (kept,) = half_expert([half] * 2, swapped, near, split=1)
-
-    late = []
-    earlier = kept
-    for c in chains:
-        first = (1 - c) * half
-        mine = after(kept[first : first + half], earlier)
-        earlier = weighted(expert, ring[1], c, mine, given, first=first, more=GATE_ROWS)
-        late.append(send(earlier, back, f"back_{far}_{c}"))
+        (kept,) = half_expert([rows], [swapped], near, split=1)
+    earlier = rounded(total(kept, given))
+    sums.append(send(earlier, back, f"back_{far}_1"))
     earlier = expert_rows(far - 1, 1, [after(last[0], earlier), last[1]], cost=0.2)
-    sums = []
-    for c in chains:
-        mine, theirs = results[far - 1, c]
-        low = half if c == 0 else 0
-        earlier = weighted(expert, holders[far - 1], c, after(mine, earlier), theirs, late[c], low=low, part=half)
-        sums.append(send(earlier, back, f"back_{far - 1}_{c}"))
-        if c == 0:
-            swapped = send(after(delayed, earlier), cores, "swap_1_1")
-            for step in range(far - 2, 1, -1):
-                for c2 in chains:
-                    give(step, c2, earlier)
-    give(1, 0, earlier)
-    give(0, 0, earlier)
-    earlier = expert_rows(1, 1, [after(delayed, earlier), swapped])
-    for step in range(far - 2, 0, -1):
+    for step in range(far - 2, 1, -1):
         for c in chains:
-            mine, theirs = results[step, c]
-            earlier = weighted(expert, holders[step], c, after(mine, earlier), theirs, sums[c])
-            sums[c] = send(earlier, across if (step, c) == (1, 1) else back, f"back_{step}_{c}")
-    own = weighted(expert, packed, 0, *results[0, 0], sums[0], dtype=jnp.float32)
+            give(step, c, earlier)
+    swapped = send(after(delayed, earlier), cores, "swap_1_1")
+    steps = [(step, c) for step in range(far - 1, 0, -1) for c in chains][1:]
+    for order_place in range(0, len(steps) - 1, 2):
+        steps[order_place : order_place + 2] = steps[order_place : order_place + 2][::-1]
+    for step, c in steps:
+        mine, theirs = results[step, c]
+        far_sum = (step, c) == (far - 1, 1)
+        mine = after(mine, earlier, sums[0]) if (step, c) == (1, 1) else after(mine, earlier)
+        if far_sum:
+            part = weighted(expert, holders[step], c, [mine], [sums[c]], dtype=jnp.float32)
+            earlier = weighted(expert, holders[step], c, [after(theirs, part)], plain=[part])
+        else:
+            earlier = weighted(expert, holders[step], c, [mine, theirs], plain=[sums[c]])
+        sums[c] = send(earlier, across if (step, c) == (1, 1) else back, f"back_{step}_{c}")
+        if (step, c) == (far - 2, 0):
+            give(1, 0, earlier)
+        if far_sum:
+            give(0, 0, earlier)
+            earlier = expert_rows(1, 1, [after(delayed, earlier), swapped])
+    own = weighted(expert, packed, 0, results[0, 0], plain=[sums[0]], dtype=jnp.float32)
     return rounded(total(own, sums[1]))
 
 

time: 98.4 us -> 99.3 us (level)
  starting transfers between devices: 33.2 us -> 27 us
  Pallas kernels: 29.2 us -> 33.4 us
  waiting for transfers between devices: 32 us -> 34.1 us
    ppermute x34 -> x31, starting transfers between devices: 33.2 us -> 27 us  [send(): return lax.ppermute(value, 'blk', pairs)]
    pallas_call x9 -> x8, Pallas kernels: 2.43 us -> 6.67 us  [weighted(): pl.pallas_call(functools.partial(weighted_kernel, kind, len(own), len(dis...]
    ppermute x34 -> x31, waiting for transfers between devices: 32 us -> 34.1 us  [send(): return lax.ppermute(value, 'blk', pairs)]
  transfers between devices with their start and end apart: 34 -> 31, of which waited for: 15 -> 11; matrix products, arithmetic and copies ran while one was open for 1% -> 2% of each run, Pallas kernels for 30% -> 34%
where the time goes in v15:
time: 99.3 us; the launch traced here: 99.1 us
  waiting for transfers between devices  34.1 us (34%)
  Pallas kernels  33.4 us (34%)
  starting transfers between devices  27 us (27%)
  local copies, waits for them, and re-layouts  2.59 us (3%)
  other arithmetic  1.78 us (2%)
    ppermute x31, waiting for transfers between devices, send(): return lax.ppermute(value, 'blk', pairs)  34.1 us
    ppermute x31, starting transfers between devices, send(): return lax.ppermute(value, 'blk', pairs)  27 us
    pallas_call x9, Pallas kernels, half_expert(): pl.pallas_call(functools.partial(half_expert_kernel, tuple(heights), load...  23.9 us
    pallas_call x8, Pallas kernels, weighted(): pl.pallas_call(functools.partial(weighted_kernel, kind, len(own), len(dis...  6.67 us
    pallas_call x1, Pallas kernels, loaded(): pl.pallas_call(load_kernel, out_shape=[jax.ShapeDtypeStruct(array.shape,...  2.86 us
  transfers between devices with their start and end apart: 31, of which 11 were waited for; matrix products, arithmetic and copies ran while one was open for 2% of the time, Pallas kernels for 34%

profile of v15, /device:TPU:0, one launch (start us, length us, event | category | flops | bytes accessed | tf_op | source)
XLA Modules:
  0.0 99.1 jit_solution(4737077362029902396)
XLA Ops:
  0.5 2.6 %collective-permute-start.2 = (bf16[128,2048]{1,0:T(8,128)(2,1)}, bf16[128,2048]{1,0:T(8,128)(2,1)S(1)}, u32[]{:S(2)}, u32[]{:S(2)}) collective-permute-start(bf16[128,2048]{1,0:T(8,128)(2,1)} %refs_0_.1), channel_id=1, source_target_pairs={{0,4},{1,3},{4,8},{5,1},{8,12},{9,5},{12,14},{13,9},{14,10},{15,13... | collective-permute-start | bytes 1572872 | tf_op jit(solution)/shard_map/ring_1_0/ppermute | solution.py:220
  7.4 1.9 %copy-done = bf16[768,2048]{1,0:T(8,128)(2,1)S(1)} copy-done((bf16[768,2048]{1,0:T(8,128)(2,1)S(1)}, bf16[768,2048]{1,0:T(8,128)(2,1)}, u32[]{:S(2)}) %copy-start) | copy-done | bytes 3145752
  9.2 2.9 %shard_map.65 = (bf16[2,768,2048]{2,1,0:T(8,128)(2,1)S(1)}, bf16[768,2048]{1,0:T(8,128)(2,1)S(1)}) custom-call(bf16[2,768,2048]{2,1,0:T(8,128)(2,1)} %refs_0_, bf16[768,2048]{1,0:T(8,128)(2,1)S(1)} %copy-done), custom_call_target="tpu_custom_call" | custom-call | flops 268435456 | bytes 1048576 | tf_op jit(solution)/shard_map/pallas_call | solution.py:111
  13.8 2.7 %expert_0.1 = (bf16[128,2048]{1,0:T(8,128)(2,1)S(1)}, bf16[128,2048]{1,0:T(8,128)(2,1)S(1)}) custom-call(bf16[128,2048]{1,0:T(8,128)(2,1)S(1)} %copy-done.1, bf16[136,2048]{1,0:T(8,128)(2,1)S(1)} %maximum_maximum_fusion.refs_1_.holder, bf16[2,768,2048]{2,1,0:T(8,128)(2,1)S(1)} %get-tuple-element.52.refs_2_.refs_1_, ...), custom_call_target="tpu_custom_call" | custom-call | flops 805306368 | bytes 3145728 | tf_op jit(solution)/shard_map/expert_0/pallas_call | solution.py:150
  16.5 1.9 %collective-permute-start.4 = (bf16[136,2048]{1,0:T(8,128)(2,1)S(1)}, bf16[136,2048]{1,0:T(8,128)(2,1)S(1)}, u32[]{:S(2)}, u32[]{:S(2)}) collective-permute-start(bf16[136,2048]{1,0:T(8,128)(2,1)S(1)} %collective-permute-done.3.refs_0_.holder), channel_id=1, source_target_pairs={{0,4},{1,3},{4,8},{5,1},{8,12},{9,5},{12,14},{13,9},{14,10},{15,13... | collective-permute-start | bytes 1671176 | tf_op jit(solution)/shard_map/ring_2_1/ppermute | solution.py:220
  18.4 2.7 %expert_1_0.1 = (bf16[128,2048]{1,0:T(8,128)(2,1)S(1)}, bf16[128,2048]{1,0:T(8,128)(2,1)S(1)}) custom-call(bf16[128,2048]{1,0:T(8,128)(2,1)S(1)} %collective-permute-done.2.refs_0_, bf16[128,2048]{1,0:T(8,128)(2,1)S(1)} %collective-permute-done.7.refs_1_, bf16[2,768,2048]{2,1,0:T(8,128)(2,1)S(1)} %get-tuple-element.52.refs_2_.refs_1_, ...), custom_call_target="tpu_custom_call" | custom-call | flops 805306368 | bytes 3145728 | tf_op jit(solution)/shard_map/expert_1_0/pallas_call | solution.py:150
  21.9 2.1 %collective-permute-start.8 = (bf16[128,2048]{1,0:T(8,128)(2,1)S(1)}, bf16[128,2048]{1,0:T(8,128)(2,1)S(1)}, u32[]{:S(2)}, u32[]{:S(2)}) collective-permute-start(bf16[128,2048]{1,0:T(8,128)(2,1)S(1)} %collective-permute-done.6.refs_0_), channel_id=1, source_target_pairs={{0,4},{1,3},{4,8},{5,1},{8,12},{9,5},{12,14},{13,9},{14,10},{15,13... | collective-permute-start | bytes 1572872 | tf_op jit(solution)/shard_map/ring_3_0/ppermute | solution.py:220
  24.0 3.9 %collective-permute-done.4.refs_0_.holder = bf16[136,2048]{1,0:T(8,128)(2,1)S(1)} collective-permute-done((bf16[136,2048]{1,0:T(8,128)(2,1)S(1)}, bf16[136,2048]{1,0:T(8,128)(2,1)S(1)}, u32[]{:S(2)}, u32[]{:S(2)}) %collective-permute-start.4) | collective-permute-done | bytes 557088 | tf_op jit(solution)/shard_map/ring_2_1/ppermute | solution.py:220
  27.9 2.1 %collective-permute-start.5 = (bf16[136,2048]{1,0:T(8,128)(2,1)S(1)}, bf16[136,2048]{1,0:T(8,128)(2,1)S(1)}, u32[]{:S(2)}, u32[]{:S(2)}) collective-permute-start(bf16[136,2048]{1,0:T(8,128)(2,1)S(1)} %collective-permute-done.4.refs_0_.holder), channel_id=1, source_target_pairs={{0,4},{1,3},{4,8},{5,1},{8,12},{9,5},{12,14},{13,9},{14,10},{15,13... | collective-permute-start | bytes 1671176 | tf_op jit(solution)/shard_map/ring_3_1/ppermute | solution.py:220
  30.0 2.6 %expert_2_0.1 = (bf16[128,2048]{1,0:T(8,128)(2,1)S(1)}, bf16[128,2048]{1,0:T(8,128)(2,1)S(1)}) custom-call(bf16[128,2048]{1,0:T(8,128)(2,1)S(1)} %collective-permute-done.6.refs_0_, bf16[128,2048]{1,0:T(8,128)(2,1)S(1)} %collective-permute-done.9.refs_1_, bf16[2,768,2048]{2,1,0:T(8,128)(2,1)S(1)} %get-tuple-element.52.refs_2_.refs_1_, ...), custom_call_target="tpu_custom_call" | custom-call | flops 805306368 | bytes 3145728 | tf_op jit(solution)/shard_map/expert_2_0/pallas_call | solution.py:150
  33.5 2.1 %collective-permute-start.11 = (bf16[128,2048]{1,0:T(8,128)(2,1)S(1)}, bf16[128,2048]{1,0:T(8,128)(2,1)S(1)}, u32[]{:S(2)}, u32[]{:S(2)}) collective-permute-start(bf16[128,2048]{1,0:T(8,128)(2,1)S(1)} %collective-permute-done.8.refs_0_), channel_id=1, source_target_pairs={{0,4},{1,3},{4,8},{5,1},{8,12},{9,5},{12,14},{13,9},{14,10},{15,13... | collective-permute-start | bytes 1572872 | tf_op jit(solution)/shard_map/ring_4_0/ppermute | solution.py:220
  35.6 2.6 %expert_2_1.1 = (bf16[128,2048]{1,0:T(8,128)(2,1)S(1)}, bf16[128,2048]{1,0:T(8,128)(2,1)S(1)}) custom-call(bf16[136,2048]{1,0:T(8,128)(2,1)S(1)} %collective-permute-done.4.refs_0_.holder, bf16[136,2048]{1,0:T(8,128)(2,1)S(1)} %collective-permute-done.10.refs_1_, bf16[2,768,2048]{2,1,0:T(8,128)(2,1)S(1)} %get-tuple-element.52.refs_2_.refs_1_, ...), custom_call_target="tpu_custom_call" | custom-call | flops 805306368 | bytes 3145728 | tf_op jit(solution)/shard_map/expert_2_1/pallas_call | solution.py:150
  39.5 2.6 %expert_3_0.1 = (bf16[128,2048]{1,0:T(8,128)(2,1)S(1)}, bf16[128,2048]{1,0:T(8,128)(2,1)S(1)}) custom-call(bf16[128,2048]{1,0:T(8,128)(2,1)S(1)} %collective-permute-done.8.refs_0_, bf16[128,2048]{1,0:T(8,128)(2,1)S(1)} %collective-permute-done.12.refs_1_, bf16[2,768,2048]{2,1,0:T(8,128)(2,1)S(1)} %get-tuple-element.52.refs_2_.refs_1_, ...), custom_call_target="tpu_custom_call" | custom-call | flops 805306368 | bytes 3145728 | tf_op jit(solution)/shard_map/expert_3_0/pallas_call | solution.py:150
  42.2 2.9 %collective-permute-done.11.refs_0_ = bf16[128,2048]{1,0:T(8,128)(2,1)S(1)} collective-permute-done((bf16[128,2048]{1,0:T(8,128)(2,1)S(1)}, bf16[128,2048]{1,0:T(8,128)(2,1)S(1)}, u32[]{:S(2)}, u32[]{:S(2)}) %collective-permute-start.11) | collective-permute-done | bytes 524320 | tf_op jit(solution)/shard_map/ring_4_0/ppermute | solution.py:220
  45.1 2.7 %expert_far_ring.1 = bf16[128,2048]{1,0:T(8,128)(2,1)S(1)} custom-call(bf16[128,2048]{1,0:T(8,128)(2,1)S(1)} %collective-permute-done.11.refs_0_, bf16[2,768,2048]{2,1,0:T(8,128)(2,1)S(1)} %get-tuple-element.52.refs_2_.refs_1_, bf16[768,2048]{1,0:T(8,128)(2,1)S(1)} %get-tuple-element.49.refs_3_.refs_2_), custom_call_target="tpu_custom_call" | custom-call | flops 402653184 | bytes 3145728 | tf_op jit(solution)/shard_map/expert_far_ring/pallas_call | solution.py:150
  49.2 2.1 %collective-permute-start.19 = (bf16[128,2048]{1,0:T(8,128)(2,1)S(1)}, bf16[128,2048]{1,0:T(8,128)(2,1)S(1)}, u32[]{:S(2)}, u32[]{:S(2)}) collective-permute-start(bf16[128,2048]{1,0:T(8,128)(2,1)S(1)} %shard_map.66), channel_id=1, source_target_pairs={{0,2},{1,5},{4,0},{5,9},{8,4},{9,13},{12,8},{13,15},{14,12},{15,11... | collective-permute-start | bytes 1572872 | tf_op jit(solution)/shard_map/back_3_0/ppermute | solution.py:220
  51.3 2.7 %expert_far_swapped.1 = bf16[128,2048]{1,0:T(8,128)(2,1)S(1)} custom-call(bf16[128,2048]{1,0:T(8,128)(2,1)S(1)} %collective-permute-done.13.refs_0_, bf16[2,768,2048]{2,1,0:T(8,128)(2,1)S(1)} %get-tuple-element.52.refs_2_.refs_1_, bf16[768,2048]{1,0:T(8,128)(2,1)S(1)} %get-tuple-element.49.refs_3_.refs_2_), custom_call_target="tpu_custom_call" | custom-call | flops 402653184 | bytes 3145728 | tf_op jit(solution)/shard_map/expert_far_swapped/pallas_call | solution.py:150
  54.1 2.7 %expert_3_1.1 = (bf16[128,2048]{1,0:T(8,128)(2,1)S(1)}, bf16[128,2048]{1,0:T(8,128)(2,1)S(1)}) custom-call(bf16[136,2048]{1,0:T(8,128)(2,1)S(1)} %collective-permute-done.5.holder.refs_0_, bf16[136,2048]{1,0:T(8,128)(2,1)S(1)} %collective-permute-done.16.refs_1_, bf16[2,768,2048]{2,1,0:T(8,128)(2,1)S(1)} %get-tuple-element.52.refs_2_.refs_1_, ...), custom_call_target="tpu_custom_call" | custom-call | flops 80530640 | bytes 314572 | tf_op jit(solution)/shard_map/expert_3_1/pallas_call | solution.py:150
  61.5 4.7 %collective-permute-done.20.refs_1_ = bf16[128,2048]{1,0:T(8,128)(2,1)S(1)} collective-permute-done((bf16[128,2048]{1,0:T(8,128)(2,1)S(1)}, bf16[128,2048]{1,0:T(8,128)(2,1)S(1)}, u32[]{:S(2)}, u32[]{:S(2)}) %collective-permute-start.20) | collective-permute-done | bytes 524320 | tf_op jit(solution)/shard_map/back_4_1/ppermute | solution.py:220
  69.6 2.7 %expert_1_1.1 = (bf16[128,2048]{1,0:T(8,128)(2,1)S(1)}, bf16[128,2048]{1,0:T(8,128)(2,1)S(1)}) custom-call(bf16[136,2048]{1,0:T(8,128)(2,1)S(1)} %collective-permute-done.3.refs_0_.holder, bf16[136,2048]{1,0:T(8,128)(2,1)S(1)} %collective-permute-done.22.refs_1_, bf16[2,768,2048]{2,1,0:T(8,128)(2,1)S(1)} %get-tuple-element.52.refs_2_.refs_1_, ...), custom_call_target="tpu_custom_call" | custom-call | flops 805306368 | bytes 3145728 | tf_op jit(solution)/shard_map/expert_1_1/pallas_call | solution.py:150
  74.9 2.6 %collective-permute-done.27.refs_2_ = bf16[128,2048]{1,0:T(8,128)(2,1)S(1)} collective-permute-done((bf16[128,2048]{1,0:T(8,128)(2,1)S(1)}, bf16[128,2048]{1,0:T(8,128)(2,1)S(1)}, u32[]{:S(2)}, u32[]{:S(2)}) %collective-permute-start.27) | collective-permute-done | bytes 524320 | tf_op jit(solution)/shard_map/back_3_1/ppermute | solution.py:220
  79.8 3.3 %collective-permute-done.25.refs_2_ = bf16[128,2048]{1,0:T(8,128)(2,1)S(1)} collective-permute-done((bf16[128,2048]{1,0:T(8,128)(2,1)S(1)}, bf16[128,2048]{1,0:T(8,128)(2,1)S(1)}, u32[]{:S(2)}, u32[]{:S(2)}) %collective-permute-start.25) | collective-permute-done | bytes 524320 | tf_op jit(solution)/shard_map/back_1_0/ppermute | solution.py:220
  83.1 5.6 %collective-permute-done.29.refs_2_ = bf16[128,2048]{1,0:T(8,128)(2,1)S(1)} collective-permute-done((bf16[128,2048]{1,0:T(8,128)(2,1)S(1)}, bf16[128,2048]{1,0:T(8,128)(2,1)S(1)}, u32[]{:S(2)}, u32[]{:S(2)}) %collective-permute-start.29) | collective-permute-done | bytes 524320 | tf_op jit(solution)/shard_map/back_2_1/ppermute | solution.py:220
  91.1 7.1 %collective-permute-done.30 = bf16[128,2048]{1,0:T(8,128)(2,1)S(1)} collective-permute-done((bf16[128,2048]{1,0:T(8,128)(2,1)S(1)}, bf16[128,2048]{1,0:T(8,128)(2,1)S(1)}, u32[]{:S(2)}, u32[]{:S(2)}) %collective-permute-start.30) | collective-permute-done | bytes 524320 | tf_op jit(solution)/shard_map/back_1_1/ppermute | solution.py:220
  (70 shorter events, 27.4 us)
Async XLA Ops:
  0.5 11.7 %collective-permute-start.2 = (bf16[128,2048]{1,0:T(8,128)(2,1)}, bf16[128,2048]{1,0:T(8,128)(2,1)S(1)}, u32[]{:S(2)}, u32[]{:S(2)}) collective-permute-start(bf16[128,2048]{1,0:T(8,128)(2,1)} %refs_0_.1), channel_id=1, source_target_pairs={{0,4},{1,3},{4,8},{5,1},{8,12},{9,5},{12,14},{13,9},{14,10},{15,13... | collective-permute-start | bytes 1572872 | tf_op jit(solution)/shard_map/ring_1_0/ppermute | solution.py:220
  5.0 11.5 %collective-permute-start.3 = (bf16[136,2048]{1,0:T(8,128)(2,1)S(1)}, bf16[136,2048]{1,0:T(8,128)(2,1)S(1)}, u32[]{:S(2)}, u32[]{:S(2)}) collective-permute-start(bf16[136,2048]{1,0:T(8,128)(2,1)S(1)} %maximum_maximum_fusion.refs_1_.holder), channel_id=1, source_target_pairs={{0,4},{1,3},{4,8},{5,1},{8,12},{9,5},{12,14},{13,9},{14,10},{15,13... | collective-permute-start | bytes 1671176 | tf_op jit(solution)/shard_map/ring_1_1/ppermute | solution.py:220
  12.1 6.3 %collective-permute-start.7 = (bf16[128,2048]{1,0:T(8,128)(2,1)S(1)}, bf16[128,2048]{1,0:T(8,128)(2,1)S(1)}, u32[]{:S(2)}, u32[]{:S(2)}) collective-permute-start(bf16[128,2048]{1,0:T(8,128)(2,1)S(1)} %collective-permute-done.2.refs_0_), channel_id=1, source_target_pairs={{0,1},{1,0},{4,5},{5,4},{8,9},{9,8},{12,13},{13,12},{14,15},{15,14... | collective-permute-start | bytes 1572872 | tf_op jit(solution)/shard_map/swap_1_0/ppermute | solution.py:220
  12.2 9.7 %collective-permute-start.6 = (bf16[128,2048]{1,0:T(8,128)(2,1)S(1)}, bf16[128,2048]{1,0:T(8,128)(2,1)S(1)}, u32[]{:S(2)}, u32[]{:S(2)}) collective-permute-start(bf16[128,2048]{1,0:T(8,128)(2,1)S(1)} %collective-permute-done.2.refs_0_), channel_id=1, source_target_pairs={{0,4},{1,3},{4,8},{5,1},{8,12},{9,5},{12,14},{13,9},{14,10},{15,13... | collective-permute-start | bytes 1572872 | tf_op jit(solution)/shard_map/ring_2_0/ppermute | solution.py:220
  16.5 11.4 %collective-permute-start.4 = (bf16[136,2048]{1,0:T(8,128)(2,1)S(1)}, bf16[136,2048]{1,0:T(8,128)(2,1)S(1)}, u32[]{:S(2)}, u32[]{:S(2)}) collective-permute-start(bf16[136,2048]{1,0:T(8,128)(2,1)S(1)} %collective-permute-done.3.refs_0_.holder), channel_id=1, source_target_pairs={{0,4},{1,3},{4,8},{5,1},{8,12},{9,5},{12,14},{13,9},{14,10},{15,13... | collective-permute-start | bytes 1671176 | tf_op jit(solution)/shard_map/ring_2_1/ppermute | solution.py:220
  21.9 8.1 %collective-permute-start.9 = (bf16[128,2048]{1,0:T(8,128)(2,1)S(1)}, bf16[128,2048]{1,0:T(8,128)(2,1)S(1)}, u32[]{:S(2)}, u32[]{:S(2)}) collective-permute-start(bf16[128,2048]{1,0:T(8,128)(2,1)S(1)} %collective-permute-done.6.refs_0_), channel_id=1, source_target_pairs={{0,1},{1,0},{4,5},{5,4},{8,9},{9,8},{12,13},{13,12},{14,15},{15,14... | collective-permute-start | bytes 1572872 | tf_op jit(solution)/shard_map/swap_2_0/ppermute | solution.py:220
  21.9 11.6 %collective-permute-start.8 = (bf16[128,2048]{1,0:T(8,128)(2,1)S(1)}, bf16[128,2048]{1,0:T(8,128)(2,1)S(1)}, u32[]{:S(2)}, u32[]{:S(2)}) collective-permute-start(bf16[128,2048]{1,0:T(8,128)(2,1)S(1)} %collective-permute-done.6.refs_0_), channel_id=1, source_target_pairs={{0,4},{1,3},{4,8},{5,1},{8,12},{9,5},{12,14},{13,9},{14,10},{15,13... | collective-permute-start | bytes 1572872 | tf_op jit(solution)/shard_map/ring_3_0/ppermute | solution.py:220
  27.9 7.7 %collective-permute-start.10 = (bf16[136,2048]{1,0:T(8,128)(2,1)S(1)}, bf16[136,2048]{1,0:T(8,128)(2,1)S(1)}, u32[]{:S(2)}, u32[]{:S(2)}) collective-permute-start(bf16[136,2048]{1,0:T(8,128)(2,1)S(1)} %collective-permute-done.4.refs_0_.holder), channel_id=1, source_target_pairs={{0,1},{1,0},{4,5},{5,4},{8,9},{9,8},{12,13},{13,12},{14,15},{15,14... | collective-permute-start | bytes 1671176 | tf_op jit(solution)/shard_map/swap_2_1/ppermute | solution.py:220
  27.9 11.6 %collective-permute-start.5 = (bf16[136,2048]{1,0:T(8,128)(2,1)S(1)}, bf16[136,2048]{1,0:T(8,128)(2,1)S(1)}, u32[]{:S(2)}, u32[]{:S(2)}) collective-permute-start(bf16[136,2048]{1,0:T(8,128)(2,1)S(1)} %collective-permute-done.4.refs_0_.holder), channel_id=1, source_target_pairs={{0,4},{1,3},{4,8},{5,1},{8,12},{9,5},{12,14},{13,9},{14,10},{15,13... | collective-permute-start | bytes 1671176 | tf_op jit(solution)/shard_map/ring_3_1/ppermute | solution.py:220
  33.5 11.6 %collective-permute-start.11 = (bf16[128,2048]{1,0:T(8,128)(2,1)S(1)}, bf16[128,2048]{1,0:T(8,128)(2,1)S(1)}, u32[]{:S(2)}, u32[]{:S(2)}) collective-permute-start(bf16[128,2048]{1,0:T(8,128)(2,1)S(1)} %collective-permute-done.8.refs_0_), channel_id=1, source_target_pairs={{0,4},{1,3},{4,8},{5,1},{8,12},{9,5},{12,14},{13,9},{14,10},{15,13... | collective-permute-start | bytes 1572872 | tf_op jit(solution)/shard_map/ring_4_0/ppermute | solution.py:220
  42.1 6.3 %collective-permute-start.14 = (bf16[128,2048]{1,0:T(8,128)(2,1)S(1)}, bf16[128,2048]{1,0:T(8,128)(2,1)S(1)}, u32[]{:S(2)}, u32[]{:S(2)}) collective-permute-start(bf16[128,2048]{1,0:T(8,128)(2,1)S(1)} %get-tuple-element.69), channel_id=1, source_target_pairs={{0,1},{1,0},{4,5},{5,4},{8,9},{9,8},{12,13},{13,12},{14,15},{15,14... | collective-permute-start | bytes 1572872 | tf_op jit(solution)/shard_map/give_3_0/ppermute | solution.py:220
  49.2 9.8 %collective-permute-start.19 = (bf16[128,2048]{1,0:T(8,128)(2,1)S(1)}, bf16[128,2048]{1,0:T(8,128)(2,1)S(1)}, u32[]{:S(2)}, u32[]{:S(2)}) collective-permute-start(bf16[128,2048]{1,0:T(8,128)(2,1)S(1)} %shard_map.66), channel_id=1, source_target_pairs={{0,2},{1,5},{4,0},{5,9},{8,4},{9,13},{12,8},{13,15},{14,12},{15,11... | collective-permute-start | bytes 1572872 | tf_op jit(solution)/shard_map/back_3_0/ppermute | solution.py:220
  57.0 9.2 %collective-permute-start.20 = (bf16[128,2048]{1,0:T(8,128)(2,1)S(1)}, bf16[128,2048]{1,0:T(8,128)(2,1)S(1)}, u32[]{:S(2)}, u32[]{:S(2)}) collective-permute-start(bf16[128,2048]{1,0:T(8,128)(2,1)S(1)} %add_convert_fusion.1), channel_id=1, source_target_pairs={{0,2},{1,5},{4,0},{5,9},{8,4},{9,13},{12,8},{13,15},{14,12},{15,11... | collective-permute-start | bytes 1572872 | tf_op jit(solution)/shard_map/back_4_1/ppermute | solution.py:220
  58.5 16.4 %collective-permute-start.26 = (bf16[128,2048]{1,0:T(8,128)(2,1)S(1)}, bf16[128,2048]{1,0:T(8,128)(2,1)S(1)}, u32[]{:S(2)}, u32[]{:S(2)}) collective-permute-start(bf16[128,2048]{1,0:T(8,128)(2,1)S(1)} %get-tuple-element.88), channel_id=1, source_target_pairs={{0,1},{1,0},{4,5},{5,4},{8,9},{9,8},{12,13},{13,12},{14,15},{15,14... | collective-permute-start | bytes 1572872 | tf_op jit(solution)/shard_map/give_2_1/ppermute | solution.py:220
  58.5 8.6 %collective-permute-start.17 = (bf16[128,2048]{1,0:T(8,128)(2,1)S(1)}, bf16[128,2048]{1,0:T(8,128)(2,1)S(1)}, u32[]{:S(2)}, u32[]{:S(2)}) collective-permute-start(bf16[128,2048]{1,0:T(8,128)(2,1)S(1)} %get-tuple-element.72), channel_id=1, source_target_pairs={{0,1},{1,0},{4,5},{5,4},{8,9},{9,8},{12,13},{13,12},{14,15},{15,14... | collective-permute-start | bytes 1572872 | tf_op jit(solution)/shard_map/give_3_1/ppermute | solution.py:220
  59.0 10.6 %collective-permute-start.22 = (bf16[136,2048]{1,0:T(8,128)(2,1)S(1)}, bf16[136,2048]{1,0:T(8,128)(2,1)S(1)}, u32[]{:S(2)}, u32[]{:S(2)}) collective-permute-start(bf16[136,2048]{1,0:T(8,128)(2,1)S(1)} %collective-permute-done.3.refs_0_.holder), channel_id=1, source_target_pairs={{0,1},{1,0},{4,5},{5,4},{8,9},{9,8},{12,13},{13,12},{14,15},{15,14... | collective-permute-start | bytes 1671176 | tf_op jit(solution)/shard_map/swap_1_1/ppermute | solution.py:220
  59.9 12.9 %collective-permute-start.24 = (bf16[128,2048]{1,0:T(8,128)(2,1)S(1)}, bf16[128,2048]{1,0:T(8,128)(2,1)S(1)}, u32[]{:S(2)}, u32[]{:S(2)}) collective-permute-start(bf16[128,2048]{1,0:T(8,128)(2,1)S(1)} %shard_map.67), channel_id=1, source_target_pairs={{0,2},{1,5},{4,0},{5,9},{8,4},{9,13},{12,8},{13,15},{14,12},{15,11... | collective-permute-start | bytes 1572872 | tf_op jit(solution)/shard_map/back_2_0/ppermute | solution.py:220
  66.2 6.5 %collective-permute-start.23 = (bf16[128,2048]{1,0:T(8,128)(2,1)S(1)}, bf16[128,2048]{1,0:T(8,128)(2,1)S(1)}, u32[]{:S(2)}, u32[]{:S(2)}) collective-permute-start(bf16[128,2048]{1,0:T(8,128)(2,1)S(1)} %get-tuple-element.85), channel_id=1, source_target_pairs={{0,1},{1,0},{4,5},{5,4},{8,9},{9,8},{12,13},{13,12},{14,15},{15,14... | collective-permute-start | bytes 1572872 | tf_op jit(solution)/shard_map/give_1_0/ppermute | solution.py:220
  67.9 9.5 %collective-permute-start.27 = (bf16[128,2048]{1,0:T(8,128)(2,1)S(1)}, bf16[128,2048]{1,0:T(8,128)(2,1)S(1)}, u32[]{:S(2)}, u32[]{:S(2)}) collective-permute-start(bf16[128,2048]{1,0:T(8,128)(2,1)S(1)} %shard_map.69), channel_id=1, source_target_pairs={{0,2},{1,5},{4,0},{5,9},{8,4},{9,13},{12,8},{13,15},{14,12},{15,11... | collective-permute-start | bytes 1572872 | tf_op jit(solution)/shard_map/back_3_1/ppermute | solution.py:220
  72.3 10.8 %collective-permute-start.28 = (bf16[128,2048]{1,0:T(8,128)(2,1)S(1)}, bf16[128,2048]{1,0:T(8,128)(2,1)S(1)}, u32[]{:S(2)}, u32[]{:S(2)}) collective-permute-start(bf16[128,2048]{1,0:T(8,128)(2,1)S(1)} %get-tuple-element.90), channel_id=1, source_target_pairs={{0,1},{1,0},{4,5},{5,4},{8,9},{9,8},{12,13},{13,12},{14,15},{15,14... | collective-permute-start | bytes 1572872 | tf_op jit(solution)/shard_map/give_1_1/ppermute | solution.py:220
  73.6 9.5 %collective-permute-start.25 = (bf16[128,2048]{1,0:T(8,128)(2,1)S(1)}, bf16[128,2048]{1,0:T(8,128)(2,1)S(1)}, u32[]{:S(2)}, u32[]{:S(2)}) collective-permute-start(bf16[128,2048]{1,0:T(8,128)(2,1)S(1)} %shard_map.70), channel_id=1, source_target_pairs={{0,2},{1,5},{4,0},{5,9},{8,4},{9,13},{12,8},{13,15},{14,12},{15,11... | collective-permute-start | bytes 1572872 | tf_op jit(solution)/shard_map/back_1_0/ppermute | solution.py:220
  78.3 10.4 %collective-permute-start.29 = (bf16[128,2048]{1,0:T(8,128)(2,1)S(1)}, bf16[128,2048]{1,0:T(8,128)(2,1)S(1)}, u32[]{:S(2)}, u32[]{:S(2)}) collective-permute-start(bf16[128,2048]{1,0:T(8,128)(2,1)S(1)} %shard_map.72), channel_id=1, source_target_pairs={{0,2},{1,5},{4,0},{5,9},{8,4},{9,13},{12,8},{13,15},{14,12},{15,11... | collective-permute-start | bytes 1572872 | tf_op jit(solution)/shard_map/back_2_1/ppermute | solution.py:220
  79.8 10.4 %collective-permute-start.21 = (bf16[128,2048]{1,0:T(8,128)(2,1)S(1)}, bf16[128,2048]{1,0:T(8,128)(2,1)S(1)}, u32[]{:S(2)}, u32[]{:S(2)}) collective-permute-start(bf16[128,2048]{1,0:T(8,128)(2,1)S(1)} %get-tuple-element.79), channel_id=1, source_target_pairs={{0,1},{1,0},{4,5},{5,4},{8,9},{9,8},{12,13},{13,12},{14,15},{15,14... | collective-permute-start | bytes 1572872 | tf_op jit(solution)/shard_map/give_0_0/ppermute | solution.py:220
  89.6 8.7 %collective-permute-start.30 = (bf16[128,2048]{1,0:T(8,128)(2,1)S(1)}, bf16[128,2048]{1,0:T(8,128)(2,1)S(1)}, u32[]{:S(2)}, u32[]{:S(2)}) collective-permute-start(bf16[128,2048]{1,0:T(8,128)(2,1)S(1)} %shard_map.73), channel_id=1, source_target_pairs={{0,3},{1,4},{4,1},{5,8},{8,5},{9,12},{12,9},{13,14},{14,13},{15,10... | collective-permute-start | bytes 1572872 | tf_op jit(solution)/shard_map/back_1_1/ppermute | solution.py:220
  (9 other events, 39.0 us)

commit v16 on v15

--- a/solution.py
+++ b/solution.py
@@ -162,14 +162,14 @@
     )(*blocks, *weights)
 
 
-def weighted_kernel(kind, own, distant, experts_ref, holder, *refs):
-    *terms, out = refs
+def weighted_kernel(kind, own, distant, *refs):
+    experts, holder, terms, out = refs[: 1 + bool(distant)], refs[1 + bool(distant)], refs[2 + bool(distant) : -1], refs[-1]
     rows = out.shape[0]
     last = holder.shape[0] - GATE_ROWS
     near, far = (holder[last:, (2 * kind + i) * LANES : (2 * kind + i + 1) * LANES].astype(jnp.float32) for i in (0, 1))
 
     def weight(place):
-        wanted = lax.broadcasted_iota(jnp.int32, near.shape, 0) == experts_ref[place]
+        wanted = lax.broadcasted_iota(jnp.int32, near.shape, 0) == experts[place][0]
         line = jnp.sum(jnp.where(wanted, near + far, 0.0), axis=0, keepdims=True)
         return jnp.broadcast_to(line, near.shape).T[:rows, :1]
 
@@ -187,15 +187,16 @@
 def weighted(experts, holder, kind, own, distant=(), plain=(), dtype=jnp.bfloat16):
     whole = pl.BlockSpec(memory_space=pltpu.VMEM)
     terms = [*own, *distant, *plain]
+    experts = experts[: 1 + bool(distant)]
     size = own[0].size
     return pl.pallas_call(
         functools.partial(weighted_kernel, kind, len(own), len(distant)),
         out_shape=jax.ShapeDtypeStruct(own[0].shape, dtype),
-        in_specs=[pl.BlockSpec(memory_space=pltpu.SMEM)] + [whole] * (1 + len(terms)),
+        in_specs=[pl.BlockSpec(memory_space=pltpu.SMEM)] * len(experts) + [whole] * (1 + len(terms)),
         out_specs=whole,
         compiler_params=pltpu.CompilerParams(vmem_limit_bytes=10 << 20),
         cost_estimate=pl.CostEstimate(flops=size * 20000, bytes_accessed=size, transcendentals=0),
-    )(experts, holder, *terms)
+    )(*experts, holder, *terms)
 
 
 def by_tokens(tokens, expert_ids, route_gate, gate_up, down_proj):
@@ -228,11 +229,14 @@
     def after(value, *earlier):
         return lax.optimization_barrier((value, *earlier))[0]
 
-    table = np.zeros((2 * chips, 2), np.int32)
-    for place in range(chips):
-        for core in (0, 1):
-            table[2 * order[place] + core] = order[place], order[(place + 1 - 2 * core) % chips]
-    expert = lax.dynamic_index_in_dim(jnp.asarray(table), lax.axis_index("blk"), 0, keepdims=False)
+    device = lax.axis_index("blk").astype(jnp.int32)
+    chip, core = jnp.right_shift(device, 1), jnp.bitwise_and(device, 1)
+    odd = jnp.bitwise_and(chip, 1)
+    place = jnp.where(odd == 1, chips - 1 - jnp.right_shift(chip, 1), jnp.right_shift(chip, 1))
+    ahead = place + 1 - 2 * core
+    ahead = jnp.where(ahead < 0, chips - 1, jnp.where(ahead == chips, 0, ahead))
+    ahead = jnp.where(ahead < far, 2 * ahead, 2 * (chips - 1 - ahead) + 1)
+    expert = [chip.reshape(1), ahead.reshape(1)]
     ring = [send(tokens, forth, "ring_1_0"), None]
     others = send(tokens, cores, "swap_0_0")
     chosen = jnp.arange(GATE_ROWS, dtype=jnp.int32)[:, None, None] == expert_ids.T[None]
@@ -242,7 +246,7 @@
     packed = jnp.concatenate([others, widened(gates, send(gates, cores, "swap_0_1"), tokens.shape[1])])
     ring[1] = send(packed, forth, "ring_1_1")
 
-    near = loaded(after(gate_up, expert), down_proj)
+    near = loaded(after(gate_up, *expert), down_proj)
     ring[0] = after(ring[0], near[1])
     results, holders = {}, {0: packed}
     with jax.named_scope("expert_0"):
@@ -288,27 +292,25 @@
     with jax.named_scope("expert_far_ring"):
         (given,) = half_expert([rows], ring, near, split=1)
     swapped = send(ring[0], cores, f"swap_{far}")
-    mine, theirs = results[far - 1, 0]
-    earlier = weighted(expert, holders[far - 1], 0, [after(mine, given), theirs])
-    sums = [send(earlier, back, f"back_{far - 1}_0")]
-    swapped = after(swapped, earlier)
+    swapped = after(swapped, given)
     given = send(given, cores, "give_far")
     with jax.named_scope("expert_far_swapped"):
         (kept,) = half_expert([rows], [swapped], near, split=1)
     earlier = rounded(total(kept, given))
-    sums.append(send(earlier, back, f"back_{far}_1"))
+    sums = [None, send(earlier, back, f"back_{far}_1")]
+    mine, theirs = results[far - 1, 0]
+    earlier = weighted(expert, holders[far - 1], 0, [after(mine, earlier), theirs])
+    sums[0] = send(earlier, back, f"back_{far - 1}_0")
     earlier = expert_rows(far - 1, 1, [after(last[0], earlier), last[1]], cost=0.2)
     for step in range(far - 2, 1, -1):
         for c in chains:
             give(step, c, earlier)
     swapped = send(after(delayed, earlier), cores, "swap_1_1")
     steps = [(step, c) for step in range(far - 1, 0, -1) for c in chains][1:]
-    for order_place in range(0, len(steps) - 1, 2):
-        steps[order_place : order_place + 2] = steps[order_place : order_place + 2][::-1]
     for step, c in steps:
         mine, theirs = results[step, c]
         far_sum = (step, c) == (far - 1, 1)
-        mine = after(mine, earlier, sums[0]) if (step, c) == (1, 1) else after(mine, earlier)
+        mine = after(mine, earlier)
         if far_sum:
             part = weighted(expert, holders[step], c, [mine], [sums[c]], dtype=jnp.float32)
             earlier = weighted(expert, holders[step], c, [after(theirs, part)], plain=[part])

time: 99.3 us -> 95.2 us (0.959)
  Pallas kernels: 33.4 us -> 29.1 us
  starting transfers between devices: 27 us -> 30 us
  waiting for transfers between devices: 34.1 us -> 32.1 us
    pallas_call x8, Pallas kernels: 6.67 us -> 2.34 us  [weighted(): pl.pallas_call(functools.partial(weighted_kernel, kind, len(own), len(dis...]
    ppermute x31, starting transfers between devices: 27 us -> 30 us  [send(): return lax.ppermute(value, 'blk', pairs)]
    ppermute x31, waiting for transfers between devices: 34.1 us -> 32.1 us  [send(): return lax.ppermute(value, 'blk', pairs)]
  transfers between devices with their start and end apart: 31 -> 31, of which waited for: 11 -> 14; matrix products, arithmetic and copies ran while one was open for 2% -> 1% of each run, Pallas kernels for 34% -> 31%
where the time goes in v16:
time: 95.2 us; the launch traced here: 95.1 us
  waiting for transfers between devices  32.1 us (34%)
  starting transfers between devices  30 us (32%)
  Pallas kernels  29.1 us (31%)
  local copies, waits for them, and re-layouts  1.9 us (2%)
  other arithmetic  1.79 us (2%)
    ppermute x31, waiting for transfers between devices, send(): return lax.ppermute(value, 'blk', pairs)  32.1 us
    ppermute x31, starting transfers between devices, send(): return lax.ppermute(value, 'blk', pairs)  30 us
    pallas_call x9, Pallas kernels, half_expert(): pl.pallas_call(functools.partial(half_expert_kernel, tuple(heights), load...  23.9 us
    pallas_call x1, Pallas kernels, loaded(): pl.pallas_call(load_kernel, out_shape=[jax.ShapeDtypeStruct(array.shape,...  2.86 us
    pallas_call x8, Pallas kernels, weighted(): pl.pallas_call(functools.partial(weighted_kernel, kind, len(own), len(dis...  2.34 us
  transfers between devices with their start and end apart: 31, of which 14 were waited for; matrix products, arithmetic and copies ran while one was open for 1% of the time, Pallas kernels for 31%

profile of v16, /device:TPU:0, one launch (start us, length us, event | category | flops | bytes accessed | tf_op | source)
XLA Modules:
  0.0 95.1 jit_solution(10883029510649964698)
XLA Ops:
  0.5 2.6 %collective-permute-start.2 = (bf16[128,2048]{1,0:T(8,128)(2,1)}, bf16[128,2048]{1,0:T(8,128)(2,1)S(1)}, u32[]{:S(2)}, u32[]{:S(2)}) collective-permute-start(bf16[128,2048]{1,0:T(8,128)(2,1)} %refs_0_.1), channel_id=1, source_target_pairs={{0,4},{1,3},{4,8},{5,1},{8,12},{9,5},{12,14},{13,9},{14,10},{15,13... | collective-permute-start | bytes 1572872 | tf_op jit(solution)/shard_map/ring_1_0/ppermute | solution.py:221
  8.6 2.9 %shard_map.56 = (bf16[2,768,2048]{2,1,0:T(8,128)(2,1)S(1)}, bf16[768,2048]{1,0:T(8,128)(2,1)S(1)}) custom-call(bf16[2,768,2048]{2,1,0:T(8,128)(2,1)} %refs_0_, bf16[768,2048]{1,0:T(8,128)(2,1)S(1)} %copy-done), custom_call_target="tpu_custom_call" | custom-call | flops 268435456 | bytes 1048576 | tf_op jit(solution)/shard_map/pallas_call | solution.py:111
  13.2 2.6 %expert_0.1 = (bf16[128,2048]{1,0:T(8,128)(2,1)S(1)}, bf16[128,2048]{1,0:T(8,128)(2,1)S(1)}) custom-call(bf16[128,2048]{1,0:T(8,128)(2,1)S(1)} %copy-done.1, bf16[136,2048]{1,0:T(8,128)(2,1)S(1)} %maximum_maximum_fusion.refs_1_, bf16[2,768,2048]{2,1,0:T(8,128)(2,1)S(1)} %get-tuple-element.52.refs_2_.refs_1_, ...), custom_call_target="tpu_custom_call" | custom-call | flops 805306368 | bytes 3145728 | tf_op jit(solution)/shard_map/expert_0/pallas_call | solution.py:150
  16.3 2.1 %collective-permute-start.4 = (bf16[136,2048]{1,0:T(8,128)(2,1)S(1)}, bf16[136,2048]{1,0:T(8,128)(2,1)S(1)}, u32[]{:S(2)}, u32[]{:S(2)}) collective-permute-start(bf16[136,2048]{1,0:T(8,128)(2,1)S(1)} %collective-permute-done.3.refs_0_.refs_1_), channel_id=1, source_target_pairs={{0,4},{1,3},{4,8},{5,1},{8,12},{9,5},{12,14},{13,9},{14,10},{15,13... | collective-permute-start | bytes 1671176 | tf_op jit(solution)/shard_map/ring_2_1/ppermute | solution.py:221
  18.4 2.7 %expert_1_0.1 = (bf16[128,2048]{1,0:T(8,128)(2,1)S(1)}, bf16[128,2048]{1,0:T(8,128)(2,1)S(1)}) custom-call(bf16[128,2048]{1,0:T(8,128)(2,1)S(1)} %collective-permute-done.2.refs_0_, bf16[128,2048]{1,0:T(8,128)(2,1)S(1)} %collective-permute-done.7.refs_1_, bf16[2,768,2048]{2,1,0:T(8,128)(2,1)S(1)} %get-tuple-element.52.refs_2_.refs_1_, ...), custom_call_target="tpu_custom_call" | custom-call | flops 805306368 | bytes 3145728 | tf_op jit(solution)/shard_map/expert_1_0/pallas_call | solution.py:150
  21.9 2.1 %collective-permute-start.8 = (bf16[128,2048]{1,0:T(8,128)(2,1)S(1)}, bf16[128,2048]{1,0:T(8,128)(2,1)S(1)}, u32[]{:S(2)}, u32[]{:S(2)}) collective-permute-start(bf16[128,2048]{1,0:T(8,128)(2,1)S(1)} %collective-permute-done.6.refs_0_), channel_id=1, source_target_pairs={{0,4},{1,3},{4,8},{5,1},{8,12},{9,5},{12,14},{13,9},{14,10},{15,13... | collective-permute-start | bytes 1572872 | tf_op jit(solution)/shard_map/ring_3_0/ppermute | solution.py:221
  24.0 3.9 %collective-permute-done.4.refs_0_.refs_1_ = bf16[136,2048]{1,0:T(8,128)(2,1)S(1)} collective-permute-done((bf16[136,2048]{1,0:T(8,128)(2,1)S(1)}, bf16[136,2048]{1,0:T(8,128)(2,1)S(1)}, u32[]{:S(2)}, u32[]{:S(2)}) %collective-permute-start.4) | collective-permute-done | bytes 557088 | tf_op jit(solution)/shard_map/ring_2_1/ppermute | solution.py:221
  27.9 2.1 %collective-permute-start.5 = (bf16[136,2048]{1,0:T(8,128)(2,1)S(1)}, bf16[136,2048]{1,0:T(8,128)(2,1)S(1)}, u32[]{:S(2)}, u32[]{:S(2)}) collective-permute-start(bf16[136,2048]{1,0:T(8,128)(2,1)S(1)} %collective-permute-done.4.refs_0_.refs_1_), channel_id=1, source_target_pairs={{0,4},{1,3},{4,8},{5,1},{8,12},{9,5},{12,14},{13,9},{14,10},{15,13... | collective-permute-start | bytes 1671176 | tf_op jit(solution)/shard_map/ring_3_1/ppermute | solution.py:221
  30.0 2.6 %expert_2_0.1 = (bf16[128,2048]{1,0:T(8,128)(2,1)S(1)}, bf16[128,2048]{1,0:T(8,128)(2,1)S(1)}) custom-call(bf16[128,2048]{1,0:T(8,128)(2,1)S(1)} %collective-permute-done.6.refs_0_, bf16[128,2048]{1,0:T(8,128)(2,1)S(1)} %collective-permute-done.9.refs_1_, bf16[2,768,2048]{2,1,0:T(8,128)(2,1)S(1)} %get-tuple-element.52.refs_2_.refs_1_, ...), custom_call_target="tpu_custom_call" | custom-call | flops 805306368 | bytes 3145728 | tf_op jit(solution)/shard_map/expert_2_0/pallas_call | solution.py:150
  33.5 2.1 %collective-permute-start.12 = (bf16[128,2048]{1,0:T(8,128)(2,1)S(1)}, bf16[128,2048]{1,0:T(8,128)(2,1)S(1)}, u32[]{:S(2)}, u32[]{:S(2)}) collective-permute-start(bf16[128,2048]{1,0:T(8,128)(2,1)S(1)} %collective-permute-done.8.refs_0_), channel_id=1, source_target_pairs={{0,4},{1,3},{4,8},{5,1},{8,12},{9,5},{12,14},{13,9},{14,10},{15,13... | collective-permute-start | bytes 1572872 | tf_op jit(solution)/shard_map/ring_4_0/ppermute | solution.py:221
  35.6 2.6 %expert_2_1.1 = (bf16[128,2048]{1,0:T(8,128)(2,1)S(1)}, bf16[128,2048]{1,0:T(8,128)(2,1)S(1)}) custom-call(bf16[136,2048]{1,0:T(8,128)(2,1)S(1)} %collective-permute-done.4.refs_0_.refs_1_, bf16[136,2048]{1,0:T(8,128)(2,1)S(1)} %collective-permute-done.10.refs_1_, bf16[2,768,2048]{2,1,0:T(8,128)(2,1)S(1)} %get-tuple-element.52.refs_2_.refs_1_, ...), custom_call_target="tpu_custom_call" | custom-call | flops 805306368 | bytes 3145728 | tf_op jit(solution)/shard_map/expert_2_1/pallas_call | solution.py:150
  39.5 2.6 %expert_3_0.1 = (bf16[128,2048]{1,0:T(8,128)(2,1)S(1)}, bf16[128,2048]{1,0:T(8,128)(2,1)S(1)}) custom-call(bf16[128,2048]{1,0:T(8,128)(2,1)S(1)} %collective-permute-done.8.refs_0_, bf16[128,2048]{1,0:T(8,128)(2,1)S(1)} %collective-permute-done.11.refs_1_, bf16[2,768,2048]{2,1,0:T(8,128)(2,1)S(1)} %get-tuple-element.52.refs_2_.refs_1_, ...), custom_call_target="tpu_custom_call" | custom-call | flops 805306368 | bytes 3145728 | tf_op jit(solution)/shard_map/expert_3_0/pallas_call | solution.py:150
  42.1 3.0 %collective-permute-done.12.refs_0_ = bf16[128,2048]{1,0:T(8,128)(2,1)S(1)} collective-permute-done((bf16[128,2048]{1,0:T(8,128)(2,1)S(1)}, bf16[128,2048]{1,0:T(8,128)(2,1)S(1)}, u32[]{:S(2)}, u32[]{:S(2)}) %collective-permute-start.12) | collective-permute-done | bytes 524320 | tf_op jit(solution)/shard_map/ring_4_0/ppermute | solution.py:221
  45.1 2.7 %expert_far_ring.1 = bf16[128,2048]{1,0:T(8,128)(2,1)S(1)} custom-call(bf16[128,2048]{1,0:T(8,128)(2,1)S(1)} %collective-permute-done.12.refs_0_, bf16[2,768,2048]{2,1,0:T(8,128)(2,1)S(1)} %get-tuple-element.52.refs_2_.refs_1_, bf16[768,2048]{1,0:T(8,128)(2,1)S(1)} %get-tuple-element.49.refs_3_.refs_2_), custom_call_target="tpu_custom_call" | custom-call | flops 402653184 | bytes 3145728 | tf_op jit(solution)/shard_map/expert_far_ring/pallas_call | solution.py:150
  48.9 2.7 %expert_far_swapped.1 = bf16[128,2048]{1,0:T(8,128)(2,1)S(1)} custom-call(bf16[128,2048]{1,0:T(8,128)(2,1)S(1)} %collective-permute-done.13.refs_0_, bf16[2,768,2048]{2,1,0:T(8,128)(2,1)S(1)} %get-tuple-element.52.refs_2_.refs_1_, bf16[768,2048]{1,0:T(8,128)(2,1)S(1)} %get-tuple-element.49.refs_3_.refs_2_), custom_call_target="tpu_custom_call" | custom-call | flops 402653184 | bytes 3145728 | tf_op jit(solution)/shard_map/expert_far_swapped/pallas_call | solution.py:150
  54.0 2.7 %expert_3_1.1 = (bf16[128,2048]{1,0:T(8,128)(2,1)S(1)}, bf16[128,2048]{1,0:T(8,128)(2,1)S(1)}) custom-call(bf16[136,2048]{1,0:T(8,128)(2,1)S(1)} %collective-permute-done.5.refs_1_.refs_0_.refs_2_, bf16[136,2048]{1,0:T(8,128)(2,1)S(1)} %collective-permute-done.16.refs_1_, bf16[2,768,2048]{2,1,0:T(8,128)(2,1)S(1)} %get-tuple-element.52.refs_2_.refs_1_, ...), custom_call_target="tpu_custom_call" | custom-call | flops 80530640 | bytes 314572 | tf_op jit(solution)/shard_map/expert_3_1/pallas_call | solution.py:150
  58.9 2.1 %collective-permute-done.18.refs_4_ = bf16[128,2048]{1,0:T(8,128)(2,1)S(1)} collective-permute-done((bf16[128,2048]{1,0:T(8,128)(2,1)S(1)}, bf16[128,2048]{1,0:T(8,128)(2,1)S(1)}, u32[]{:S(2)}, u32[]{:S(2)}) %collective-permute-start.18) | collective-permute-done | bytes 524320 | tf_op jit(solution)/shard_map/back_4_1/ppermute | solution.py:221
  61.6 2.2 %collective-permute-start.24 = (bf16[128,2048]{1,0:T(8,128)(2,1)S(1)}, bf16[128,2048]{1,0:T(8,128)(2,1)S(1)}, u32[]{:S(2)}, u32[]{:S(2)}) collective-permute-start(bf16[128,2048]{1,0:T(8,128)(2,1)S(1)} %shard_map.59), channel_id=1, source_target_pairs={{0,2},{1,5},{4,0},{5,9},{8,4},{9,13},{12,8},{13,15},{14,12},{15,11... | collective-permute-start | bytes 1572872 | tf_op jit(solution)/shard_map/back_3_1/ppermute | solution.py:221
  63.8 2.6 %expert_1_1.1 = (bf16[128,2048]{1,0:T(8,128)(2,1)S(1)}, bf16[128,2048]{1,0:T(8,128)(2,1)S(1)}) custom-call(bf16[136,2048]{1,0:T(8,128)(2,1)S(1)} %collective-permute-done.3.refs_0_.refs_1_, bf16[136,2048]{1,0:T(8,128)(2,1)S(1)} %collective-permute-done.20.refs_1_, bf16[2,768,2048]{2,1,0:T(8,128)(2,1)S(1)} %get-tuple-element.52.refs_2_.refs_1_, ...), custom_call_target="tpu_custom_call" | custom-call | flops 805306368 | bytes 3145728 | tf_op jit(solution)/shard_map/expert_1_1/pallas_call | solution.py:150
  69.4 2.8 %collective-permute-done.24.refs_4_ = bf16[128,2048]{1,0:T(8,128)(2,1)S(1)} collective-permute-done((bf16[128,2048]{1,0:T(8,128)(2,1)S(1)}, bf16[128,2048]{1,0:T(8,128)(2,1)S(1)}, u32[]{:S(2)}, u32[]{:S(2)}) %collective-permute-start.24) | collective-permute-done | bytes 524320 | tf_op jit(solution)/shard_map/back_3_1/ppermute | solution.py:221
  74.5 3.3 %collective-permute-done.26.refs_4_ = bf16[128,2048]{1,0:T(8,128)(2,1)S(1)} collective-permute-done((bf16[128,2048]{1,0:T(8,128)(2,1)S(1)}, bf16[128,2048]{1,0:T(8,128)(2,1)S(1)}, u32[]{:S(2)}, u32[]{:S(2)}) %collective-permute-start.26) | collective-permute-done | bytes 524320 | tf_op jit(solution)/shard_map/back_2_0/ppermute | solution.py:221
  80.2 3.3 %collective-permute-done.29.refs_4_ = bf16[128,2048]{1,0:T(8,128)(2,1)S(1)} collective-permute-done((bf16[128,2048]{1,0:T(8,128)(2,1)S(1)}, bf16[128,2048]{1,0:T(8,128)(2,1)S(1)}, u32[]{:S(2)}, u32[]{:S(2)}) %collective-permute-start.29) | collective-permute-done | bytes 524320 | tf_op jit(solution)/shard_map/back_2_1/ppermute | solution.py:221
  84.6 4.4 %collective-permute-done.27.refs_4_ = bf16[128,2048]{1,0:T(8,128)(2,1)S(1)} collective-permute-done((bf16[128,2048]{1,0:T(8,128)(2,1)S(1)}, bf16[128,2048]{1,0:T(8,128)(2,1)S(1)}, u32[]{:S(2)}, u32[]{:S(2)}) %collective-permute-start.27) | collective-permute-done | bytes 524320 | tf_op jit(solution)/shard_map/back_1_0/ppermute | solution.py:221
  89.4 4.8 %collective-permute-done.30 = bf16[128,2048]{1,0:T(8,128)(2,1)S(1)} collective-permute-done((bf16[128,2048]{1,0:T(8,128)(2,1)S(1)}, bf16[128,2048]{1,0:T(8,128)(2,1)S(1)}, u32[]{:S(2)}, u32[]{:S(2)}) %collective-permute-start.30) | collective-permute-done | bytes 524320 | tf_op jit(solution)/shard_map/back_1_1/ppermute | solution.py:221
  (69 shorter events, 27.5 us)
Async XLA Ops:
  0.5 11.0 %collective-permute-start.2 = (bf16[128,2048]{1,0:T(8,128)(2,1)}, bf16[128,2048]{1,0:T(8,128)(2,1)S(1)}, u32[]{:S(2)}, u32[]{:S(2)}) collective-permute-start(bf16[128,2048]{1,0:T(8,128)(2,1)} %refs_0_.1), channel_id=1, source_target_pairs={{0,4},{1,3},{4,8},{5,1},{8,12},{9,5},{12,14},{13,9},{14,10},{15,13... | collective-permute-start | bytes 1572872 | tf_op jit(solution)/shard_map/ring_1_0/ppermute | solution.py:221
  5.0 11.3 %collective-permute-start.3 = (bf16[136,2048]{1,0:T(8,128)(2,1)S(1)}, bf16[136,2048]{1,0:T(8,128)(2,1)S(1)}, u32[]{:S(2)}, u32[]{:S(2)}) collective-permute-start(bf16[136,2048]{1,0:T(8,128)(2,1)S(1)} %maximum_maximum_fusion.refs_1_), channel_id=1, source_target_pairs={{0,4},{1,3},{4,8},{5,1},{8,12},{9,5},{12,14},{13,9},{14,10},{15,13... | collective-permute-start | bytes 1671176 | tf_op jit(solution)/shard_map/ring_1_1/ppermute | solution.py:221
  11.4 6.9 %collective-permute-start.7 = (bf16[128,2048]{1,0:T(8,128)(2,1)S(1)}, bf16[128,2048]{1,0:T(8,128)(2,1)S(1)}, u32[]{:S(2)}, u32[]{:S(2)}) collective-permute-start(bf16[128,2048]{1,0:T(8,128)(2,1)S(1)} %collective-permute-done.2.refs_0_), channel_id=1, source_target_pairs={{0,1},{1,0},{4,5},{5,4},{8,9},{9,8},{12,13},{13,12},{14,15},{15,14... | collective-permute-start | bytes 1572872 | tf_op jit(solution)/shard_map/swap_1_0/ppermute | solution.py:221
  11.5 10.4 %collective-permute-start.6 = (bf16[128,2048]{1,0:T(8,128)(2,1)S(1)}, bf16[128,2048]{1,0:T(8,128)(2,1)S(1)}, u32[]{:S(2)}, u32[]{:S(2)}) collective-permute-start(bf16[128,2048]{1,0:T(8,128)(2,1)S(1)} %collective-permute-done.2.refs_0_), channel_id=1, source_target_pairs={{0,4},{1,3},{4,8},{5,1},{8,12},{9,5},{12,14},{13,9},{14,10},{15,13... | collective-permute-start | bytes 1572872 | tf_op jit(solution)/shard_map/ring_2_0/ppermute | solution.py:221
  16.3 11.6 %collective-permute-start.4 = (bf16[136,2048]{1,0:T(8,128)(2,1)S(1)}, bf16[136,2048]{1,0:T(8,128)(2,1)S(1)}, u32[]{:S(2)}, u32[]{:S(2)}) collective-permute-start(bf16[136,2048]{1,0:T(8,128)(2,1)S(1)} %collective-permute-done.3.refs_0_.refs_1_), channel_id=1, source_target_pairs={{0,4},{1,3},{4,8},{5,1},{8,12},{9,5},{12,14},{13,9},{14,10},{15,13... | collective-permute-start | bytes 1671176 | tf_op jit(solution)/shard_map/ring_2_1/ppermute | solution.py:221
  21.9 8.1 %collective-permute-start.9 = (bf16[128,2048]{1,0:T(8,128)(2,1)S(1)}, bf16[128,2048]{1,0:T(8,128)(2,1)S(1)}, u32[]{:S(2)}, u32[]{:S(2)}) collective-permute-start(bf16[128,2048]{1,0:T(8,128)(2,1)S(1)} %collective-permute-done.6.refs_0_), channel_id=1, source_target_pairs={{0,1},{1,0},{4,5},{5,4},{8,9},{9,8},{12,13},{13,12},{14,15},{15,14... | collective-permute-start | bytes 1572872 | tf_op jit(solution)/shard_map/swap_2_0/ppermute | solution.py:221
  21.9 11.6 %collective-permute-start.8 = (bf16[128,2048]{1,0:T(8,128)(2,1)S(1)}, bf16[128,2048]{1,0:T(8,128)(2,1)S(1)}, u32[]{:S(2)}, u32[]{:S(2)}) collective-permute-start(bf16[128,2048]{1,0:T(8,128)(2,1)S(1)} %collective-permute-done.6.refs_0_), channel_id=1, source_target_pairs={{0,4},{1,3},{4,8},{5,1},{8,12},{9,5},{12,14},{13,9},{14,10},{15,13... | collective-permute-start | bytes 1572872 | tf_op jit(solution)/shard_map/ring_3_0/ppermute | solution.py:221
  27.9 7.7 %collective-permute-start.10 = (bf16[136,2048]{1,0:T(8,128)(2,1)S(1)}, bf16[136,2048]{1,0:T(8,128)(2,1)S(1)}, u32[]{:S(2)}, u32[]{:S(2)}) collective-permute-start(bf16[136,2048]{1,0:T(8,128)(2,1)S(1)} %collective-permute-done.4.refs_0_.refs_1_), channel_id=1, source_target_pairs={{0,1},{1,0},{4,5},{5,4},{8,9},{9,8},{12,13},{13,12},{14,15},{15,14... | collective-permute-start | bytes 1671176 | tf_op jit(solution)/shard_map/swap_2_1/ppermute | solution.py:221
  27.9 11.6 %collective-permute-start.5 = (bf16[136,2048]{1,0:T(8,128)(2,1)S(1)}, bf16[136,2048]{1,0:T(8,128)(2,1)S(1)}, u32[]{:S(2)}, u32[]{:S(2)}) collective-permute-start(bf16[136,2048]{1,0:T(8,128)(2,1)S(1)} %collective-permute-done.4.refs_0_.refs_1_), channel_id=1, source_target_pairs={{0,4},{1,3},{4,8},{5,1},{8,12},{9,5},{12,14},{13,9},{14,10},{15,13... | collective-permute-start | bytes 1671176 | tf_op jit(solution)/shard_map/ring_3_1/ppermute | solution.py:221
  33.5 6.0 %collective-permute-start.11 = (bf16[128,2048]{1,0:T(8,128)(2,1)S(1)}, bf16[128,2048]{1,0:T(8,128)(2,1)S(1)}, u32[]{:S(2)}, u32[]{:S(2)}) collective-permute-start(bf16[128,2048]{1,0:T(8,128)(2,1)S(1)} %collective-permute-done.8.refs_0_), channel_id=1, source_target_pairs={{0,1},{1,0},{4,5},{5,4},{8,9},{9,8},{12,13},{13,12},{14,15},{15,14... | collective-permute-start | bytes 1572872 | tf_op jit(solution)/shard_map/swap_3_0/ppermute | solution.py:221
  33.5 11.6 %collective-permute-start.12 = (bf16[128,2048]{1,0:T(8,128)(2,1)S(1)}, bf16[128,2048]{1,0:T(8,128)(2,1)S(1)}, u32[]{:S(2)}, u32[]{:S(2)}) collective-permute-start(bf16[128,2048]{1,0:T(8,128)(2,1)S(1)} %collective-permute-done.8.refs_0_), channel_id=1, source_target_pairs={{0,4},{1,3},{4,8},{5,1},{8,12},{9,5},{12,14},{13,9},{14,10},{15,13... | collective-permute-start | bytes 1572872 | tf_op jit(solution)/shard_map/ring_4_0/ppermute | solution.py:221
  48.3 5.6 %collective-permute-start.16 = (bf16[136,2048]{1,0:T(8,128)(2,1)S(1)}, bf16[136,2048]{1,0:T(8,128)(2,1)S(1)}, u32[]{:S(2)}, u32[]{:S(2)}) collective-permute-start(bf16[136,2048]{1,0:T(8,128)(2,1)S(1)} %collective-permute-done.5.refs_1_.refs_0_.refs_2_), channel_id=1, source_target_pairs={{0,1},{1,0},{4,5},{5,4},{8,9},{9,8},{12,13},{13,12},{14,15},{15,14... | collective-permute-start | bytes 1671176 | tf_op jit(solution)/shard_map/swap_3_1/ppermute | solution.py:221
  51.7 9.3 %collective-permute-start.18 = (bf16[128,2048]{1,0:T(8,128)(2,1)S(1)}, bf16[128,2048]{1,0:T(8,128)(2,1)S(1)}, u32[]{:S(2)}, u32[]{:S(2)}) collective-permute-start(bf16[128,2048]{1,0:T(8,128)(2,1)S(1)} %add_convert_fusion.1), channel_id=1, source_target_pairs={{0,2},{1,5},{4,0},{5,9},{8,4},{9,13},{12,8},{13,15},{14,12},{15,11... | collective-permute-start | bytes 1572872 | tf_op jit(solution)/shard_map/back_4_1/ppermute | solution.py:221
  56.7 9.8 %collective-permute-start.22 = (bf16[128,2048]{1,0:T(8,128)(2,1)S(1)}, bf16[128,2048]{1,0:T(8,128)(2,1)S(1)}, u32[]{:S(2)}, u32[]{:S(2)}) collective-permute-start(bf16[128,2048]{1,0:T(8,128)(2,1)S(1)} %shard_map.57), channel_id=1, source_target_pairs={{0,2},{1,5},{4,0},{5,9},{8,4},{9,13},{12,8},{13,15},{14,12},{15,11... | collective-permute-start | bytes 1572872 | tf_op jit(solution)/shard_map/back_3_0/ppermute | solution.py:221
  58.4 8.2 %collective-permute-start.21 = (bf16[128,2048]{1,0:T(8,128)(2,1)S(1)}, bf16[128,2048]{1,0:T(8,128)(2,1)S(1)}, u32[]{:S(2)}, u32[]{:S(2)}) collective-permute-start(bf16[128,2048]{1,0:T(8,128)(2,1)S(1)} %get-tuple-element.82), channel_id=1, source_target_pairs={{0,1},{1,0},{4,5},{5,4},{8,9},{9,8},{12,13},{13,12},{14,15},{15,14... | collective-permute-start | bytes 1572872 | tf_op jit(solution)/shard_map/give_2_0/ppermute | solution.py:221
  58.4 11.1 %collective-permute-start.23 = (bf16[128,2048]{1,0:T(8,128)(2,1)S(1)}, bf16[128,2048]{1,0:T(8,128)(2,1)S(1)}, u32[]{:S(2)}, u32[]{:S(2)}) collective-permute-start(bf16[128,2048]{1,0:T(8,128)(2,1)S(1)} %get-tuple-element.85), channel_id=1, source_target_pairs={{0,1},{1,0},{4,5},{5,4},{8,9},{9,8},{12,13},{13,12},{14,15},{15,14... | collective-permute-start | bytes 1572872 | tf_op jit(solution)/shard_map/give_2_1/ppermute | solution.py:221
  61.6 10.6 %collective-permute-start.24 = (bf16[128,2048]{1,0:T(8,128)(2,1)S(1)}, bf16[128,2048]{1,0:T(8,128)(2,1)S(1)}, u32[]{:S(2)}, u32[]{:S(2)}) collective-permute-start(bf16[128,2048]{1,0:T(8,128)(2,1)S(1)} %shard_map.59), channel_id=1, source_target_pairs={{0,2},{1,5},{4,0},{5,9},{8,4},{9,13},{12,8},{13,15},{14,12},{15,11... | collective-permute-start | bytes 1572872 | tf_op jit(solution)/shard_map/back_3_1/ppermute | solution.py:221
  66.9 10.9 %collective-permute-start.26 = (bf16[128,2048]{1,0:T(8,128)(2,1)S(1)}, bf16[128,2048]{1,0:T(8,128)(2,1)S(1)}, u32[]{:S(2)}, u32[]{:S(2)}) collective-permute-start(bf16[128,2048]{1,0:T(8,128)(2,1)S(1)} %shard_map.60), channel_id=1, source_target_pairs={{0,2},{1,5},{4,0},{5,9},{8,4},{9,13},{12,8},{13,15},{14,12},{15,11... | collective-permute-start | bytes 1572872 | tf_op jit(solution)/shard_map/back_2_0/ppermute | solution.py:221
  68.9 5.6 %collective-permute-start.25 = (bf16[128,2048]{1,0:T(8,128)(2,1)S(1)}, bf16[128,2048]{1,0:T(8,128)(2,1)S(1)}, u32[]{:S(2)}, u32[]{:S(2)}) collective-permute-start(bf16[128,2048]{1,0:T(8,128)(2,1)S(1)} %get-tuple-element.88), channel_id=1, source_target_pairs={{0,1},{1,0},{4,5},{5,4},{8,9},{9,8},{12,13},{13,12},{14,15},{15,14... | collective-permute-start | bytes 1572872 | tf_op jit(solution)/shard_map/give_1_0/ppermute | solution.py:221
  68.9 11.2 %collective-permute-start.28 = (bf16[128,2048]{1,0:T(8,128)(2,1)S(1)}, bf16[128,2048]{1,0:T(8,128)(2,1)S(1)}, u32[]{:S(2)}, u32[]{:S(2)}) collective-permute-start(bf16[128,2048]{1,0:T(8,128)(2,1)S(1)} %get-tuple-element.90), channel_id=1, source_target_pairs={{0,1},{1,0},{4,5},{5,4},{8,9},{9,8},{12,13},{13,12},{14,15},{15,14... | collective-permute-start | bytes 1572872 | tf_op jit(solution)/shard_map/give_1_1/ppermute | solution.py:221
  72.5 10.9 %collective-permute-start.29 = (bf16[128,2048]{1,0:T(8,128)(2,1)S(1)}, bf16[128,2048]{1,0:T(8,128)(2,1)S(1)}, u32[]{:S(2)}, u32[]{:S(2)}) collective-permute-start(bf16[128,2048]{1,0:T(8,128)(2,1)S(1)} %shard_map.61), channel_id=1, source_target_pairs={{0,2},{1,5},{4,0},{5,9},{8,4},{9,13},{12,8},{13,15},{14,12},{15,11... | collective-permute-start | bytes 1572872 | tf_op jit(solution)/shard_map/back_2_1/ppermute | solution.py:221
  74.5 10.1 %collective-permute-start.19 = (bf16[128,2048]{1,0:T(8,128)(2,1)S(1)}, bf16[128,2048]{1,0:T(8,128)(2,1)S(1)}, u32[]{:S(2)}, u32[]{:S(2)}) collective-permute-start(bf16[128,2048]{1,0:T(8,128)(2,1)S(1)} %get-tuple-element.76), channel_id=1, source_target_pairs={{0,1},{1,0},{4,5},{5,4},{8,9},{9,8},{12,13},{13,12},{14,15},{15,14... | collective-permute-start | bytes 1572872 | tf_op jit(solution)/shard_map/give_0_0/ppermute | solution.py:221
  78.1 10.9 %collective-permute-start.27 = (bf16[128,2048]{1,0:T(8,128)(2,1)S(1)}, bf16[128,2048]{1,0:T(8,128)(2,1)S(1)}, u32[]{:S(2)}, u32[]{:S(2)}) collective-permute-start(bf16[128,2048]{1,0:T(8,128)(2,1)S(1)} %shard_map.62), channel_id=1, source_target_pairs={{0,2},{1,5},{4,0},{5,9},{8,4},{9,13},{12,8},{13,15},{14,12},{15,11... | collective-permute-start | bytes 1572872 | tf_op jit(solution)/shard_map/back_1_0/ppermute | solution.py:221
  83.8 10.4 %collective-permute-start.30 = (bf16[128,2048]{1,0:T(8,128)(2,1)S(1)}, bf16[128,2048]{1,0:T(8,128)(2,1)S(1)}, u32[]{:S(2)}, u32[]{:S(2)}) collective-permute-start(bf16[128,2048]{1,0:T(8,128)(2,1)S(1)} %shard_map.64), channel_id=1, source_target_pairs={{0,3},{1,4},{4,1},{5,8},{8,5},{9,12},{12,9},{13,14},{14,13},{15,10... | collective-permute-start | bytes 1572872 | tf_op jit(solution)/shard_map/back_1_1/ppermute | solution.py:221
  (9 other events, 33.0 us)

commit v17 on v16

--- a/solution.py
+++ b/solution.py
@@ -266,36 +266,40 @@
         results[step, c] = kept, send(after(given, *earlier) if earlier else given, cores, f"give_{step}_{c}")
 
     earlier = ring[1]
-    for step in range(1, far):
+    for step in range(1, far - 1):
         holders[step] = ring[1]
         swapped = [
             send(block, cores, f"swap_{step}_{c}") for c, block in enumerate(ring[: 1 if step == 1 else 2])
         ]
         blocks = list(ring)
-        if step < far - 1:
-            ring = [send(block, forth, f"ring_{step + 1}_{c}") for c, block in enumerate(ring)]
-        else:
-            ring = [send(ring[0], forth, f"ring_{far}_0")]
+        ring[0] = send(blocks[0], forth, f"ring_{step + 1}_0")
+        if step < far - 2:
+            ring[1] = send(blocks[1], forth, f"ring_{step + 1}_1")
         for c in chains:
             if (step, c) == (1, 1):
                 delayed = blocks[1]
                 earlier = ring[1]
                 continue
-            if (step, c) == (far - 1, 1):
-                last = blocks[1], swapped[1]
-                continue
             kept = expert_rows(step, c, [after(blocks[c], earlier), swapped[c]])
-            place = c if step < far - 1 else 0
-            ring[place] = after(ring[place], kept)
-            earlier = ring[place]
+            if (step, c) == (far - 2, 1):
+                ring[1] = send(after(blocks[1], kept), forth, f"ring_{step + 1}_1")
+            else:
+                ring[c] = after(ring[c], kept)
+                earlier = ring[c]
+    holders[far - 1] = blocks[1] = ring[1]
+    swapped = send(ring[0], cores, f"swap_{far - 1}_0")
+    block, ring = ring[0], [send(ring[0], forth, f"ring_{far}_0")]
+    kept = expert_rows(far - 1, 0, [after(block, kept), swapped])
+    ring[0] = after(ring[0], kept)
 
     with jax.named_scope("expert_far_ring"):
-        (given,) = half_expert([rows], ring, near, split=1)
+        (given,) = half_expert([rows], ring, near, split=1, cost=0.3)
     swapped = send(ring[0], cores, f"swap_{far}")
     swapped = after(swapped, given)
     given = send(given, cores, "give_far")
     with jax.named_scope("expert_far_swapped"):
-        (kept,) = half_expert([rows], [swapped], near, split=1)
+        (kept,) = half_expert([rows], [swapped], near, split=1, cost=0.3)
+    last = blocks[1], send(after(blocks[1], kept), cores, f"swap_{far - 1}_1")
     earlier = rounded(total(kept, given))
     sums = [None, send(earlier, back, f"back_{far}_1")]
     mine, theirs = results[far - 1, 0]

time: 95.2 us -> 92.9 us (0.976)
  waiting for transfers between devices: 32.1 us -> 30.4 us
    ppermute x31, waiting for transfers between devices: 32.1 us -> 30.4 us  [send(): return lax.ppermute(value, 'blk', pairs)]
  transfers between devices with their start and end apart: 31 -> 31, of which waited for: 14 -> 12; matrix products, arithmetic and copies ran while one was open for 1% -> 1% of each run, Pallas kernels for 31% -> 31%
where the time goes in v17:
time: 92.9 us; the launch traced here: 92.7 us
  waiting for transfers between devices  30.4 us (33%)
  starting transfers between devices  29.3 us (32%)
  Pallas kernels  29.1 us (31%)
  local copies, waits for them, and re-layouts  1.9 us (2%)
  other arithmetic  1.79 us (2%)
    ppermute x31, waiting for transfers between devices, send(): return lax.ppermute(value, 'blk', pairs)  30.4 us
    ppermute x31, starting transfers between devices, send(): return lax.ppermute(value, 'blk', pairs)  29.3 us
    pallas_call x9, Pallas kernels, half_expert(): pl.pallas_call(functools.partial(half_expert_kernel, tuple(heights), load...  23.9 us
    pallas_call x1, Pallas kernels, loaded(): pl.pallas_call(load_kernel, out_shape=[jax.ShapeDtypeStruct(array.shape,...  2.86 us
    pallas_call x8, Pallas kernels, weighted(): pl.pallas_call(functools.partial(weighted_kernel, kind, len(own), len(dis...  2.34 us
    unnamed x4, local copies, waits for them, and re-layouts  1.89 us
  transfers between devices with their start and end apart: 31, of which 12 were waited for; matrix products, arithmetic and copies ran while one was open for 1% of the time, Pallas kernels for 31%

profile of v17, /device:TPU:0, one launch (start us, length us, event | category | flops | bytes accessed | tf_op | source)
XLA Modules:
  0.0 92.7 jit_solution(2188823597394091570)
XLA Ops:
  0.5 2.6 %collective-permute-start.2 = (bf16[128,2048]{1,0:T(8,128)(2,1)}, bf16[128,2048]{1,0:T(8,128)(2,1)S(1)}, u32[]{:S(2)}, u32[]{:S(2)}) collective-permute-start(bf16[128,2048]{1,0:T(8,128)(2,1)} %refs_0_.1), channel_id=1, source_target_pairs={{0,4},{1,3},{4,8},{5,1},{8,12},{9,5},{12,14},{13,9},{14,10},{15,13... | collective-permute-start | bytes 1572872 | tf_op jit(solution)/shard_map/ring_1_0/ppermute | solution.py:221
  8.6 2.9 %shard_map.56 = (bf16[2,768,2048]{2,1,0:T(8,128)(2,1)S(1)}, bf16[768,2048]{1,0:T(8,128)(2,1)S(1)}) custom-call(bf16[2,768,2048]{2,1,0:T(8,128)(2,1)} %refs_0_, bf16[768,2048]{1,0:T(8,128)(2,1)S(1)} %copy-done), custom_call_target="tpu_custom_call" | custom-call | flops 268435456 | bytes 1048576 | tf_op jit(solution)/shard_map/pallas_call | solution.py:111
  13.2 2.6 %expert_0.1 = (bf16[128,2048]{1,0:T(8,128)(2,1)S(1)}, bf16[128,2048]{1,0:T(8,128)(2,1)S(1)}) custom-call(bf16[128,2048]{1,0:T(8,128)(2,1)S(1)} %copy-done.1, bf16[136,2048]{1,0:T(8,128)(2,1)S(1)} %maximum_maximum_fusion.refs_1_, bf16[2,768,2048]{2,1,0:T(8,128)(2,1)S(1)} %get-tuple-element.53.refs_2_.refs_1_, ...), custom_call_target="tpu_custom_call" | custom-call | flops 805306368 | bytes 3145728 | tf_op jit(solution)/shard_map/expert_0/pallas_call | solution.py:150
  16.3 2.1 %collective-permute-start.4 = (bf16[136,2048]{1,0:T(8,128)(2,1)S(1)}, bf16[136,2048]{1,0:T(8,128)(2,1)S(1)}, u32[]{:S(2)}, u32[]{:S(2)}) collective-permute-start(bf16[136,2048]{1,0:T(8,128)(2,1)S(1)} %collective-permute-done.3.refs_0_.refs_1_), channel_id=1, source_target_pairs={{0,4},{1,3},{4,8},{5,1},{8,12},{9,5},{12,14},{13,9},{14,10},{15,13... | collective-permute-start | bytes 1671176 | tf_op jit(solution)/shard_map/ring_2_1/ppermute | solution.py:221
  18.4 2.7 %expert_1_0.1 = (bf16[128,2048]{1,0:T(8,128)(2,1)S(1)}, bf16[128,2048]{1,0:T(8,128)(2,1)S(1)}) custom-call(bf16[128,2048]{1,0:T(8,128)(2,1)S(1)} %collective-permute-done.2.refs_0_, bf16[128,2048]{1,0:T(8,128)(2,1)S(1)} %collective-permute-done.6.refs_1_, bf16[2,768,2048]{2,1,0:T(8,128)(2,1)S(1)} %get-tuple-element.53.refs_2_.refs_1_, ...), custom_call_target="tpu_custom_call" | custom-call | flops 805306368 | bytes 3145728 | tf_op jit(solution)/shard_map/expert_1_0/pallas_call | solution.py:150
  21.9 2.1 %collective-permute-start.7 = (bf16[128,2048]{1,0:T(8,128)(2,1)S(1)}, bf16[128,2048]{1,0:T(8,128)(2,1)S(1)}, u32[]{:S(2)}, u32[]{:S(2)}) collective-permute-start(bf16[128,2048]{1,0:T(8,128)(2,1)S(1)} %collective-permute-done.5.refs_0_), channel_id=1, source_target_pairs={{0,4},{1,3},{4,8},{5,1},{8,12},{9,5},{12,14},{13,9},{14,10},{15,13... | collective-permute-start | bytes 1572872 | tf_op jit(solution)/shard_map/ring_3_0/ppermute | solution.py:221
  24.0 3.9 %collective-permute-done.4.refs_0_.refs_1_ = bf16[136,2048]{1,0:T(8,128)(2,1)S(1)} collective-permute-done((bf16[136,2048]{1,0:T(8,128)(2,1)S(1)}, bf16[136,2048]{1,0:T(8,128)(2,1)S(1)}, u32[]{:S(2)}, u32[]{:S(2)}) %collective-permute-start.4) | collective-permute-done | bytes 557088 | tf_op jit(solution)/shard_map/ring_2_1/ppermute | solution.py:221
  27.9 2.7 %expert_2_0.1 = (bf16[128,2048]{1,0:T(8,128)(2,1)S(1)}, bf16[128,2048]{1,0:T(8,128)(2,1)S(1)}) custom-call(bf16[128,2048]{1,0:T(8,128)(2,1)S(1)} %collective-permute-done.5.refs_0_, bf16[128,2048]{1,0:T(8,128)(2,1)S(1)} %collective-permute-done.8.refs_1_, bf16[2,768,2048]{2,1,0:T(8,128)(2,1)S(1)} %get-tuple-element.53.refs_2_.refs_1_, ...), custom_call_target="tpu_custom_call" | custom-call | flops 805306368 | bytes 3145728 | tf_op jit(solution)/shard_map/expert_2_0/pallas_call | solution.py:150
  30.6 3.0 %collective-permute-done.7.refs_0_ = bf16[128,2048]{1,0:T(8,128)(2,1)S(1)} collective-permute-done((bf16[128,2048]{1,0:T(8,128)(2,1)S(1)}, bf16[128,2048]{1,0:T(8,128)(2,1)S(1)}, u32[]{:S(2)}, u32[]{:S(2)}) %collective-permute-start.7) | collective-permute-done | bytes 524320 | tf_op jit(solution)/shard_map/ring_3_0/ppermute | solution.py:221
  33.5 2.1 %collective-permute-start.12 = (bf16[128,2048]{1,0:T(8,128)(2,1)S(1)}, bf16[128,2048]{1,0:T(8,128)(2,1)S(1)}, u32[]{:S(2)}, u32[]{:S(2)}) collective-permute-start(bf16[128,2048]{1,0:T(8,128)(2,1)S(1)} %collective-permute-done.7.refs_0_), channel_id=1, source_target_pairs={{0,4},{1,3},{4,8},{5,1},{8,12},{9,5},{12,14},{13,9},{14,10},{15,13... | collective-permute-start | bytes 1572872 | tf_op jit(solution)/shard_map/ring_4_0/ppermute | solution.py:221
  35.6 2.6 %expert_2_1.1 = (bf16[128,2048]{1,0:T(8,128)(2,1)S(1)}, bf16[128,2048]{1,0:T(8,128)(2,1)S(1)}) custom-call(bf16[136,2048]{1,0:T(8,128)(2,1)S(1)} %collective-permute-done.4.refs_0_.refs_1_, bf16[136,2048]{1,0:T(8,128)(2,1)S(1)} %collective-permute-done.9.refs_1_, bf16[2,768,2048]{2,1,0:T(8,128)(2,1)S(1)} %get-tuple-element.53.refs_2_.refs_1_, ...), custom_call_target="tpu_custom_call" | custom-call | flops 805306368 | bytes 3145728 | tf_op jit(solution)/shard_map/expert_2_1/pallas_call | solution.py:150
  40.1 2.6 %expert_3_0.1 = (bf16[128,2048]{1,0:T(8,128)(2,1)S(1)}, bf16[128,2048]{1,0:T(8,128)(2,1)S(1)}) custom-call(bf16[128,2048]{1,0:T(8,128)(2,1)S(1)} %collective-permute-done.7.refs_0_, bf16[128,2048]{1,0:T(8,128)(2,1)S(1)} %collective-permute-done.11.refs_1_, bf16[2,768,2048]{2,1,0:T(8,128)(2,1)S(1)} %get-tuple-element.53.refs_2_.refs_1_, ...), custom_call_target="tpu_custom_call" | custom-call | flops 805306368 | bytes 3145728 | tf_op jit(solution)/shard_map/expert_3_0/pallas_call | solution.py:150
  42.8 2.7 %expert_far_ring.1 = bf16[128,2048]{1,0:T(8,128)(2,1)S(1)} custom-call(bf16[128,2048]{1,0:T(8,128)(2,1)S(1)} %collective-permute-done.12.refs_0_, bf16[2,768,2048]{2,1,0:T(8,128)(2,1)S(1)} %get-tuple-element.53.refs_2_.refs_1_, bf16[768,2048]{1,0:T(8,128)(2,1)S(1)} %get-tuple-element.50.refs_3_.refs_2_), custom_call_target="tpu_custom_call" | custom-call | flops 60397976 | bytes 471859 | tf_op jit(solution)/shard_map/expert_far_ring/pallas_call | solution.py:150
  46.1 2.7 %expert_far_swapped.1 = bf16[128,2048]{1,0:T(8,128)(2,1)S(1)} custom-call(bf16[128,2048]{1,0:T(8,128)(2,1)S(1)} %collective-permute-done.13.refs_0_, bf16[2,768,2048]{2,1,0:T(8,128)(2,1)S(1)} %get-tuple-element.53.refs_2_.refs_1_, bf16[768,2048]{1,0:T(8,128)(2,1)S(1)} %get-tuple-element.50.refs_3_.refs_2_), custom_call_target="tpu_custom_call" | custom-call | flops 60397976 | bytes 471859 | tf_op jit(solution)/shard_map/expert_far_swapped/pallas_call | solution.py:150
  49.4 2.0 %collective-permute-start.18 = (bf16[128,2048]{1,0:T(8,128)(2,1)S(1)}, bf16[128,2048]{1,0:T(8,128)(2,1)S(1)}, u32[]{:S(2)}, u32[]{:S(2)}) collective-permute-start(bf16[128,2048]{1,0:T(8,128)(2,1)S(1)} %add_convert_fusion.1), channel_id=1, source_target_pairs={{0,2},{1,5},{4,0},{5,9},{8,4},{9,13},{12,8},{13,15},{14,12},{15,11... | collective-permute-start | bytes 1572872 | tf_op jit(solution)/shard_map/back_4_1/ppermute | solution.py:221
  51.7 2.6 %expert_3_1.1 = (bf16[128,2048]{1,0:T(8,128)(2,1)S(1)}, bf16[128,2048]{1,0:T(8,128)(2,1)S(1)}) custom-call(bf16[136,2048]{1,0:T(8,128)(2,1)S(1)} %collective-permute-done.10.refs_1_.refs_0_.refs_2_, bf16[136,2048]{1,0:T(8,128)(2,1)S(1)} %collective-permute-done.16.refs_1_, bf16[2,768,2048]{2,1,0:T(8,128)(2,1)S(1)} %get-tuple-element.53.refs_2_.refs_1_, ...), custom_call_target="tpu_custom_call" | custom-call | flops 80530640 | bytes 314572 | tf_op jit(solution)/shard_map/expert_3_1/pallas_call | solution.py:150
  56.5 2.1 %collective-permute-done.18.refs_4_ = bf16[128,2048]{1,0:T(8,128)(2,1)S(1)} collective-permute-done((bf16[128,2048]{1,0:T(8,128)(2,1)S(1)}, bf16[128,2048]{1,0:T(8,128)(2,1)S(1)}, u32[]{:S(2)}, u32[]{:S(2)}) %collective-permute-start.18) | collective-permute-done | bytes 524320 | tf_op jit(solution)/shard_map/back_4_1/ppermute | solution.py:221
  59.3 2.0 %collective-permute-start.24 = (bf16[128,2048]{1,0:T(8,128)(2,1)S(1)}, bf16[128,2048]{1,0:T(8,128)(2,1)S(1)}, u32[]{:S(2)}, u32[]{:S(2)}) collective-permute-start(bf16[128,2048]{1,0:T(8,128)(2,1)S(1)} %shard_map.59), channel_id=1, source_target_pairs={{0,2},{1,5},{4,0},{5,9},{8,4},{9,13},{12,8},{13,15},{14,12},{15,11... | collective-permute-start | bytes 1572872 | tf_op jit(solution)/shard_map/back_3_1/ppermute | solution.py:221
  61.3 2.7 %expert_1_1.1 = (bf16[128,2048]{1,0:T(8,128)(2,1)S(1)}, bf16[128,2048]{1,0:T(8,128)(2,1)S(1)}) custom-call(bf16[136,2048]{1,0:T(8,128)(2,1)S(1)} %collective-permute-done.3.refs_0_.refs_1_, bf16[136,2048]{1,0:T(8,128)(2,1)S(1)} %collective-permute-done.20.refs_1_, bf16[2,768,2048]{2,1,0:T(8,128)(2,1)S(1)} %get-tuple-element.53.refs_2_.refs_1_, ...), custom_call_target="tpu_custom_call" | custom-call | flops 805306368 | bytes 3145728 | tf_op jit(solution)/shard_map/expert_1_1/pallas_call | solution.py:150
  67.1 2.8 %collective-permute-done.24.refs_4_ = bf16[128,2048]{1,0:T(8,128)(2,1)S(1)} collective-permute-done((bf16[128,2048]{1,0:T(8,128)(2,1)S(1)}, bf16[128,2048]{1,0:T(8,128)(2,1)S(1)}, u32[]{:S(2)}, u32[]{:S(2)}) %collective-permute-start.24) | collective-permute-done | bytes 524320 | tf_op jit(solution)/shard_map/back_3_1/ppermute | solution.py:221
  72.2 3.3 %collective-permute-done.26.refs_4_ = bf16[128,2048]{1,0:T(8,128)(2,1)S(1)} collective-permute-done((bf16[128,2048]{1,0:T(8,128)(2,1)S(1)}, bf16[128,2048]{1,0:T(8,128)(2,1)S(1)}, u32[]{:S(2)}, u32[]{:S(2)}) %collective-permute-start.26) | collective-permute-done | bytes 524320 | tf_op jit(solution)/shard_map/back_2_0/ppermute | solution.py:221
  77.8 3.3 %collective-permute-done.29.refs_4_ = bf16[128,2048]{1,0:T(8,128)(2,1)S(1)} collective-permute-done((bf16[128,2048]{1,0:T(8,128)(2,1)S(1)}, bf16[128,2048]{1,0:T(8,128)(2,1)S(1)}, u32[]{:S(2)}, u32[]{:S(2)}) %collective-permute-start.29) | collective-permute-done | bytes 524320 | tf_op jit(solution)/shard_map/back_2_1/ppermute | solution.py:221
  82.3 4.5 %collective-permute-done.27.refs_4_ = bf16[128,2048]{1,0:T(8,128)(2,1)S(1)} collective-permute-done((bf16[128,2048]{1,0:T(8,128)(2,1)S(1)}, bf16[128,2048]{1,0:T(8,128)(2,1)S(1)}, u32[]{:S(2)}, u32[]{:S(2)}) %collective-permute-start.27) | collective-permute-done | bytes 524320 | tf_op jit(solution)/shard_map/back_1_0/ppermute | solution.py:221
  87.1 4.8 %collective-permute-done.30 = bf16[128,2048]{1,0:T(8,128)(2,1)S(1)} collective-permute-done((bf16[128,2048]{1,0:T(8,128)(2,1)S(1)}, bf16[128,2048]{1,0:T(8,128)(2,1)S(1)}, u32[]{:S(2)}, u32[]{:S(2)}) %collective-permute-start.30) | collective-permute-done | bytes 524320 | tf_op jit(solution)/shard_map/back_1_1/ppermute | solution.py:221
  (69 shorter events, 25.3 us)
Async XLA Ops:
  0.5 11.0 %collective-permute-start.2 = (bf16[128,2048]{1,0:T(8,128)(2,1)}, bf16[128,2048]{1,0:T(8,128)(2,1)S(1)}, u32[]{:S(2)}, u32[]{:S(2)}) collective-permute-start(bf16[128,2048]{1,0:T(8,128)(2,1)} %refs_0_.1), channel_id=1, source_target_pairs={{0,4},{1,3},{4,8},{5,1},{8,12},{9,5},{12,14},{13,9},{14,10},{15,13... | collective-permute-start | bytes 1572872 | tf_op jit(solution)/shard_map/ring_1_0/ppermute | solution.py:221
  5.0 11.3 %collective-permute-start.3 = (bf16[136,2048]{1,0:T(8,128)(2,1)S(1)}, bf16[136,2048]{1,0:T(8,128)(2,1)S(1)}, u32[]{:S(2)}, u32[]{:S(2)}) collective-permute-start(bf16[136,2048]{1,0:T(8,128)(2,1)S(1)} %maximum_maximum_fusion.refs_1_), channel_id=1, source_target_pairs={{0,4},{1,3},{4,8},{5,1},{8,12},{9,5},{12,14},{13,9},{14,10},{15,13... | collective-permute-start | bytes 1671176 | tf_op jit(solution)/shard_map/ring_1_1/ppermute | solution.py:221
  11.4 6.9 %collective-permute-start.6 = (bf16[128,2048]{1,0:T(8,128)(2,1)S(1)}, bf16[128,2048]{1,0:T(8,128)(2,1)S(1)}, u32[]{:S(2)}, u32[]{:S(2)}) collective-permute-start(bf16[128,2048]{1,0:T(8,128)(2,1)S(1)} %collective-permute-done.2.refs_0_), channel_id=1, source_target_pairs={{0,1},{1,0},{4,5},{5,4},{8,9},{9,8},{12,13},{13,12},{14,15},{15,14... | collective-permute-start | bytes 1572872 | tf_op jit(solution)/shard_map/swap_1_0/ppermute | solution.py:221
  11.5 10.4 %collective-permute-start.5 = (bf16[128,2048]{1,0:T(8,128)(2,1)S(1)}, bf16[128,2048]{1,0:T(8,128)(2,1)S(1)}, u32[]{:S(2)}, u32[]{:S(2)}) collective-permute-start(bf16[128,2048]{1,0:T(8,128)(2,1)S(1)} %collective-permute-done.2.refs_0_), channel_id=1, source_target_pairs={{0,4},{1,3},{4,8},{5,1},{8,12},{9,5},{12,14},{13,9},{14,10},{15,13... | collective-permute-start | bytes 1572872 | tf_op jit(solution)/shard_map/ring_2_0/ppermute | solution.py:221
  16.3 11.6 %collective-permute-start.4 = (bf16[136,2048]{1,0:T(8,128)(2,1)S(1)}, bf16[136,2048]{1,0:T(8,128)(2,1)S(1)}, u32[]{:S(2)}, u32[]{:S(2)}) collective-permute-start(bf16[136,2048]{1,0:T(8,128)(2,1)S(1)} %collective-permute-done.3.refs_0_.refs_1_), channel_id=1, source_target_pairs={{0,4},{1,3},{4,8},{5,1},{8,12},{9,5},{12,14},{13,9},{14,10},{15,13... | collective-permute-start | bytes 1671176 | tf_op jit(solution)/shard_map/ring_2_1/ppermute | solution.py:221
  21.9 6.0 %collective-permute-start.8 = (bf16[128,2048]{1,0:T(8,128)(2,1)S(1)}, bf16[128,2048]{1,0:T(8,128)(2,1)S(1)}, u32[]{:S(2)}, u32[]{:S(2)}) collective-permute-start(bf16[128,2048]{1,0:T(8,128)(2,1)S(1)} %collective-permute-done.5.refs_0_), channel_id=1, source_target_pairs={{0,1},{1,0},{4,5},{5,4},{8,9},{9,8},{12,13},{13,12},{14,15},{15,14... | collective-permute-start | bytes 1572872 | tf_op jit(solution)/shard_map/swap_2_0/ppermute | solution.py:221
  21.9 11.6 %collective-permute-start.7 = (bf16[128,2048]{1,0:T(8,128)(2,1)S(1)}, bf16[128,2048]{1,0:T(8,128)(2,1)S(1)}, u32[]{:S(2)}, u32[]{:S(2)}) collective-permute-start(bf16[128,2048]{1,0:T(8,128)(2,1)S(1)} %collective-permute-done.5.refs_0_), channel_id=1, source_target_pairs={{0,4},{1,3},{4,8},{5,1},{8,12},{9,5},{12,14},{13,9},{14,10},{15,13... | collective-permute-start | bytes 1572872 | tf_op jit(solution)/shard_map/ring_3_0/ppermute | solution.py:221
  27.9 7.7 %collective-permute-start.9 = (bf16[136,2048]{1,0:T(8,128)(2,1)S(1)}, bf16[136,2048]{1,0:T(8,128)(2,1)S(1)}, u32[]{:S(2)}, u32[]{:S(2)}) collective-permute-start(bf16[136,2048]{1,0:T(8,128)(2,1)S(1)} %collective-permute-done.4.refs_0_.refs_1_), channel_id=1, source_target_pairs={{0,1},{1,0},{4,5},{5,4},{8,9},{9,8},{12,13},{13,12},{14,15},{15,14... | collective-permute-start | bytes 1671176 | tf_op jit(solution)/shard_map/swap_2_1/ppermute | solution.py:221
  33.5 6.6 %collective-permute-start.11 = (bf16[128,2048]{1,0:T(8,128)(2,1)S(1)}, bf16[128,2048]{1,0:T(8,128)(2,1)S(1)}, u32[]{:S(2)}, u32[]{:S(2)}) collective-permute-start(bf16[128,2048]{1,0:T(8,128)(2,1)S(1)} %collective-permute-done.7.refs_0_), channel_id=1, source_target_pairs={{0,1},{1,0},{4,5},{5,4},{8,9},{9,8},{12,13},{13,12},{14,15},{15,14... | collective-permute-start | bytes 1572872 | tf_op jit(solution)/shard_map/swap_3_0/ppermute | solution.py:221
  33.5 9.2 %collective-permute-start.12 = (bf16[128,2048]{1,0:T(8,128)(2,1)S(1)}, bf16[128,2048]{1,0:T(8,128)(2,1)S(1)}, u32[]{:S(2)}, u32[]{:S(2)}) collective-permute-start(bf16[128,2048]{1,0:T(8,128)(2,1)S(1)} %collective-permute-done.7.refs_0_), channel_id=1, source_target_pairs={{0,4},{1,3},{4,8},{5,1},{8,12},{9,5},{12,14},{13,9},{14,10},{15,13... | collective-permute-start | bytes 1572872 | tf_op jit(solution)/shard_map/ring_4_0/ppermute | solution.py:221
  38.3 10.6 %collective-permute-start.10 = (bf16[136,2048]{1,0:T(8,128)(2,1)S(1)}, bf16[136,2048]{1,0:T(8,128)(2,1)S(1)}, u32[]{:S(2)}, u32[]{:S(2)}) collective-permute-start(bf16[136,2048]{1,0:T(8,128)(2,1)S(1)} %collective-permute-done.4.refs_0_.refs_1_), channel_id=1, source_target_pairs={{0,4},{1,3},{4,8},{5,1},{8,12},{9,5},{12,14},{13,9},{14,10},{15,13... | collective-permute-start | bytes 1671176 | tf_op jit(solution)/shard_map/ring_3_1/ppermute | solution.py:221
  46.0 5.4 %collective-permute-start.15 = (bf16[128,2048]{1,0:T(8,128)(2,1)S(1)}, bf16[128,2048]{1,0:T(8,128)(2,1)S(1)}, u32[]{:S(2)}, u32[]{:S(2)}) collective-permute-start(bf16[128,2048]{1,0:T(8,128)(2,1)S(1)} %get-tuple-element.71), channel_id=1, source_target_pairs={{0,1},{1,0},{4,5},{5,4},{8,9},{9,8},{12,13},{13,12},{14,15},{15,14... | collective-permute-start | bytes 1572872 | tf_op jit(solution)/shard_map/give_3_0/ppermute | solution.py:221
  49.4 9.2 %collective-permute-start.18 = (bf16[128,2048]{1,0:T(8,128)(2,1)S(1)}, bf16[128,2048]{1,0:T(8,128)(2,1)S(1)}, u32[]{:S(2)}, u32[]{:S(2)}) collective-permute-start(bf16[128,2048]{1,0:T(8,128)(2,1)S(1)} %add_convert_fusion.1), channel_id=1, source_target_pairs={{0,2},{1,5},{4,0},{5,9},{8,4},{9,13},{12,8},{13,15},{14,12},{15,11... | collective-permute-start | bytes 1572872 | tf_op jit(solution)/shard_map/back_4_1/ppermute | solution.py:221
  54.4 9.9 %collective-permute-start.22 = (bf16[128,2048]{1,0:T(8,128)(2,1)S(1)}, bf16[128,2048]{1,0:T(8,128)(2,1)S(1)}, u32[]{:S(2)}, u32[]{:S(2)}) collective-permute-start(bf16[128,2048]{1,0:T(8,128)(2,1)S(1)} %shard_map.57), channel_id=1, source_target_pairs={{0,2},{1,5},{4,0},{5,9},{8,4},{9,13},{12,8},{13,15},{14,12},{15,11... | collective-permute-start | bytes 1572872 | tf_op jit(solution)/shard_map/back_3_0/ppermute | solution.py:221
  56.0 8.3 %collective-permute-start.21 = (bf16[128,2048]{1,0:T(8,128)(2,1)S(1)}, bf16[128,2048]{1,0:T(8,128)(2,1)S(1)}, u32[]{:S(2)}, u32[]{:S(2)}) collective-permute-start(bf16[128,2048]{1,0:T(8,128)(2,1)S(1)} %get-tuple-element.84), channel_id=1, source_target_pairs={{0,1},{1,0},{4,5},{5,4},{8,9},{9,8},{12,13},{13,12},{14,15},{15,14... | collective-permute-start | bytes 1572872 | tf_op jit(solution)/shard_map/give_2_0/ppermute | solution.py:221
  56.0 11.1 %collective-permute-start.23 = (bf16[128,2048]{1,0:T(8,128)(2,1)S(1)}, bf16[128,2048]{1,0:T(8,128)(2,1)S(1)}, u32[]{:S(2)}, u32[]{:S(2)}) collective-permute-start(bf16[128,2048]{1,0:T(8,128)(2,1)S(1)} %get-tuple-element.87), channel_id=1, source_target_pairs={{0,1},{1,0},{4,5},{5,4},{8,9},{9,8},{12,13},{13,12},{14,15},{15,14... | collective-permute-start | bytes 1572872 | tf_op jit(solution)/shard_map/give_2_1/ppermute | solution.py:221
  59.3 10.6 %collective-permute-start.24 = (bf16[128,2048]{1,0:T(8,128)(2,1)S(1)}, bf16[128,2048]{1,0:T(8,128)(2,1)S(1)}, u32[]{:S(2)}, u32[]{:S(2)}) collective-permute-start(bf16[128,2048]{1,0:T(8,128)(2,1)S(1)} %shard_map.59), channel_id=1, source_target_pairs={{0,2},{1,5},{4,0},{5,9},{8,4},{9,13},{12,8},{13,15},{14,12},{15,11... | collective-permute-start | bytes 1572872 | tf_op jit(solution)/shard_map/back_3_1/ppermute | solution.py:221
  64.6 10.9 %collective-permute-start.26 = (bf16[128,2048]{1,0:T(8,128)(2,1)S(1)}, bf16[128,2048]{1,0:T(8,128)(2,1)S(1)}, u32[]{:S(2)}, u32[]{:S(2)}) collective-permute-start(bf16[128,2048]{1,0:T(8,128)(2,1)S(1)} %shard_map.60), channel_id=1, source_target_pairs={{0,2},{1,5},{4,0},{5,9},{8,4},{9,13},{12,8},{13,15},{14,12},{15,11... | collective-permute-start | bytes 1572872 | tf_op jit(solution)/shard_map/back_2_0/ppermute | solution.py:221
  66.6 5.6 %collective-permute-start.25 = (bf16[128,2048]{1,0:T(8,128)(2,1)S(1)}, bf16[128,2048]{1,0:T(8,128)(2,1)S(1)}, u32[]{:S(2)}, u32[]{:S(2)}) collective-permute-start(bf16[128,2048]{1,0:T(8,128)(2,1)S(1)} %get-tuple-element.90), channel_id=1, source_target_pairs={{0,1},{1,0},{4,5},{5,4},{8,9},{9,8},{12,13},{13,12},{14,15},{15,14... | collective-permute-start | bytes 1572872 | tf_op jit(solution)/shard_map/give_1_0/ppermute | solution.py:221
  66.6 11.2 %collective-permute-start.28 = (bf16[128,2048]{1,0:T(8,128)(2,1)S(1)}, bf16[128,2048]{1,0:T(8,128)(2,1)S(1)}, u32[]{:S(2)}, u32[]{:S(2)}) collective-permute-start(bf16[128,2048]{1,0:T(8,128)(2,1)S(1)} %get-tuple-element.92), channel_id=1, source_target_pairs={{0,1},{1,0},{4,5},{5,4},{8,9},{9,8},{12,13},{13,12},{14,15},{15,14... | collective-permute-start | bytes 1572872 | tf_op jit(solution)/shard_map/give_1_1/ppermute | solution.py:221
  70.2 10.9 %collective-permute-start.29 = (bf16[128,2048]{1,0:T(8,128)(2,1)S(1)}, bf16[128,2048]{1,0:T(8,128)(2,1)S(1)}, u32[]{:S(2)}, u32[]{:S(2)}) collective-permute-start(bf16[128,2048]{1,0:T(8,128)(2,1)S(1)} %shard_map.61), channel_id=1, source_target_pairs={{0,2},{1,5},{4,0},{5,9},{8,4},{9,13},{12,8},{13,15},{14,12},{15,11... | collective-permute-start | bytes 1572872 | tf_op jit(solution)/shard_map/back_2_1/ppermute | solution.py:221
  72.2 10.1 %collective-permute-start.19 = (bf16[128,2048]{1,0:T(8,128)(2,1)S(1)}, bf16[128,2048]{1,0:T(8,128)(2,1)S(1)}, u32[]{:S(2)}, u32[]{:S(2)}) collective-permute-start(bf16[128,2048]{1,0:T(8,128)(2,1)S(1)} %get-tuple-element.78), channel_id=1, source_target_pairs={{0,1},{1,0},{4,5},{5,4},{8,9},{9,8},{12,13},{13,12},{14,15},{15,14... | collective-permute-start | bytes 1572872 | tf_op jit(solution)/shard_map/give_0_0/ppermute | solution.py:221
  75.8 10.9 %collective-permute-start.27 = (bf16[128,2048]{1,0:T(8,128)(2,1)S(1)}, bf16[128,2048]{1,0:T(8,128)(2,1)S(1)}, u32[]{:S(2)}, u32[]{:S(2)}) collective-permute-start(bf16[128,2048]{1,0:T(8,128)(2,1)S(1)} %shard_map.62), channel_id=1, source_target_pairs={{0,2},{1,5},{4,0},{5,9},{8,4},{9,13},{12,8},{13,15},{14,12},{15,11... | collective-permute-start | bytes 1572872 | tf_op jit(solution)/shard_map/back_1_0/ppermute | solution.py:221
  81.5 10.4 %collective-permute-start.30 = (bf16[128,2048]{1,0:T(8,128)(2,1)S(1)}, bf16[128,2048]{1,0:T(8,128)(2,1)S(1)}, u32[]{:S(2)}, u32[]{:S(2)}) collective-permute-start(bf16[128,2048]{1,0:T(8,128)(2,1)S(1)} %shard_map.64), channel_id=1, source_target_pairs={{0,3},{1,4},{4,1},{5,8},{8,5},{9,12},{12,9},{13,14},{14,13},{15,10... | collective-permute-start | bytes 1572872 | tf_op jit(solution)/shard_map/back_1_1/ppermute | solution.py:221
  (9 other events, 30.0 us)

commit v18 on v17

--- a/solution.py
+++ b/solution.py
@@ -8,7 +8,7 @@
 from jax.experimental.pallas import tpu as pltpu
 from jax.sharding import PartitionSpec as P
 
-GATE_ROWS, LANES = 8, 128
+GATE_ROWS, LANES = 16, 128
 
 
 def expert_half(slot_block, gate_up, down_proj):

time: 92.9 us -> 93.7 us (level)
  transfers between devices with their start and end apart: 31 -> 31, of which waited for: 12 -> 13; matrix products, arithmetic and copies ran while one was open for 1% -> 1% of each run, Pallas kernels for 31% -> 31%
where the time goes in v18:
time: 93.7 us; the launch traced here: 93.5 us
  waiting for transfers between devices  31.2 us (33%)
  starting transfers between devices  29.3 us (31%)
  Pallas kernels  29.1 us (31%)
  local copies, waits for them, and re-layouts  1.9 us (2%)
  other arithmetic  1.79 us (2%)
    ppermute x31, waiting for transfers between devices, send(): return lax.ppermute(value, 'blk', pairs)  31.2 us
    ppermute x31, starting transfers between devices, send(): return lax.ppermute(value, 'blk', pairs)  29.3 us
    pallas_call x9, Pallas kernels, half_expert(): pl.pallas_call(functools.partial(half_expert_kernel, tuple(heights), load...  23.9 us
    pallas_call x1, Pallas kernels, loaded(): pl.pallas_call(load_kernel, out_shape=[jax.ShapeDtypeStruct(array.shape,...  2.86 us
    pallas_call x8, Pallas kernels, weighted(): pl.pallas_call(functools.partial(weighted_kernel, kind, len(own), len(dis...  2.35 us
    unnamed x4, local copies, waits for them, and re-layouts  1.89 us
  transfers between devices with their start and end apart: 31, of which 13 were waited for; matrix products, arithmetic and copies ran while one was open for 1% of the time, Pallas kernels for 31%

profile of v18, /device:TPU:0, one launch (start us, length us, event | category | flops | bytes accessed | tf_op | source)
XLA Modules:
  0.0 93.5 jit_solution(14000326750743563864)
XLA Ops:
  0.5 2.6 %collective-permute-start.2 = (bf16[128,2048]{1,0:T(8,128)(2,1)}, bf16[128,2048]{1,0:T(8,128)(2,1)S(1)}, u32[]{:S(2)}, u32[]{:S(2)}) collective-permute-start(bf16[128,2048]{1,0:T(8,128)(2,1)} %refs_0_.1), channel_id=1, source_target_pairs={{0,4},{1,3},{4,8},{5,1},{8,12},{9,5},{12,14},{13,9},{14,10},{15,13... | collective-permute-start | bytes 1572872 | tf_op jit(solution)/shard_map/ring_1_0/ppermute | solution.py:221
  8.6 2.9 %shard_map.56 = (bf16[2,768,2048]{2,1,0:T(8,128)(2,1)S(1)}, bf16[768,2048]{1,0:T(8,128)(2,1)S(1)}) custom-call(bf16[2,768,2048]{2,1,0:T(8,128)(2,1)} %refs_0_, bf16[768,2048]{1,0:T(8,128)(2,1)S(1)} %copy-done), custom_call_target="tpu_custom_call" | custom-call | flops 268435456 | bytes 1048576 | tf_op jit(solution)/shard_map/pallas_call | solution.py:111
  13.2 2.7 %expert_0.1 = (bf16[128,2048]{1,0:T(8,128)(2,1)S(1)}, bf16[128,2048]{1,0:T(8,128)(2,1)S(1)}) custom-call(bf16[128,2048]{1,0:T(8,128)(2,1)S(1)} %copy-done.1, bf16[144,2048]{1,0:T(8,128)(2,1)S(1)} %maximum_maximum_fusion.refs_1_, bf16[2,768,2048]{2,1,0:T(8,128)(2,1)S(1)} %get-tuple-element.53.refs_2_.refs_1_, ...), custom_call_target="tpu_custom_call" | custom-call | flops 805306368 | bytes 3145728 | tf_op jit(solution)/shard_map/expert_0/pallas_call | solution.py:150
  16.7 2.1 %collective-permute-start.4 = (bf16[144,2048]{1,0:T(8,128)(2,1)S(1)}, bf16[144,2048]{1,0:T(8,128)(2,1)S(1)}, u32[]{:S(2)}, u32[]{:S(2)}) collective-permute-start(bf16[144,2048]{1,0:T(8,128)(2,1)S(1)} %collective-permute-done.3.refs_0_.refs_1_), channel_id=1, source_target_pairs={{0,4},{1,3},{4,8},{5,1},{8,12},{9,5},{12,14},{13,9},{14,10},{15,13... | collective-permute-start | bytes 1769480 | tf_op jit(solution)/shard_map/ring_2_1/ppermute | solution.py:221
  18.7 2.6 %expert_1_0.1 = (bf16[128,2048]{1,0:T(8,128)(2,1)S(1)}, bf16[128,2048]{1,0:T(8,128)(2,1)S(1)}) custom-call(bf16[128,2048]{1,0:T(8,128)(2,1)S(1)} %collective-permute-done.2.refs_0_, bf16[128,2048]{1,0:T(8,128)(2,1)S(1)} %collective-permute-done.6.refs_1_, bf16[2,768,2048]{2,1,0:T(8,128)(2,1)S(1)} %get-tuple-element.53.refs_2_.refs_1_, ...), custom_call_target="tpu_custom_call" | custom-call | flops 805306368 | bytes 3145728 | tf_op jit(solution)/shard_map/expert_1_0/pallas_call | solution.py:150
  22.3 2.1 %collective-permute-start.7 = (bf16[128,2048]{1,0:T(8,128)(2,1)S(1)}, bf16[128,2048]{1,0:T(8,128)(2,1)S(1)}, u32[]{:S(2)}, u32[]{:S(2)}) collective-permute-start(bf16[128,2048]{1,0:T(8,128)(2,1)S(1)} %collective-permute-done.5.refs_0_), channel_id=1, source_target_pairs={{0,4},{1,3},{4,8},{5,1},{8,12},{9,5},{12,14},{13,9},{14,10},{15,13... | collective-permute-start | bytes 1572872 | tf_op jit(solution)/shard_map/ring_3_0/ppermute | solution.py:221
  24.4 4.2 %collective-permute-done.4.refs_0_.refs_1_ = bf16[144,2048]{1,0:T(8,128)(2,1)S(1)} collective-permute-done((bf16[144,2048]{1,0:T(8,128)(2,1)S(1)}, bf16[144,2048]{1,0:T(8,128)(2,1)S(1)}, u32[]{:S(2)}, u32[]{:S(2)}) %collective-permute-start.4) | collective-permute-done | bytes 589856 | tf_op jit(solution)/shard_map/ring_2_1/ppermute | solution.py:221
  28.6 2.6 %expert_2_0.1 = (bf16[128,2048]{1,0:T(8,128)(2,1)S(1)}, bf16[128,2048]{1,0:T(8,128)(2,1)S(1)}) custom-call(bf16[128,2048]{1,0:T(8,128)(2,1)S(1)} %collective-permute-done.5.refs_0_, bf16[128,2048]{1,0:T(8,128)(2,1)S(1)} %collective-permute-done.8.refs_1_, bf16[2,768,2048]{2,1,0:T(8,128)(2,1)S(1)} %get-tuple-element.53.refs_2_.refs_1_, ...), custom_call_target="tpu_custom_call" | custom-call | flops 805306368 | bytes 3145728 | tf_op jit(solution)/shard_map/expert_2_0/pallas_call | solution.py:150
  31.3 3.0 %collective-permute-done.7.refs_0_ = bf16[128,2048]{1,0:T(8,128)(2,1)S(1)} collective-permute-done((bf16[128,2048]{1,0:T(8,128)(2,1)S(1)}, bf16[128,2048]{1,0:T(8,128)(2,1)S(1)}, u32[]{:S(2)}, u32[]{:S(2)}) %collective-permute-start.7) | collective-permute-done | bytes 524320 | tf_op jit(solution)/shard_map/ring_3_0/ppermute | solution.py:221
  34.2 2.1 %collective-permute-start.12 = (bf16[128,2048]{1,0:T(8,128)(2,1)S(1)}, bf16[128,2048]{1,0:T(8,128)(2,1)S(1)}, u32[]{:S(2)}, u32[]{:S(2)}) collective-permute-start(bf16[128,2048]{1,0:T(8,128)(2,1)S(1)} %collective-permute-done.7.refs_0_), channel_id=1, source_target_pairs={{0,4},{1,3},{4,8},{5,1},{8,12},{9,5},{12,14},{13,9},{14,10},{15,13... | collective-permute-start | bytes 1572872 | tf_op jit(solution)/shard_map/ring_4_0/ppermute | solution.py:221
  36.3 2.6 %expert_2_1.1 = (bf16[128,2048]{1,0:T(8,128)(2,1)S(1)}, bf16[128,2048]{1,0:T(8,128)(2,1)S(1)}) custom-call(bf16[144,2048]{1,0:T(8,128)(2,1)S(1)} %collective-permute-done.4.refs_0_.refs_1_, bf16[144,2048]{1,0:T(8,128)(2,1)S(1)} %collective-permute-done.9.refs_1_, bf16[2,768,2048]{2,1,0:T(8,128)(2,1)S(1)} %get-tuple-element.53.refs_2_.refs_1_, ...), custom_call_target="tpu_custom_call" | custom-call | flops 805306368 | bytes 3145728 | tf_op jit(solution)/shard_map/expert_2_1/pallas_call | solution.py:150
  40.8 2.6 %expert_3_0.1 = (bf16[128,2048]{1,0:T(8,128)(2,1)S(1)}, bf16[128,2048]{1,0:T(8,128)(2,1)S(1)}) custom-call(bf16[128,2048]{1,0:T(8,128)(2,1)S(1)} %collective-permute-done.7.refs_0_, bf16[128,2048]{1,0:T(8,128)(2,1)S(1)} %collective-permute-done.11.refs_1_, bf16[2,768,2048]{2,1,0:T(8,128)(2,1)S(1)} %get-tuple-element.53.refs_2_.refs_1_, ...), custom_call_target="tpu_custom_call" | custom-call | flops 805306368 | bytes 3145728 | tf_op jit(solution)/shard_map/expert_3_0/pallas_call | solution.py:150
  43.5 2.7 %expert_far_ring.1 = bf16[128,2048]{1,0:T(8,128)(2,1)S(1)} custom-call(bf16[128,2048]{1,0:T(8,128)(2,1)S(1)} %collective-permute-done.12.refs_0_, bf16[2,768,2048]{2,1,0:T(8,128)(2,1)S(1)} %get-tuple-element.53.refs_2_.refs_1_, bf16[768,2048]{1,0:T(8,128)(2,1)S(1)} %get-tuple-element.50.refs_3_.refs_2_), custom_call_target="tpu_custom_call" | custom-call | flops 60397976 | bytes 471859 | tf_op jit(solution)/shard_map/expert_far_ring/pallas_call | solution.py:150
  46.8 2.7 %expert_far_swapped.1 = bf16[128,2048]{1,0:T(8,128)(2,1)S(1)} custom-call(bf16[128,2048]{1,0:T(8,128)(2,1)S(1)} %collective-permute-done.13.refs_0_, bf16[2,768,2048]{2,1,0:T(8,128)(2,1)S(1)} %get-tuple-element.53.refs_2_.refs_1_, bf16[768,2048]{1,0:T(8,128)(2,1)S(1)} %get-tuple-element.50.refs_3_.refs_2_), custom_call_target="tpu_custom_call" | custom-call | flops 60397976 | bytes 471859 | tf_op jit(solution)/shard_map/expert_far_swapped/pallas_call | solution.py:150
  50.1 2.0 %collective-permute-start.18 = (bf16[128,2048]{1,0:T(8,128)(2,1)S(1)}, bf16[128,2048]{1,0:T(8,128)(2,1)S(1)}, u32[]{:S(2)}, u32[]{:S(2)}) collective-permute-start(bf16[128,2048]{1,0:T(8,128)(2,1)S(1)} %add_convert_fusion.1), channel_id=1, source_target_pairs={{0,2},{1,5},{4,0},{5,9},{8,4},{9,13},{12,8},{13,15},{14,12},{15,11... | collective-permute-start | bytes 1572872 | tf_op jit(solution)/shard_map/back_4_1/ppermute | solution.py:221
  52.4 2.7 %expert_3_1.1 = (bf16[128,2048]{1,0:T(8,128)(2,1)S(1)}, bf16[128,2048]{1,0:T(8,128)(2,1)S(1)}) custom-call(bf16[144,2048]{1,0:T(8,128)(2,1)S(1)} %collective-permute-done.10.refs_1_.refs_0_.refs_2_, bf16[144,2048]{1,0:T(8,128)(2,1)S(1)} %collective-permute-done.16.refs_1_, bf16[2,768,2048]{2,1,0:T(8,128)(2,1)S(1)} %get-tuple-element.53.refs_2_.refs_1_, ...), custom_call_target="tpu_custom_call" | custom-call | flops 80530640 | bytes 314572 | tf_op jit(solution)/shard_map/expert_3_1/pallas_call | solution.py:150
  57.2 2.1 %collective-permute-done.18.refs_4_ = bf16[128,2048]{1,0:T(8,128)(2,1)S(1)} collective-permute-done((bf16[128,2048]{1,0:T(8,128)(2,1)S(1)}, bf16[128,2048]{1,0:T(8,128)(2,1)S(1)}, u32[]{:S(2)}, u32[]{:S(2)}) %collective-permute-start.18) | collective-permute-done | bytes 524320 | tf_op jit(solution)/shard_map/back_4_1/ppermute | solution.py:221
  60.0 2.0 %collective-permute-start.24 = (bf16[128,2048]{1,0:T(8,128)(2,1)S(1)}, bf16[128,2048]{1,0:T(8,128)(2,1)S(1)}, u32[]{:S(2)}, u32[]{:S(2)}) collective-permute-start(bf16[128,2048]{1,0:T(8,128)(2,1)S(1)} %shard_map.59), channel_id=1, source_target_pairs={{0,2},{1,5},{4,0},{5,9},{8,4},{9,13},{12,8},{13,15},{14,12},{15,11... | collective-permute-start | bytes 1572872 | tf_op jit(solution)/shard_map/back_3_1/ppermute | solution.py:221
  62.0 2.6 %expert_1_1.1 = (bf16[128,2048]{1,0:T(8,128)(2,1)S(1)}, bf16[128,2048]{1,0:T(8,128)(2,1)S(1)}) custom-call(bf16[144,2048]{1,0:T(8,128)(2,1)S(1)} %collective-permute-done.3.refs_0_.refs_1_, bf16[144,2048]{1,0:T(8,128)(2,1)S(1)} %collective-permute-done.20.refs_1_, bf16[2,768,2048]{2,1,0:T(8,128)(2,1)S(1)} %get-tuple-element.53.refs_2_.refs_1_, ...), custom_call_target="tpu_custom_call" | custom-call | flops 805306368 | bytes 3145728 | tf_op jit(solution)/shard_map/expert_1_1/pallas_call | solution.py:150
  67.8 2.8 %collective-permute-done.24.refs_4_ = bf16[128,2048]{1,0:T(8,128)(2,1)S(1)} collective-permute-done((bf16[128,2048]{1,0:T(8,128)(2,1)S(1)}, bf16[128,2048]{1,0:T(8,128)(2,1)S(1)}, u32[]{:S(2)}, u32[]{:S(2)}) %collective-permute-start.24) | collective-permute-done | bytes 524320 | tf_op jit(solution)/shard_map/back_3_1/ppermute | solution.py:221
  72.9 3.3 %collective-permute-done.26.refs_4_ = bf16[128,2048]{1,0:T(8,128)(2,1)S(1)} collective-permute-done((bf16[128,2048]{1,0:T(8,128)(2,1)S(1)}, bf16[128,2048]{1,0:T(8,128)(2,1)S(1)}, u32[]{:S(2)}, u32[]{:S(2)}) %collective-permute-start.26) | collective-permute-done | bytes 524320 | tf_op jit(solution)/shard_map/back_2_0/ppermute | solution.py:221
  78.5 3.3 %collective-permute-done.29.refs_4_ = bf16[128,2048]{1,0:T(8,128)(2,1)S(1)} collective-permute-done((bf16[128,2048]{1,0:T(8,128)(2,1)S(1)}, bf16[128,2048]{1,0:T(8,128)(2,1)S(1)}, u32[]{:S(2)}, u32[]{:S(2)}) %collective-permute-start.29) | collective-permute-done | bytes 524320 | tf_op jit(solution)/shard_map/back_2_1/ppermute | solution.py:221
  83.2 4.2 %collective-permute-done.27.refs_4_ = bf16[128,2048]{1,0:T(8,128)(2,1)S(1)} collective-permute-done((bf16[128,2048]{1,0:T(8,128)(2,1)S(1)}, bf16[128,2048]{1,0:T(8,128)(2,1)S(1)}, u32[]{:S(2)}, u32[]{:S(2)}) %collective-permute-start.27) | collective-permute-done | bytes 524320 | tf_op jit(solution)/shard_map/back_1_0/ppermute | solution.py:221
  87.8 4.8 %collective-permute-done.30 = bf16[128,2048]{1,0:T(8,128)(2,1)S(1)} collective-permute-done((bf16[128,2048]{1,0:T(8,128)(2,1)S(1)}, bf16[128,2048]{1,0:T(8,128)(2,1)S(1)}, u32[]{:S(2)}, u32[]{:S(2)}) %collective-permute-start.30) | collective-permute-done | bytes 524320 | tf_op jit(solution)/shard_map/back_1_1/ppermute | solution.py:221
  (69 shorter events, 25.9 us)
Async XLA Ops:
  0.5 11.0 %collective-permute-start.2 = (bf16[128,2048]{1,0:T(8,128)(2,1)}, bf16[128,2048]{1,0:T(8,128)(2,1)S(1)}, u32[]{:S(2)}, u32[]{:S(2)}) collective-permute-start(bf16[128,2048]{1,0:T(8,128)(2,1)} %refs_0_.1), channel_id=1, source_target_pairs={{0,4},{1,3},{4,8},{5,1},{8,12},{9,5},{12,14},{13,9},{14,10},{15,13... | collective-permute-start | bytes 1572872 | tf_op jit(solution)/shard_map/ring_1_0/ppermute | solution.py:221
  5.1 11.6 %collective-permute-start.3 = (bf16[144,2048]{1,0:T(8,128)(2,1)S(1)}, bf16[144,2048]{1,0:T(8,128)(2,1)S(1)}, u32[]{:S(2)}, u32[]{:S(2)}) collective-permute-start(bf16[144,2048]{1,0:T(8,128)(2,1)S(1)} %maximum_maximum_fusion.refs_1_), channel_id=1, source_target_pairs={{0,4},{1,3},{4,8},{5,1},{8,12},{9,5},{12,14},{13,9},{14,10},{15,13... | collective-permute-start | bytes 1769480 | tf_op jit(solution)/shard_map/ring_1_1/ppermute | solution.py:221
  11.5 7.3 %collective-permute-start.6 = (bf16[128,2048]{1,0:T(8,128)(2,1)S(1)}, bf16[128,2048]{1,0:T(8,128)(2,1)S(1)}, u32[]{:S(2)}, u32[]{:S(2)}) collective-permute-start(bf16[128,2048]{1,0:T(8,128)(2,1)S(1)} %collective-permute-done.2.refs_0_), channel_id=1, source_target_pairs={{0,1},{1,0},{4,5},{5,4},{8,9},{9,8},{12,13},{13,12},{14,15},{15,14... | collective-permute-start | bytes 1572872 | tf_op jit(solution)/shard_map/swap_1_0/ppermute | solution.py:221
  11.5 10.7 %collective-permute-start.5 = (bf16[128,2048]{1,0:T(8,128)(2,1)S(1)}, bf16[128,2048]{1,0:T(8,128)(2,1)S(1)}, u32[]{:S(2)}, u32[]{:S(2)}) collective-permute-start(bf16[128,2048]{1,0:T(8,128)(2,1)S(1)} %collective-permute-done.2.refs_0_), channel_id=1, source_target_pairs={{0,4},{1,3},{4,8},{5,1},{8,12},{9,5},{12,14},{13,9},{14,10},{15,13... | collective-permute-start | bytes 1572872 | tf_op jit(solution)/shard_map/ring_2_0/ppermute | solution.py:221
  16.7 11.9 %collective-permute-start.4 = (bf16[144,2048]{1,0:T(8,128)(2,1)S(1)}, bf16[144,2048]{1,0:T(8,128)(2,1)S(1)}, u32[]{:S(2)}, u32[]{:S(2)}) collective-permute-start(bf16[144,2048]{1,0:T(8,128)(2,1)S(1)} %collective-permute-done.3.refs_0_.refs_1_), channel_id=1, source_target_pairs={{0,4},{1,3},{4,8},{5,1},{8,12},{9,5},{12,14},{13,9},{14,10},{15,13... | collective-permute-start | bytes 1769480 | tf_op jit(solution)/shard_map/ring_2_1/ppermute | solution.py:221
  22.3 6.3 %collective-permute-start.8 = (bf16[128,2048]{1,0:T(8,128)(2,1)S(1)}, bf16[128,2048]{1,0:T(8,128)(2,1)S(1)}, u32[]{:S(2)}, u32[]{:S(2)}) collective-permute-start(bf16[128,2048]{1,0:T(8,128)(2,1)S(1)} %collective-permute-done.5.refs_0_), channel_id=1, source_target_pairs={{0,1},{1,0},{4,5},{5,4},{8,9},{9,8},{12,13},{13,12},{14,15},{15,14... | collective-permute-start | bytes 1572872 | tf_op jit(solution)/shard_map/swap_2_0/ppermute | solution.py:221
  22.3 11.9 %collective-permute-start.7 = (bf16[128,2048]{1,0:T(8,128)(2,1)S(1)}, bf16[128,2048]{1,0:T(8,128)(2,1)S(1)}, u32[]{:S(2)}, u32[]{:S(2)}) collective-permute-start(bf16[128,2048]{1,0:T(8,128)(2,1)S(1)} %collective-permute-done.5.refs_0_), channel_id=1, source_target_pairs={{0,4},{1,3},{4,8},{5,1},{8,12},{9,5},{12,14},{13,9},{14,10},{15,13... | collective-permute-start | bytes 1572872 | tf_op jit(solution)/shard_map/ring_3_0/ppermute | solution.py:221
  28.6 7.7 %collective-permute-start.9 = (bf16[144,2048]{1,0:T(8,128)(2,1)S(1)}, bf16[144,2048]{1,0:T(8,128)(2,1)S(1)}, u32[]{:S(2)}, u32[]{:S(2)}) collective-permute-start(bf16[144,2048]{1,0:T(8,128)(2,1)S(1)} %collective-permute-done.4.refs_0_.refs_1_), channel_id=1, source_target_pairs={{0,1},{1,0},{4,5},{5,4},{8,9},{9,8},{12,13},{13,12},{14,15},{15,14... | collective-permute-start | bytes 1769480 | tf_op jit(solution)/shard_map/swap_2_1/ppermute | solution.py:221
  34.2 6.6 %collective-permute-start.11 = (bf16[128,2048]{1,0:T(8,128)(2,1)S(1)}, bf16[128,2048]{1,0:T(8,128)(2,1)S(1)}, u32[]{:S(2)}, u32[]{:S(2)}) collective-permute-start(bf16[128,2048]{1,0:T(8,128)(2,1)S(1)} %collective-permute-done.7.refs_0_), channel_id=1, source_target_pairs={{0,1},{1,0},{4,5},{5,4},{8,9},{9,8},{12,13},{13,12},{14,15},{15,14... | collective-permute-start | bytes 1572872 | tf_op jit(solution)/shard_map/swap_3_0/ppermute | solution.py:221
  34.2 9.2 %collective-permute-start.12 = (bf16[128,2048]{1,0:T(8,128)(2,1)S(1)}, bf16[128,2048]{1,0:T(8,128)(2,1)S(1)}, u32[]{:S(2)}, u32[]{:S(2)}) collective-permute-start(bf16[128,2048]{1,0:T(8,128)(2,1)S(1)} %collective-permute-done.7.refs_0_), channel_id=1, source_target_pairs={{0,4},{1,3},{4,8},{5,1},{8,12},{9,5},{12,14},{13,9},{14,10},{15,13... | collective-permute-start | bytes 1572872 | tf_op jit(solution)/shard_map/ring_4_0/ppermute | solution.py:221
  39.0 10.8 %collective-permute-start.10 = (bf16[144,2048]{1,0:T(8,128)(2,1)S(1)}, bf16[144,2048]{1,0:T(8,128)(2,1)S(1)}, u32[]{:S(2)}, u32[]{:S(2)}) collective-permute-start(bf16[144,2048]{1,0:T(8,128)(2,1)S(1)} %collective-permute-done.4.refs_0_.refs_1_), channel_id=1, source_target_pairs={{0,4},{1,3},{4,8},{5,1},{8,12},{9,5},{12,14},{13,9},{14,10},{15,13... | collective-permute-start | bytes 1769480 | tf_op jit(solution)/shard_map/ring_3_1/ppermute | solution.py:221
  46.8 5.4 %collective-permute-start.15 = (bf16[128,2048]{1,0:T(8,128)(2,1)S(1)}, bf16[128,2048]{1,0:T(8,128)(2,1)S(1)}, u32[]{:S(2)}, u32[]{:S(2)}) collective-permute-start(bf16[128,2048]{1,0:T(8,128)(2,1)S(1)} %get-tuple-element.71), channel_id=1, source_target_pairs={{0,1},{1,0},{4,5},{5,4},{8,9},{9,8},{12,13},{13,12},{14,15},{15,14... | collective-permute-start | bytes 1572872 | tf_op jit(solution)/shard_map/give_3_0/ppermute | solution.py:221
  50.1 9.2 %collective-permute-start.18 = (bf16[128,2048]{1,0:T(8,128)(2,1)S(1)}, bf16[128,2048]{1,0:T(8,128)(2,1)S(1)}, u32[]{:S(2)}, u32[]{:S(2)}) collective-permute-start(bf16[128,2048]{1,0:T(8,128)(2,1)S(1)} %add_convert_fusion.1), channel_id=1, source_target_pairs={{0,2},{1,5},{4,0},{5,9},{8,4},{9,13},{12,8},{13,15},{14,12},{15,11... | collective-permute-start | bytes 1572872 | tf_op jit(solution)/shard_map/back_4_1/ppermute | solution.py:221
  55.2 9.8 %collective-permute-start.22 = (bf16[128,2048]{1,0:T(8,128)(2,1)S(1)}, bf16[128,2048]{1,0:T(8,128)(2,1)S(1)}, u32[]{:S(2)}, u32[]{:S(2)}) collective-permute-start(bf16[128,2048]{1,0:T(8,128)(2,1)S(1)} %shard_map.57), channel_id=1, source_target_pairs={{0,2},{1,5},{4,0},{5,9},{8,4},{9,13},{12,8},{13,15},{14,12},{15,11... | collective-permute-start | bytes 1572872 | tf_op jit(solution)/shard_map/back_3_0/ppermute | solution.py:221
  56.7 8.3 %collective-permute-start.21 = (bf16[128,2048]{1,0:T(8,128)(2,1)S(1)}, bf16[128,2048]{1,0:T(8,128)(2,1)S(1)}, u32[]{:S(2)}, u32[]{:S(2)}) collective-permute-start(bf16[128,2048]{1,0:T(8,128)(2,1)S(1)} %get-tuple-element.84), channel_id=1, source_target_pairs={{0,1},{1,0},{4,5},{5,4},{8,9},{9,8},{12,13},{13,12},{14,15},{15,14... | collective-permute-start | bytes 1572872 | tf_op jit(solution)/shard_map/give_2_0/ppermute | solution.py:221
  56.8 11.0 %collective-permute-start.23 = (bf16[128,2048]{1,0:T(8,128)(2,1)S(1)}, bf16[128,2048]{1,0:T(8,128)(2,1)S(1)}, u32[]{:S(2)}, u32[]{:S(2)}) collective-permute-start(bf16[128,2048]{1,0:T(8,128)(2,1)S(1)} %get-tuple-element.87), channel_id=1, source_target_pairs={{0,1},{1,0},{4,5},{5,4},{8,9},{9,8},{12,13},{13,12},{14,15},{15,14... | collective-permute-start | bytes 1572872 | tf_op jit(solution)/shard_map/give_2_1/ppermute | solution.py:221
  60.0 10.6 %collective-permute-start.24 = (bf16[128,2048]{1,0:T(8,128)(2,1)S(1)}, bf16[128,2048]{1,0:T(8,128)(2,1)S(1)}, u32[]{:S(2)}, u32[]{:S(2)}) collective-permute-start(bf16[128,2048]{1,0:T(8,128)(2,1)S(1)} %shard_map.59), channel_id=1, source_target_pairs={{0,2},{1,5},{4,0},{5,9},{8,4},{9,13},{12,8},{13,15},{14,12},{15,11... | collective-permute-start | bytes 1572872 | tf_op jit(solution)/shard_map/back_3_1/ppermute | solution.py:221
  65.3 10.9 %collective-permute-start.26 = (bf16[128,2048]{1,0:T(8,128)(2,1)S(1)}, bf16[128,2048]{1,0:T(8,128)(2,1)S(1)}, u32[]{:S(2)}, u32[]{:S(2)}) collective-permute-start(bf16[128,2048]{1,0:T(8,128)(2,1)S(1)} %shard_map.60), channel_id=1, source_target_pairs={{0,2},{1,5},{4,0},{5,9},{8,4},{9,13},{12,8},{13,15},{14,12},{15,11... | collective-permute-start | bytes 1572872 | tf_op jit(solution)/shard_map/back_2_0/ppermute | solution.py:221
  67.3 5.6 %collective-permute-start.25 = (bf16[128,2048]{1,0:T(8,128)(2,1)S(1)}, bf16[128,2048]{1,0:T(8,128)(2,1)S(1)}, u32[]{:S(2)}, u32[]{:S(2)}) collective-permute-start(bf16[128,2048]{1,0:T(8,128)(2,1)S(1)} %get-tuple-element.90), channel_id=1, source_target_pairs={{0,1},{1,0},{4,5},{5,4},{8,9},{9,8},{12,13},{13,12},{14,15},{15,14... | collective-permute-start | bytes 1572872 | tf_op jit(solution)/shard_map/give_1_0/ppermute | solution.py:221
  67.3 11.2 %collective-permute-start.28 = (bf16[128,2048]{1,0:T(8,128)(2,1)S(1)}, bf16[128,2048]{1,0:T(8,128)(2,1)S(1)}, u32[]{:S(2)}, u32[]{:S(2)}) collective-permute-start(bf16[128,2048]{1,0:T(8,128)(2,1)S(1)} %get-tuple-element.92), channel_id=1, source_target_pairs={{0,1},{1,0},{4,5},{5,4},{8,9},{9,8},{12,13},{13,12},{14,15},{15,14... | collective-permute-start | bytes 1572872 | tf_op jit(solution)/shard_map/give_1_1/ppermute | solution.py:221
  70.9 10.9 %collective-permute-start.29 = (bf16[128,2048]{1,0:T(8,128)(2,1)S(1)}, bf16[128,2048]{1,0:T(8,128)(2,1)S(1)}, u32[]{:S(2)}, u32[]{:S(2)}) collective-permute-start(bf16[128,2048]{1,0:T(8,128)(2,1)S(1)} %shard_map.61), channel_id=1, source_target_pairs={{0,2},{1,5},{4,0},{5,9},{8,4},{9,13},{12,8},{13,15},{14,12},{15,11... | collective-permute-start | bytes 1572872 | tf_op jit(solution)/shard_map/back_2_1/ppermute | solution.py:221
  72.9 10.3 %collective-permute-start.19 = (bf16[128,2048]{1,0:T(8,128)(2,1)S(1)}, bf16[128,2048]{1,0:T(8,128)(2,1)S(1)}, u32[]{:S(2)}, u32[]{:S(2)}) collective-permute-start(bf16[128,2048]{1,0:T(8,128)(2,1)S(1)} %get-tuple-element.78), channel_id=1, source_target_pairs={{0,1},{1,0},{4,5},{5,4},{8,9},{9,8},{12,13},{13,12},{14,15},{15,14... | collective-permute-start | bytes 1572872 | tf_op jit(solution)/shard_map/give_0_0/ppermute | solution.py:221
  76.6 10.9 %collective-permute-start.27 = (bf16[128,2048]{1,0:T(8,128)(2,1)S(1)}, bf16[128,2048]{1,0:T(8,128)(2,1)S(1)}, u32[]{:S(2)}, u32[]{:S(2)}) collective-permute-start(bf16[128,2048]{1,0:T(8,128)(2,1)S(1)} %shard_map.62), channel_id=1, source_target_pairs={{0,2},{1,5},{4,0},{5,9},{8,4},{9,13},{12,8},{13,15},{14,12},{15,11... | collective-permute-start | bytes 1572872 | tf_op jit(solution)/shard_map/back_1_0/ppermute | solution.py:221
  82.2 10.4 %collective-permute-start.30 = (bf16[128,2048]{1,0:T(8,128)(2,1)S(1)}, bf16[128,2048]{1,0:T(8,128)(2,1)S(1)}, u32[]{:S(2)}, u32[]{:S(2)}) collective-permute-start(bf16[128,2048]{1,0:T(8,128)(2,1)S(1)} %shard_map.64), channel_id=1, source_target_pairs={{0,3},{1,4},{4,1},{5,8},{8,5},{9,12},{12,9},{13,14},{14,13},{15,10... | collective-permute-start | bytes 1572872 | tf_op jit(solution)/shard_map/back_1_1/ppermute | solution.py:221
  (9 other events, 29.8 us)

commit v19 on v18

--- a/solution.py
+++ b/solution.py
@@ -197,6 +197,35 @@
         compiler_params=pltpu.CompilerParams(vmem_limit_bytes=10 << 20),
         cost_estimate=pl.CostEstimate(flops=size * 20000, bytes_accessed=size, transcendentals=0),
     )(*experts, holder, *terms)
+
+
+def last_sum_kernel(own, arrived, out, parts, done):
+    chunks, height = parts.shape[:2]
+    copies = []
+    for i in range(chunks):
+        near = slice(i * height, (i + 1) * height)
+        parts[i] = (own[near, :] + arrived[near, :].astype(jnp.float32)).astype(out.dtype)
+        copies.append(pltpu.make_async_copy(parts.at[i], out.at[pl.ds(i * height, height)], done.at[i]))
+        copies[-1].start()
+    for copy in copies:
+        copy.wait()
+
+
+def last_sum(own, arrived):
+    whole = pl.BlockSpec(memory_space=pltpu.VMEM)
+    rows, width = own.shape
+    chunks = 4
+    return pl.pallas_call(
+        last_sum_kernel,
+        out_shape=jax.ShapeDtypeStruct((rows, width), jnp.bfloat16),
+        in_specs=[whole, whole],
+        out_specs=pl.BlockSpec(memory_space=pltpu.HBM),
+        scratch_shapes=[
+            pltpu.VMEM((chunks, rows // chunks, width), jnp.bfloat16),
+            pltpu.SemaphoreType.DMA((chunks,)),
+        ],
+        compiler_params=pltpu.CompilerParams(vmem_limit_bytes=8 << 20),
+    )(own, arrived)
 
 
 def by_tokens(tokens, expert_ids, route_gate, gate_up, down_proj):
@@ -327,7 +356,7 @@
             give(0, 0, earlier)
             earlier = expert_rows(1, 1, [after(delayed, earlier), swapped])
     own = weighted(expert, packed, 0, results[0, 0], plain=[sums[0]], dtype=jnp.float32)
-    return rounded(total(own, sums[1]))
+    return last_sum(own, sums[1])
 
 
 def solution(mesh):

time: 93.7 us -> 93.8 us (level)
  no operation moved by 1% of the time
where the time goes in v19:
time: 93.8 us; the launch traced here: 93.6 us
  waiting for transfers between devices  31.2 us (33%)
  Pallas kernels  29.9 us (32%)
  starting transfers between devices  29.3 us (31%)
  local copies, waits for them, and re-layouts  1.9 us (2%)
    ppermute x31, waiting for transfers between devices, send(): return lax.ppermute(value, 'blk', pairs)  31.2 us
    ppermute x31, starting transfers between devices, send(): return lax.ppermute(value, 'blk', pairs)  29.3 us
    pallas_call x9, Pallas kernels, half_expert(): pl.pallas_call(functools.partial(half_expert_kernel, tuple(heights), load...  23.9 us
    pallas_call x1, Pallas kernels, loaded(): pl.pallas_call(load_kernel, out_shape=[jax.ShapeDtypeStruct(array.shape,...  2.86 us
    pallas_call x8, Pallas kernels, weighted(): pl.pallas_call(functools.partial(weighted_kernel, kind, len(own), len(dis...  2.35 us
    unnamed x4, local copies, waits for them, and re-layouts  1.89 us
  transfers between devices with their start and end apart: 31, of which 13 were waited for; matrix products, arithmetic and copies ran while one was open for 1% of the time, Pallas kernels for 31%

profile of v19, /device:TPU:0, one launch (start us, length us, event | category | flops | bytes accessed | tf_op | source)
XLA Modules:
  0.0 93.6 jit_solution(13259678626990920627)
XLA Ops:
  0.5 2.6 %collective-permute-start.2 = (bf16[128,2048]{1,0:T(8,128)(2,1)}, bf16[128,2048]{1,0:T(8,128)(2,1)S(1)}, u32[]{:S(2)}, u32[]{:S(2)}) collective-permute-start(bf16[128,2048]{1,0:T(8,128)(2,1)} %refs_0_.1), channel_id=1, source_target_pairs={{0,4},{1,3},{4,8},{5,1},{8,12},{9,5},{12,14},{13,9},{14,10},{15,13... | collective-permute-start | bytes 1572872 | tf_op jit(solution)/shard_map/ring_1_0/ppermute | solution.py:250
  8.6 2.9 %shard_map.56 = (bf16[2,768,2048]{2,1,0:T(8,128)(2,1)S(1)}, bf16[768,2048]{1,0:T(8,128)(2,1)S(1)}) custom-call(bf16[2,768,2048]{2,1,0:T(8,128)(2,1)} %refs_0_, bf16[768,2048]{1,0:T(8,128)(2,1)S(1)} %copy-done), custom_call_target="tpu_custom_call" | custom-call | flops 268435456 | bytes 1048576 | tf_op jit(solution)/shard_map/pallas_call | solution.py:111
  13.2 2.7 %expert_0.1 = (bf16[128,2048]{1,0:T(8,128)(2,1)S(1)}, bf16[128,2048]{1,0:T(8,128)(2,1)S(1)}) custom-call(bf16[128,2048]{1,0:T(8,128)(2,1)S(1)} %copy-done.1, bf16[144,2048]{1,0:T(8,128)(2,1)S(1)} %maximum_maximum_fusion.refs_1_, bf16[2,768,2048]{2,1,0:T(8,128)(2,1)S(1)} %get-tuple-element.53.refs_2_.refs_1_, ...), custom_call_target="tpu_custom_call" | custom-call | flops 805306368 | bytes 3145728 | tf_op jit(solution)/shard_map/expert_0/pallas_call | solution.py:150
  16.7 2.1 %collective-permute-start.4 = (bf16[144,2048]{1,0:T(8,128)(2,1)S(1)}, bf16[144,2048]{1,0:T(8,128)(2,1)S(1)}, u32[]{:S(2)}, u32[]{:S(2)}) collective-permute-start(bf16[144,2048]{1,0:T(8,128)(2,1)S(1)} %collective-permute-done.3.refs_0_.refs_1_), channel_id=1, source_target_pairs={{0,4},{1,3},{4,8},{5,1},{8,12},{9,5},{12,14},{13,9},{14,10},{15,13... | collective-permute-start | bytes 1769480 | tf_op jit(solution)/shard_map/ring_2_1/ppermute | solution.py:250
  18.7 2.6 %expert_1_0.1 = (bf16[128,2048]{1,0:T(8,128)(2,1)S(1)}, bf16[128,2048]{1,0:T(8,128)(2,1)S(1)}) custom-call(bf16[128,2048]{1,0:T(8,128)(2,1)S(1)} %collective-permute-done.2.refs_0_, bf16[128,2048]{1,0:T(8,128)(2,1)S(1)} %collective-permute-done.6.refs_1_, bf16[2,768,2048]{2,1,0:T(8,128)(2,1)S(1)} %get-tuple-element.53.refs_2_.refs_1_, ...), custom_call_target="tpu_custom_call" | custom-call | flops 805306368 | bytes 3145728 | tf_op jit(solution)/shard_map/expert_1_0/pallas_call | solution.py:150
  22.3 2.1 %collective-permute-start.7 = (bf16[128,2048]{1,0:T(8,128)(2,1)S(1)}, bf16[128,2048]{1,0:T(8,128)(2,1)S(1)}, u32[]{:S(2)}, u32[]{:S(2)}) collective-permute-start(bf16[128,2048]{1,0:T(8,128)(2,1)S(1)} %collective-permute-done.5.refs_0_), channel_id=1, source_target_pairs={{0,4},{1,3},{4,8},{5,1},{8,12},{9,5},{12,14},{13,9},{14,10},{15,13... | collective-permute-start | bytes 1572872 | tf_op jit(solution)/shard_map/ring_3_0/ppermute | solution.py:250
  24.4 4.2 %collective-permute-done.4.refs_0_.refs_1_ = bf16[144,2048]{1,0:T(8,128)(2,1)S(1)} collective-permute-done((bf16[144,2048]{1,0:T(8,128)(2,1)S(1)}, bf16[144,2048]{1,0:T(8,128)(2,1)S(1)}, u32[]{:S(2)}, u32[]{:S(2)}) %collective-permute-start.4) | collective-permute-done | bytes 589856 | tf_op jit(solution)/shard_map/ring_2_1/ppermute | solution.py:250
  28.6 2.6 %expert_2_0.1 = (bf16[128,2048]{1,0:T(8,128)(2,1)S(1)}, bf16[128,2048]{1,0:T(8,128)(2,1)S(1)}) custom-call(bf16[128,2048]{1,0:T(8,128)(2,1)S(1)} %collective-permute-done.5.refs_0_, bf16[128,2048]{1,0:T(8,128)(2,1)S(1)} %collective-permute-done.8.refs_1_, bf16[2,768,2048]{2,1,0:T(8,128)(2,1)S(1)} %get-tuple-element.53.refs_2_.refs_1_, ...), custom_call_target="tpu_custom_call" | custom-call | flops 805306368 | bytes 3145728 | tf_op jit(solution)/shard_map/expert_2_0/pallas_call | solution.py:150
  31.3 3.0 %collective-permute-done.7.refs_0_ = bf16[128,2048]{1,0:T(8,128)(2,1)S(1)} collective-permute-done((bf16[128,2048]{1,0:T(8,128)(2,1)S(1)}, bf16[128,2048]{1,0:T(8,128)(2,1)S(1)}, u32[]{:S(2)}, u32[]{:S(2)}) %collective-permute-start.7) | collective-permute-done | bytes 524320 | tf_op jit(solution)/shard_map/ring_3_0/ppermute | solution.py:250
  34.2 2.1 %collective-permute-start.12 = (bf16[128,2048]{1,0:T(8,128)(2,1)S(1)}, bf16[128,2048]{1,0:T(8,128)(2,1)S(1)}, u32[]{:S(2)}, u32[]{:S(2)}) collective-permute-start(bf16[128,2048]{1,0:T(8,128)(2,1)S(1)} %collective-permute-done.7.refs_0_), channel_id=1, source_target_pairs={{0,4},{1,3},{4,8},{5,1},{8,12},{9,5},{12,14},{13,9},{14,10},{15,13... | collective-permute-start | bytes 1572872 | tf_op jit(solution)/shard_map/ring_4_0/ppermute | solution.py:250
  36.3 2.6 %expert_2_1.1 = (bf16[128,2048]{1,0:T(8,128)(2,1)S(1)}, bf16[128,2048]{1,0:T(8,128)(2,1)S(1)}) custom-call(bf16[144,2048]{1,0:T(8,128)(2,1)S(1)} %collective-permute-done.4.refs_0_.refs_1_, bf16[144,2048]{1,0:T(8,128)(2,1)S(1)} %collective-permute-done.9.refs_1_, bf16[2,768,2048]{2,1,0:T(8,128)(2,1)S(1)} %get-tuple-element.53.refs_2_.refs_1_, ...), custom_call_target="tpu_custom_call" | custom-call | flops 805306368 | bytes 3145728 | tf_op jit(solution)/shard_map/expert_2_1/pallas_call | solution.py:150
  40.8 2.6 %expert_3_0.1 = (bf16[128,2048]{1,0:T(8,128)(2,1)S(1)}, bf16[128,2048]{1,0:T(8,128)(2,1)S(1)}) custom-call(bf16[128,2048]{1,0:T(8,128)(2,1)S(1)} %collective-permute-done.7.refs_0_, bf16[128,2048]{1,0:T(8,128)(2,1)S(1)} %collective-permute-done.11.refs_1_, bf16[2,768,2048]{2,1,0:T(8,128)(2,1)S(1)} %get-tuple-element.53.refs_2_.refs_1_, ...), custom_call_target="tpu_custom_call" | custom-call | flops 805306368 | bytes 3145728 | tf_op jit(solution)/shard_map/expert_3_0/pallas_call | solution.py:150
  43.5 2.7 %expert_far_ring.1 = bf16[128,2048]{1,0:T(8,128)(2,1)S(1)} custom-call(bf16[128,2048]{1,0:T(8,128)(2,1)S(1)} %collective-permute-done.12.refs_0_, bf16[2,768,2048]{2,1,0:T(8,128)(2,1)S(1)} %get-tuple-element.53.refs_2_.refs_1_, bf16[768,2048]{1,0:T(8,128)(2,1)S(1)} %get-tuple-element.50.refs_3_.refs_2_), custom_call_target="tpu_custom_call" | custom-call | flops 60397976 | bytes 471859 | tf_op jit(solution)/shard_map/expert_far_ring/pallas_call | solution.py:150
  46.8 2.7 %expert_far_swapped.1 = bf16[128,2048]{1,0:T(8,128)(2,1)S(1)} custom-call(bf16[128,2048]{1,0:T(8,128)(2,1)S(1)} %collective-permute-done.13.refs_0_, bf16[2,768,2048]{2,1,0:T(8,128)(2,1)S(1)} %get-tuple-element.53.refs_2_.refs_1_, bf16[768,2048]{1,0:T(8,128)(2,1)S(1)} %get-tuple-element.50.refs_3_.refs_2_), custom_call_target="tpu_custom_call" | custom-call | flops 60397976 | bytes 471859 | tf_op jit(solution)/shard_map/expert_far_swapped/pallas_call | solution.py:150
  52.4 2.7 %expert_3_1.1 = (bf16[128,2048]{1,0:T(8,128)(2,1)S(1)}, bf16[128,2048]{1,0:T(8,128)(2,1)S(1)}) custom-call(bf16[144,2048]{1,0:T(8,128)(2,1)S(1)} %collective-permute-done.10.refs_1_.refs_0_.refs_2_, bf16[144,2048]{1,0:T(8,128)(2,1)S(1)} %collective-permute-done.16.refs_1_, bf16[2,768,2048]{2,1,0:T(8,128)(2,1)S(1)} %get-tuple-element.53.refs_2_.refs_1_, ...), custom_call_target="tpu_custom_call" | custom-call | flops 80530640 | bytes 314572 | tf_op jit(solution)/shard_map/expert_3_1/pallas_call | solution.py:150
  57.2 2.1 %collective-permute-done.18.refs_4_ = bf16[128,2048]{1,0:T(8,128)(2,1)S(1)} collective-permute-done((bf16[128,2048]{1,0:T(8,128)(2,1)S(1)}, bf16[128,2048]{1,0:T(8,128)(2,1)S(1)}, u32[]{:S(2)}, u32[]{:S(2)}) %collective-permute-start.18) | collective-permute-done | bytes 524320 | tf_op jit(solution)/shard_map/back_4_1/ppermute | solution.py:250
  60.0 2.0 %collective-permute-start.24 = (bf16[128,2048]{1,0:T(8,128)(2,1)S(1)}, bf16[128,2048]{1,0:T(8,128)(2,1)S(1)}, u32[]{:S(2)}, u32[]{:S(2)}) collective-permute-start(bf16[128,2048]{1,0:T(8,128)(2,1)S(1)} %shard_map.59), channel_id=1, source_target_pairs={{0,2},{1,5},{4,0},{5,9},{8,4},{9,13},{12,8},{13,15},{14,12},{15,11... | collective-permute-start | bytes 1572872 | tf_op jit(solution)/shard_map/back_3_1/ppermute | solution.py:250
  62.0 2.6 %expert_1_1.1 = (bf16[128,2048]{1,0:T(8,128)(2,1)S(1)}, bf16[128,2048]{1,0:T(8,128)(2,1)S(1)}) custom-call(bf16[144,2048]{1,0:T(8,128)(2,1)S(1)} %collective-permute-done.3.refs_0_.refs_1_, bf16[144,2048]{1,0:T(8,128)(2,1)S(1)} %collective-permute-done.20.refs_1_, bf16[2,768,2048]{2,1,0:T(8,128)(2,1)S(1)} %get-tuple-element.53.refs_2_.refs_1_, ...), custom_call_target="tpu_custom_call" | custom-call | flops 805306368 | bytes 3145728 | tf_op jit(solution)/shard_map/expert_1_1/pallas_call | solution.py:150
  65.3 2.0 %collective-permute-start.26 = (bf16[128,2048]{1,0:T(8,128)(2,1)S(1)}, bf16[128,2048]{1,0:T(8,128)(2,1)S(1)}, u32[]{:S(2)}, u32[]{:S(2)}) collective-permute-start(bf16[128,2048]{1,0:T(8,128)(2,1)S(1)} %shard_map.60), channel_id=1, source_target_pairs={{0,2},{1,5},{4,0},{5,9},{8,4},{9,13},{12,8},{13,15},{14,12},{15,11... | collective-permute-start | bytes 1572872 | tf_op jit(solution)/shard_map/back_2_0/ppermute | solution.py:250
  67.8 2.8 %collective-permute-done.24.refs_4_ = bf16[128,2048]{1,0:T(8,128)(2,1)S(1)} collective-permute-done((bf16[128,2048]{1,0:T(8,128)(2,1)S(1)}, bf16[128,2048]{1,0:T(8,128)(2,1)S(1)}, u32[]{:S(2)}, u32[]{:S(2)}) %collective-permute-start.24) | collective-permute-done | bytes 524320 | tf_op jit(solution)/shard_map/back_3_1/ppermute | solution.py:250
  72.9 3.3 %collective-permute-done.26.refs_4_ = bf16[128,2048]{1,0:T(8,128)(2,1)S(1)} collective-permute-done((bf16[128,2048]{1,0:T(8,128)(2,1)S(1)}, bf16[128,2048]{1,0:T(8,128)(2,1)S(1)}, u32[]{:S(2)}, u32[]{:S(2)}) %collective-permute-start.26) | collective-permute-done | bytes 524320 | tf_op jit(solution)/shard_map/back_2_0/ppermute | solution.py:250
  78.5 3.3 %collective-permute-done.29.refs_4_ = bf16[128,2048]{1,0:T(8,128)(2,1)S(1)} collective-permute-done((bf16[128,2048]{1,0:T(8,128)(2,1)S(1)}, bf16[128,2048]{1,0:T(8,128)(2,1)S(1)}, u32[]{:S(2)}, u32[]{:S(2)}) %collective-permute-start.29) | collective-permute-done | bytes 524320 | tf_op jit(solution)/shard_map/back_2_1/ppermute | solution.py:250
  83.2 4.2 %collective-permute-done.27.refs_4_ = bf16[128,2048]{1,0:T(8,128)(2,1)S(1)} collective-permute-done((bf16[128,2048]{1,0:T(8,128)(2,1)S(1)}, bf16[128,2048]{1,0:T(8,128)(2,1)S(1)}, u32[]{:S(2)}, u32[]{:S(2)}) %collective-permute-start.27) | collective-permute-done | bytes 524320 | tf_op jit(solution)/shard_map/back_1_0/ppermute | solution.py:250
  87.8 4.8 %collective-permute-done.30.arrived = bf16[128,2048]{1,0:T(8,128)(2,1)S(1)} collective-permute-done((bf16[128,2048]{1,0:T(8,128)(2,1)S(1)}, bf16[128,2048]{1,0:T(8,128)(2,1)S(1)}, u32[]{:S(2)}, u32[]{:S(2)}) %collective-permute-start.30) | collective-permute-done | bytes 524320 | tf_op jit(solution)/shard_map/back_1_1/ppermute | solution.py:250
  (69 shorter events, 25.9 us)
Async XLA Ops:
  0.5 11.0 %collective-permute-start.2 = (bf16[128,2048]{1,0:T(8,128)(2,1)}, bf16[128,2048]{1,0:T(8,128)(2,1)S(1)}, u32[]{:S(2)}, u32[]{:S(2)}) collective-permute-start(bf16[128,2048]{1,0:T(8,128)(2,1)} %refs_0_.1), channel_id=1, source_target_pairs={{0,4},{1,3},{4,8},{5,1},{8,12},{9,5},{12,14},{13,9},{14,10},{15,13... | collective-permute-start | bytes 1572872 | tf_op jit(solution)/shard_map/ring_1_0/ppermute | solution.py:250
  5.1 11.6 %collective-permute-start.3 = (bf16[144,2048]{1,0:T(8,128)(2,1)S(1)}, bf16[144,2048]{1,0:T(8,128)(2,1)S(1)}, u32[]{:S(2)}, u32[]{:S(2)}) collective-permute-start(bf16[144,2048]{1,0:T(8,128)(2,1)S(1)} %maximum_maximum_fusion.refs_1_), channel_id=1, source_target_pairs={{0,4},{1,3},{4,8},{5,1},{8,12},{9,5},{12,14},{13,9},{14,10},{15,13... | collective-permute-start | bytes 1769480 | tf_op jit(solution)/shard_map/ring_1_1/ppermute | solution.py:250
  11.5 7.3 %collective-permute-start.6 = (bf16[128,2048]{1,0:T(8,128)(2,1)S(1)}, bf16[128,2048]{1,0:T(8,128)(2,1)S(1)}, u32[]{:S(2)}, u32[]{:S(2)}) collective-permute-start(bf16[128,2048]{1,0:T(8,128)(2,1)S(1)} %collective-permute-done.2.refs_0_), channel_id=1, source_target_pairs={{0,1},{1,0},{4,5},{5,4},{8,9},{9,8},{12,13},{13,12},{14,15},{15,14... | collective-permute-start | bytes 1572872 | tf_op jit(solution)/shard_map/swap_1_0/ppermute | solution.py:250
  11.5 10.7 %collective-permute-start.5 = (bf16[128,2048]{1,0:T(8,128)(2,1)S(1)}, bf16[128,2048]{1,0:T(8,128)(2,1)S(1)}, u32[]{:S(2)}, u32[]{:S(2)}) collective-permute-start(bf16[128,2048]{1,0:T(8,128)(2,1)S(1)} %collective-permute-done.2.refs_0_), channel_id=1, source_target_pairs={{0,4},{1,3},{4,8},{5,1},{8,12},{9,5},{12,14},{13,9},{14,10},{15,13... | collective-permute-start | bytes 1572872 | tf_op jit(solution)/shard_map/ring_2_0/ppermute | solution.py:250
  16.7 11.9 %collective-permute-start.4 = (bf16[144,2048]{1,0:T(8,128)(2,1)S(1)}, bf16[144,2048]{1,0:T(8,128)(2,1)S(1)}, u32[]{:S(2)}, u32[]{:S(2)}) collective-permute-start(bf16[144,2048]{1,0:T(8,128)(2,1)S(1)} %collective-permute-done.3.refs_0_.refs_1_), channel_id=1, source_target_pairs={{0,4},{1,3},{4,8},{5,1},{8,12},{9,5},{12,14},{13,9},{14,10},{15,13... | collective-permute-start | bytes 1769480 | tf_op jit(solution)/shard_map/ring_2_1/ppermute | solution.py:250
  22.3 6.3 %collective-permute-start.8 = (bf16[128,2048]{1,0:T(8,128)(2,1)S(1)}, bf16[128,2048]{1,0:T(8,128)(2,1)S(1)}, u32[]{:S(2)}, u32[]{:S(2)}) collective-permute-start(bf16[128,2048]{1,0:T(8,128)(2,1)S(1)} %collective-permute-done.5.refs_0_), channel_id=1, source_target_pairs={{0,1},{1,0},{4,5},{5,4},{8,9},{9,8},{12,13},{13,12},{14,15},{15,14... | collective-permute-start | bytes 1572872 | tf_op jit(solution)/shard_map/swap_2_0/ppermute | solution.py:250
  22.3 11.9 %collective-permute-start.7 = (bf16[128,2048]{1,0:T(8,128)(2,1)S(1)}, bf16[128,2048]{1,0:T(8,128)(2,1)S(1)}, u32[]{:S(2)}, u32[]{:S(2)}) collective-permute-start(bf16[128,2048]{1,0:T(8,128)(2,1)S(1)} %collective-permute-done.5.refs_0_), channel_id=1, source_target_pairs={{0,4},{1,3},{4,8},{5,1},{8,12},{9,5},{12,14},{13,9},{14,10},{15,13... | collective-permute-start | bytes 1572872 | tf_op jit(solution)/shard_map/ring_3_0/ppermute | solution.py:250
  28.6 7.7 %collective-permute-start.9 = (bf16[144,2048]{1,0:T(8,128)(2,1)S(1)}, bf16[144,2048]{1,0:T(8,128)(2,1)S(1)}, u32[]{:S(2)}, u32[]{:S(2)}) collective-permute-start(bf16[144,2048]{1,0:T(8,128)(2,1)S(1)} %collective-permute-done.4.refs_0_.refs_1_), channel_id=1, source_target_pairs={{0,1},{1,0},{4,5},{5,4},{8,9},{9,8},{12,13},{13,12},{14,15},{15,14... | collective-permute-start | bytes 1769480 | tf_op jit(solution)/shard_map/swap_2_1/ppermute | solution.py:250
  34.2 6.6 %collective-permute-start.11 = (bf16[128,2048]{1,0:T(8,128)(2,1)S(1)}, bf16[128,2048]{1,0:T(8,128)(2,1)S(1)}, u32[]{:S(2)}, u32[]{:S(2)}) collective-permute-start(bf16[128,2048]{1,0:T(8,128)(2,1)S(1)} %collective-permute-done.7.refs_0_), channel_id=1, source_target_pairs={{0,1},{1,0},{4,5},{5,4},{8,9},{9,8},{12,13},{13,12},{14,15},{15,14... | collective-permute-start | bytes 1572872 | tf_op jit(solution)/shard_map/swap_3_0/ppermute | solution.py:250
  34.2 9.2 %collective-permute-start.12 = (bf16[128,2048]{1,0:T(8,128)(2,1)S(1)}, bf16[128,2048]{1,0:T(8,128)(2,1)S(1)}, u32[]{:S(2)}, u32[]{:S(2)}) collective-permute-start(bf16[128,2048]{1,0:T(8,128)(2,1)S(1)} %collective-permute-done.7.refs_0_), channel_id=1, source_target_pairs={{0,4},{1,3},{4,8},{5,1},{8,12},{9,5},{12,14},{13,9},{14,10},{15,13... | collective-permute-start | bytes 1572872 | tf_op jit(solution)/shard_map/ring_4_0/ppermute | solution.py:250
  39.0 10.8 %collective-permute-start.10 = (bf16[144,2048]{1,0:T(8,128)(2,1)S(1)}, bf16[144,2048]{1,0:T(8,128)(2,1)S(1)}, u32[]{:S(2)}, u32[]{:S(2)}) collective-permute-start(bf16[144,2048]{1,0:T(8,128)(2,1)S(1)} %collective-permute-done.4.refs_0_.refs_1_), channel_id=1, source_target_pairs={{0,4},{1,3},{4,8},{5,1},{8,12},{9,5},{12,14},{13,9},{14,10},{15,13... | collective-permute-start | bytes 1769480 | tf_op jit(solution)/shard_map/ring_3_1/ppermute | solution.py:250
  46.8 5.4 %collective-permute-start.15 = (bf16[128,2048]{1,0:T(8,128)(2,1)S(1)}, bf16[128,2048]{1,0:T(8,128)(2,1)S(1)}, u32[]{:S(2)}, u32[]{:S(2)}) collective-permute-start(bf16[128,2048]{1,0:T(8,128)(2,1)S(1)} %get-tuple-element.71), channel_id=1, source_target_pairs={{0,1},{1,0},{4,5},{5,4},{8,9},{9,8},{12,13},{13,12},{14,15},{15,14... | collective-permute-start | bytes 1572872 | tf_op jit(solution)/shard_map/give_3_0/ppermute | solution.py:250
  50.1 9.2 %collective-permute-start.18 = (bf16[128,2048]{1,0:T(8,128)(2,1)S(1)}, bf16[128,2048]{1,0:T(8,128)(2,1)S(1)}, u32[]{:S(2)}, u32[]{:S(2)}) collective-permute-start(bf16[128,2048]{1,0:T(8,128)(2,1)S(1)} %add_convert_fusion), channel_id=1, source_target_pairs={{0,2},{1,5},{4,0},{5,9},{8,4},{9,13},{12,8},{13,15},{14,12},{15,11... | collective-permute-start | bytes 1572872 | tf_op jit(solution)/shard_map/back_4_1/ppermute | solution.py:250
  55.2 9.8 %collective-permute-start.22 = (bf16[128,2048]{1,0:T(8,128)(2,1)S(1)}, bf16[128,2048]{1,0:T(8,128)(2,1)S(1)}, u32[]{:S(2)}, u32[]{:S(2)}) collective-permute-start(bf16[128,2048]{1,0:T(8,128)(2,1)S(1)} %shard_map.57), channel_id=1, source_target_pairs={{0,2},{1,5},{4,0},{5,9},{8,4},{9,13},{12,8},{13,15},{14,12},{15,11... | collective-permute-start | bytes 1572872 | tf_op jit(solution)/shard_map/back_3_0/ppermute | solution.py:250
  56.7 8.3 %collective-permute-start.21 = (bf16[128,2048]{1,0:T(8,128)(2,1)S(1)}, bf16[128,2048]{1,0:T(8,128)(2,1)S(1)}, u32[]{:S(2)}, u32[]{:S(2)}) collective-permute-start(bf16[128,2048]{1,0:T(8,128)(2,1)S(1)} %get-tuple-element.84), channel_id=1, source_target_pairs={{0,1},{1,0},{4,5},{5,4},{8,9},{9,8},{12,13},{13,12},{14,15},{15,14... | collective-permute-start | bytes 1572872 | tf_op jit(solution)/shard_map/give_2_0/ppermute | solution.py:250
  56.8 11.0 %collective-permute-start.23 = (bf16[128,2048]{1,0:T(8,128)(2,1)S(1)}, bf16[128,2048]{1,0:T(8,128)(2,1)S(1)}, u32[]{:S(2)}, u32[]{:S(2)}) collective-permute-start(bf16[128,2048]{1,0:T(8,128)(2,1)S(1)} %get-tuple-element.87), channel_id=1, source_target_pairs={{0,1},{1,0},{4,5},{5,4},{8,9},{9,8},{12,13},{13,12},{14,15},{15,14... | collective-permute-start | bytes 1572872 | tf_op jit(solution)/shard_map/give_2_1/ppermute | solution.py:250
  60.0 10.6 %collective-permute-start.24 = (bf16[128,2048]{1,0:T(8,128)(2,1)S(1)}, bf16[128,2048]{1,0:T(8,128)(2,1)S(1)}, u32[]{:S(2)}, u32[]{:S(2)}) collective-permute-start(bf16[128,2048]{1,0:T(8,128)(2,1)S(1)} %shard_map.59), channel_id=1, source_target_pairs={{0,2},{1,5},{4,0},{5,9},{8,4},{9,13},{12,8},{13,15},{14,12},{15,11... | collective-permute-start | bytes 1572872 | tf_op jit(solution)/shard_map/back_3_1/ppermute | solution.py:250
  65.3 10.9 %collective-permute-start.26 = (bf16[128,2048]{1,0:T(8,128)(2,1)S(1)}, bf16[128,2048]{1,0:T(8,128)(2,1)S(1)}, u32[]{:S(2)}, u32[]{:S(2)}) collective-permute-start(bf16[128,2048]{1,0:T(8,128)(2,1)S(1)} %shard_map.60), channel_id=1, source_target_pairs={{0,2},{1,5},{4,0},{5,9},{8,4},{9,13},{12,8},{13,15},{14,12},{15,11... | collective-permute-start | bytes 1572872 | tf_op jit(solution)/shard_map/back_2_0/ppermute | solution.py:250
  67.3 5.6 %collective-permute-start.25 = (bf16[128,2048]{1,0:T(8,128)(2,1)S(1)}, bf16[128,2048]{1,0:T(8,128)(2,1)S(1)}, u32[]{:S(2)}, u32[]{:S(2)}) collective-permute-start(bf16[128,2048]{1,0:T(8,128)(2,1)S(1)} %get-tuple-element.90), channel_id=1, source_target_pairs={{0,1},{1,0},{4,5},{5,4},{8,9},{9,8},{12,13},{13,12},{14,15},{15,14... | collective-permute-start | bytes 1572872 | tf_op jit(solution)/shard_map/give_1_0/ppermute | solution.py:250
  67.3 11.2 %collective-permute-start.28 = (bf16[128,2048]{1,0:T(8,128)(2,1)S(1)}, bf16[128,2048]{1,0:T(8,128)(2,1)S(1)}, u32[]{:S(2)}, u32[]{:S(2)}) collective-permute-start(bf16[128,2048]{1,0:T(8,128)(2,1)S(1)} %get-tuple-element.92), channel_id=1, source_target_pairs={{0,1},{1,0},{4,5},{5,4},{8,9},{9,8},{12,13},{13,12},{14,15},{15,14... | collective-permute-start | bytes 1572872 | tf_op jit(solution)/shard_map/give_1_1/ppermute | solution.py:250
  70.9 10.9 %collective-permute-start.29 = (bf16[128,2048]{1,0:T(8,128)(2,1)S(1)}, bf16[128,2048]{1,0:T(8,128)(2,1)S(1)}, u32[]{:S(2)}, u32[]{:S(2)}) collective-permute-start(bf16[128,2048]{1,0:T(8,128)(2,1)S(1)} %shard_map.61), channel_id=1, source_target_pairs={{0,2},{1,5},{4,0},{5,9},{8,4},{9,13},{12,8},{13,15},{14,12},{15,11... | collective-permute-start | bytes 1572872 | tf_op jit(solution)/shard_map/back_2_1/ppermute | solution.py:250
  72.9 10.3 %collective-permute-start.19 = (bf16[128,2048]{1,0:T(8,128)(2,1)S(1)}, bf16[128,2048]{1,0:T(8,128)(2,1)S(1)}, u32[]{:S(2)}, u32[]{:S(2)}) collective-permute-start(bf16[128,2048]{1,0:T(8,128)(2,1)S(1)} %get-tuple-element.78), channel_id=1, source_target_pairs={{0,1},{1,0},{4,5},{5,4},{8,9},{9,8},{12,13},{13,12},{14,15},{15,14... | collective-permute-start | bytes 1572872 | tf_op jit(solution)/shard_map/give_0_0/ppermute | solution.py:250
  76.6 10.9 %collective-permute-start.27 = (bf16[128,2048]{1,0:T(8,128)(2,1)S(1)}, bf16[128,2048]{1,0:T(8,128)(2,1)S(1)}, u32[]{:S(2)}, u32[]{:S(2)}) collective-permute-start(bf16[128,2048]{1,0:T(8,128)(2,1)S(1)} %shard_map.62), channel_id=1, source_target_pairs={{0,2},{1,5},{4,0},{5,9},{8,4},{9,13},{12,8},{13,15},{14,12},{15,11... | collective-permute-start | bytes 1572872 | tf_op jit(solution)/shard_map/back_1_0/ppermute | solution.py:250
  82.2 10.4 %collective-permute-start.30 = (bf16[128,2048]{1,0:T(8,128)(2,1)S(1)}, bf16[128,2048]{1,0:T(8,128)(2,1)S(1)}, u32[]{:S(2)}, u32[]{:S(2)}) collective-permute-start(bf16[128,2048]{1,0:T(8,128)(2,1)S(1)} %shard_map.64), channel_id=1, source_target_pairs={{0,3},{1,4},{4,1},{5,8},{8,5},{9,12},{12,9},{13,14},{14,13},{15,10... | collective-permute-start | bytes 1572872 | tf_op jit(solution)/shard_map/back_1_1/ppermute | solution.py:250
  (9 other events, 29.8 us)

commit v20 on v19

--- a/solution.py
+++ b/solution.py
@@ -62,7 +62,8 @@
     else:
         (gate_up_ref, down_ref), outs, (rows, hidden) = refs[:2], refs[2:-2], refs[-2:]
     units, width = down_ref.shape
-    tile = 256 if units % 256 == 0 else units
+    small = len(heights) == 1
+    tile = 256 if units % 256 == 0 and not small else units
     tiles = units // tile
     copies = []
     if load:
@@ -75,11 +76,12 @@
 
     at = 0
     for block, height in zip(blocks, heights):
-        rows[at : at + height, :] = block[:height, :]
+        if not small:
+            rows[at : at + height, :] = block[:height, :]
         at += height
 
     contract = (((1,), (1,)), ((), ()))
-    taken = rows[...]
+    taken = blocks[0][...] if small else rows[...]
     for t in range(tiles):
         if load:
             copies[t].wait()
@@ -91,7 +93,7 @@
         copies[tiles].wait()
     inner = hidden[...]
     share = outs[0].shape[0]
-    tile = 512 if width % 512 == 0 else width
+    tile = 512 if width % 512 == 0 and not small else width
     for low in range(0, width, tile):
         product = jnp.dot(inner, down_ref[:, low : low + tile], preferred_element_type=jnp.float32)
         product = product.astype(jnp.bfloat16)

time: 93.8 us -> 93.8 us (level)
  no operation moved by 1% of the time
where the time goes in v20:
time: 93.8 us; the launch traced here: 93.6 us
  waiting for transfers between devices  31.2 us (33%)
  Pallas kernels  30 us (32%)
  starting transfers between devices  29.3 us (31%)
  local copies, waits for them, and re-layouts  1.9 us (2%)
    ppermute x31, waiting for transfers between devices, send(): return lax.ppermute(value, 'blk', pairs)  31.2 us
    ppermute x31, starting transfers between devices, send(): return lax.ppermute(value, 'blk', pairs)  29.3 us
    pallas_call x9, Pallas kernels, half_expert(): pl.pallas_call(functools.partial(half_expert_kernel, tuple(heights), load...  23.9 us
    pallas_call x1, Pallas kernels, loaded(): pl.pallas_call(load_kernel, out_shape=[jax.ShapeDtypeStruct(array.shape,...  2.86 us
    pallas_call x8, Pallas kernels, weighted(): pl.pallas_call(functools.partial(weighted_kernel, kind, len(own), len(dis...  2.35 us
    unnamed x4, local copies, waits for them, and re-layouts  1.89 us
  transfers between devices with their start and end apart: 31, of which 13 were waited for; matrix products, arithmetic and copies ran while one was open for 1% of the time, Pallas kernels for 31%

profile of v20, /device:TPU:0, one launch (start us, length us, event | category | flops | bytes accessed | tf_op | source)
XLA Modules:
  0.0 93.6 jit_solution(8594059099330665245)
XLA Ops:
  0.5 2.6 %collective-permute-start.2 = (bf16[128,2048]{1,0:T(8,128)(2,1)}, bf16[128,2048]{1,0:T(8,128)(2,1)S(1)}, u32[]{:S(2)}, u32[]{:S(2)}) collective-permute-start(bf16[128,2048]{1,0:T(8,128)(2,1)} %refs_0_.1), channel_id=1, source_target_pairs={{0,4},{1,3},{4,8},{5,1},{8,12},{9,5},{12,14},{13,9},{14,10},{15,13... | collective-permute-start | bytes 1572872 | tf_op jit(solution)/shard_map/ring_1_0/ppermute | solution.py:252
  8.6 2.9 %shard_map.56 = (bf16[2,768,2048]{2,1,0:T(8,128)(2,1)S(1)}, bf16[768,2048]{1,0:T(8,128)(2,1)S(1)}) custom-call(bf16[2,768,2048]{2,1,0:T(8,128)(2,1)} %refs_0_, bf16[768,2048]{1,0:T(8,128)(2,1)S(1)} %copy-done), custom_call_target="tpu_custom_call" | custom-call | flops 268435456 | bytes 1048576 | tf_op jit(solution)/shard_map/pallas_call | solution.py:113
  13.2 2.7 %expert_0.1 = (bf16[128,2048]{1,0:T(8,128)(2,1)S(1)}, bf16[128,2048]{1,0:T(8,128)(2,1)S(1)}) custom-call(bf16[128,2048]{1,0:T(8,128)(2,1)S(1)} %copy-done.1, bf16[144,2048]{1,0:T(8,128)(2,1)S(1)} %maximum_maximum_fusion.refs_1_, bf16[2,768,2048]{2,1,0:T(8,128)(2,1)S(1)} %get-tuple-element.53.refs_2_.refs_1_, ...), custom_call_target="tpu_custom_call" | custom-call | flops 805306368 | bytes 3145728 | tf_op jit(solution)/shard_map/expert_0/pallas_call | solution.py:152
  16.7 2.1 %collective-permute-start.4 = (bf16[144,2048]{1,0:T(8,128)(2,1)S(1)}, bf16[144,2048]{1,0:T(8,128)(2,1)S(1)}, u32[]{:S(2)}, u32[]{:S(2)}) collective-permute-start(bf16[144,2048]{1,0:T(8,128)(2,1)S(1)} %collective-permute-done.3.refs_0_.refs_1_), channel_id=1, source_target_pairs={{0,4},{1,3},{4,8},{5,1},{8,12},{9,5},{12,14},{13,9},{14,10},{15,13... | collective-permute-start | bytes 1769480 | tf_op jit(solution)/shard_map/ring_2_1/ppermute | solution.py:252
  18.7 2.6 %expert_1_0.1 = (bf16[128,2048]{1,0:T(8,128)(2,1)S(1)}, bf16[128,2048]{1,0:T(8,128)(2,1)S(1)}) custom-call(bf16[128,2048]{1,0:T(8,128)(2,1)S(1)} %collective-permute-done.2.refs_0_, bf16[128,2048]{1,0:T(8,128)(2,1)S(1)} %collective-permute-done.6.refs_1_, bf16[2,768,2048]{2,1,0:T(8,128)(2,1)S(1)} %get-tuple-element.53.refs_2_.refs_1_, ...), custom_call_target="tpu_custom_call" | custom-call | flops 805306368 | bytes 3145728 | tf_op jit(solution)/shard_map/expert_1_0/pallas_call | solution.py:152
  22.3 2.1 %collective-permute-start.7 = (bf16[128,2048]{1,0:T(8,128)(2,1)S(1)}, bf16[128,2048]{1,0:T(8,128)(2,1)S(1)}, u32[]{:S(2)}, u32[]{:S(2)}) collective-permute-start(bf16[128,2048]{1,0:T(8,128)(2,1)S(1)} %collective-permute-done.5.refs_0_), channel_id=1, source_target_pairs={{0,4},{1,3},{4,8},{5,1},{8,12},{9,5},{12,14},{13,9},{14,10},{15,13... | collective-permute-start | bytes 1572872 | tf_op jit(solution)/shard_map/ring_3_0/ppermute | solution.py:252
  24.4 4.2 %collective-permute-done.4.refs_0_.refs_1_ = bf16[144,2048]{1,0:T(8,128)(2,1)S(1)} collective-permute-done((bf16[144,2048]{1,0:T(8,128)(2,1)S(1)}, bf16[144,2048]{1,0:T(8,128)(2,1)S(1)}, u32[]{:S(2)}, u32[]{:S(2)}) %collective-permute-start.4) | collective-permute-done | bytes 589856 | tf_op jit(solution)/shard_map/ring_2_1/ppermute | solution.py:252
  28.6 2.6 %expert_2_0.1 = (bf16[128,2048]{1,0:T(8,128)(2,1)S(1)}, bf16[128,2048]{1,0:T(8,128)(2,1)S(1)}) custom-call(bf16[128,2048]{1,0:T(8,128)(2,1)S(1)} %collective-permute-done.5.refs_0_, bf16[128,2048]{1,0:T(8,128)(2,1)S(1)} %collective-permute-done.8.refs_1_, bf16[2,768,2048]{2,1,0:T(8,128)(2,1)S(1)} %get-tuple-element.53.refs_2_.refs_1_, ...), custom_call_target="tpu_custom_call" | custom-call | flops 805306368 | bytes 3145728 | tf_op jit(solution)/shard_map/expert_2_0/pallas_call | solution.py:152
  31.3 3.0 %collective-permute-done.7.refs_0_ = bf16[128,2048]{1,0:T(8,128)(2,1)S(1)} collective-permute-done((bf16[128,2048]{1,0:T(8,128)(2,1)S(1)}, bf16[128,2048]{1,0:T(8,128)(2,1)S(1)}, u32[]{:S(2)}, u32[]{:S(2)}) %collective-permute-start.7) | collective-permute-done | bytes 524320 | tf_op jit(solution)/shard_map/ring_3_0/ppermute | solution.py:252
  34.2 2.1 %collective-permute-start.12 = (bf16[128,2048]{1,0:T(8,128)(2,1)S(1)}, bf16[128,2048]{1,0:T(8,128)(2,1)S(1)}, u32[]{:S(2)}, u32[]{:S(2)}) collective-permute-start(bf16[128,2048]{1,0:T(8,128)(2,1)S(1)} %collective-permute-done.7.refs_0_), channel_id=1, source_target_pairs={{0,4},{1,3},{4,8},{5,1},{8,12},{9,5},{12,14},{13,9},{14,10},{15,13... | collective-permute-start | bytes 1572872 | tf_op jit(solution)/shard_map/ring_4_0/ppermute | solution.py:252
  36.3 2.6 %expert_2_1.1 = (bf16[128,2048]{1,0:T(8,128)(2,1)S(1)}, bf16[128,2048]{1,0:T(8,128)(2,1)S(1)}) custom-call(bf16[144,2048]{1,0:T(8,128)(2,1)S(1)} %collective-permute-done.4.refs_0_.refs_1_, bf16[144,2048]{1,0:T(8,128)(2,1)S(1)} %collective-permute-done.9.refs_1_, bf16[2,768,2048]{2,1,0:T(8,128)(2,1)S(1)} %get-tuple-element.53.refs_2_.refs_1_, ...), custom_call_target="tpu_custom_call" | custom-call | flops 805306368 | bytes 3145728 | tf_op jit(solution)/shard_map/expert_2_1/pallas_call | solution.py:152
  40.8 2.6 %expert_3_0.1 = (bf16[128,2048]{1,0:T(8,128)(2,1)S(1)}, bf16[128,2048]{1,0:T(8,128)(2,1)S(1)}) custom-call(bf16[128,2048]{1,0:T(8,128)(2,1)S(1)} %collective-permute-done.7.refs_0_, bf16[128,2048]{1,0:T(8,128)(2,1)S(1)} %collective-permute-done.11.refs_1_, bf16[2,768,2048]{2,1,0:T(8,128)(2,1)S(1)} %get-tuple-element.53.refs_2_.refs_1_, ...), custom_call_target="tpu_custom_call" | custom-call | flops 805306368 | bytes 3145728 | tf_op jit(solution)/shard_map/expert_3_0/pallas_call | solution.py:152
  43.5 2.7 %expert_far_ring.1 = bf16[128,2048]{1,0:T(8,128)(2,1)S(1)} custom-call(bf16[128,2048]{1,0:T(8,128)(2,1)S(1)} %collective-permute-done.12.refs_0_, bf16[2,768,2048]{2,1,0:T(8,128)(2,1)S(1)} %get-tuple-element.53.refs_2_.refs_1_, bf16[768,2048]{1,0:T(8,128)(2,1)S(1)} %get-tuple-element.50.refs_3_.refs_2_), custom_call_target="tpu_custom_call" | custom-call | flops 60397976 | bytes 471859 | tf_op jit(solution)/shard_map/expert_far_ring/pallas_call | solution.py:152
  46.8 2.7 %expert_far_swapped.1 = bf16[128,2048]{1,0:T(8,128)(2,1)S(1)} custom-call(bf16[128,2048]{1,0:T(8,128)(2,1)S(1)} %collective-permute-done.13.refs_0_, bf16[2,768,2048]{2,1,0:T(8,128)(2,1)S(1)} %get-tuple-element.53.refs_2_.refs_1_, bf16[768,2048]{1,0:T(8,128)(2,1)S(1)} %get-tuple-element.50.refs_3_.refs_2_), custom_call_target="tpu_custom_call" | custom-call | flops 60397976 | bytes 471859 | tf_op jit(solution)/shard_map/expert_far_swapped/pallas_call | solution.py:152
  50.2 2.0 %collective-permute-start.18 = (bf16[128,2048]{1,0:T(8,128)(2,1)S(1)}, bf16[128,2048]{1,0:T(8,128)(2,1)S(1)}, u32[]{:S(2)}, u32[]{:S(2)}) collective-permute-start(bf16[128,2048]{1,0:T(8,128)(2,1)S(1)} %add_convert_fusion), channel_id=1, source_target_pairs={{0,2},{1,5},{4,0},{5,9},{8,4},{9,13},{12,8},{13,15},{14,12},{15,11... | collective-permute-start | bytes 1572872 | tf_op jit(solution)/shard_map/back_4_1/ppermute | solution.py:252
  52.4 2.6 %expert_3_1.1 = (bf16[128,2048]{1,0:T(8,128)(2,1)S(1)}, bf16[128,2048]{1,0:T(8,128)(2,1)S(1)}) custom-call(bf16[144,2048]{1,0:T(8,128)(2,1)S(1)} %collective-permute-done.10.refs_1_.refs_0_.refs_2_, bf16[144,2048]{1,0:T(8,128)(2,1)S(1)} %collective-permute-done.16.refs_1_, bf16[2,768,2048]{2,1,0:T(8,128)(2,1)S(1)} %get-tuple-element.53.refs_2_.refs_1_, ...), custom_call_target="tpu_custom_call" | custom-call | flops 80530640 | bytes 314572 | tf_op jit(solution)/shard_map/expert_3_1/pallas_call | solution.py:152
  57.3 2.1 %collective-permute-done.18.refs_4_ = bf16[128,2048]{1,0:T(8,128)(2,1)S(1)} collective-permute-done((bf16[128,2048]{1,0:T(8,128)(2,1)S(1)}, bf16[128,2048]{1,0:T(8,128)(2,1)S(1)}, u32[]{:S(2)}, u32[]{:S(2)}) %collective-permute-start.18) | collective-permute-done | bytes 524320 | tf_op jit(solution)/shard_map/back_4_1/ppermute | solution.py:252
  60.0 2.0 %collective-permute-start.24 = (bf16[128,2048]{1,0:T(8,128)(2,1)S(1)}, bf16[128,2048]{1,0:T(8,128)(2,1)S(1)}, u32[]{:S(2)}, u32[]{:S(2)}) collective-permute-start(bf16[128,2048]{1,0:T(8,128)(2,1)S(1)} %shard_map.59), channel_id=1, source_target_pairs={{0,2},{1,5},{4,0},{5,9},{8,4},{9,13},{12,8},{13,15},{14,12},{15,11... | collective-permute-start | bytes 1572872 | tf_op jit(solution)/shard_map/back_3_1/ppermute | solution.py:252
  62.0 2.6 %expert_1_1.1 = (bf16[128,2048]{1,0:T(8,128)(2,1)S(1)}, bf16[128,2048]{1,0:T(8,128)(2,1)S(1)}) custom-call(bf16[144,2048]{1,0:T(8,128)(2,1)S(1)} %collective-permute-done.3.refs_0_.refs_1_, bf16[144,2048]{1,0:T(8,128)(2,1)S(1)} %collective-permute-done.20.refs_1_, bf16[2,768,2048]{2,1,0:T(8,128)(2,1)S(1)} %get-tuple-element.53.refs_2_.refs_1_, ...), custom_call_target="tpu_custom_call" | custom-call | flops 805306368 | bytes 3145728 | tf_op jit(solution)/shard_map/expert_1_1/pallas_call | solution.py:152
  67.8 2.8 %collective-permute-done.24.refs_4_ = bf16[128,2048]{1,0:T(8,128)(2,1)S(1)} collective-permute-done((bf16[128,2048]{1,0:T(8,128)(2,1)S(1)}, bf16[128,2048]{1,0:T(8,128)(2,1)S(1)}, u32[]{:S(2)}, u32[]{:S(2)}) %collective-permute-start.24) | collective-permute-done | bytes 524320 | tf_op jit(solution)/shard_map/back_3_1/ppermute | solution.py:252
  72.9 3.3 %collective-permute-done.26.refs_4_ = bf16[128,2048]{1,0:T(8,128)(2,1)S(1)} collective-permute-done((bf16[128,2048]{1,0:T(8,128)(2,1)S(1)}, bf16[128,2048]{1,0:T(8,128)(2,1)S(1)}, u32[]{:S(2)}, u32[]{:S(2)}) %collective-permute-start.26) | collective-permute-done | bytes 524320 | tf_op jit(solution)/shard_map/back_2_0/ppermute | solution.py:252
  78.5 3.3 %collective-permute-done.29.refs_4_ = bf16[128,2048]{1,0:T(8,128)(2,1)S(1)} collective-permute-done((bf16[128,2048]{1,0:T(8,128)(2,1)S(1)}, bf16[128,2048]{1,0:T(8,128)(2,1)S(1)}, u32[]{:S(2)}, u32[]{:S(2)}) %collective-permute-start.29) | collective-permute-done | bytes 524320 | tf_op jit(solution)/shard_map/back_2_1/ppermute | solution.py:252
  83.2 4.3 %collective-permute-done.27.refs_4_ = bf16[128,2048]{1,0:T(8,128)(2,1)S(1)} collective-permute-done((bf16[128,2048]{1,0:T(8,128)(2,1)S(1)}, bf16[128,2048]{1,0:T(8,128)(2,1)S(1)}, u32[]{:S(2)}, u32[]{:S(2)}) %collective-permute-start.27) | collective-permute-done | bytes 524320 | tf_op jit(solution)/shard_map/back_1_0/ppermute | solution.py:252
  87.8 4.8 %collective-permute-done.30.arrived = bf16[128,2048]{1,0:T(8,128)(2,1)S(1)} collective-permute-done((bf16[128,2048]{1,0:T(8,128)(2,1)S(1)}, bf16[128,2048]{1,0:T(8,128)(2,1)S(1)}, u32[]{:S(2)}, u32[]{:S(2)}) %collective-permute-start.30) | collective-permute-done | bytes 524320 | tf_op jit(solution)/shard_map/back_1_1/ppermute | solution.py:252
  (69 shorter events, 25.8 us)
Async XLA Ops:
  0.5 11.0 %collective-permute-start.2 = (bf16[128,2048]{1,0:T(8,128)(2,1)}, bf16[128,2048]{1,0:T(8,128)(2,1)S(1)}, u32[]{:S(2)}, u32[]{:S(2)}) collective-permute-start(bf16[128,2048]{1,0:T(8,128)(2,1)} %refs_0_.1), channel_id=1, source_target_pairs={{0,4},{1,3},{4,8},{5,1},{8,12},{9,5},{12,14},{13,9},{14,10},{15,13... | collective-permute-start | bytes 1572872 | tf_op jit(solution)/shard_map/ring_1_0/ppermute | solution.py:252
  5.1 11.6 %collective-permute-start.3 = (bf16[144,2048]{1,0:T(8,128)(2,1)S(1)}, bf16[144,2048]{1,0:T(8,128)(2,1)S(1)}, u32[]{:S(2)}, u32[]{:S(2)}) collective-permute-start(bf16[144,2048]{1,0:T(8,128)(2,1)S(1)} %maximum_maximum_fusion.refs_1_), channel_id=1, source_target_pairs={{0,4},{1,3},{4,8},{5,1},{8,12},{9,5},{12,14},{13,9},{14,10},{15,13... | collective-permute-start | bytes 1769480 | tf_op jit(solution)/shard_map/ring_1_1/ppermute | solution.py:252
  11.5 7.3 %collective-permute-start.6 = (bf16[128,2048]{1,0:T(8,128)(2,1)S(1)}, bf16[128,2048]{1,0:T(8,128)(2,1)S(1)}, u32[]{:S(2)}, u32[]{:S(2)}) collective-permute-start(bf16[128,2048]{1,0:T(8,128)(2,1)S(1)} %collective-permute-done.2.refs_0_), channel_id=1, source_target_pairs={{0,1},{1,0},{4,5},{5,4},{8,9},{9,8},{12,13},{13,12},{14,15},{15,14... | collective-permute-start | bytes 1572872 | tf_op jit(solution)/shard_map/swap_1_0/ppermute | solution.py:252
  11.5 10.7 %collective-permute-start.5 = (bf16[128,2048]{1,0:T(8,128)(2,1)S(1)}, bf16[128,2048]{1,0:T(8,128)(2,1)S(1)}, u32[]{:S(2)}, u32[]{:S(2)}) collective-permute-start(bf16[128,2048]{1,0:T(8,128)(2,1)S(1)} %collective-permute-done.2.refs_0_), channel_id=1, source_target_pairs={{0,4},{1,3},{4,8},{5,1},{8,12},{9,5},{12,14},{13,9},{14,10},{15,13... | collective-permute-start | bytes 1572872 | tf_op jit(solution)/shard_map/ring_2_0/ppermute | solution.py:252
  16.7 11.9 %collective-permute-start.4 = (bf16[144,2048]{1,0:T(8,128)(2,1)S(1)}, bf16[144,2048]{1,0:T(8,128)(2,1)S(1)}, u32[]{:S(2)}, u32[]{:S(2)}) collective-permute-start(bf16[144,2048]{1,0:T(8,128)(2,1)S(1)} %collective-permute-done.3.refs_0_.refs_1_), channel_id=1, source_target_pairs={{0,4},{1,3},{4,8},{5,1},{8,12},{9,5},{12,14},{13,9},{14,10},{15,13... | collective-permute-start | bytes 1769480 | tf_op jit(solution)/shard_map/ring_2_1/ppermute | solution.py:252
  22.3 6.3 %collective-permute-start.8 = (bf16[128,2048]{1,0:T(8,128)(2,1)S(1)}, bf16[128,2048]{1,0:T(8,128)(2,1)S(1)}, u32[]{:S(2)}, u32[]{:S(2)}) collective-permute-start(bf16[128,2048]{1,0:T(8,128)(2,1)S(1)} %collective-permute-done.5.refs_0_), channel_id=1, source_target_pairs={{0,1},{1,0},{4,5},{5,4},{8,9},{9,8},{12,13},{13,12},{14,15},{15,14... | collective-permute-start | bytes 1572872 | tf_op jit(solution)/shard_map/swap_2_0/ppermute | solution.py:252
  22.3 11.9 %collective-permute-start.7 = (bf16[128,2048]{1,0:T(8,128)(2,1)S(1)}, bf16[128,2048]{1,0:T(8,128)(2,1)S(1)}, u32[]{:S(2)}, u32[]{:S(2)}) collective-permute-start(bf16[128,2048]{1,0:T(8,128)(2,1)S(1)} %collective-permute-done.5.refs_0_), channel_id=1, source_target_pairs={{0,4},{1,3},{4,8},{5,1},{8,12},{9,5},{12,14},{13,9},{14,10},{15,13... | collective-permute-start | bytes 1572872 | tf_op jit(solution)/shard_map/ring_3_0/ppermute | solution.py:252
  28.6 7.7 %collective-permute-start.9 = (bf16[144,2048]{1,0:T(8,128)(2,1)S(1)}, bf16[144,2048]{1,0:T(8,128)(2,1)S(1)}, u32[]{:S(2)}, u32[]{:S(2)}) collective-permute-start(bf16[144,2048]{1,0:T(8,128)(2,1)S(1)} %collective-permute-done.4.refs_0_.refs_1_), channel_id=1, source_target_pairs={{0,1},{1,0},{4,5},{5,4},{8,9},{9,8},{12,13},{13,12},{14,15},{15,14... | collective-permute-start | bytes 1769480 | tf_op jit(solution)/shard_map/swap_2_1/ppermute | solution.py:252
  34.2 6.6 %collective-permute-start.11 = (bf16[128,2048]{1,0:T(8,128)(2,1)S(1)}, bf16[128,2048]{1,0:T(8,128)(2,1)S(1)}, u32[]{:S(2)}, u32[]{:S(2)}) collective-permute-start(bf16[128,2048]{1,0:T(8,128)(2,1)S(1)} %collective-permute-done.7.refs_0_), channel_id=1, source_target_pairs={{0,1},{1,0},{4,5},{5,4},{8,9},{9,8},{12,13},{13,12},{14,15},{15,14... | collective-permute-start | bytes 1572872 | tf_op jit(solution)/shard_map/swap_3_0/ppermute | solution.py:252
  34.2 9.2 %collective-permute-start.12 = (bf16[128,2048]{1,0:T(8,128)(2,1)S(1)}, bf16[128,2048]{1,0:T(8,128)(2,1)S(1)}, u32[]{:S(2)}, u32[]{:S(2)}) collective-permute-start(bf16[128,2048]{1,0:T(8,128)(2,1)S(1)} %collective-permute-done.7.refs_0_), channel_id=1, source_target_pairs={{0,4},{1,3},{4,8},{5,1},{8,12},{9,5},{12,14},{13,9},{14,10},{15,13... | collective-permute-start | bytes 1572872 | tf_op jit(solution)/shard_map/ring_4_0/ppermute | solution.py:252
  39.0 10.8 %collective-permute-start.10 = (bf16[144,2048]{1,0:T(8,128)(2,1)S(1)}, bf16[144,2048]{1,0:T(8,128)(2,1)S(1)}, u32[]{:S(2)}, u32[]{:S(2)}) collective-permute-start(bf16[144,2048]{1,0:T(8,128)(2,1)S(1)} %collective-permute-done.4.refs_0_.refs_1_), channel_id=1, source_target_pairs={{0,4},{1,3},{4,8},{5,1},{8,12},{9,5},{12,14},{13,9},{14,10},{15,13... | collective-permute-start | bytes 1769480 | tf_op jit(solution)/shard_map/ring_3_1/ppermute | solution.py:252
  46.8 5.4 %collective-permute-start.15 = (bf16[128,2048]{1,0:T(8,128)(2,1)S(1)}, bf16[128,2048]{1,0:T(8,128)(2,1)S(1)}, u32[]{:S(2)}, u32[]{:S(2)}) collective-permute-start(bf16[128,2048]{1,0:T(8,128)(2,1)S(1)} %get-tuple-element.71), channel_id=1, source_target_pairs={{0,1},{1,0},{4,5},{5,4},{8,9},{9,8},{12,13},{13,12},{14,15},{15,14... | collective-permute-start | bytes 1572872 | tf_op jit(solution)/shard_map/give_3_0/ppermute | solution.py:252
  50.2 9.2 %collective-permute-start.18 = (bf16[128,2048]{1,0:T(8,128)(2,1)S(1)}, bf16[128,2048]{1,0:T(8,128)(2,1)S(1)}, u32[]{:S(2)}, u32[]{:S(2)}) collective-permute-start(bf16[128,2048]{1,0:T(8,128)(2,1)S(1)} %add_convert_fusion), channel_id=1, source_target_pairs={{0,2},{1,5},{4,0},{5,9},{8,4},{9,13},{12,8},{13,15},{14,12},{15,11... | collective-permute-start | bytes 1572872 | tf_op jit(solution)/shard_map/back_4_1/ppermute | solution.py:252
  55.2 9.8 %collective-permute-start.22 = (bf16[128,2048]{1,0:T(8,128)(2,1)S(1)}, bf16[128,2048]{1,0:T(8,128)(2,1)S(1)}, u32[]{:S(2)}, u32[]{:S(2)}) collective-permute-start(bf16[128,2048]{1,0:T(8,128)(2,1)S(1)} %shard_map.57), channel_id=1, source_target_pairs={{0,2},{1,5},{4,0},{5,9},{8,4},{9,13},{12,8},{13,15},{14,12},{15,11... | collective-permute-start | bytes 1572872 | tf_op jit(solution)/shard_map/back_3_0/ppermute | solution.py:252
  56.8 8.3 %collective-permute-start.21 = (bf16[128,2048]{1,0:T(8,128)(2,1)S(1)}, bf16[128,2048]{1,0:T(8,128)(2,1)S(1)}, u32[]{:S(2)}, u32[]{:S(2)}) collective-permute-start(bf16[128,2048]{1,0:T(8,128)(2,1)S(1)} %get-tuple-element.84), channel_id=1, source_target_pairs={{0,1},{1,0},{4,5},{5,4},{8,9},{9,8},{12,13},{13,12},{14,15},{15,14... | collective-permute-start | bytes 1572872 | tf_op jit(solution)/shard_map/give_2_0/ppermute | solution.py:252
  56.8 11.1 %collective-permute-start.23 = (bf16[128,2048]{1,0:T(8,128)(2,1)S(1)}, bf16[128,2048]{1,0:T(8,128)(2,1)S(1)}, u32[]{:S(2)}, u32[]{:S(2)}) collective-permute-start(bf16[128,2048]{1,0:T(8,128)(2,1)S(1)} %get-tuple-element.87), channel_id=1, source_target_pairs={{0,1},{1,0},{4,5},{5,4},{8,9},{9,8},{12,13},{13,12},{14,15},{15,14... | collective-permute-start | bytes 1572872 | tf_op jit(solution)/shard_map/give_2_1/ppermute | solution.py:252
  60.0 10.6 %collective-permute-start.24 = (bf16[128,2048]{1,0:T(8,128)(2,1)S(1)}, bf16[128,2048]{1,0:T(8,128)(2,1)S(1)}, u32[]{:S(2)}, u32[]{:S(2)}) collective-permute-start(bf16[128,2048]{1,0:T(8,128)(2,1)S(1)} %shard_map.59), channel_id=1, source_target_pairs={{0,2},{1,5},{4,0},{5,9},{8,4},{9,13},{12,8},{13,15},{14,12},{15,11... | collective-permute-start | bytes 1572872 | tf_op jit(solution)/shard_map/back_3_1/ppermute | solution.py:252
  65.3 10.9 %collective-permute-start.26 = (bf16[128,2048]{1,0:T(8,128)(2,1)S(1)}, bf16[128,2048]{1,0:T(8,128)(2,1)S(1)}, u32[]{:S(2)}, u32[]{:S(2)}) collective-permute-start(bf16[128,2048]{1,0:T(8,128)(2,1)S(1)} %shard_map.60), channel_id=1, source_target_pairs={{0,2},{1,5},{4,0},{5,9},{8,4},{9,13},{12,8},{13,15},{14,12},{15,11... | collective-permute-start | bytes 1572872 | tf_op jit(solution)/shard_map/back_2_0/ppermute | solution.py:252
  67.3 5.6 %collective-permute-start.25 = (bf16[128,2048]{1,0:T(8,128)(2,1)S(1)}, bf16[128,2048]{1,0:T(8,128)(2,1)S(1)}, u32[]{:S(2)}, u32[]{:S(2)}) collective-permute-start(bf16[128,2048]{1,0:T(8,128)(2,1)S(1)} %get-tuple-element.90), channel_id=1, source_target_pairs={{0,1},{1,0},{4,5},{5,4},{8,9},{9,8},{12,13},{13,12},{14,15},{15,14... | collective-permute-start | bytes 1572872 | tf_op jit(solution)/shard_map/give_1_0/ppermute | solution.py:252
  67.3 11.2 %collective-permute-start.28 = (bf16[128,2048]{1,0:T(8,128)(2,1)S(1)}, bf16[128,2048]{1,0:T(8,128)(2,1)S(1)}, u32[]{:S(2)}, u32[]{:S(2)}) collective-permute-start(bf16[128,2048]{1,0:T(8,128)(2,1)S(1)} %get-tuple-element.92), channel_id=1, source_target_pairs={{0,1},{1,0},{4,5},{5,4},{8,9},{9,8},{12,13},{13,12},{14,15},{15,14... | collective-permute-start | bytes 1572872 | tf_op jit(solution)/shard_map/give_1_1/ppermute | solution.py:252
  71.0 10.9 %collective-permute-start.29 = (bf16[128,2048]{1,0:T(8,128)(2,1)S(1)}, bf16[128,2048]{1,0:T(8,128)(2,1)S(1)}, u32[]{:S(2)}, u32[]{:S(2)}) collective-permute-start(bf16[128,2048]{1,0:T(8,128)(2,1)S(1)} %shard_map.61), channel_id=1, source_target_pairs={{0,2},{1,5},{4,0},{5,9},{8,4},{9,13},{12,8},{13,15},{14,12},{15,11... | collective-permute-start | bytes 1572872 | tf_op jit(solution)/shard_map/back_2_1/ppermute | solution.py:252
  72.9 10.3 %collective-permute-start.19 = (bf16[128,2048]{1,0:T(8,128)(2,1)S(1)}, bf16[128,2048]{1,0:T(8,128)(2,1)S(1)}, u32[]{:S(2)}, u32[]{:S(2)}) collective-permute-start(bf16[128,2048]{1,0:T(8,128)(2,1)S(1)} %get-tuple-element.78), channel_id=1, source_target_pairs={{0,1},{1,0},{4,5},{5,4},{8,9},{9,8},{12,13},{13,12},{14,15},{15,14... | collective-permute-start | bytes 1572872 | tf_op jit(solution)/shard_map/give_0_0/ppermute | solution.py:252
  76.6 10.9 %collective-permute-start.27 = (bf16[128,2048]{1,0:T(8,128)(2,1)S(1)}, bf16[128,2048]{1,0:T(8,128)(2,1)S(1)}, u32[]{:S(2)}, u32[]{:S(2)}) collective-permute-start(bf16[128,2048]{1,0:T(8,128)(2,1)S(1)} %shard_map.62), channel_id=1, source_target_pairs={{0,2},{1,5},{4,0},{5,9},{8,4},{9,13},{12,8},{13,15},{14,12},{15,11... | collective-permute-start | bytes 1572872 | tf_op jit(solution)/shard_map/back_1_0/ppermute | solution.py:252
  82.2 10.4 %collective-permute-start.30 = (bf16[128,2048]{1,0:T(8,128)(2,1)S(1)}, bf16[128,2048]{1,0:T(8,128)(2,1)S(1)}, u32[]{:S(2)}, u32[]{:S(2)}) collective-permute-start(bf16[128,2048]{1,0:T(8,128)(2,1)S(1)} %shard_map.64), channel_id=1, source_target_pairs={{0,3},{1,4},{4,1},{5,8},{8,5},{9,12},{12,9},{13,14},{14,13},{15,10... | collective-permute-start | bytes 1572872 | tf_op jit(solution)/shard_map/back_1_1/ppermute | solution.py:252
  (9 other events, 29.9 us)
